TPU v7x, 128 devices: a whole 4x4x4 slice. The times are simulated.
128 devices in a mesh: grp: 8 (over z, core), ctx: 16 (over x, y).
Axes of the slice: x: 4, y: 4, z: 4, core: 2. Of those that a mesh axis runs over, the one named last changes fastest.
Arguments:
- query_rows: bfloat16 [131072, 512], P(('grp', 'ctx')), may hold values from -6 to 6
- key_rows: bfloat16 [131072, 512], P(('grp', 'ctx')), may hold values from -6 to 6
- value_rows: bfloat16 [131072, 512], P(('grp', 'ctx')), may hold values from -6 to 6
- cluster_ids: int32 [4, 131072], P(None, ('grp', 'ctx')), may hold values from 0 to 1023, as said below
Outputs:
- attended: bfloat16 [131072, 512], P(('grp', 'ctx'))
Inputs may be any that keep to these rules, and one draw needn't show every extreme that they name: `cluster_ids`: for each head, the tokens of one device whose clusters share one value of id // 8 number at most 24; for each head one such range receives exactly 24 tokens from every device, and every other range at most 8 from one device. For each head and range, the sum over its clusters of their token counts rounded up to multiples of 128 is at most 3072, with equality for the range that is full.
All inputs are finite; a program needn't handle non-finite values.
Results may differ from a plain program's by a relative error of at most 0.0034.
Values may be sent and summed in bfloat16 or wider, within the bound.
No kernel may reach another device: no remote copies, remote signals or barrier semaphores. Data moves between devices by JAX's collectives and lax.ppermute only.
A program may use at most 128 MiB of HBM per device.

v0:
```python
import math

import jax
import jax.numpy as jnp
from jax import lax
from jax.sharding import PartitionSpec as P

CL_DEV = 8
TILE = 128
WORK = 3072


NEG_FILL = -1e30


def cluster_attention(packed_rows, labels, used_rows):
    head_width = packed_rows.shape[1] // 3
    total_rows = packed_rows.shape[0]
    block_rows = math.gcd(total_rows, 512)
    score_scale = head_width ** (-0.5)
    queries = packed_rows[:, :head_width]
    keys_all = packed_rows[:, head_width : 2 * head_width]
    values_all = packed_rows[:, 2 * head_width :]
    positions = jnp.arange(total_rows, dtype=jnp.int32)
    previous = jnp.concatenate([jnp.full((1,), -2, jnp.int32), labels[:-1]])
    starts_here = (labels != previous) & (labels >= 0)
    region_start = lax.cummax(jnp.where(starts_here, positions, 0), axis=0)
    first_live = jnp.min(
        jnp.where(labels >= 0, region_start, total_rows).reshape(-1, block_rows), axis=1
    )
    block_count = (used_rows + block_rows - 1) // block_rows

    def query_block(block_index, result):
        row_start = block_index * block_rows
        query_part = lax.dynamic_slice_in_dim(queries, row_start, block_rows, 0)
        query_label = lax.dynamic_slice_in_dim(labels, row_start, block_rows, 0)
        query_pos = row_start + jnp.arange(block_rows, dtype=jnp.int32)

        def key_block(key_index, state_now):
            run_max, run_sum, weighted = state_now
            key_start = key_index * block_rows
            key_part = lax.dynamic_slice_in_dim(keys_all, key_start, block_rows, 0)
            value_part = lax.dynamic_slice_in_dim(values_all, key_start, block_rows, 0)
            key_label = lax.dynamic_slice_in_dim(labels, key_start, block_rows, 0)
            key_pos = key_start + jnp.arange(block_rows, dtype=jnp.int32)
            scores = (
                jnp.dot(query_part, key_part.T, preferred_element_type=jnp.float32) * score_scale
            )
            allowed = (
                (query_label[:, None] == key_label[None, :])
                & (key_pos[None, :] <= query_pos[:, None])
                & (query_label[:, None] >= 0)
            )
            masked = jnp.where(allowed, scores, NEG_FILL)
            new_max = jnp.maximum(run_max, jnp.max(masked, axis=1))
            weights = jnp.where(allowed, jnp.exp(masked - new_max[:, None]), 0.0)
            factor = jnp.exp(run_max - new_max)
            run_sum = run_sum * factor + jnp.sum(weights, axis=1)
            weighted = weighted * factor[:, None] + jnp.dot(
                weights.astype(jnp.bfloat16), value_part, preferred_element_type=jnp.float32
            )
            return (new_max, run_sum, weighted)

        start_state = (
            jnp.full((block_rows,), NEG_FILL, jnp.float32),
            jnp.zeros((block_rows,), jnp.float32),
            jnp.zeros((block_rows, head_width), jnp.float32),
        )
        first_block = jnp.minimum(first_live[block_index], row_start) // block_rows
        run_max, run_sum, weighted = lax.fori_loop(
            first_block, block_index + 1, key_block, start_state
        )
        output = (weighted / jnp.where(run_sum > 0.0, run_sum, 1.0)[:, None]).astype(jnp.bfloat16)
        return lax.dynamic_update_slice_in_dim(result, output, row_start, 0)

    return lax.fori_loop(
        0, block_count, query_block, jnp.zeros((total_rows, head_width), jnp.bfloat16)
    )


def serve_items(payload, labels_in):
    lead_shape = labels_in.shape[:-2]
    item_count = labels_in.shape[-2]
    capacity = labels_in.shape[-1]
    source_count = math.prod(lead_shape)
    local_ids = jnp.where(labels_in >= 0, labels_in % CL_DEV, -1)
    member = (local_ids[..., None] == jnp.arange(CL_DEV, dtype=jnp.int32)).astype(jnp.int32)
    per_source = jnp.sum(member, axis=2)
    totals = jnp.sum(per_source, axis=0)
    padded = (totals + TILE - 1) // TILE * TILE
    region = jnp.cumsum(padded, axis=1) - padded
    earlier_sources = jnp.cumsum(per_source, axis=0) - per_source
    within = jnp.cumsum(member, axis=2) - member
    offset = region[None, :, None, :] + earlier_sources[:, :, None, :] + within
    target = jnp.where(local_ids >= 0, jnp.sum(offset * member, axis=3), WORK)
    row_total = source_count * capacity
    replies = []
    for item_pos in range(item_count):
        target_rows = target[:, item_pos].reshape(-1)
        row_data = payload[:, item_pos].reshape(-1, payload.shape[-1])
        label_data = labels_in[:, item_pos].reshape(-1)
        source_of_row = (
            jnp.full((WORK,), row_total, jnp.int32)
            .at[target_rows]
            .set(jnp.arange(row_total, dtype=jnp.int32), mode="drop")
        )
        work_rows = jnp.take(row_data, source_of_row, axis=0, mode="fill", fill_value=0)
        work_labels = jnp.take(label_data, source_of_row, axis=0, mode="fill", fill_value=-1)
        used_rows = jnp.max(jnp.where(target_rows < WORK, target_rows + 1, 0))
        attended = cluster_attention(work_rows, work_labels, used_rows)
        answer_rows = jnp.take(attended, target_rows, axis=0, mode="fill", fill_value=0)
        replies.append(answer_rows.reshape(source_count, capacity, -1))
    answer = jnp.stack(replies, axis=1)
    return answer


def local(query_rows, key_rows, value_rows, cluster_ids):
    groups = lax.axis_size("grp")
    members = lax.axis_size("ctx")
    devices = groups * members
    head_count, tokens = cluster_ids.shape
    head_width = query_rows.shape[1] // head_count
    capacity = 3 * tokens // devices
    owners = cluster_ids // CL_DEV
    onehot = (owners[:, :, None] == jnp.arange(devices, dtype=jnp.int32)).astype(jnp.int32)
    slot_ids = jnp.sum((jnp.cumsum(onehot, axis=1) - onehot) * onehot, axis=2)
    packed = jnp.concatenate(
        [
            query_rows.reshape(tokens, head_count, head_width),
            key_rows.reshape(tokens, head_count, head_width),
            value_rows.reshape(tokens, head_count, head_width),
        ],
        axis=2,
    )
    packed_flat = packed.reshape(tokens * head_count, 3 * head_width)
    head_rows = jnp.broadcast_to(
        jnp.arange(head_count, dtype=jnp.int32)[None, :], (tokens, head_count)
    )
    flat_slot = ((owners.T * head_count + head_rows) * capacity + slot_ids.T).reshape(-1)
    slot_total = devices * head_count * capacity
    source_of_slot = (
        jnp.full((slot_total,), tokens * head_count, jnp.int32)
        .at[flat_slot]
        .set(jnp.arange(tokens * head_count, dtype=jnp.int32))
    )
    outgoing = jnp.take(packed_flat, source_of_slot, axis=0, mode="fill", fill_value=0).reshape(
        devices, head_count, capacity, 3 * head_width
    )
    tagged = jnp.take(
        cluster_ids.T.reshape(-1), source_of_slot, axis=0, mode="fill", fill_value=-1
    ).reshape(devices, head_count, capacity)
    answer = serve_items(
        lax.all_to_all(outgoing, ("grp", "ctx"), split_axis=0, concat_axis=0, tiled=True),
        lax.all_to_all(tagged, ("grp", "ctx"), split_axis=0, concat_axis=0, tiled=True),
    )
    back = lax.all_to_all(answer, ("grp", "ctx"), split_axis=0, concat_axis=0, tiled=True)
    back_flat = back.reshape(slot_total, head_width)
    result = jnp.take(back_flat, flat_slot, axis=0)
    return result.reshape(tokens, head_count * head_width)


def solution(mesh):
    return jax.shard_map(
        local,
        mesh=mesh,
        in_specs=(
            P(("grp", "ctx"), None),
            P(("grp", "ctx"), None),
            P(("grp", "ctx"), None),
            P(None, ("grp", "ctx")),
        ),
        out_specs=P(("grp", "ctx"), None),
        check_vma=False,
    )
```

profile of v0, /device:TPU:0, one launch (start us, length us, event | category | flops | bytes accessed | tf_op | source)
XLA Modules:
  0.0 667.6 jit_solution(10844521373816654233)
XLA Ops:
  5.8 15.5 %scatter_custom_fusion = s32[12288]{0:T(1024)S(1)} fusion(s32[4096]{0:T(1024)S(1)} %bitcast.142, s32[4096]{0:T(1024)S(1)} %iota.84, s32[]{:T(128)} %constant.512.clone.1), kind=kCustom, calls=%fused_computation.186 | custom fusion | bytes 49156 | tf_op jit(solution)/shard_map/scatter | solution.py:144
  21.9 68.0 %gather_fusion = s32[12288]{0:T(1024)S(1)} fusion(s32[4096]{0:T(1024)S(1)} %reshape.395, s32[12288]{0:T(1024)S(1)} %fusion.71), kind=kCustom, calls=%fused_computation.12 | custom fusion | bytes 147456 | tf_op jit(solution)/shard_map/jit(_take)/gather | solution.py:149
  91.7 11.1 %all-to-all-start = ((s32[128,4,24]{2,1,0:T(4,128)}), s32[128,4,24]{2,1,0:T(4,128)S(1)}, u32[]{:S(2)}, u32[]{:S(2)}) async-start(s32[128,4,24]{2,1,0:T(4,128)} %copy.105), calls=%async_computation | async-start | bytes 524288 | tf_op jit(solution)/shard_map/all_to_all | solution.py:154
  110.5 49.2 %gather_fusion.1 = bf16[12288,384]{1,0:T(8,128)(2,1)} fusion(bf16[4096,384]{1,0:T(8,128)(2,1)S(1)} %pad_maximum_fusion, s32[12288]{0:T(1024)S(1)} %fusion.71), kind=kCustom, calls=%fused_computation.13 | custom fusion | bytes 18923520 | tf_op jit(solution)/shard_map/jit(_take)/gather | solution.py:146
  159.7 9.9 %broadcast_select_fusion = bf16[128,4,24,384]{3,2,1,0:T(8,128)(2,1)} fusion(bf16[128,4,24,384]{3,2,1,0:T(8,128)(2,1)} %bitcast.134, pred[128,4,24]{2,1,0:T(4,128)(4,1)S(1)} %reduce_and.9), kind=kLoop, calls=%fused_computation.120 | loop fusion | flops 4718592 | bytes 18886656 | tf_op jit(solution)/shard_map/jit(_take)/select_n | solution.py:146
  169.6 10.2 %all-to-all-start.1 = ((bf16[128,4,24,384]{3,2,1,0:T(8,128)(2,1)}), bf16[128,4,24,384]{3,2,1,0:T(8,128)(2,1)}, u32[]{:S(2)}, u32[]{:S(2)}) async-start(bf16[128,4,24,384]{3,2,1,0:T(8,128)(2,1)} %broadcast_select_fusion), calls=%async_computation.1 | async-start | bytes 18874368 | tf_op jit(solution)/shard_map/all_to_all | solution.py:153
  186.5 12.3 %scatter_custom_fusion.2 = s32[3072]{0:T(1024)S(1)} fusion(s32[3072]{0:T(1024)S(1)} %bitcast.144, s32[3072]{0:T(1024)S(1)} %iota.87, s32[]{:T(128)} %constant.517.clone.1), kind=kCustom, calls=%fused_computation.246 | custom fusion | bytes 12292 | tf_op jit(solution)/shard_map/scatter | solution.py:105
  198.8 17.4 %gather_fusion.6 = s32[3072]{0:T(1024)S(1)} fusion(s32[3072]{0:T(1024)S(1)} %reshape_squeeze.48, s32[3072]{0:T(1024)S(1)} %fusion.91), kind=kCustom, calls=%fused_computation.6.clone | custom fusion | bytes 36864 | tf_op jit(solution)/shard_map/jit(_take)/gather | solution.py:108
  216.3 11.8 %scatter_custom_fusion.1 = s32[3072]{0:T(1024)S(1)} fusion(s32[3072]{0:T(1024)S(1)} %bitcast.145, s32[3072]{0:T(1024)S(1)} %iota.85, s32[]{:T(128)} %constant.517.clone.1), kind=kCustom, calls=%fused_computation.248 | custom fusion | bytes 12292 | tf_op jit(solution)/shard_map/scatter | solution.py:105
  228.1 17.4 %gather_fusion.3 = s32[3072]{0:T(1024)S(1)} fusion(s32[3072]{0:T(1024)S(1)} %reshape_squeeze.44, s32[3072]{0:T(1024)S(1)} %fusion.89), kind=kCustom, calls=%fused_computation.1.clone | custom fusion | bytes 36864 | tf_op jit(solution)/shard_map/jit(_take)/gather | solution.py:108
  251.7 11.8 %scatter_custom_fusion.3 = s32[3072]{0:T(1024)S(1)} fusion(s32[3072]{0:T(1024)S(1)} %bitcast.146, s32[3072]{0:T(1024)S(1)} %iota.89, s32[]{:T(128)} %constant.517.clone.1), kind=kCustom, calls=%fused_computation.244 | custom fusion | bytes 12292 | tf_op jit(solution)/shard_map/scatter | solution.py:105
  263.5 17.4 %gather_fusion.9 = s32[3072]{0:T(1024)S(1)} fusion(s32[3072]{0:T(1024)S(1)} %reshape_squeeze.52, s32[3072]{0:T(1024)S(1)} %fusion.93), kind=kCustom, calls=%fused_computation.7.clone | custom fusion | bytes 36864 | tf_op jit(solution)/shard_map/jit(_take)/gather | solution.py:108
  281.0 11.8 %scatter_custom_fusion.4 = s32[3072]{0:T(1024)S(1)} fusion(s32[3072]{0:T(1024)S(1)} %bitcast.147, s32[3072]{0:T(1024)S(1)} %iota.91, s32[]{:T(128)} %constant.517.clone.1), kind=kCustom, calls=%fused_computation.242 | custom fusion | bytes 12292 | tf_op jit(solution)/shard_map/scatter | solution.py:105
  292.8 17.4 %gather_fusion.12 = s32[3072]{0:T(1024)S(1)} fusion(s32[3072]{0:T(1024)S(1)} %reshape_squeeze.56, s32[3072]{0:T(1024)S(1)} %fusion.95), kind=kCustom, calls=%fused_computation.8.clone | custom fusion | bytes 36864 | tf_op jit(solution)/shard_map/jit(_take)/gather | solution.py:108
  321.2 6.4 fusion.112
  327.6 14.7 %gather_fusion.4 = bf16[3072,384]{1,0:T(8,128)(2,1)} fusion(bf16[3072,384]{1,0:T(8,128)(2,1)} %bitcast.132, s32[3072]{0:T(1024)S(1)} %fusion.89), kind=kCustom, calls=%fused_computation.clone | custom fusion | bytes 4730880 | tf_op jit(solution)/shard_map/jit(_take)/gather | solution.py:107
  347.0 24.6 %while.157 = (s32[]{:T(128)}, bf16[3072,128]{1,0:T(8,128)(2,1)S(1)}, s32[]{:T(128)}, s32[6]{0:T(128)}, bf16[3072,128]{1,0:T(8,128)(2,1)}, /*index=5*/s32[3072]{0...) while((s32[]{:T(128)}, bf16[3072,128]{1,0:T(8,128)(2,1)S(1)}, ...), condition=%wide.region_20.23_spmd, body=%wide.region_15.22_spmd.sunk | while | flops 139988512 | bytes 5065506 | solution.py:76
  366.9 4.3 while.164
  371.6 16.1 %gather_fusion.7 = bf16[3072,384]{1,0:T(8,128)(2,1)} fusion(bf16[3072,384]{1,0:T(8,128)(2,1)} %bitcast.131, s32[3072]{0:T(1024)} %copy-done.9), kind=kCustom, calls=%fused_computation.3.clone | custom fusion | bytes 4730880 | tf_op jit(solution)/shard_map/jit(_take)/gather | solution.py:107
  392.1 24.6 %while.159 = (s32[]{:T(128)}, bf16[3072,128]{1,0:T(8,128)(2,1)S(1)}, s32[]{:T(128)}, s32[6]{0:T(128)}, bf16[3072,128]{1,0:T(8,128)(2,1)}, /*index=5*/s32[3072]{0...) while((s32[]{:T(128)}, bf16[3072,128]{1,0:T(8,128)(2,1)S(1)}, ...), condition=%wide.region_31.35_spmd, body=%wide.region_26.34_spmd.sunk | while | flops 139988512 | bytes 5065506 | solution.py:76
  412.2 4.3 while.165
  416.7 14.0 %gather_fusion.10 = bf16[3072,384]{1,0:T(8,128)(2,1)} fusion(bf16[3072,384]{1,0:T(8,128)(2,1)S(1)} %bitcast.130, s32[3072]{0:T(1024)} %copy-done.8), kind=kCustom, calls=%fused_computation.4.clone | custom fusion | bytes 4730880 | tf_op jit(solution)/shard_map/jit(_take)/gather | solution.py:107
  436.2 24.1 %while.161 = (s32[]{:T(128)}, bf16[3072,128]{1,0:T(8,128)(2,1)}, s32[]{:T(128)}, s32[6]{0:T(128)S(1)}, bf16[3072,128]{1,0:T(8,128)(2,1)}, /*index=5*/s32[3072]{0...) while((s32[]{:T(128)}, bf16[3072,128]{1,0:T(8,128)(2,1)}, ...), condition=%wide.region_42.46_spmd, body=%wide.region_37.45_spmd.sunk | while | flops 139988512 | bytes 5065506 | solution.py:76
  460.2 14.0 %gather_fusion.13 = bf16[3072,384]{1,0:T(8,128)(2,1)} fusion(bf16[3072,384]{1,0:T(8,128)(2,1)S(1)} %bitcast.129, s32[3072]{0:T(1024)} %copy-done.7), kind=kCustom, calls=%fused_computation.5.clone | custom fusion | bytes 4730880 | tf_op jit(solution)/shard_map/jit(_take)/gather | solution.py:107
  478.8 19.7 %while.163 = (s32[]{:T(128)}, bf16[3072,128]{1,0:T(8,128)(2,1)S(1)}, s32[]{:T(128)}, s32[6]{0:T(128)S(1)}, bf16[3072,128]{1,0:T(8,128)(2,1)S(1)}, /*index=5*/s32...) while((s32[]{:T(128)}, bf16[3072,128]{1,0:T(8,128)(2,1)S(1)}, ...), condition=%wide.region_53.57_spmd, body=%wide.region_48.56_spmd.sunk | while | flops 139988512 | bytes 5065506 | solution.py:76
  498.6 10.6 %gather_fusion.5 = bf16[3072,128]{1,0:T(8,128)(2,1)S(1)} fusion(bf16[3072,128]{1,0:T(8,128)(2,1)S(1)} %copy-done.2, s32[3072]{0:T(1024)} %fusion.90), kind=kCustom, calls=%fused_computation.2.clone | custom fusion | bytes 1585152 | tf_op jit(solution)/shard_map/jit(_take)/gather | solution.py:111
  510.9 11.5 %gather_fusion.8 = bf16[3072,128]{1,0:T(8,128)(2,1)} fusion(bf16[3072,128]{1,0:T(8,128)(2,1)S(1)} %get-tuple-element.665, s32[3072]{0:T(1024)S(1)} %copy-done.14), kind=kCustom, calls=%fused_computation.9.clone | custom fusion | bytes 1585152 | tf_op jit(solution)/shard_map/jit(_take)/gather | solution.py:111
  525.1 11.5 %gather_fusion.11 = bf16[3072,128]{1,0:T(8,128)(2,1)} fusion(bf16[3072,128]{1,0:T(8,128)(2,1)S(1)} %copy-done.3, s32[3072]{0:T(1024)S(1)} %copy-done.13), kind=kCustom, calls=%fused_computation.10.clone | custom fusion | bytes 1585152 | tf_op jit(solution)/shard_map/jit(_take)/gather | solution.py:111
  539.2 11.5 %gather_fusion.14 = bf16[3072,128]{1,0:T(8,128)(2,1)} fusion(bf16[3072,128]{1,0:T(8,128)(2,1)S(1)} %get-tuple-element.667, s32[3072]{0:T(1024)S(1)} %copy-done.12), kind=kCustom, calls=%fused_computation.11.clone | custom fusion | bytes 1585152 | tf_op jit(solution)/shard_map/jit(_take)/gather | solution.py:111
  555.2 50.5 %all-to-all-start.2 = ((bf16[128,4,24,128]{3,2,1,0:T(8,128)(2,1)}), bf16[128,4,24,128]{3,2,1,0:T(8,128)(2,1)S(1)}, u32[]{:S(2)}, u32[]{:S(2)}) async-start(bf16[128,4,24,128]{3,2,1,0:T(8,128)(2,1)} %pad_maximum_fusion.1), calls=%async_computation.2 | async-start | bytes 6291456 | tf_op jit(solution)/shard_map/all_to_all | solution.py:156
  606.1 40.2 %all-to-all-done.2 = bf16[128,4,24,128]{3,2,1,0:T(8,128)(2,1)S(1)} async-done(((bf16[128,4,24,128]{3,2,1,0:T(8,128)(2,1)}), bf16[128,4,24,128]{3,2,1,0:T(8,128)(2,1)S(1)}, u32[]{:S(2)}, u32[]{:S(2)}) %all-to-all-start.2) | async-done | bytes 3145760 | tf_op jit(solution)/shard_map/all_to_all | solution.py:156
  646.2 15.0 %gather_fusion.2 = bf16[4096,128]{1,0:T(8,128)(2,1)} fusion(bf16[12288,128]{1,0:T(8,128)(2,1)S(1)} %bitcast.133, s32[4096]{0:T(1024)S(1)} %broadcast_clamp_fusion), kind=kCustom, calls=%fused_computation.14 | custom fusion | bytes 2113536 | tf_op jit(solution)/shard_map/jit(_take)/gather | solution.py:158
  (399 shorter events, 199.9 us)
Async XLA Ops:
  2.7 1.8 copy-start.6
  5.8 15.6 %copy-start.10 = (s32[4096,1]{0,1:T(1,128)}, s32[4096,1]{0,1:T(1,128)S(1)}, u32[]{:S(2)}) copy-start(s32[4096,1]{0,1:T(1,128)S(1)} %compare_select_fusion.5) | copy-start | bytes 49156
  89.9 12.9 %copy-start.4 = (bf16[1024,512]{1,0:T(8,128)(2,1)S(1)}, bf16[1024,512]{1,0:T(8,128)(2,1)}, u32[]{:S(2)}) copy-start(bf16[1024,512]{1,0:T(8,128)(2,1)} %param.26) | copy-start | bytes 3145732
  90.0 14.4 %copy-start.5 = (bf16[1024,512]{1,0:T(8,128)(2,1)S(1)}, bf16[1024,512]{1,0:T(8,128)(2,1)}, u32[]{:S(2)}) copy-start(bf16[1024,512]{1,0:T(8,128)(2,1)} %param.27) | copy-start | bytes 3145732
  91.7 77.9 %all-to-all-start = ((s32[128,4,24]{2,1,0:T(4,128)}), s32[128,4,24]{2,1,0:T(4,128)S(1)}, u32[]{:S(2)}, u32[]{:S(2)}) async-start(s32[128,4,24]{2,1,0:T(4,128)} %copy.105), calls=%async_computation | async-start | bytes 524288 | tf_op jit(solution)/shard_map/all_to_all | solution.py:154
  169.6 151.6 %all-to-all-start.1 = ((bf16[128,4,24,384]{3,2,1,0:T(8,128)(2,1)}), bf16[128,4,24,384]{3,2,1,0:T(8,128)(2,1)}, u32[]{:S(2)}, u32[]{:S(2)}) async-start(bf16[128,4,24,384]{3,2,1,0:T(8,128)(2,1)} %broadcast_select_fusion), calls=%async_computation.1 | async-start | bytes 18874368 | tf_op jit(solution)/shard_map/all_to_all | solution.py:153
  198.8 17.4 %copy-start.9 = (s32[3072]{0:T(1024)}, s32[3072]{0:T(1024)S(1)}, u32[]{:S(2)}) copy-start(s32[3072]{0:T(1024)S(1)} %fusion.91) | copy-start | bytes 36868
  263.5 17.4 %copy-start.8 = (s32[3072]{0:T(1024)}, s32[3072]{0:T(1024)S(1)}, u32[]{:S(2)}) copy-start(s32[3072]{0:T(1024)S(1)} %fusion.93) | copy-start | bytes 36868
  292.8 17.4 %copy-start.7 = (s32[3072]{0:T(1024)}, s32[3072]{0:T(1024)S(1)}, u32[]{:S(2)}) copy-start(s32[3072]{0:T(1024)S(1)} %fusion.95) | copy-start | bytes 36868
  371.5 16.1 %copy-start.1 = (bf16[3072,128]{1,0:T(8,128)(2,1)}, bf16[3072,128]{1,0:T(8,128)(2,1)S(1)}, u32[]{:S(2)}) copy-start(bf16[3072,128]{1,0:T(8,128)(2,1)S(1)} %get-tuple-element.664) | copy-start | bytes 2359300
  371.6 16.1 %copy-start.17 = (pred[3072]{0:T(1024)(128)(4,1)S(1)}, pred[3072]{0:T(1024)(128)(4,1)}, u32[]{:S(2)}) copy-start(pred[3072]{0:T(1024)(128)(4,1)} %get-tuple-element.947) | copy-start | bytes 9220
  433.6 2.5 copy-start.23
  436.2 24.1 %copy-start = (bf16[128,1,24,384]{3,2,1,0:T(8,128)(2,1)S(1)}, bf16[128,1,24,384]{3,2,1,0:T(8,128)(2,1)}, u32[]{:S(2)}) copy-start(bf16[128,1,24,384]{3,2,1,0:T(8,128)(2,1)} %get-tuple-element.969) | copy-start | bytes 7077892
  460.2 14.0 %copy-start.16 = (pred[3072]{0:T(1024)(128)(4,1)S(1)}, pred[3072]{0:T(1024)(128)(4,1)}, u32[]{:S(2)}) copy-start(pred[3072]{0:T(1024)(128)(4,1)} %get-tuple-element.951) | copy-start | bytes 9220
  477.1 1.7 copy-start.22
  478.8 19.8 %copy-start.2 = (bf16[3072,128]{1,0:T(8,128)(2,1)S(1)}, bf16[3072,128]{1,0:T(8,128)(2,1)}, u32[]{:S(2)}) copy-start(bf16[3072,128]{1,0:T(8,128)(2,1)} %copy-done.1) | copy-start | bytes 2359300
  498.6 10.7 %copy-start.21 = (pred[3072]{0:T(1024)(128)(4,1)S(1)}, pred[3072]{0:T(1024)(128)(4,1)}, u32[]{:S(2)}) copy-start(pred[3072]{0:T(1024)(128)(4,1)} %compare_and_fusion.8) | copy-start | bytes 9220
  498.6 12.3 %copy-start.14 = (s32[3072]{0:T(1024)S(1)}, s32[3072]{0:T(1024)}, u32[]{:S(2)}) copy-start(s32[3072]{0:T(1024)} %fusion.92) | copy-start | bytes 36868
  510.8 11.6 %copy-start.20 = (pred[3072]{0:T(1024)(128)(4,1)S(1)}, pred[3072]{0:T(1024)(128)(4,1)}, u32[]{:S(2)}) copy-start(pred[3072]{0:T(1024)(128)(4,1)} %compare_and_fusion.6) | copy-start | bytes 9220
  510.9 14.2 %copy-start.13 = (s32[3072]{0:T(1024)S(1)}, s32[3072]{0:T(1024)}, u32[]{:S(2)}) copy-start(s32[3072]{0:T(1024)} %fusion.94) | copy-start | bytes 36868
  522.4 2.7 copy-start.3
  525.1 11.6 %copy-start.19 = (pred[3072]{0:T(1024)(128)(4,1)S(1)}, pred[3072]{0:T(1024)(128)(4,1)}, u32[]{:S(2)}) copy-start(pred[3072]{0:T(1024)(128)(4,1)} %compare_and_fusion.4) | copy-start | bytes 9220
  525.1 14.1 %copy-start.12 = (s32[3072]{0:T(1024)S(1)}, s32[3072]{0:T(1024)}, u32[]{:S(2)}) copy-start(s32[3072]{0:T(1024)} %fusion.96) | copy-start | bytes 36868
  539.2 11.6 %copy-start.18 = (pred[3072]{0:T(1024)(128)(4,1)S(1)}, pred[3072]{0:T(1024)(128)(4,1)}, u32[]{:S(2)}) copy-start(pred[3072]{0:T(1024)(128)(4,1)} %compare_and_fusion.2) | copy-start | bytes 9220
  555.2 50.5 %copy-start.15 = (pred[1024,4]{0,1:T(4,128)(4,1)S(1)}, pred[1024,4]{0,1:T(4,128)(4,1)}, u32[]{:S(2)}) copy-start(pred[1024,4]{0,1:T(4,128)(4,1)} %get-tuple-element.942) | copy-start | bytes 12292
  555.2 50.8 %copy-start.11 = (s32[4096,1]{0,1:T(1,128)S(1)}, s32[4096,1]{0,1:T(1,128)}, u32[]{:S(2)}) copy-start(s32[4096,1]{0,1:T(1,128)} %copy-done.10) | copy-start | bytes 49156
  555.2 91.0 %all-to-all-start.2 = ((bf16[128,4,24,128]{3,2,1,0:T(8,128)(2,1)}), bf16[128,4,24,128]{3,2,1,0:T(8,128)(2,1)S(1)}, u32[]{:S(2)}, u32[]{:S(2)}) async-start(bf16[128,4,24,128]{3,2,1,0:T(8,128)(2,1)} %pad_maximum_fusion.1), calls=%async_computation.2 | async-start | bytes 6291456 | tf_op jit(solution)/shard_map/all_to_all | solution.py:156
where the time goes:
time: 681 us; the launch traced here: 668 us
  local copies, waits for them, and re-layouts  438 us (64%)
  starting transfers between devices  71.9 us (11%)
  other arithmetic  68.1 us (10%)
  waiting for transfers between devices  40.2 us (6%)
  matrix products  36.3 us (5%)
  loops' own time  9.62 us (1%)
    gather x4, local copies, waits for them, and re-layouts, serve_items(): jnp.take(label_data, source_of_row, axis=0, mode='fill', fill_value=-1)  69.6 us
    gather x3, local copies, waits for them, and re-layouts, local(): jnp.take(cluster_ids.T.reshape(-1), source_of_slot, axis=0, mode='fill',...  68.5 us
    gather x4, local copies, waits for them, and re-layouts, serve_items(): jnp.take(row_data, source_of_row, axis=0, mode='fill', fill_value=0)  58.9 us
    all_to_all x1, starting transfers between devices, local(): lax.all_to_all(answer, ('grp', 'ctx'), split_axis=0, concat_axis=0, tiled...  50.5 us
    gather x1, local copies, waits for them, and re-layouts, local(): jnp.take(packed_flat, source_of_slot, axis=0, mode='fill', fill_value=0)  49.2 us
    scatter x4, local copies, waits for them, and re-layouts, serve_items(): source_of_row = jnp.full((WORK,), row_total, jnp.int32).at[target_rows].s...  47.6 us
    gather x4, local copies, waits for them, and re-layouts, serve_items(): jnp.take(attended, target_rows, axis=0, mode='fill', fill_value=0)  45.3 us
    all_to_all x1, waiting for transfers between devices, local(): lax.all_to_all(answer, ('grp', 'ctx'), split_axis=0, concat_axis=0, tiled...  40.2 us
  transfers between devices with their start and end apart: 3, of which 1 were waited for; matrix products, arithmetic and copies ran while one was open for 31% of the time, Pallas kernels for 0%

commit v1 on v0

v1 whole, which is shorter than its diff:
```python
import functools

import jax
import jax.numpy as jnp
from jax import lax
from jax.experimental import pallas as pl
from jax.experimental.pallas import tpu as pltpu
from jax.sharding import PartitionSpec as P

CL_DEV = 8
COLD = 8
HOT = 24
HOT_PAD = 32
LANES = 128
NEG_FILL = -1e30
LOG2E = 1.4426950408889634
F32 = jnp.float32
BF16 = jnp.bfloat16
VMEM_LIMIT = 56 * 1024 * 1024


def pack_kernel(ids_ref, q_ref, k_ref, v_ref, send_ref, hot_kv_ref, hot_q_ref, cols_ref, x_ref):
    heads, tokens = ids_ref.shape
    devices = send_ref.shape[0]
    hd = q_ref.shape[1] // heads
    slots = devices * COLD
    step = 256
    ids = ids_ref[...]
    owner = ids // CL_DEV
    lid = ids - owner * CL_DEV
    upper = (
        lax.broadcasted_iota(jnp.int32, (step, step), 0)
        < lax.broadcasted_iota(jnp.int32, (step, step), 1)
    ).astype(BF16)
    dev_col = lax.broadcasted_iota(jnp.int32, (devices, step), 0)
    slot_rows = []
    for h in range(heads):
        carry = jnp.zeros((devices, 1), F32)
        ones, ranks = [], []
        for b in range(tokens // step):
            one = (owner[h : h + 1, b * step : (b + 1) * step] == dev_col).astype(F32)
            inside = jnp.dot(one.astype(BF16), upper, preferred_element_type=F32) + carry
            carry = carry + jnp.sum(one, axis=1, keepdims=True)
            ones.append(one)
            ranks.append(jnp.sum(one * inside, axis=0, keepdims=True))
        full = (carry > COLD).astype(F32)
        is_hot = jnp.concatenate(
            [jnp.sum(one * full, axis=0, keepdims=True) for one in ones], axis=1
        )
        rank = jnp.concatenate(ranks, axis=1).astype(jnp.int32)
        slot_rows.append(jnp.where(is_hot > 0.5, slots + rank, owner[h : h + 1] * COLD + rank))
    slot_all = jnp.concatenate(slot_rows, axis=0)
    pad = jnp.zeros((4, tokens), F32)
    table = jnp.concatenate(
        [(lid + 1).astype(F32), pad, slot_all.astype(F32), pad, jnp.zeros((LANES - 16, tokens), F32)],
        axis=0,
    )
    cols = jnp.transpose(table)
    cols_ref[...] = cols
    lane = lax.broadcasted_iota(jnp.int32, (tokens, LANES), 1)
    labels = jnp.zeros((slots, LANES), F32)
    hot_labels = jnp.zeros((HOT_PAD, LANES), F32)
    part = 256
    label_parts = [jnp.zeros((part, LANES), F32) for _ in range(slots // part)]
    for h in range(heads):
        x_ref[:, 0:hd] = q_ref[:, h * hd : (h + 1) * hd]
        x_ref[:, hd : 2 * hd] = k_ref[:, h * hd : (h + 1) * hd]
        x_ref[:, 2 * hd : 3 * hd] = v_ref[:, h * hd : (h + 1) * hd]
        x_ref[:, 3 * hd :] = jnp.where(lane == h, cols, 0.0).astype(BF16)
        rows = x_ref[...]
        slot_row = slot_all[h : h + 1]
        for c in range(slots // part):
            place = (
                slot_row == lax.broadcasted_iota(jnp.int32, (part, tokens), 0) + c * part
            ).astype(BF16)
            moved = jnp.dot(place, rows, preferred_element_type=F32)
            devs = slice(c * part // COLD, (c + 1) * part // COLD)
            for j in range(3):
                send_ref[devs, 3 * h + j] = (
                    moved[:, j * hd : (j + 1) * hd].reshape(part // COLD, COLD, hd).astype(BF16)
                )
            label_parts[c] = label_parts[c] + moved[:, 3 * hd :]
        place = (
            slot_row == lax.broadcasted_iota(jnp.int32, (HOT_PAD, tokens), 0) + slots
        ).astype(BF16)
        moved = jnp.dot(place, rows, preferred_element_type=F32)
        hot_q_ref[3 * h : 3 * h + 3] = moved[:HOT, :hd].reshape(3, COLD, hd).astype(BF16)
        hot_kv_ref[6 * h : 6 * h + 3] = moved[:HOT, hd : 2 * hd].reshape(3, COLD, hd).astype(BF16)
        hot_kv_ref[6 * h + 3 : 6 * h + 6] = (
            moved[:HOT, 2 * hd : 3 * hd].reshape(3, COLD, hd).astype(BF16)
        )
        hot_labels = hot_labels + moved[:, 3 * hd :]
    for c in range(slots // part):
        devs = slice(c * part // COLD, (c + 1) * part // COLD)
        send_ref[devs, 3 * heads] = (
            label_parts[c].reshape(part // COLD, COLD, LANES).astype(BF16)
        )
    hot_kv_ref[6 * heads :] = hot_labels[:HOT].reshape(3, COLD, LANES).astype(BF16)


def softmax_rows(scores, allowed, scale, values):
    masked = jnp.where(allowed, scores, NEG_FILL)
    top = jnp.max(masked, axis=1, keepdims=True)
    weights = jnp.exp2((masked - top) * scale)
    total = jnp.sum(weights, axis=1, keepdims=True)
    out = jnp.dot(weights.astype(BF16), values, preferred_element_type=F32)
    return out / total


NT = (((1,), (1,)), ((), ()))


def cold_kernel(got_ref, out_ref):
    devices, tiles, _, hd = got_ref.shape
    heads = tiles // 3
    slots = devices * COLD
    scale = hd ** (-0.5) * LOG2E
    labels = got_ref[:, 3 * heads].astype(F32).reshape(slots, hd)
    label_rows = jnp.transpose(labels)
    part = 256
    causal = lax.broadcasted_iota(jnp.int32, (part, part), 1) <= lax.broadcasted_iota(
        jnp.int32, (part, part), 0
    )
    for h in range(heads):
        q, k, v = (
            got_ref[:, 3 * h + j].astype(F32).reshape(slots, hd).astype(BF16) for j in range(3)
        )
        row = label_rows[h : h + 1]
        for c in range(slots // part):
            stop = (c + 1) * part
            col = labels[c * part : stop, h : h + 1]
            scores = lax.dot_general(
                q[c * part : stop], k[:stop], NT, preferred_element_type=F32
            )
            allowed = col == row[:, :stop]
            last = allowed[:, c * part :] & causal
            allowed = last if c == 0 else jnp.concatenate([allowed[:, : c * part], last], axis=1)
            out = softmax_rows(scores, allowed, scale, v[:stop])
            devs = slice(c * part // COLD, stop // COLD)
            out_ref[devs, h] = out.reshape(part // COLD, COLD, hd).astype(BF16)


def hot_kernel(me_ref, q_ref, own_ref, all_ref, out_ref):
    devices, tiles, _, hd = all_ref.shape
    heads = tiles // 6
    keys = devices * HOT
    scale = hd ** (-0.5) * LOG2E
    own_labels = own_ref[6 * heads :].astype(F32).reshape(HOT, hd)
    labels = all_ref[:, 6 * heads :].astype(F32).reshape(keys, hd)
    label_rows = jnp.transpose(labels)
    first = me_ref[0] * HOT
    before = lax.broadcasted_iota(jnp.int32, (HOT, keys), 1) <= first + lax.broadcasted_iota(
        jnp.int32, (HOT, keys), 0
    )
    for h in range(heads):
        q = q_ref[3 * h : 3 * h + 3].astype(F32).reshape(HOT, hd).astype(BF16)
        k = all_ref[:, 6 * h : 6 * h + 3].astype(F32).reshape(keys, hd).astype(BF16)
        v = all_ref[:, 6 * h + 3 : 6 * h + 6].astype(F32).reshape(keys, hd).astype(BF16)
        scores = lax.dot_general(q, k, NT, preferred_element_type=F32)
        allowed = (own_labels[:, h : h + 1] == label_rows[h : h + 1]) & before
        out = softmax_rows(scores, allowed, scale, v)
        out_ref[3 * h : 3 * h + 3] = out.reshape(3, COLD, hd)


def unpack_kernel(cols_ref, back_ref, hot_ref, out_ref):
    devices, heads, _, hd = back_ref.shape
    tokens = cols_ref.shape[0]
    slots = devices * COLD
    part = 256
    for h in range(heads):
        rows = back_ref[:, h].astype(F32).reshape(slots, hd).astype(BF16)
        hot = hot_ref[3 * h : 3 * h + 3].reshape(HOT, hd)
        hot = jnp.concatenate([hot, jnp.zeros((LANES - HOT, hd), F32)], axis=0).astype(BF16)
        for c in range(tokens // part):
            slot = cols_ref[c * part : (c + 1) * part, 8 + h : 9 + h].astype(jnp.int32)
            place = (slot == lax.broadcasted_iota(jnp.int32, (part, slots), 1)).astype(BF16)
            hot_place = (
                slot == lax.broadcasted_iota(jnp.int32, (part, LANES), 1) + slots
            ).astype(BF16)
            got = jnp.dot(place, rows, preferred_element_type=F32) + jnp.dot(
                hot_place, hot, preferred_element_type=F32
            )
            out_ref[c * part : (c + 1) * part, h * hd : (h + 1) * hd] = got.astype(BF16)


def vmem(count):
    return [pl.BlockSpec(memory_space=pltpu.VMEM)] * count


PARAMS = pltpu.CompilerParams(vmem_limit_bytes=VMEM_LIMIT)


def local(query_rows, key_rows, value_rows, cluster_ids):
    devices = lax.axis_size("grp") * lax.axis_size("ctx")
    heads, tokens = cluster_ids.shape
    hd = query_rows.shape[1] // heads
    axes = ("grp", "ctx")
    send, hot_kv, hot_q, cols = pl.pallas_call(
        pack_kernel,
        out_shape=(
            jax.ShapeDtypeStruct((devices, 3 * heads + 1, COLD, hd), BF16),
            jax.ShapeDtypeStruct((6 * heads + 3, COLD, hd), BF16),
            jax.ShapeDtypeStruct((3 * heads, COLD, hd), BF16),
            jax.ShapeDtypeStruct((tokens, LANES), F32),
        ),
        in_specs=vmem(4),
        out_specs=tuple(vmem(4)),
        scratch_shapes=[pltpu.VMEM((tokens, 3 * hd + LANES), BF16)],
        compiler_params=PARAMS,
        name="pack",
    )(cluster_ids, query_rows, key_rows, value_rows)
    hot_all = lax.all_gather(hot_kv, axes, axis=0, tiled=False)
    got = lax.all_to_all(send, axes, split_axis=0, concat_axis=0, tiled=True)
    me = lax.axis_index(axes).astype(jnp.int32).reshape(1)
    hot_out = pl.pallas_call(
        hot_kernel,
        out_shape=jax.ShapeDtypeStruct((3 * heads, COLD, hd), F32),
        in_specs=[pl.BlockSpec(memory_space=pltpu.SMEM)] + vmem(3),
        out_specs=vmem(1)[0],
        compiler_params=PARAMS,
        name="hot",
    )(me, hot_q, hot_kv, hot_all)
    answer = pl.pallas_call(
        cold_kernel,
        out_shape=jax.ShapeDtypeStruct((devices, heads, COLD, hd), BF16),
        in_specs=vmem(1),
        out_specs=vmem(1)[0],
        compiler_params=PARAMS,
        name="cold",
    )(got)
    back = lax.all_to_all(answer, axes, split_axis=0, concat_axis=0, tiled=True)
    return pl.pallas_call(
        unpack_kernel,
        out_shape=jax.ShapeDtypeStruct((tokens, heads * hd), BF16),
        in_specs=vmem(3),
        out_specs=vmem(1)[0],
        compiler_params=PARAMS,
        name="unpack",
    )(cols, back, hot_out)


def solution(mesh):
    return jax.shard_map(
        local,
        mesh=mesh,
        in_specs=(
            P(("grp", "ctx"), None),
            P(("grp", "ctx"), None),
            P(("grp", "ctx"), None),
            P(None, ("grp", "ctx")),
        ),
        out_specs=P(("grp", "ctx"), None),
        check_vma=False,
    )
```

time: 681 us -> 136 us (0.20); the launches traced: 668 us -> 134 us
  local copies, waits for them, and re-layouts: 438 us -> 0.97 us
  other arithmetic: 68.1 us -> 0 us
  starting transfers between devices: 71.9 us -> 5.29 us
  blocking collectives: 0 us -> 55 us
  matrix products: 36.3 us -> 0 us
  Pallas kernels: 0 us -> 31.5 us
  waiting for transfers between devices: 40.2 us -> 28.3 us
  between operations: 3.59 us -> 13.4 us
  loops' own time: 9.62 us -> 0 us
    gather x18 -> x0, local copies, waits for them, and re-layouts: 308 us -> none  [the longest x4 69.6 us: serve_items(): jnp.take(label_data, source_of_row, axis=0, mode='fill', fill_value=-1)]
    all_to_all x3 -> x1, starting transfers between devices: 71.9 us -> 5.29 us  [local(): back = lax.all_to_all(answer, axes, split_axis=0, concat_axis=0, tiled=True)]
    scatter x5 -> x0, local copies, waits for them, and re-layouts: 63.2 us -> none  [the longest x4 47.6 us: serve_items(): source_of_row = jnp.full((WORK,), row_total, jnp.int32).at[target_rows].s...]
    all_to_all x0 -> x1, blocking collectives: none -> 55 us  [local(): got = lax.all_to_all(send, axes, split_axis=0, concat_axis=0, tiled=True)]
    all_to_all x3 -> x1, waiting for transfers between devices: 40.2 us -> 0.01 us  [local(): back = lax.all_to_all(answer, axes, split_axis=0, concat_axis=0, tiled=True)]
    select_n x39 -> x0, other arithmetic: 38.5 us -> none  [the longest x4 11.5 us: serve_items(): jnp.take(row_data, source_of_row, axis=0, mode='fill', fill_value=0)]
    dynamic_slice x48 -> x0, local copies, waits for them, and re-layouts: 37.2 us -> none  [the longest x12 10.9 us: query_block(): first_block = jnp.minimum(first_live[block_index], row_start) // block_rows]
    dot_general x24 -> x0, matrix products: 36.3 us -> none  [the longest x12 19.9 us: key_block(): jnp.dot(weights.astype(jnp.bfloat16), value_part, preferred_element_type=...]
  transfers between devices with their start and end apart: 3 -> 2, of which waited for: 1 -> 1; matrix products, arithmetic and copies ran while one was open for 31% -> 0% of each run, Pallas kernels for 0% -> 12%
where the time goes in v1:
time: 136 us; the launch traced here: 134 us
  blocking collectives  55 us (40%)
  Pallas kernels  31.5 us (23%)
  waiting for transfers between devices  28.3 us (21%)
  between operations  13.4 us (10%)
  starting transfers between devices  5.29 us (4%)
    all_to_all x1, blocking collectives, local(): got = lax.all_to_all(send, axes, split_axis=0, concat_axis=0, tiled=True)  55 us
    all_gather x1, waiting for transfers between devices, local(): hot_all = lax.all_gather(hot_kv, axes, axis=0, tiled=False)  28.3 us
    pallas_call x1, Pallas kernels, local(): pl.pallas_call(pack_kernel, out_shape=(jax.ShapeDtypeStruct((devices, 3 *...  10.2 us
    pallas_call x1, Pallas kernels, local(): pl.pallas_call(cold_kernel, out_shape=jax.ShapeDtypeStruct((devices, head...  10.2 us
    pallas_call x1, Pallas kernels, local(): pl.pallas_call(hot_kernel, out_shape=jax.ShapeDtypeStruct((3 * heads, COL...  6.05 us
    all_to_all x1, starting transfers between devices, local(): back = lax.all_to_all(answer, axes, split_axis=0, concat_axis=0, tiled=True)  5.29 us
    pallas_call x1, Pallas kernels, local(): pl.pallas_call(unpack_kernel, out_shape=jax.ShapeDtypeStruct((tokens, hea...  5.02 us
  transfers between devices with their start and end apart: 2, of which 1 were waited for; matrix products, arithmetic and copies ran while one was open for 0% of the time, Pallas kernels for 12%

profile of v1, /device:TPU:0, one launch (start us, length us, event | category | flops | bytes accessed | tf_op | source)
XLA Modules:
  0.0 134.4 jit_solution(10694847317422992352)
XLA Ops:
  6.5 0.0 all-gather.3.cloned.1.call-start
  6.5 10.2 %pack.1 = (bf16[128,13,8,128]{3,2,1,0:T(8,128)(2,1)}, bf16[27,8,128]{2,1,0:T(8,128)(2,1)}, bf16[12,8,128]{2,1,0:T(8,128)(2,1)}, f32[1024,128]{1,0:T(8,128)}) custom-call(s32[4,1024]{1,0:T(4,128)} %ids_ref.1, bf16[1024,512]{1,0:T(8,128)(2,1)} %q_ref.1, bf16[1024,512]{1,0:T(8,128)(2,1)} %k_ref.1, bf16[1024,512]{1,0:T(8,128)(2,1)} %v_ref.1), custom_call_target="tpu_custom_call" | custom-call | tf_op jit(solution)/shard_map/pack/pallas_call | solution.py:198
  16.7 0.0 all-gather.3.cloned.1.call-update
  16.8 55.0 %all_to_all.10.got_ref = bf16[128,13,8,128]{3,2,1,0:T(8,128)(2,1)} all-to-all(bf16[128,13,8,128]{3,2,1,0:T(8,128)(2,1)} %get-tuple-element.10), channel_id=1, replica_groups=mesh['grp'=8,'ctx'=16] {'grp','ctx'}, dimensions={0} | all-to-all | bytes 6815744 | tf_op jit(solution)/shard_map/all_to_all | solution.py:213
  71.7 10.2 %cold.1 = bf16[128,4,8,128]{3,2,1,0:T(8,128)(2,1)} custom-call(bf16[128,13,8,128]{3,2,1,0:T(8,128)(2,1)} %all_to_all.10.got_ref), custom_call_target="tpu_custom_call" | custom-call | tf_op jit(solution)/shard_map/cold/pallas_call | solution.py:223
  81.9 5.3 %all-to-all-start.1 = ((bf16[128,4,8,128]{3,2,1,0:T(8,128)(2,1)}), bf16[128,4,8,128]{3,2,1,0:T(8,128)(2,1)S(1)}, u32[]{:S(2)}, u32[]{:S(2)}) async-start(bf16[128,4,8,128]{3,2,1,0:T(8,128)(2,1)} %cold.1), calls=%async_computation.1 | async-start | bytes 2097152 | tf_op jit(solution)/shard_map/all_to_all | solution.py:231
  87.2 28.3 %all-gather.3.cloned.1.call-done = bf16[3456,8,128]{2,1,0:T(8,128)(2,1)} async-done(((bf16[27,8,128]{2,1,0:T(8,128)(2,1)}), bf16[3456,8,128]{2,1,0:T(8,128)(2,1)}) %all-gather.3.cloned.1.call-update) | async-done | bytes 7077904 | tf_op jit(solution)/shard_map/all_gather | solution.py:212
  115.5 6.1 %hot.1.hot_ref = f32[12,8,128]{2,1,0:T(8,128)} custom-call(s32[1]{0:T(128)} %bitcast.me_ref, bf16[12,8,128]{2,1,0:T(8,128)(2,1)} %get-tuple-element.11.q_ref, bf16[27,8,128]{2,1,0:T(8,128)(2,1)} %get-tuple-element.12.own_ref, bf16[128,27,8,128]{3,2,1,0:T(8,128)(2,1)} %bitcast.2), custom_call_target="tpu_custom_call" | custom-call | tf_op jit(solution)/shard_map/hot/pallas_call | solution.py:215
  121.6 0.0 all-to-all-done.1.back_ref
  121.6 0.0 copy-start
  121.6 1.0 copy-done
  122.5 5.0 %unpack.1 = bf16[1024,512]{1,0:T(8,128)(2,1)} custom-call(f32[1024,128]{1,0:T(8,128)} %get-tuple-element.9.cols_ref, bf16[128,4,8,128]{3,2,1,0:T(8,128)(2,1)} %copy-done, f32[12,8,128]{2,1,0:T(8,128)} %hot.1.hot_ref), custom_call_target="tpu_custom_call" | custom-call | tf_op jit(solution)/shard_map/unpack/pallas_call | solution.py:232
Async XLA Ops:
  6.5 109.0 %all-gather.3.cloned.1.call-start = ((), (), s32[]{:S(2)}) async-start(), calls=%async_computation.2 | async-start | bytes 7133184 | tf_op jit(solution)/shard_map/all_gather | solution.py:212
  81.9 39.7 %all-to-all-start.1 = ((bf16[128,4,8,128]{3,2,1,0:T(8,128)(2,1)}), bf16[128,4,8,128]{3,2,1,0:T(8,128)(2,1)S(1)}, u32[]{:S(2)}, u32[]{:S(2)}) async-start(bf16[128,4,8,128]{3,2,1,0:T(8,128)(2,1)} %cold.1), calls=%async_computation.1 | async-start | bytes 2097152 | tf_op jit(solution)/shard_map/all_to_all | solution.py:231
  121.6 1.0 copy-start
Sparse Core Ops, SparseCore 0:
  16.9 98.5 all-gather.2

commit v2 on v1

--- a/solution.py
+++ b/solution.py
@@ -1,5 +1,3 @@
-import functools
-
 import jax
 import jax.numpy as jnp
 from jax import lax
@@ -16,10 +14,12 @@
 LOG2E = 1.4426950408889634
 F32 = jnp.float32
 BF16 = jnp.bfloat16
-VMEM_LIMIT = 56 * 1024 * 1024
-
-
-def pack_kernel(ids_ref, q_ref, k_ref, v_ref, send_ref, hot_kv_ref, hot_q_ref, cols_ref, x_ref):
+VMEM_LIMIT = 24 * 1024 * 1024
+
+
+def pack_kernel(
+    at_ref, ids_ref, q_ref, k_ref, v_ref, send_ref, h0_ref, h1_ref, h2_ref, h3_ref, cols_ref, x_ref, hot_ref
+):
     heads, tokens = ids_ref.shape
     devices = send_ref.shape[0]
     hd = q_ref.shape[1] // heads
@@ -58,8 +58,6 @@
     cols = jnp.transpose(table)
     cols_ref[...] = cols
     lane = lax.broadcasted_iota(jnp.int32, (tokens, LANES), 1)
-    labels = jnp.zeros((slots, LANES), F32)
-    hot_labels = jnp.zeros((HOT_PAD, LANES), F32)
     part = 256
     label_parts = [jnp.zeros((part, LANES), F32) for _ in range(slots // part)]
     for h in range(heads):
@@ -84,18 +82,18 @@
             slot_row == lax.broadcasted_iota(jnp.int32, (HOT_PAD, tokens), 0) + slots
         ).astype(BF16)
         moved = jnp.dot(place, rows, preferred_element_type=F32)
-        hot_q_ref[3 * h : 3 * h + 3] = moved[:HOT, :hd].reshape(3, COLD, hd).astype(BF16)
-        hot_kv_ref[6 * h : 6 * h + 3] = moved[:HOT, hd : 2 * hd].reshape(3, COLD, hd).astype(BF16)
-        hot_kv_ref[6 * h + 3 : 6 * h + 6] = (
-            moved[:HOT, 2 * hd : 3 * hd].reshape(3, COLD, hd).astype(BF16)
-        )
-        hot_labels = hot_labels + moved[:, 3 * hd :]
+        for j in range(4):
+            block = moved[:HOT, j * hd : (j + 1) * hd]
+            if j == 3:
+                block = jnp.broadcast_to(block[:, h : h + 1], (HOT, hd))
+            hot_ref[h, 3 * j : 3 * j + 3] = block.reshape(3, COLD, hd).astype(BF16)
     for c in range(slots // part):
         devs = slice(c * part // COLD, (c + 1) * part // COLD)
         send_ref[devs, 3 * heads] = (
             label_parts[c].reshape(part // COLD, COLD, LANES).astype(BF16)
         )
-    hot_kv_ref[6 * heads :] = hot_labels[:HOT].reshape(3, COLD, LANES).astype(BF16)
+    for d, ref in enumerate((h0_ref, h1_ref, h2_ref, h3_ref)):
+        ref[...] = hot_ref[lax.rem(at_ref[0] + d, heads)]
 
 
 def softmax_rows(scores, allowed, scale, values):
@@ -140,36 +138,67 @@
             out_ref[devs, h] = out.reshape(part // COLD, COLD, hd).astype(BF16)
 
 
-def hot_kernel(me_ref, q_ref, own_ref, all_ref, out_ref):
-    devices, tiles, _, hd = all_ref.shape
-    heads = tiles // 6
-    keys = devices * HOT
+def mid_kernel(at_ref, b0_ref, b1_ref, b2_ref, b3_ref, q_ref, kv_ref, all_ref):
+    hd = q_ref.shape[-1]
+    for d, ref in enumerate((b0_ref, b1_ref, b2_ref, b3_ref)):
+        all_ref[lax.rem(at_ref[0] - d + 4, 4)] = ref[...].astype(F32)
+    rows = 4 * HOT
+    blocks = [all_ref[:, 3 * j : 3 * j + 3] for j in range(4)]
+    labels = blocks[3].reshape(rows, hd)
+    q_ref[0:12] = blocks[0].reshape(12, COLD, hd).astype(BF16)
+    q_ref[12:24] = blocks[3].reshape(12, COLD, hd).astype(BF16)
+    kv_ref[0:12] = blocks[1].reshape(12, COLD, hd).astype(BF16)
+    kv_ref[12:24] = blocks[2].reshape(12, COLD, hd).astype(BF16)
+    flat = jnp.transpose(jnp.concatenate([labels, jnp.zeros((LANES - rows, hd), F32)], axis=0))
+    kv_ref[24] = flat[:COLD].astype(BF16)
+
+
+def hot_kernel(at_ref, q_ref, near_ref, far_ref, o0_ref, o1_ref, o2_ref, o3_ref, k_ref, v_ref, o_ref):
+    hd = q_ref.shape[-1]
+    rows = 4 * HOT
     scale = hd ** (-0.5) * LOG2E
-    own_labels = own_ref[6 * heads :].astype(F32).reshape(HOT, hd)
-    labels = all_ref[:, 6 * heads :].astype(F32).reshape(keys, hd)
-    label_rows = jnp.transpose(labels)
-    first = me_ref[0] * HOT
-    before = lax.broadcasted_iota(jnp.int32, (HOT, keys), 1) <= first + lax.broadcasted_iota(
-        jnp.int32, (HOT, keys), 0
-    )
-    for h in range(heads):
-        q = q_ref[3 * h : 3 * h + 3].astype(F32).reshape(HOT, hd).astype(BF16)
-        k = all_ref[:, 6 * h : 6 * h + 3].astype(F32).reshape(keys, hd).astype(BF16)
-        v = all_ref[:, 6 * h + 3 : 6 * h + 6].astype(F32).reshape(keys, hd).astype(BF16)
-        scores = lax.dot_general(q, k, NT, preferred_element_type=F32)
-        allowed = (own_labels[:, h : h + 1] == label_rows[h : h + 1]) & before
-        out = softmax_rows(scores, allowed, scale, v)
-        out_ref[3 * h : 3 * h + 3] = out.reshape(3, COLD, hd)
-
-
-def unpack_kernel(cols_ref, back_ref, hot_ref, out_ref):
+    y, x, core, z = (at_ref[i] for i in range(4))
+    mine = (z * 2 + core) * 4 + x
+    q = q_ref[0:12].astype(F32).reshape(rows, hd).astype(BF16)
+    label_col = q_ref[12:24].astype(F32).reshape(rows, hd)[:, 0:1]
+    zeros = jnp.zeros((LANES - rows, hd), F32)
+    allowed = []
+    for dc, ref in enumerate((near_ref, far_ref)):
+        for dz in range(4):
+            for dx in range(4):
+                n = (dc * 4 + dz) * 4 + dx
+                tile = 25 * (dz * 4 + dx)
+                at = slice(n * LANES, (n + 1) * LANES)
+                for dst_ref, first in ((k_ref, 0), (v_ref, 12)):
+                    block = ref[tile + first : tile + first + 12].astype(F32).reshape(rows, hd)
+                    dst_ref[at] = jnp.concatenate([block, zeros], axis=0).astype(BF16)
+                label_row = ref[tile + 24].astype(F32)[0:1]
+                theirs = (lax.rem(z + 4 - dz, 4) * 2 + lax.rem(core + dc, 2)) * 4 + lax.rem(x + 4 - dx, 4)
+                label_row = label_row + jnp.where(theirs > mine, 64.0, 0.0)
+                here = label_col == label_row
+                if n == 0:
+                    here = here & (
+                        lax.broadcasted_iota(jnp.int32, (rows, LANES), 1)
+                        <= lax.broadcasted_iota(jnp.int32, (rows, LANES), 0)
+                    )
+                allowed.append(here)
+    scores = lax.dot_general(q, k_ref[...], NT, preferred_element_type=F32)
+    out = softmax_rows(scores, jnp.concatenate(allowed, axis=1), scale, v_ref[...])
+    o_ref[...] = out.reshape(4, 3, COLD, hd)
+    for d, ref in enumerate((o0_ref, o1_ref, o2_ref, o3_ref)):
+        ref[...] = o_ref[lax.rem(y + 4 - d, 4)].astype(BF16)
+
+
+def unpack_kernel(at_ref, cols_ref, back_ref, o0_ref, o1_ref, o2_ref, o3_ref, out_ref, hot_ref):
     devices, heads, _, hd = back_ref.shape
     tokens = cols_ref.shape[0]
     slots = devices * COLD
     part = 256
+    for d, ref in enumerate((o0_ref, o1_ref, o2_ref, o3_ref)):
+        hot_ref[d] = ref[...].astype(F32)
     for h in range(heads):
         rows = back_ref[:, h].astype(F32).reshape(slots, hd).astype(BF16)
-        hot = hot_ref[3 * h : 3 * h + 3].reshape(HOT, hd)
+        hot = hot_ref[lax.rem(h + 4 - at_ref[0], 4)].reshape(HOT, hd)
         hot = jnp.concatenate([hot, jnp.zeros((LANES - HOT, hd), F32)], axis=0).astype(BF16)
         for c in range(tokens // part):
             slot = cols_ref[c * part : (c + 1) * part, 8 + h : 9 + h].astype(jnp.int32)
@@ -187,68 +216,71 @@
     return [pl.BlockSpec(memory_space=pltpu.VMEM)] * count
 
 
+SMEM = [pl.BlockSpec(memory_space=pltpu.SMEM)]
 PARAMS = pltpu.CompilerParams(vmem_limit_bytes=VMEM_LIMIT)
+AXES = ("z", "core", "x", "y")
+
+
+def call(kernel, name, outs, scratch, scalars, *arrays):
+    return pl.pallas_call(
+        kernel,
+        out_shape=tuple(jax.ShapeDtypeStruct(*out) for out in outs),
+        in_specs=(SMEM if scalars is not None else []) + vmem(len(arrays)),
+        out_specs=tuple(vmem(len(outs))),
+        scratch_shapes=[pltpu.VMEM(*one) for one in scratch],
+        compiler_params=PARAMS,
+        name=name,
+    )(*([scalars] if scalars is not None else []), *arrays)
+
+
+def shift(block, axis, by):
+    size = lax.axis_size(axis)
+    return lax.ppermute(block, axis, [(i, (i + by) % size) for i in range(size)])
 
 
 def local(query_rows, key_rows, value_rows, cluster_ids):
-    devices = lax.axis_size("grp") * lax.axis_size("ctx")
+    devices = lax.axis_size(AXES)
     heads, tokens = cluster_ids.shape
     hd = query_rows.shape[1] // heads
-    axes = ("grp", "ctx")
-    send, hot_kv, hot_q, cols = pl.pallas_call(
+    at = jnp.stack([lax.axis_index(a).astype(jnp.int32) for a in ("y", "x", "core", "z")])
+    block = ((12, COLD, hd), BF16)
+    send, h0, h1, h2, h3, cols = call(
         pack_kernel,
-        out_shape=(
-            jax.ShapeDtypeStruct((devices, 3 * heads + 1, COLD, hd), BF16),
-            jax.ShapeDtypeStruct((6 * heads + 3, COLD, hd), BF16),
-            jax.ShapeDtypeStruct((3 * heads, COLD, hd), BF16),
-            jax.ShapeDtypeStruct((tokens, LANES), F32),
-        ),
-        in_specs=vmem(4),
-        out_specs=tuple(vmem(4)),
-        scratch_shapes=[pltpu.VMEM((tokens, 3 * hd + LANES), BF16)],
-        compiler_params=PARAMS,
-        name="pack",
-    )(cluster_ids, query_rows, key_rows, value_rows)
-    hot_all = lax.all_gather(hot_kv, axes, axis=0, tiled=False)
-    got = lax.all_to_all(send, axes, split_axis=0, concat_axis=0, tiled=True)
-    me = lax.axis_index(axes).astype(jnp.int32).reshape(1)
-    hot_out = pl.pallas_call(
-        hot_kernel,
-        out_shape=jax.ShapeDtypeStruct((3 * heads, COLD, hd), F32),
-        in_specs=[pl.BlockSpec(memory_space=pltpu.SMEM)] + vmem(3),
-        out_specs=vmem(1)[0],
-        compiler_params=PARAMS,
-        name="hot",
-    )(me, hot_q, hot_kv, hot_all)
-    answer = pl.pallas_call(
-        cold_kernel,
-        out_shape=jax.ShapeDtypeStruct((devices, heads, COLD, hd), BF16),
-        in_specs=vmem(1),
-        out_specs=vmem(1)[0],
-        compiler_params=PARAMS,
-        name="cold",
-    )(got)
-    back = lax.all_to_all(answer, axes, split_axis=0, concat_axis=0, tiled=True)
-    return pl.pallas_call(
-        unpack_kernel,
-        out_shape=jax.ShapeDtypeStruct((tokens, heads * hd), BF16),
-        in_specs=vmem(3),
-        out_specs=vmem(1)[0],
-        compiler_params=PARAMS,
-        name="unpack",
-    )(cols, back, hot_out)
+        "pack",
+        [((devices, 3 * heads + 1, COLD, hd), BF16)] + [block] * 4 + [((tokens, LANES), F32)],
+        [((tokens, 3 * hd + LANES), BF16), ((heads, 12, COLD, hd), BF16)],
+        at, cluster_ids, query_rows, key_rows, value_rows,
+    )
+    got = lax.all_to_all(send, AXES, split_axis=0, concat_axis=0, tiled=True)
+    near = [h0] + [shift(b, "y", d + 1) for d, b in enumerate((h1, h2, h3))]
+    hot_q, kv = call(
+        mid_kernel, "mid", [((24, COLD, hd), BF16), ((25, COLD, hd), BF16)], [((4, 12, COLD, hd), F32)],
+        at, *near,
+    )
+    for axis in ("x", "z"):
+        kv = jnp.concatenate([kv] + [shift(kv, axis, d) for d in (1, 2, 3)], axis=0)
+    far = shift(kv, "core", 1)
+    outs = call(
+        hot_kernel, "hot", [((3, COLD, hd), BF16)] * 4,
+        [((32 * LANES, hd), BF16), ((32 * LANES, hd), BF16), ((4, 3, COLD, hd), F32)],
+        at, hot_q, kv, far,
+    )
+    hot_out = [outs[0]] + [shift(b, "y", 3 - d) for d, b in enumerate(outs[1:])]
+    (answer,) = call(cold_kernel, "cold", [((devices, heads, COLD, hd), BF16)], [], None, got)
+    back = lax.all_to_all(answer, AXES, split_axis=0, concat_axis=0, tiled=True)
+    (result,) = call(
+        unpack_kernel, "unpack", [((tokens, heads * hd), BF16)], [((4, 3, COLD, hd), F32)],
+        at, cols, back, *hot_out,
+    )
+    return result
 
 
 def solution(mesh):
+    split = jax.sharding.Mesh(mesh.devices.reshape(4, 2, 4, 4), AXES)
     return jax.shard_map(
         local,
-        mesh=mesh,
-        in_specs=(
-            P(("grp", "ctx"), None),
-            P(("grp", "ctx"), None),
-            P(("grp", "ctx"), None),
-            P(None, ("grp", "ctx")),
-        ),
-        out_specs=P(("grp", "ctx"), None),
+        mesh=split,
+        in_specs=(P(AXES, None), P(AXES, None), P(AXES, None), P(None, AXES)),
+        out_specs=P(AXES, None),
         check_vma=False,
     )

time: 136 us -> 127 us (0.934)
  blocking collectives: 55 us -> 0 us
  starting transfers between devices: 5.29 us -> 45.1 us
  waiting for transfers between devices: 28.3 us -> 45.3 us
  local copies, waits for them, and re-layouts: 0.97 us -> 14.4 us
  between operations: 13.4 us -> 0.07 us
  Pallas kernels: 31.5 us -> 21.8 us
    all_to_all x1 -> x0, blocking collectives: 55 us -> none  [local(): got = lax.all_to_all(send, axes, split_axis=0, concat_axis=0, tiled=True)]
    ppermute x0 -> x13, waiting for transfers between devices: none -> 42.4 us  [shift(): lax.ppermute(block, axis, [(i, (i + by) % size) for i in range(size)])]
    all_gather x1 -> x0, waiting for transfers between devices: 28.3 us -> none  [local(): hot_all = lax.all_gather(hot_kv, axes, axis=0, tiled=False)]
    ppermute x0 -> x13, starting transfers between devices: none -> 24.2 us  [shift(): lax.ppermute(block, axis, [(i, (i + by) % size) for i in range(size)])]
    all_to_all x1 -> x2, starting transfers between devices: 5.29 us -> 20.9 us  [the longest x1 11.1 us: local(): got = lax.all_to_all(send, AXES, split_axis=0, concat_axis=0, tiled=True)]
    unnamed x2 -> x21, local copies, waits for them, and re-layouts: 0.97 us -> 12.1 us
    pallas_call x4 -> x5, Pallas kernels: 31.5 us -> 21.8 us  [call(): pl.pallas_call(kernel, out_shape=tuple((jax.ShapeDtypeStruct(*out) for ou...]
    all_to_all x1 -> x2, waiting for transfers between devices: 0.01 us -> 2.87 us  [the longest x1 2.87 us: local(): back = lax.all_to_all(answer, AXES, split_axis=0, concat_axis=0, tiled=True)]
  transfers between devices with their start and end apart: 2 -> 15, of which waited for: 1 -> 11; matrix products, arithmetic and copies ran while one was open for 0% -> 5% of each run, Pallas kernels for 12% -> 8%
where the time goes in v2:
time: 127 us
  waiting for transfers between devices  45.3 us (36%)
  starting transfers between devices  45.1 us (36%)
  Pallas kernels  21.8 us (17%)
  local copies, waits for them, and re-layouts  14.4 us (11%)
    ppermute x13, waiting for transfers between devices, shift(): lax.ppermute(block, axis, [(i, (i + by) % size) for i in range(size)])  42.4 us
    ppermute x13, starting transfers between devices, shift(): lax.ppermute(block, axis, [(i, (i + by) % size) for i in range(size)])  24.2 us
    pallas_call x5, Pallas kernels, call(): pl.pallas_call(kernel, out_shape=tuple((jax.ShapeDtypeStruct(*out) for ou...  21.8 us
    unnamed x21, local copies, waits for them, and re-layouts  12.1 us
    all_to_all x1, starting transfers between devices, local(): got = lax.all_to_all(send, AXES, split_axis=0, concat_axis=0, tiled=True)  11.1 us
    all_to_all x1, starting transfers between devices, local(): back = lax.all_to_all(answer, AXES, split_axis=0, concat_axis=0, tiled=True)  9.71 us
    all_to_all x1, waiting for transfers between devices, local(): back = lax.all_to_all(answer, AXES, split_axis=0, concat_axis=0, tiled=True)  2.87 us
  transfers between devices with their start and end apart: 15, of which 11 were waited for; matrix products, arithmetic and copies ran while one was open for 5% of the time, Pallas kernels for 8%

profile of v2, /device:TPU:0, one launch (start us, length us, event | category | flops | bytes accessed | tf_op | source)
XLA Modules:
  0.0 126.8 jit_solution(9572812328653943905)
XLA Ops:
  0.1 1.2 copy-done.2
  1.3 1.2 copy-done.3
  2.5 1.2 copy-done.4
  4.5 7.3 %pack.1 = (bf16[128,13,8,128]{3,2,1,0:T(8,128)(2,1)S(1)}, bf16[12,8,128]{2,1,0:T(8,128)(2,1)S(1)}, bf16[12,8,128]{2,1,0:T(8,128)(2,1)S(1)}, bf16[12,8,128]{2,1,0...) custom-call(s32[4]{0:T(128)S(1)} %pad_add_fusion.at_ref, s32[4,1024]{1,0:T(4,128)S(1)} %copy-done.7, ...), custom_call_target="tpu_custom_call" | custom-call | tf_op jit(solution)/shard_map/pack/pallas_call | solution.py:225
  11.8 1.7 %copy-done.1 = bf16[128,13,8,128]{3,2,1,0:T(8,128)(2,1)} copy-done((bf16[128,13,8,128]{3,2,1,0:T(8,128)(2,1)}, bf16[128,13,8,128]{3,2,1,0:T(8,128)(2,1)S(1)}, u32[]{:S(2)}) %copy-start.1) | copy-done | bytes 3407896
  13.5 0.8 copy-done.5
  14.4 11.1 %all-to-all-start = ((bf16[128,13,8,128]{3,2,1,0:T(8,128)(2,1)}), bf16[128,13,8,128]{3,2,1,0:T(8,128)(2,1)S(1)}, u32[]{:S(2)}, u32[]{:S(2)}) async-start(bf16[128,13,8,128]{3,2,1,0:T(8,128)(2,1)} %copy-done.1), calls=%async_computation | async-start | bytes 6815744 | tf_op jit(solution)/shard_map/all_to_all | solution.py:254
  25.5 1.0 collective-permute-start
  26.5 2.7 %collective-permute-start.1 = (bf16[12,8,128]{2,1,0:T(8,128)(2,1)S(1)}, bf16[12,8,128]{2,1,0:T(8,128)(2,1)S(1)}, u32[]{:S(2)}, u32[]{:S(2)}) collective-permute-start(bf16[12,8,128]{2,1,0:T(8,128)(2,1)S(1)} %get-tuple-element.21), channel_id=1, source_target_pairs={{0,2},{1,3},{2,0},{3,1},{4,6},{5,7},{6,4},{7,5},{8,10},{9,11},{10,... | collective-permute-start | bytes 73736 | tf_op jit(solution)/shard_map/ppermute | solution.py:238
  29.3 1.4 %collective-permute-start.2 = (bf16[12,8,128]{2,1,0:T(8,128)(2,1)S(1)}, bf16[12,8,128]{2,1,0:T(8,128)(2,1)S(1)}, u32[]{:S(2)}, u32[]{:S(2)}) collective-permute-start(bf16[12,8,128]{2,1,0:T(8,128)(2,1)S(1)} %get-tuple-element.22), channel_id=1, source_target_pairs={{0,3},{1,0},{2,1},{3,2},{4,7},{5,4},{6,5},{7,6},{8,11},{9,8},{10,9... | collective-permute-start | bytes 73736 | tf_op jit(solution)/shard_map/ppermute | solution.py:238
  30.7 30.4 %collective-permute-done.b1_ref = bf16[12,8,128]{2,1,0:T(8,128)(2,1)S(1)} collective-permute-done((bf16[12,8,128]{2,1,0:T(8,128)(2,1)S(1)}, bf16[12,8,128]{2,1,0:T(8,128)(2,1)S(1)}, u32[]{:S(2)}, u32[]{:S(2)}) %collective-permute-start) | collective-permute-done | bytes 24608 | tf_op jit(solution)/shard_map/ppermute | solution.py:238
  61.2 1.4 %collective-permute-done.2.b3_ref = bf16[12,8,128]{2,1,0:T(8,128)(2,1)S(1)} collective-permute-done((bf16[12,8,128]{2,1,0:T(8,128)(2,1)S(1)}, bf16[12,8,128]{2,1,0:T(8,128)(2,1)S(1)}, u32[]{:S(2)}, u32[]{:S(2)}) %collective-permute-start.2) | collective-permute-done | bytes 24608 | tf_op jit(solution)/shard_map/ppermute | solution.py:238
  63.2 4.5 %collective-permute-start.3 = (bf16[25,8,128]{2,1,0:T(8,128)(2,1)S(1)}, bf16[25,8,128]{2,1,0:T(8,128)(2,1)S(1)}, u32[]{:S(2)}, u32[]{:S(2)}) collective-permute-start(bf16[25,8,128]{2,1,0:T(8,128)(2,1)S(1)} %get-tuple-element.24), channel_id=1, source_target_pairs={{0,4},{4,8},{8,12},{12,0},{1,5},{5,9},{9,13},{13,1},{2,6},{6,10},{... | collective-permute-start | bytes 153608 | tf_op jit(solution)/shard_map/ppermute | solution.py:238
  68.4 3.0 %collective-permute-start.4 = (bf16[25,8,128]{2,1,0:T(8,128)(2,1)S(1)}, bf16[25,8,128]{2,1,0:T(8,128)(2,1)S(1)}, u32[]{:S(2)}, u32[]{:S(2)}) collective-permute-start(bf16[25,8,128]{2,1,0:T(8,128)(2,1)S(1)} %get-tuple-element.24), channel_id=1, source_target_pairs={{0,8},{4,12},{8,0},{12,4},{1,9},{5,13},{9,1},{13,5},{2,10},{6,14},... | collective-permute-start | bytes 153608 | tf_op jit(solution)/shard_map/ppermute | solution.py:238
  71.3 1.5 %collective-permute-start.5 = (bf16[25,8,128]{2,1,0:T(8,128)(2,1)S(1)}, bf16[25,8,128]{2,1,0:T(8,128)(2,1)S(1)}, u32[]{:S(2)}, u32[]{:S(2)}) collective-permute-start(bf16[25,8,128]{2,1,0:T(8,128)(2,1)S(1)} %get-tuple-element.24), channel_id=1, source_target_pairs={{0,12},{4,0},{8,4},{12,8},{1,13},{5,1},{9,5},{13,9},{2,14},{6,2},{... | collective-permute-start | bytes 153608 | tf_op jit(solution)/shard_map/ppermute | solution.py:238
  74.6 0.8 collective-permute-done.5
  76.1 1.7 %collective-permute-start.6 = (bf16[100,8,128]{2,1,0:T(8,128)(2,1)}, bf16[100,8,128]{2,1,0:T(8,128)(2,1)S(1)}, u32[]{:S(2)}, u32[]{:S(2)}) collective-permute-start(bf16[100,8,128]{2,1,0:T(8,128)(2,1)} %get-tuple-element.29), channel_id=1, source_target_pairs={{0,32},{32,64},{64,96},{96,0},{1,33},{33,65},{65,97},{97,1},{2,34}... | collective-permute-start | bytes 614408 | tf_op jit(solution)/shard_map/ppermute | solution.py:238
  77.8 3.2 %collective-permute-start.7 = (bf16[100,8,128]{2,1,0:T(8,128)(2,1)}, bf16[100,8,128]{2,1,0:T(8,128)(2,1)}, u32[]{:S(2)}, u32[]{:S(2)}) collective-permute-start(bf16[100,8,128]{2,1,0:T(8,128)(2,1)} %get-tuple-element.29), channel_id=1, source_target_pairs={{0,64},{32,96},{64,0},{96,32},{1,65},{33,97},{65,1},{97,33},{2,66}... | collective-permute-start | bytes 614408 | tf_op jit(solution)/shard_map/ppermute | solution.py:238
  81.0 1.2 collective-permute-start.8
  82.2 2.6 %collective-permute-done.6 = bf16[100,8,128]{2,1,0:T(8,128)(2,1)S(1)} collective-permute-done((bf16[100,8,128]{2,1,0:T(8,128)(2,1)}, bf16[100,8,128]{2,1,0:T(8,128)(2,1)S(1)}, u32[]{:S(2)}, u32[]{:S(2)}) %collective-permute-start.6) | collective-permute-done | bytes 204832 | tf_op jit(solution)/shard_map/ppermute | solution.py:238
  85.6 7.2 %cold.1 = bf16[128,4,8,128]{3,2,1,0:T(8,128)(2,1)S(1)} custom-call(bf16[128,13,8,128]{3,2,1,0:T(8,128)(2,1)S(1)} %all-to-all-done.got_ref), custom_call_target="tpu_custom_call" | custom-call | tf_op jit(solution)/shard_map/cold/pallas_call | solution.py:225
  92.8 1.0 copy-done
  93.8 9.7 %all-to-all-start.1 = ((bf16[128,4,8,128]{3,2,1,0:T(8,128)(2,1)}), bf16[128,4,8,128]{3,2,1,0:T(8,128)(2,1)S(1)}, u32[]{:S(2)}, u32[]{:S(2)}) async-start(bf16[128,4,8,128]{3,2,1,0:T(8,128)(2,1)} %copy-done), calls=%async_computation.1 | async-start | bytes 2097152 | tf_op jit(solution)/shard_map/all_to_all | solution.py:270
  103.5 1.6 %constant_dynamic-update-slice_fusion.5 = bf16[400,8,128]{2,1,0:T(8,128)(2,1)} fusion(bf16[400,8,128]{2,1,0:T(8,128)(2,1)} %constant_dynamic-update-slice_fusion.6, bf16[100,8,128]{2,1,0:T(8,128)(2,1)} %collective-permute-done.7), kind=kLoop, calls=%fused_computation.5 | loop fusion | bytes 409600
  105.1 1.6 %constant_dynamic-update-slice_fusion.4.near_ref = bf16[400,8,128]{2,1,0:T(8,128)(2,1)} fusion(bf16[400,8,128]{2,1,0:T(8,128)(2,1)} %constant_dynamic-update-slice_fusion.5, bf16[100,8,128]{2,1,0:T(8,128)(2,1)} %collective-permute-done.8), kind=kLoop, calls=%fused_computation.4 | loop fusion | bytes 409600 | tf_op jit(solution)/shard_map/concatenate | solution.py:261
  106.8 2.5 %collective-permute-done.9.far_ref = bf16[400,8,128]{2,1,0:T(8,128)(2,1)S(1)} collective-permute-done((bf16[400,8,128]{2,1,0:T(8,128)(2,1)}, bf16[400,8,128]{2,1,0:T(8,128)(2,1)S(1)}, u32[]{:S(2)}, u32[]{:S(2)}) %collective-permute-start.9) | collective-permute-done | bytes 819232 | tf_op jit(solution)/shard_map/ppermute | solution.py:238
  109.3 2.4 %hot.1 = (bf16[3,8,128]{2,1,0:T(8,128)(2,1)S(1)}, bf16[3,8,128]{2,1,0:T(8,128)(2,1)S(1)}, bf16[3,8,128]{2,1,0:T(8,128)(2,1)S(1)}, bf16[3,8,128]{2,1,0:T(8,128)(2,1)S(1)}) custom-call(s32[4]{0:T(128)S(1)} %pad_add_fusion.at_ref, bf16[24,8,128]{2,1,0:T(8,128)(2,1)S(1)} %get-tuple-element.23.q_ref, ...), custom_call_target="tpu_custom_call" | custom-call | tf_op jit(solution)/shard_map/hot/pallas_call | solution.py:225
  111.7 2.3 %collective-permute-start.10 = (bf16[3,8,128]{2,1,0:T(8,128)(2,1)S(1)}, bf16[3,8,128]{2,1,0:T(8,128)(2,1)S(1)}, u32[]{:S(2)}, u32[]{:S(2)}) collective-permute-start(bf16[3,8,128]{2,1,0:T(8,128)(2,1)S(1)} %get-tuple-element.26), channel_id=1, source_target_pairs={{0,3},{1,0},{2,1},{3,2},{4,7},{5,4},{6,5},{7,6},{8,11},{9,8},{10,9... | collective-permute-start | bytes 18440 | tf_op jit(solution)/shard_map/ppermute | solution.py:238
  114.8 0.9 collective-permute-start.12
  116.3 2.9 %collective-permute-done.11.o2_ref = bf16[3,8,128]{2,1,0:T(8,128)(2,1)S(1)} collective-permute-done((bf16[3,8,128]{2,1,0:T(8,128)(2,1)S(1)}, bf16[3,8,128]{2,1,0:T(8,128)(2,1)S(1)}, u32[]{:S(2)}, u32[]{:S(2)}) %collective-permute-start.11) | collective-permute-done | bytes 6176 | tf_op jit(solution)/shard_map/ppermute | solution.py:238
  119.7 2.9 %all-to-all-done.1.back_ref = bf16[128,4,8,128]{3,2,1,0:T(8,128)(2,1)S(1)} async-done(((bf16[128,4,8,128]{3,2,1,0:T(8,128)(2,1)}), bf16[128,4,8,128]{3,2,1,0:T(8,128)(2,1)S(1)}, u32[]{:S(2)}, u32[]{:S(2)}) %all-to-all-start.1) | async-done | bytes 1048608 | tf_op jit(solution)/shard_map/all_to_all | solution.py:270
  122.6 4.2 %unpack.1 = bf16[1024,512]{1,0:T(8,128)(2,1)} custom-call(s32[4]{0:T(128)S(1)} %pad_add_fusion.at_ref, f32[1024,128]{1,0:T(8,128)S(1)} %copy-done.6, bf16[128,4,8,128]{3,2,1,0:T(8,128)(2,1)S(1)} %all-to-all-done.1.back_ref, bf16[3,8,128]{2,1,0:T(8,128)(2,1)S(1)} %get-tuple-element.25.o0_ref, bf16[3,8,128]{2,1,0:T(8,128)(2,1)S(1)} %collective-permute-done.10.o1_ref, ...), custom_call_target="tpu_custom_call" | custom-call | tf_op jit(solution)/shard_map/unpack/pallas_call | solution.py:225
  (27 shorter events, 7.2 us)
Async XLA Ops:
  0.1 1.2 copy-start.2
  1.3 1.2 copy-start.3
  2.5 1.2 copy-start.4
  3.8 0.7 copy-start.7
  11.8 1.7 %copy-start.1 = (bf16[128,13,8,128]{3,2,1,0:T(8,128)(2,1)}, bf16[128,13,8,128]{3,2,1,0:T(8,128)(2,1)S(1)}, u32[]{:S(2)}) copy-start(bf16[128,13,8,128]{3,2,1,0:T(8,128)(2,1)S(1)} %get-tuple-element.18) | copy-start | bytes 10223620
  13.5 0.8 copy-start.5
  14.4 71.2 %all-to-all-start = ((bf16[128,13,8,128]{3,2,1,0:T(8,128)(2,1)}), bf16[128,13,8,128]{3,2,1,0:T(8,128)(2,1)S(1)}, u32[]{:S(2)}, u32[]{:S(2)}) async-start(bf16[128,13,8,128]{3,2,1,0:T(8,128)(2,1)} %copy-done.1), calls=%async_computation | async-start | bytes 6815744 | tf_op jit(solution)/shard_map/all_to_all | solution.py:254
  25.5 35.6 %collective-permute-start = (bf16[12,8,128]{2,1,0:T(8,128)(2,1)S(1)}, bf16[12,8,128]{2,1,0:T(8,128)(2,1)S(1)}, u32[]{:S(2)}, u32[]{:S(2)}) collective-permute-start(bf16[12,8,128]{2,1,0:T(8,128)(2,1)S(1)} %get-tuple-element.20), channel_id=1, source_target_pairs={{0,1},{1,2},{2,3},{3,0},{4,5},{5,6},{6,7},{7,4},{8,9},{9,10},{10,1... | collective-permute-start | bytes 73736 | tf_op jit(solution)/shard_map/ppermute | solution.py:238
  26.5 34.6 %collective-permute-start.1 = (bf16[12,8,128]{2,1,0:T(8,128)(2,1)S(1)}, bf16[12,8,128]{2,1,0:T(8,128)(2,1)S(1)}, u32[]{:S(2)}, u32[]{:S(2)}) collective-permute-start(bf16[12,8,128]{2,1,0:T(8,128)(2,1)S(1)} %get-tuple-element.21), channel_id=1, source_target_pairs={{0,2},{1,3},{2,0},{3,1},{4,6},{5,7},{6,4},{7,5},{8,10},{9,11},{10,... | collective-permute-start | bytes 73736 | tf_op jit(solution)/shard_map/ppermute | solution.py:238
  29.3 33.3 %collective-permute-start.2 = (bf16[12,8,128]{2,1,0:T(8,128)(2,1)S(1)}, bf16[12,8,128]{2,1,0:T(8,128)(2,1)S(1)}, u32[]{:S(2)}, u32[]{:S(2)}) collective-permute-start(bf16[12,8,128]{2,1,0:T(8,128)(2,1)S(1)} %get-tuple-element.22), channel_id=1, source_target_pairs={{0,3},{1,0},{2,1},{3,2},{4,7},{5,4},{6,5},{7,6},{8,11},{9,8},{10,9... | collective-permute-start | bytes 73736 | tf_op jit(solution)/shard_map/ppermute | solution.py:238
  63.2 9.6 %collective-permute-start.3 = (bf16[25,8,128]{2,1,0:T(8,128)(2,1)S(1)}, bf16[25,8,128]{2,1,0:T(8,128)(2,1)S(1)}, u32[]{:S(2)}, u32[]{:S(2)}) collective-permute-start(bf16[25,8,128]{2,1,0:T(8,128)(2,1)S(1)} %get-tuple-element.24), channel_id=1, source_target_pairs={{0,4},{4,8},{8,12},{12,0},{1,5},{5,9},{9,13},{13,1},{2,6},{6,10},{... | collective-permute-start | bytes 153608 | tf_op jit(solution)/shard_map/ppermute | solution.py:238
  68.4 5.6 %collective-permute-start.4 = (bf16[25,8,128]{2,1,0:T(8,128)(2,1)S(1)}, bf16[25,8,128]{2,1,0:T(8,128)(2,1)S(1)}, u32[]{:S(2)}, u32[]{:S(2)}) collective-permute-start(bf16[25,8,128]{2,1,0:T(8,128)(2,1)S(1)} %get-tuple-element.24), channel_id=1, source_target_pairs={{0,8},{4,12},{8,0},{12,4},{1,9},{5,13},{9,1},{13,5},{2,10},{6,14},... | collective-permute-start | bytes 153608 | tf_op jit(solution)/shard_map/ppermute | solution.py:238
  71.3 4.1 %collective-permute-start.5 = (bf16[25,8,128]{2,1,0:T(8,128)(2,1)S(1)}, bf16[25,8,128]{2,1,0:T(8,128)(2,1)S(1)}, u32[]{:S(2)}, u32[]{:S(2)}) collective-permute-start(bf16[25,8,128]{2,1,0:T(8,128)(2,1)S(1)} %get-tuple-element.24), channel_id=1, source_target_pairs={{0,12},{4,0},{8,4},{12,8},{1,13},{5,1},{9,5},{13,9},{2,14},{6,2},{... | collective-permute-start | bytes 153608 | tf_op jit(solution)/shard_map/ppermute | solution.py:238
  76.1 8.8 %collective-permute-start.6 = (bf16[100,8,128]{2,1,0:T(8,128)(2,1)}, bf16[100,8,128]{2,1,0:T(8,128)(2,1)S(1)}, u32[]{:S(2)}, u32[]{:S(2)}) collective-permute-start(bf16[100,8,128]{2,1,0:T(8,128)(2,1)} %get-tuple-element.29), channel_id=1, source_target_pairs={{0,32},{32,64},{64,96},{96,0},{1,33},{33,65},{65,97},{97,1},{2,34}... | collective-permute-start | bytes 614408 | tf_op jit(solution)/shard_map/ppermute | solution.py:238
  77.8 25.7 %collective-permute-start.7 = (bf16[100,8,128]{2,1,0:T(8,128)(2,1)}, bf16[100,8,128]{2,1,0:T(8,128)(2,1)}, u32[]{:S(2)}, u32[]{:S(2)}) collective-permute-start(bf16[100,8,128]{2,1,0:T(8,128)(2,1)} %get-tuple-element.29), channel_id=1, source_target_pairs={{0,64},{32,96},{64,0},{96,32},{1,65},{33,97},{65,1},{97,33},{2,66}... | collective-permute-start | bytes 614408 | tf_op jit(solution)/shard_map/ppermute | solution.py:238
  81.0 24.1 %collective-permute-start.8 = (bf16[100,8,128]{2,1,0:T(8,128)(2,1)}, bf16[100,8,128]{2,1,0:T(8,128)(2,1)}, u32[]{:S(2)}, u32[]{:S(2)}) collective-permute-start(bf16[100,8,128]{2,1,0:T(8,128)(2,1)} %get-tuple-element.29), channel_id=1, source_target_pairs={{0,96},{32,0},{64,32},{96,64},{1,97},{33,1},{65,33},{97,65},{2,98}... | collective-permute-start | bytes 614408 | tf_op jit(solution)/shard_map/ppermute | solution.py:238
  92.8 1.0 copy-start
  93.8 28.8 %copy-start.6 = (f32[1024,128]{1,0:T(8,128)S(1)}, f32[1024,128]{1,0:T(8,128)}, u32[]{:S(2)}) copy-start(f32[1024,128]{1,0:T(8,128)} %copy-done.5) | copy-start | bytes 1572868
  93.8 28.8 %all-to-all-start.1 = ((bf16[128,4,8,128]{3,2,1,0:T(8,128)(2,1)}), bf16[128,4,8,128]{3,2,1,0:T(8,128)(2,1)S(1)}, u32[]{:S(2)}, u32[]{:S(2)}) async-start(bf16[128,4,8,128]{3,2,1,0:T(8,128)(2,1)} %copy-done), calls=%async_computation.1 | async-start | bytes 2097152 | tf_op jit(solution)/shard_map/all_to_all | solution.py:270
  106.8 2.5 %collective-permute-start.9 = (bf16[400,8,128]{2,1,0:T(8,128)(2,1)}, bf16[400,8,128]{2,1,0:T(8,128)(2,1)S(1)}, u32[]{:S(2)}, u32[]{:S(2)}) collective-permute-start(bf16[400,8,128]{2,1,0:T(8,128)(2,1)} %constant_dynamic-update-slice_fusion.4.near_ref), channel_id=1, source_target_pairs={{0,16},{16,0},{1,17},{17,1},{2,18},{18,2},{3,19},{19,3},{4,20},{20... | collective-permute-start | bytes 2457608 | tf_op jit(solution)/shard_map/ppermute | solution.py:238
  111.7 4.6 %collective-permute-start.10 = (bf16[3,8,128]{2,1,0:T(8,128)(2,1)S(1)}, bf16[3,8,128]{2,1,0:T(8,128)(2,1)S(1)}, u32[]{:S(2)}, u32[]{:S(2)}) collective-permute-start(bf16[3,8,128]{2,1,0:T(8,128)(2,1)S(1)} %get-tuple-element.26), channel_id=1, source_target_pairs={{0,3},{1,0},{2,1},{3,2},{4,7},{5,4},{6,5},{7,6},{8,11},{9,8},{10,9... | collective-permute-start | bytes 18440 | tf_op jit(solution)/shard_map/ppermute | solution.py:238
  114.0 5.2 %collective-permute-start.11 = (bf16[3,8,128]{2,1,0:T(8,128)(2,1)S(1)}, bf16[3,8,128]{2,1,0:T(8,128)(2,1)S(1)}, u32[]{:S(2)}, u32[]{:S(2)}) collective-permute-start(bf16[3,8,128]{2,1,0:T(8,128)(2,1)S(1)} %get-tuple-element.27), channel_id=1, source_target_pairs={{0,2},{1,3},{2,0},{3,1},{4,6},{5,7},{6,4},{7,5},{8,10},{9,11},{10,... | collective-permute-start | bytes 18440 | tf_op jit(solution)/shard_map/ppermute | solution.py:238
  114.8 4.8 %collective-permute-start.12 = (bf16[3,8,128]{2,1,0:T(8,128)(2,1)S(1)}, bf16[3,8,128]{2,1,0:T(8,128)(2,1)S(1)}, u32[]{:S(2)}, u32[]{:S(2)}) collective-permute-start(bf16[3,8,128]{2,1,0:T(8,128)(2,1)S(1)} %get-tuple-element.28), channel_id=1, source_target_pairs={{0,1},{1,2},{2,3},{3,0},{4,5},{5,6},{6,7},{7,4},{8,9},{9,10},{10,1... | collective-permute-start | bytes 18440 | tf_op jit(solution)/shard_map/ppermute | solution.py:238

commit v3 on v2

--- a/solution.py
+++ b/solution.py
@@ -14,17 +14,42 @@
 LOG2E = 1.4426950408889634
 F32 = jnp.float32
 BF16 = jnp.bfloat16
-VMEM_LIMIT = 24 * 1024 * 1024
-
-
-def pack_kernel(
-    at_ref, ids_ref, q_ref, k_ref, v_ref, send_ref, h0_ref, h1_ref, h2_ref, h3_ref, cols_ref, x_ref, hot_ref
+
+
+def load_heads(q_hbm, k_hbm, v_hbm, x_ref, sems):
+    heads = x_ref.shape[0]
+    hd = q_hbm.shape[1] // heads
+    copies = []
+    for h in range(heads):
+        copies.append([
+            pltpu.make_async_copy(
+                src.at[:, h * hd : (h + 1) * hd],
+                x_ref.at[h, :, j * hd : (j + 1) * hd],
+                sems.at[3 * h + j],
+            )
+            for j, src in enumerate((q_hbm, k_hbm, v_hbm))
+        ])
+        for one in copies[h]:
+            one.start()
+    return copies
+
+
+def columns_of(table):
+    tokens = table.shape[1]
+    return jnp.transpose(
+        jnp.concatenate([table, jnp.zeros((LANES - table.shape[0], tokens), F32)], axis=0)
+    )
+
+
+def rank_kernel(
+    at_ref, ids_ref, q_hbm, k_hbm, v_hbm, table_ref, h0_ref, h1_ref, h2_ref, h3_ref, x_ref, hot_ref, sems
 ):
     heads, tokens = ids_ref.shape
-    devices = send_ref.shape[0]
-    hd = q_ref.shape[1] // heads
+    hd = q_hbm.shape[1] // heads
+    devices = tokens // COLD
     slots = devices * COLD
     step = 256
+    copies = load_heads(q_hbm, k_hbm, v_hbm, x_ref, sems)
     ids = ids_ref[...]
     owner = ids // CL_DEV
     lid = ids - owner * CL_DEV
@@ -50,23 +75,46 @@
         rank = jnp.concatenate(ranks, axis=1).astype(jnp.int32)
         slot_rows.append(jnp.where(is_hot > 0.5, slots + rank, owner[h : h + 1] * COLD + rank))
     slot_all = jnp.concatenate(slot_rows, axis=0)
-    pad = jnp.zeros((4, tokens), F32)
-    table = jnp.concatenate(
-        [(lid + 1).astype(F32), pad, slot_all.astype(F32), pad, jnp.zeros((LANES - 16, tokens), F32)],
-        axis=0,
-    )
-    cols = jnp.transpose(table)
-    cols_ref[...] = cols
+    table = jnp.concatenate([slot_all.astype(F32), (lid + 1).astype(F32)], axis=0)
+    table_ref[...] = table
+    label_cols = columns_of(table).astype(BF16)
+    for h in range(heads):
+        place = (
+            slot_all[h : h + 1] == lax.broadcasted_iota(jnp.int32, (HOT_PAD, tokens), 0) + slots
+        ).astype(BF16)
+        tags = jnp.dot(place, label_cols, preferred_element_type=F32)
+        tags = jnp.broadcast_to(tags[:HOT, heads + h : heads + h + 1], (HOT, hd))
+        for one in copies[h]:
+            one.wait()
+        moved = jnp.dot(place, x_ref[h], preferred_element_type=F32)
+        for j in range(3):
+            hot_ref[h, 3 * j : 3 * j + 3] = (
+                moved[:HOT, j * hd : (j + 1) * hd].reshape(3, COLD, hd).astype(BF16)
+            )
+        hot_ref[h, 9:12] = tags.reshape(3, COLD, hd).astype(BF16)
+    for d, ref in enumerate((h0_ref, h1_ref, h2_ref, h3_ref)):
+        ref[...] = hot_ref[lax.rem(at_ref[0] + d, heads)]
+
+
+def pack_kernel(table_ref, q_hbm, k_hbm, v_hbm, send_hbm, x_ref, e_ref, send_ref, sems, out_sems):
+    heads = x_ref.shape[0]
+    tokens = table_ref.shape[1]
+    hd = q_hbm.shape[1] // heads
+    devices = send_ref.shape[0]
+    slots = devices * COLD
+    part = 256
+    copies = load_heads(q_hbm, k_hbm, v_hbm, x_ref, sems)
+    cols = columns_of(table_ref[...])
     lane = lax.broadcasted_iota(jnp.int32, (tokens, LANES), 1)
-    part = 256
+    for h in range(heads):
+        e_ref[h] = jnp.where(lane == heads + h, cols, 0.0).astype(BF16)
     label_parts = [jnp.zeros((part, LANES), F32) for _ in range(slots // part)]
-    for h in range(heads):
-        x_ref[:, 0:hd] = q_ref[:, h * hd : (h + 1) * hd]
-        x_ref[:, hd : 2 * hd] = k_ref[:, h * hd : (h + 1) * hd]
-        x_ref[:, 2 * hd : 3 * hd] = v_ref[:, h * hd : (h + 1) * hd]
-        x_ref[:, 3 * hd :] = jnp.where(lane == h, cols, 0.0).astype(BF16)
-        rows = x_ref[...]
-        slot_row = slot_all[h : h + 1]
+    sent = []
+    for h in range(heads):
+        slot_row = table_ref[h : h + 1].astype(jnp.int32)
+        for one in copies[h]:
+            one.wait()
+        rows = jnp.concatenate([x_ref[h], e_ref[h]], axis=1)
         for c in range(slots // part):
             place = (
                 slot_row == lax.broadcasted_iota(jnp.int32, (part, tokens), 0) + c * part
@@ -78,22 +126,18 @@
                     moved[:, j * hd : (j + 1) * hd].reshape(part // COLD, COLD, hd).astype(BF16)
                 )
             label_parts[c] = label_parts[c] + moved[:, 3 * hd :]
-        place = (
-            slot_row == lax.broadcasted_iota(jnp.int32, (HOT_PAD, tokens), 0) + slots
-        ).astype(BF16)
-        moved = jnp.dot(place, rows, preferred_element_type=F32)
-        for j in range(4):
-            block = moved[:HOT, j * hd : (j + 1) * hd]
-            if j == 3:
-                block = jnp.broadcast_to(block[:, h : h + 1], (HOT, hd))
-            hot_ref[h, 3 * j : 3 * j + 3] = block.reshape(3, COLD, hd).astype(BF16)
-    for c in range(slots // part):
-        devs = slice(c * part // COLD, (c + 1) * part // COLD)
-        send_ref[devs, 3 * heads] = (
-            label_parts[c].reshape(part // COLD, COLD, LANES).astype(BF16)
+            if h == heads - 1:
+                send_ref[devs, 3 * heads] = (
+                    label_parts[c].reshape(part // COLD, COLD, LANES).astype(BF16)
+                )
+        last = 3 * h + 3 + (h == heads - 1)
+        out = pltpu.make_async_copy(
+            send_ref.at[:, 3 * h : last], send_hbm.at[:, 3 * h : last], out_sems.at[h]
         )
-    for d, ref in enumerate((h0_ref, h1_ref, h2_ref, h3_ref)):
-        ref[...] = hot_ref[lax.rem(at_ref[0] + d, heads)]
+        out.start()
+        sent.append(out)
+    for out in sent:
+        out.wait()
 
 
 def softmax_rows(scores, allowed, scale, values):
@@ -108,25 +152,35 @@
 NT = (((1,), (1,)), ((), ()))
 
 
-def cold_kernel(got_ref, out_ref):
+def cold_kernel(got_hbm, out_hbm, got_ref, out_ref, sems, out_sems):
     devices, tiles, _, hd = got_ref.shape
     heads = tiles // 3
     slots = devices * COLD
     scale = hd ** (-0.5) * LOG2E
+    ranges = [slice(3 * heads, 3 * heads + 1)] + [slice(3 * h, 3 * h + 3) for h in range(heads)]
+    loads = [
+        pltpu.make_async_copy(got_hbm.at[:, r], got_ref.at[:, r], sems.at[i])
+        for i, r in enumerate(ranges)
+    ]
+    for load in loads:
+        load.start()
+    loads[0].wait()
     labels = got_ref[:, 3 * heads].astype(F32).reshape(slots, hd)
     label_rows = jnp.transpose(labels)
     part = 256
     causal = lax.broadcasted_iota(jnp.int32, (part, part), 1) <= lax.broadcasted_iota(
         jnp.int32, (part, part), 0
     )
-    for h in range(heads):
+    sent = []
+    for h in range(heads):
+        loads[1 + h].wait()
         q, k, v = (
             got_ref[:, 3 * h + j].astype(F32).reshape(slots, hd).astype(BF16) for j in range(3)
         )
-        row = label_rows[h : h + 1]
+        row = label_rows[heads + h : heads + h + 1]
         for c in range(slots // part):
             stop = (c + 1) * part
-            col = labels[c * part : stop, h : h + 1]
+            col = labels[c * part : stop, heads + h : heads + h + 1]
             scores = lax.dot_general(
                 q[c * part : stop], k[:stop], NT, preferred_element_type=F32
             )
@@ -136,6 +190,11 @@
             out = softmax_rows(scores, allowed, scale, v[:stop])
             devs = slice(c * part // COLD, stop // COLD)
             out_ref[devs, h] = out.reshape(part // COLD, COLD, hd).astype(BF16)
+        out = pltpu.make_async_copy(out_ref.at[:, h], out_hbm.at[:, h], out_sems.at[h])
+        out.start()
+        sent.append(out)
+    for out in sent:
+        out.wait()
 
 
 def mid_kernel(at_ref, b0_ref, b1_ref, b2_ref, b3_ref, q_ref, kv_ref, all_ref):
@@ -189,9 +248,10 @@
         ref[...] = o_ref[lax.rem(y + 4 - d, 4)].astype(BF16)
 
 
-def unpack_kernel(at_ref, cols_ref, back_ref, o0_ref, o1_ref, o2_ref, o3_ref, out_ref, hot_ref):
+def unpack_kernel(at_ref, table_ref, back_ref, o0_ref, o1_ref, o2_ref, o3_ref, out_ref, hot_ref):
     devices, heads, _, hd = back_ref.shape
-    tokens = cols_ref.shape[0]
+    tokens = table_ref.shape[1]
+    cols = columns_of(table_ref[...])
     slots = devices * COLD
     part = 256
     for d, ref in enumerate((o0_ref, o1_ref, o2_ref, o3_ref)):
@@ -201,7 +261,7 @@
         hot = hot_ref[lax.rem(h + 4 - at_ref[0], 4)].reshape(HOT, hd)
         hot = jnp.concatenate([hot, jnp.zeros((LANES - HOT, hd), F32)], axis=0).astype(BF16)
         for c in range(tokens // part):
-            slot = cols_ref[c * part : (c + 1) * part, 8 + h : 9 + h].astype(jnp.int32)
+            slot = cols[c * part : (c + 1) * part, h : h + 1].astype(jnp.int32)
             place = (slot == lax.broadcasted_iota(jnp.int32, (part, slots), 1)).astype(BF16)
             hot_place = (
                 slot == lax.broadcasted_iota(jnp.int32, (part, LANES), 1) + slots
@@ -212,25 +272,23 @@
             out_ref[c * part : (c + 1) * part, h * hd : (h + 1) * hd] = got.astype(BF16)
 
 
-def vmem(count):
-    return [pl.BlockSpec(memory_space=pltpu.VMEM)] * count
-
-
-SMEM = [pl.BlockSpec(memory_space=pltpu.SMEM)]
-PARAMS = pltpu.CompilerParams(vmem_limit_bytes=VMEM_LIMIT)
+SMEM = pl.BlockSpec(memory_space=pltpu.SMEM)
+VMEM = pl.BlockSpec(memory_space=pltpu.VMEM)
+HBM = pl.BlockSpec(memory_space=pltpu.HBM)
 AXES = ("z", "core", "x", "y")
-
-
-def call(kernel, name, outs, scratch, scalars, *arrays):
+MIB = 1024 * 1024
+
+
+def call(kernel, name, limit, ins, outs, scratch, *arrays):
     return pl.pallas_call(
         kernel,
-        out_shape=tuple(jax.ShapeDtypeStruct(*out) for out in outs),
-        in_specs=(SMEM if scalars is not None else []) + vmem(len(arrays)),
-        out_specs=tuple(vmem(len(outs))),
-        scratch_shapes=[pltpu.VMEM(*one) for one in scratch],
-        compiler_params=PARAMS,
+        out_shape=tuple(jax.ShapeDtypeStruct(*out[1:]) for out in outs),
+        in_specs=ins,
+        out_specs=tuple(out[0] for out in outs),
+        scratch_shapes=scratch,
+        compiler_params=pltpu.CompilerParams(vmem_limit_bytes=limit * MIB),
         name=name,
-    )(*([scalars] if scalars is not None else []), *arrays)
+    )(*arrays)
 
 
 def shift(block, axis, by):
@@ -243,34 +301,61 @@
     heads, tokens = cluster_ids.shape
     hd = query_rows.shape[1] // heads
     at = jnp.stack([lax.axis_index(a).astype(jnp.int32) for a in ("y", "x", "core", "z")])
-    block = ((12, COLD, hd), BF16)
-    send, h0, h1, h2, h3, cols = call(
-        pack_kernel,
-        "pack",
-        [((devices, 3 * heads + 1, COLD, hd), BF16)] + [block] * 4 + [((tokens, LANES), F32)],
-        [((tokens, 3 * hd + LANES), BF16), ((heads, 12, COLD, hd), BF16)],
+    tile = (COLD, hd)
+    x_scratch = pltpu.VMEM((heads, tokens, 3 * hd), BF16)
+    x_sems = pltpu.SemaphoreType.DMA((3 * heads,))
+    table, h0, h1, h2, h3 = call(
+        rank_kernel, "rank", 58, [SMEM, VMEM, HBM, HBM, HBM],
+        [(VMEM, (2 * heads, tokens), F32)] + [(VMEM, (12, *tile), BF16)] * 4,
+        [x_scratch, pltpu.VMEM((heads, 12, *tile), BF16), x_sems],
         at, cluster_ids, query_rows, key_rows, value_rows,
     )
+    near = [h0] + [shift(b, "y", d + 1) for d, b in enumerate((h1, h2, h3))]
+    (send,) = call(
+        pack_kernel, "pack", 58, [VMEM, HBM, HBM, HBM],
+        [(HBM, (devices, 3 * heads + 1, *tile), BF16)],
+        [
+            x_scratch, pltpu.VMEM((heads, tokens, LANES), BF16),
+            pltpu.VMEM((devices, 3 * heads + 1, *tile), BF16), x_sems,
+            pltpu.SemaphoreType.DMA((heads,)),
+        ],
+        table, query_rows, key_rows, value_rows,
+    )
+    send, near = lax.optimization_barrier((send, near))
     got = lax.all_to_all(send, AXES, split_axis=0, concat_axis=0, tiled=True)
-    near = [h0] + [shift(b, "y", d + 1) for d, b in enumerate((h1, h2, h3))]
     hot_q, kv = call(
-        mid_kernel, "mid", [((24, COLD, hd), BF16), ((25, COLD, hd), BF16)], [((4, 12, COLD, hd), F32)],
+        mid_kernel, "mid", 24, [SMEM] + [VMEM] * 4,
+        [(VMEM, (24, *tile), BF16), (VMEM, (25, *tile), BF16)],
+        [pltpu.VMEM((4, 12, *tile), F32)],
         at, *near,
     )
-    for axis in ("x", "z"):
-        kv = jnp.concatenate([kv] + [shift(kv, axis, d) for d in (1, 2, 3)], axis=0)
+    kv = jnp.concatenate([kv] + [shift(kv, "x", d) for d in (1, 2, 3)], axis=0)
+    along_z = [kv] + [shift(kv, "z", d) for d in (1, 2, 3)]
+    (answer,) = call(
+        cold_kernel, "cold", 58, [HBM], [(HBM, (devices, heads, *tile), BF16)],
+        [
+            pltpu.VMEM((devices, 3 * heads + 1, *tile), BF16), pltpu.VMEM((devices, heads, *tile), BF16),
+            pltpu.SemaphoreType.DMA((heads + 1,)), pltpu.SemaphoreType.DMA((heads,)),
+        ],
+        got,
+    )
+    along_z, _ = lax.optimization_barrier((along_z, answer))
+    kv = jnp.concatenate(along_z, axis=0)
     far = shift(kv, "core", 1)
     outs = call(
-        hot_kernel, "hot", [((3, COLD, hd), BF16)] * 4,
-        [((32 * LANES, hd), BF16), ((32 * LANES, hd), BF16), ((4, 3, COLD, hd), F32)],
+        hot_kernel, "hot", 24, [SMEM] + [VMEM] * 3, [(VMEM, (3, *tile), BF16)] * 4,
+        [
+            pltpu.VMEM((32 * LANES, hd), BF16), pltpu.VMEM((32 * LANES, hd), BF16),
+            pltpu.VMEM((4, 3, *tile), F32),
+        ],
         at, hot_q, kv, far,
     )
     hot_out = [outs[0]] + [shift(b, "y", 3 - d) for d, b in enumerate(outs[1:])]
-    (answer,) = call(cold_kernel, "cold", [((devices, heads, COLD, hd), BF16)], [], None, got)
     back = lax.all_to_all(answer, AXES, split_axis=0, concat_axis=0, tiled=True)
     (result,) = call(
-        unpack_kernel, "unpack", [((tokens, heads * hd), BF16)], [((4, 3, COLD, hd), F32)],
-        at, cols, back, *hot_out,
+        unpack_kernel, "unpack", 24, [SMEM] + [VMEM] * 6, [(VMEM, (tokens, heads * hd), BF16)],
+        [pltpu.VMEM((4, 3, *tile), F32)],
+        at, table, back, *hot_out,
     )
     return result
 

time: 127 us -> 115 us (0.906)
  local copies, waits for them, and re-layouts: 14.4 us -> 0.16 us
  starting transfers between devices: 45.1 us -> 35.4 us
  Pallas kernels: 21.8 us -> 28.4 us
  waiting for transfers between devices: 45.3 us -> 49.2 us
    unnamed x21 -> x12, local copies, waits for them, and re-layouts: 12.1 us -> 0.12 us
    pallas_call x5 -> x6, Pallas kernels: 21.8 us -> 28.4 us  [call(): pl.pallas_call(kernel, out_shape=tuple((jax.ShapeDtypeStruct(*out[1:]) fo...]
    ppermute x13, starting transfers between devices: 24.2 us -> 18.8 us  [shift(): lax.ppermute(block, axis, [(i, (i + by) % size) for i in range(size)])]
    all_to_all x1, waiting for transfers between devices: 2.87 us -> 6.21 us  [local(): back = lax.all_to_all(answer, AXES, split_axis=0, concat_axis=0, tiled=True)]
    concatenate x2, local copies, waits for them, and re-layouts: 2.3 us -> 0.04 us  [the longest x1 0.03 us: local(): kv = jnp.concatenate(along_z, axis=0)]
    all_to_all x1, starting transfers between devices: 9.71 us -> 7.58 us  [local(): back = lax.all_to_all(answer, AXES, split_axis=0, concat_axis=0, tiled=True)]
    all_to_all x1, starting transfers between devices: 11.1 us -> 9.01 us  [local(): got = lax.all_to_all(send, AXES, split_axis=0, concat_axis=0, tiled=True)]
  transfers between devices with their start and end apart: 15 -> 15, of which waited for: 11 -> 6; matrix products, arithmetic and copies ran while one was open for 5% -> 0% of each run, Pallas kernels for 8% -> 18%
where the time goes in v3:
time: 115 us; the launch traced here: 114 us
  waiting for transfers between devices  49.2 us (43%)
  starting transfers between devices  35.4 us (31%)
  Pallas kernels  28.4 us (25%)
    ppermute x13, waiting for transfers between devices, shift(): lax.ppermute(block, axis, [(i, (i + by) % size) for i in range(size)])  43 us
    pallas_call x6, Pallas kernels, call(): pl.pallas_call(kernel, out_shape=tuple((jax.ShapeDtypeStruct(*out[1:]) fo...  28.4 us
    ppermute x13, starting transfers between devices, shift(): lax.ppermute(block, axis, [(i, (i + by) % size) for i in range(size)])  18.8 us
    all_to_all x1, starting transfers between devices, local(): got = lax.all_to_all(send, AXES, split_axis=0, concat_axis=0, tiled=True)  9.01 us
    all_to_all x1, starting transfers between devices, local(): back = lax.all_to_all(answer, AXES, split_axis=0, concat_axis=0, tiled=True)  7.58 us
    all_to_all x1, waiting for transfers between devices, local(): back = lax.all_to_all(answer, AXES, split_axis=0, concat_axis=0, tiled=True)  6.21 us
  transfers between devices with their start and end apart: 15, of which 6 were waited for; matrix products, arithmetic and copies ran while one was open for 0% of the time, Pallas kernels for 18%

profile of v3, /device:TPU:0, one launch (start us, length us, event | category | flops | bytes accessed | tf_op | source)
XLA Modules:
  0.0 114.0 jit_solution(3469572430947831499)
XLA Ops:
  0.0 0.7 pad_add_fusion.at_ref
  0.7 3.9 %rank.1 = (f32[8,1024]{1,0:T(8,128)}, bf16[12,8,128]{2,1,0:T(8,128)(2,1)}, bf16[12,8,128]{2,1,0:T(8,128)(2,1)}, bf16[12,8,128]{2,1,0:T(8,128)(2,1)}, bf16[12,8,128]{2,1,0:T(8,128)(2,1)}) custom-call(s32[4]{0:T(128)} %pad_add_fusion.at_ref, s32[4,1024]{1,0:T(4,128)} %ids_ref.1, bf16[1024,512]{1,0:T(8,128)(2,1)} %q_hbm.3, bf16[1024,512]{1,0:T(8,128)(2,1)} %k_hbm.3, ...), custom_call_target="tpu_custom_call" | custom-call | tf_op jit(solution)/shard_map/rank/pallas_call | solution.py:283
  4.6 1.7 %collective-permute-start = (bf16[12,8,128]{2,1,0:T(8,128)(2,1)}, bf16[12,8,128]{2,1,0:T(8,128)(2,1)S(1)}, u32[]{:S(2)}, u32[]{:S(2)}) collective-permute-start(bf16[12,8,128]{2,1,0:T(8,128)(2,1)} %get-tuple-element.27), channel_id=1, source_target_pairs={{0,1},{1,2},{2,3},{3,0},{4,5},{5,6},{6,7},{7,4},{8,9},{9,10},{10,1... | collective-permute-start | bytes 73736 | tf_op jit(solution)/shard_map/ppermute | solution.py:296
  6.3 2.9 %collective-permute-start.1 = (bf16[12,8,128]{2,1,0:T(8,128)(2,1)}, bf16[12,8,128]{2,1,0:T(8,128)(2,1)S(1)}, u32[]{:S(2)}, u32[]{:S(2)}) collective-permute-start(bf16[12,8,128]{2,1,0:T(8,128)(2,1)} %get-tuple-element.28), channel_id=1, source_target_pairs={{0,2},{1,3},{2,0},{3,1},{4,6},{5,7},{6,4},{7,5},{8,10},{9,11},{10,... | collective-permute-start | bytes 73736 | tf_op jit(solution)/shard_map/ppermute | solution.py:296
  9.2 1.3 %collective-permute-start.2 = (bf16[12,8,128]{2,1,0:T(8,128)(2,1)}, bf16[12,8,128]{2,1,0:T(8,128)(2,1)S(1)}, u32[]{:S(2)}, u32[]{:S(2)}) collective-permute-start(bf16[12,8,128]{2,1,0:T(8,128)(2,1)} %get-tuple-element.29), channel_id=1, source_target_pairs={{0,3},{1,0},{2,1},{3,2},{4,7},{5,4},{6,5},{7,6},{8,11},{9,8},{10,9... | collective-permute-start | bytes 73736 | tf_op jit(solution)/shard_map/ppermute | solution.py:296
  10.6 8.1 %pack.1 = bf16[128,13,8,128]{3,2,1,0:T(8,128)(2,1)} custom-call(f32[8,1024]{1,0:T(8,128)} %get-tuple-element.25.table_ref, bf16[1024,512]{1,0:T(8,128)(2,1)} %q_hbm.3, bf16[1024,512]{1,0:T(8,128)(2,1)} %k_hbm.3, bf16[1024,512]{1,0:T(8,128)(2,1)} %v_hbm.3), custom_call_target="tpu_custom_call" | custom-call | tf_op jit(solution)/shard_map/pack/pallas_call | solution.py:283
  18.7 0.0 collective-permute-done.1.b2_ref
  18.7 0.0 collective-permute-done.2.b3_ref
  18.7 0.0 copy-start.1
  18.7 9.0 %all-to-all-start = ((bf16[128,13,8,128]{3,2,1,0:T(8,128)(2,1)}), bf16[128,13,8,128]{3,2,1,0:T(8,128)(2,1)}, u32[]{:S(2)}, u32[]{:S(2)}) async-start(bf16[128,13,8,128]{3,2,1,0:T(8,128)(2,1)} %pack.1), calls=%async_computation | async-start | bytes 6815744 | tf_op jit(solution)/shard_map/all_to_all | solution.py:325
  27.8 0.6 mid.1
  28.4 2.1 %collective-permute-start.5 = (bf16[25,8,128]{2,1,0:T(8,128)(2,1)S(1)}, bf16[25,8,128]{2,1,0:T(8,128)(2,1)S(1)}, u32[]{:S(2)}, u32[]{:S(2)}) collective-permute-start(bf16[25,8,128]{2,1,0:T(8,128)(2,1)S(1)} %get-tuple-element.36), channel_id=1, source_target_pairs={{0,12},{4,0},{8,4},{12,8},{1,13},{5,1},{9,5},{13,9},{2,14},{6,2},{... | collective-permute-start | bytes 153608 | tf_op jit(solution)/shard_map/ppermute | solution.py:296
  30.5 0.9 collective-permute-start.4
  31.4 0.9 collective-permute-start.3
  32.2 36.2 %collective-permute-done.3 = bf16[25,8,128]{2,1,0:T(8,128)(2,1)S(1)} collective-permute-done((bf16[25,8,128]{2,1,0:T(8,128)(2,1)S(1)}, bf16[25,8,128]{2,1,0:T(8,128)(2,1)S(1)}, u32[]{:S(2)}, u32[]{:S(2)}) %collective-permute-start.3) | collective-permute-done | bytes 51232 | tf_op jit(solution)/shard_map/ppermute | solution.py:296
  68.5 0.0 collective-permute-done.4
  68.6 3.5 %collective-permute-start.8 = (bf16[100,8,128]{2,1,0:T(8,128)(2,1)S(1)}, bf16[100,8,128]{2,1,0:T(8,128)(2,1)S(1)}, u32[]{:S(2)}, u32[]{:S(2)}) collective-permute-start(bf16[100,8,128]{2,1,0:T(8,128)(2,1)S(1)} %constant_dynamic-update-slice_fusion), channel_id=1, source_target_pairs={{0,96},{32,0},{64,32},{96,64},{1,97},{33,1},{65,33},{97,65},{2,98}... | collective-permute-start | bytes 614408 | tf_op jit(solution)/shard_map/ppermute | solution.py:296
  72.0 0.3 collective-permute-start.7
  72.3 1.1 collective-permute-start.6
  73.5 9.4 %cold.1 = bf16[128,4,8,128]{3,2,1,0:T(8,128)(2,1)} custom-call(bf16[128,13,8,128]{3,2,1,0:T(8,128)(2,1)} %all-to-all-done.got_hbm), custom_call_target="tpu_custom_call" | custom-call | tf_op jit(solution)/shard_map/cold/pallas_call | solution.py:283
  82.9 7.6 %all-to-all-start.1 = ((bf16[128,4,8,128]{3,2,1,0:T(8,128)(2,1)}), bf16[128,4,8,128]{3,2,1,0:T(8,128)(2,1)S(1)}, u32[]{:S(2)}, u32[]{:S(2)}) async-start(bf16[128,4,8,128]{3,2,1,0:T(8,128)(2,1)} %cold.1), calls=%async_computation.1 | async-start | bytes 2097152 | tf_op jit(solution)/shard_map/all_to_all | solution.py:354
  90.7 0.1 collective-permute-start.9
  90.8 2.3 %collective-permute-done.9.far_ref = bf16[400,8,128]{2,1,0:T(8,128)(2,1)S(1)} collective-permute-done((bf16[400,8,128]{2,1,0:T(8,128)(2,1)S(1)}, bf16[400,8,128]{2,1,0:T(8,128)(2,1)S(1)}, u32[]{:S(2)}, u32[]{:S(2)}) %collective-permute-start.9) | collective-permute-done | bytes 819232 | tf_op jit(solution)/shard_map/ppermute | solution.py:296
  93.1 1.9 %hot.1 = (bf16[3,8,128]{2,1,0:T(8,128)(2,1)S(1)}, bf16[3,8,128]{2,1,0:T(8,128)(2,1)S(1)}, bf16[3,8,128]{2,1,0:T(8,128)(2,1)S(1)}, bf16[3,8,128]{2,1,0:T(8,128)(2,1)S(1)}) custom-call(s32[4]{0:T(128)S(1)} %copy-done.2, bf16[24,8,128]{2,1,0:T(8,128)(2,1)S(1)} %get-tuple-element.35.q_ref, bf16[400,8,128]{2,1,0:T(8,128)(2,1)S(1)} %constant_dynamic-update-slice_fusion.4.near_ref, ...), custom_call_target="tpu_custom_call" | custom-call | tf_op jit(solution)/shard_map/hot/pallas_call | solution.py:283
  95.0 2.3 %collective-permute-start.10 = (bf16[3,8,128]{2,1,0:T(8,128)(2,1)S(1)}, bf16[3,8,128]{2,1,0:T(8,128)(2,1)S(1)}, u32[]{:S(2)}, u32[]{:S(2)}) collective-permute-start(bf16[3,8,128]{2,1,0:T(8,128)(2,1)S(1)} %get-tuple-element.42), channel_id=1, source_target_pairs={{0,3},{1,0},{2,1},{3,2},{4,7},{5,4},{6,5},{7,6},{8,11},{9,8},{10,9... | collective-permute-start | bytes 18440 | tf_op jit(solution)/shard_map/ppermute | solution.py:296
  97.2 0.8 collective-permute-start.11
  98.0 0.9 collective-permute-start.12
  98.9 0.1 collective-permute-done.10.o1_ref
  99.0 3.5 %collective-permute-done.11.o2_ref = bf16[3,8,128]{2,1,0:T(8,128)(2,1)S(1)} collective-permute-done((bf16[3,8,128]{2,1,0:T(8,128)(2,1)S(1)}, bf16[3,8,128]{2,1,0:T(8,128)(2,1)S(1)}, u32[]{:S(2)}, u32[]{:S(2)}) %collective-permute-start.11) | collective-permute-done | bytes 6176 | tf_op jit(solution)/shard_map/ppermute | solution.py:296
  102.6 0.8 collective-permute-done.12.o3_ref
  103.4 6.2 %all-to-all-done.1.back_ref = bf16[128,4,8,128]{3,2,1,0:T(8,128)(2,1)S(1)} async-done(((bf16[128,4,8,128]{3,2,1,0:T(8,128)(2,1)}), bf16[128,4,8,128]{3,2,1,0:T(8,128)(2,1)S(1)}, u32[]{:S(2)}, u32[]{:S(2)}) %all-to-all-start.1) | async-done | bytes 1048608 | tf_op jit(solution)/shard_map/all_to_all | solution.py:354
  109.6 4.5 %unpack.1 = bf16[1024,512]{1,0:T(8,128)(2,1)} custom-call(s32[4]{0:T(128)S(1)} %copy-done.2, f32[8,1024]{1,0:T(8,128)S(1)} %copy-done, bf16[128,4,8,128]{3,2,1,0:T(8,128)(2,1)S(1)} %all-to-all-done.1.back_ref, bf16[3,8,128]{2,1,0:T(8,128)(2,1)S(1)} %get-tuple-element.41.o0_ref, bf16[3,8,128]{2,1,0:T(8,128)(2,1)S(1)} %collective-permute-done.10.o1_ref, ...), custom_call_target="tpu_custom_call" | custom-call | tf_op jit(solution)/shard_map/unpack/pallas_call | solution.py:283
  (19 shorter events, 0.2 us)
Async XLA Ops:
  4.6 14.1 %collective-permute-start = (bf16[12,8,128]{2,1,0:T(8,128)(2,1)}, bf16[12,8,128]{2,1,0:T(8,128)(2,1)S(1)}, u32[]{:S(2)}, u32[]{:S(2)}) collective-permute-start(bf16[12,8,128]{2,1,0:T(8,128)(2,1)} %get-tuple-element.27), channel_id=1, source_target_pairs={{0,1},{1,2},{2,3},{3,0},{4,5},{5,6},{6,7},{7,4},{8,9},{9,10},{10,1... | collective-permute-start | bytes 73736 | tf_op jit(solution)/shard_map/ppermute | solution.py:296
  6.3 12.3 %collective-permute-start.1 = (bf16[12,8,128]{2,1,0:T(8,128)(2,1)}, bf16[12,8,128]{2,1,0:T(8,128)(2,1)S(1)}, u32[]{:S(2)}, u32[]{:S(2)}) collective-permute-start(bf16[12,8,128]{2,1,0:T(8,128)(2,1)} %get-tuple-element.28), channel_id=1, source_target_pairs={{0,2},{1,3},{2,0},{3,1},{4,6},{5,7},{6,4},{7,5},{8,10},{9,11},{10,... | collective-permute-start | bytes 73736 | tf_op jit(solution)/shard_map/ppermute | solution.py:296
  9.2 9.4 %collective-permute-start.2 = (bf16[12,8,128]{2,1,0:T(8,128)(2,1)}, bf16[12,8,128]{2,1,0:T(8,128)(2,1)S(1)}, u32[]{:S(2)}, u32[]{:S(2)}) collective-permute-start(bf16[12,8,128]{2,1,0:T(8,128)(2,1)} %get-tuple-element.29), channel_id=1, source_target_pairs={{0,3},{1,0},{2,1},{3,2},{4,7},{5,4},{6,5},{7,6},{8,11},{9,8},{10,9... | collective-permute-start | bytes 73736 | tf_op jit(solution)/shard_map/ppermute | solution.py:296
  18.7 9.0 %copy-start.1 = (bf16[12,8,128]{2,1,0:T(8,128)(2,1)S(1)}, bf16[12,8,128]{2,1,0:T(8,128)(2,1)}, u32[]{:S(2)}) copy-start(bf16[12,8,128]{2,1,0:T(8,128)(2,1)} %get-tuple-element.31.b0_ref) | copy-start | bytes 73732
  18.7 9.0 %copy-start.2 = (s32[4]{0:T(128)S(1)}, s32[4]{0:T(128)}, u32[]{:S(2)}) copy-start(s32[4]{0:T(128)} %pad_add_fusion.at_ref) | copy-start | bytes 52
  18.7 54.7 %all-to-all-start = ((bf16[128,13,8,128]{3,2,1,0:T(8,128)(2,1)}), bf16[128,13,8,128]{3,2,1,0:T(8,128)(2,1)}, u32[]{:S(2)}, u32[]{:S(2)}) async-start(bf16[128,13,8,128]{3,2,1,0:T(8,128)(2,1)} %pack.1), calls=%async_computation | async-start | bytes 6815744 | tf_op jit(solution)/shard_map/all_to_all | solution.py:325
  28.4 40.1 %collective-permute-start.5 = (bf16[25,8,128]{2,1,0:T(8,128)(2,1)S(1)}, bf16[25,8,128]{2,1,0:T(8,128)(2,1)S(1)}, u32[]{:S(2)}, u32[]{:S(2)}) collective-permute-start(bf16[25,8,128]{2,1,0:T(8,128)(2,1)S(1)} %get-tuple-element.36), channel_id=1, source_target_pairs={{0,12},{4,0},{8,4},{12,8},{1,13},{5,1},{9,5},{13,9},{2,14},{6,2},{... | collective-permute-start | bytes 153608 | tf_op jit(solution)/shard_map/ppermute | solution.py:296
  30.5 38.0 %collective-permute-start.4 = (bf16[25,8,128]{2,1,0:T(8,128)(2,1)S(1)}, bf16[25,8,128]{2,1,0:T(8,128)(2,1)S(1)}, u32[]{:S(2)}, u32[]{:S(2)}) collective-permute-start(bf16[25,8,128]{2,1,0:T(8,128)(2,1)S(1)} %get-tuple-element.36), channel_id=1, source_target_pairs={{0,8},{4,12},{8,0},{12,4},{1,9},{5,13},{9,1},{13,5},{2,10},{6,14},... | collective-permute-start | bytes 153608 | tf_op jit(solution)/shard_map/ppermute | solution.py:296
  31.4 37.1 %collective-permute-start.3 = (bf16[25,8,128]{2,1,0:T(8,128)(2,1)S(1)}, bf16[25,8,128]{2,1,0:T(8,128)(2,1)S(1)}, u32[]{:S(2)}, u32[]{:S(2)}) collective-permute-start(bf16[25,8,128]{2,1,0:T(8,128)(2,1)S(1)} %get-tuple-element.36), channel_id=1, source_target_pairs={{0,4},{4,8},{8,12},{12,0},{1,5},{5,9},{9,13},{13,1},{2,6},{6,10},{... | collective-permute-start | bytes 153608 | tf_op jit(solution)/shard_map/ppermute | solution.py:296
  68.6 22.0 %collective-permute-start.8 = (bf16[100,8,128]{2,1,0:T(8,128)(2,1)S(1)}, bf16[100,8,128]{2,1,0:T(8,128)(2,1)S(1)}, u32[]{:S(2)}, u32[]{:S(2)}) collective-permute-start(bf16[100,8,128]{2,1,0:T(8,128)(2,1)S(1)} %constant_dynamic-update-slice_fusion), channel_id=1, source_target_pairs={{0,96},{32,0},{64,32},{96,64},{1,97},{33,1},{65,33},{97,65},{2,98}... | collective-permute-start | bytes 614408 | tf_op jit(solution)/shard_map/ppermute | solution.py:296
  72.0 18.5 %collective-permute-start.7 = (bf16[100,8,128]{2,1,0:T(8,128)(2,1)S(1)}, bf16[100,8,128]{2,1,0:T(8,128)(2,1)S(1)}, u32[]{:S(2)}, u32[]{:S(2)}) collective-permute-start(bf16[100,8,128]{2,1,0:T(8,128)(2,1)S(1)} %constant_dynamic-update-slice_fusion), channel_id=1, source_target_pairs={{0,64},{32,96},{64,0},{96,32},{1,65},{33,97},{65,1},{97,33},{2,66}... | collective-permute-start | bytes 614408 | tf_op jit(solution)/shard_map/ppermute | solution.py:296
  72.3 18.2 %collective-permute-start.6 = (bf16[100,8,128]{2,1,0:T(8,128)(2,1)S(1)}, bf16[100,8,128]{2,1,0:T(8,128)(2,1)S(1)}, u32[]{:S(2)}, u32[]{:S(2)}) collective-permute-start(bf16[100,8,128]{2,1,0:T(8,128)(2,1)S(1)} %constant_dynamic-update-slice_fusion), channel_id=1, source_target_pairs={{0,32},{32,64},{64,96},{96,0},{1,33},{33,65},{65,97},{97,1},{2,34}... | collective-permute-start | bytes 614408 | tf_op jit(solution)/shard_map/ppermute | solution.py:296
  82.9 26.6 %copy-start = (f32[8,1024]{1,0:T(8,128)S(1)}, f32[8,1024]{1,0:T(8,128)}, u32[]{:S(2)}) copy-start(f32[8,1024]{1,0:T(8,128)} %get-tuple-element.25.table_ref) | copy-start | bytes 98308
  82.9 26.6 %all-to-all-start.1 = ((bf16[128,4,8,128]{3,2,1,0:T(8,128)(2,1)}), bf16[128,4,8,128]{3,2,1,0:T(8,128)(2,1)S(1)}, u32[]{:S(2)}, u32[]{:S(2)}) async-start(bf16[128,4,8,128]{3,2,1,0:T(8,128)(2,1)} %cold.1), calls=%async_computation.1 | async-start | bytes 2097152 | tf_op jit(solution)/shard_map/all_to_all | solution.py:354
  90.7 2.4 %collective-permute-start.9 = (bf16[400,8,128]{2,1,0:T(8,128)(2,1)S(1)}, bf16[400,8,128]{2,1,0:T(8,128)(2,1)S(1)}, u32[]{:S(2)}, u32[]{:S(2)}) collective-permute-start(bf16[400,8,128]{2,1,0:T(8,128)(2,1)S(1)} %constant_dynamic-update-slice_fusion.4.near_ref), channel_id=1, source_target_pairs={{0,16},{16,0},{1,17},{17,1},{2,18},{18,2},{3,19},{19,3},{4,20},{20... | collective-permute-start | bytes 2457608 | tf_op jit(solution)/shard_map/ppermute | solution.py:296
  95.0 4.1 %collective-permute-start.10 = (bf16[3,8,128]{2,1,0:T(8,128)(2,1)S(1)}, bf16[3,8,128]{2,1,0:T(8,128)(2,1)S(1)}, u32[]{:S(2)}, u32[]{:S(2)}) collective-permute-start(bf16[3,8,128]{2,1,0:T(8,128)(2,1)S(1)} %get-tuple-element.42), channel_id=1, source_target_pairs={{0,3},{1,0},{2,1},{3,2},{4,7},{5,4},{6,5},{7,6},{8,11},{9,8},{10,9... | collective-permute-start | bytes 18440 | tf_op jit(solution)/shard_map/ppermute | solution.py:296
  97.2 5.3 %collective-permute-start.11 = (bf16[3,8,128]{2,1,0:T(8,128)(2,1)S(1)}, bf16[3,8,128]{2,1,0:T(8,128)(2,1)S(1)}, u32[]{:S(2)}, u32[]{:S(2)}) collective-permute-start(bf16[3,8,128]{2,1,0:T(8,128)(2,1)S(1)} %get-tuple-element.43), channel_id=1, source_target_pairs={{0,2},{1,3},{2,0},{3,1},{4,6},{5,7},{6,4},{7,5},{8,10},{9,11},{10,... | collective-permute-start | bytes 18440 | tf_op jit(solution)/shard_map/ppermute | solution.py:296
  98.0 5.3 %collective-permute-start.12 = (bf16[3,8,128]{2,1,0:T(8,128)(2,1)S(1)}, bf16[3,8,128]{2,1,0:T(8,128)(2,1)S(1)}, u32[]{:S(2)}, u32[]{:S(2)}) collective-permute-start(bf16[3,8,128]{2,1,0:T(8,128)(2,1)S(1)} %get-tuple-element.44), channel_id=1, source_target_pairs={{0,1},{1,2},{2,3},{3,0},{4,5},{5,6},{6,7},{7,4},{8,9},{9,10},{10,1... | collective-permute-start | bytes 18440 | tf_op jit(solution)/shard_map/ppermute | solution.py:296

commit v4 on v3

--- a/solution.py
+++ b/solution.py
@@ -11,6 +11,8 @@
 HOT_PAD = 32
 LANES = 128
 NEG_FILL = -1e30
+TAGS = 16
+MARK = 128.0
 LOG2E = 1.4426950408889634
 F32 = jnp.float32
 BF16 = jnp.bfloat16
@@ -42,7 +44,7 @@
 
 
 def rank_kernel(
-    at_ref, ids_ref, q_hbm, k_hbm, v_hbm, table_ref, h0_ref, h1_ref, h2_ref, h3_ref, x_ref, hot_ref, sems
+    ids_ref, q_hbm, k_hbm, v_hbm, table_ref, h0_ref, h1_ref, h2_ref, h3_ref, x_ref, hot_ref, sems
 ):
     heads, tokens = ids_ref.shape
     hd = q_hbm.shape[1] // heads
@@ -92,8 +94,9 @@
                 moved[:HOT, j * hd : (j + 1) * hd].reshape(3, COLD, hd).astype(BF16)
             )
         hot_ref[h, 9:12] = tags.reshape(3, COLD, hd).astype(BF16)
+    y = lax.axis_index("y")
     for d, ref in enumerate((h0_ref, h1_ref, h2_ref, h3_ref)):
-        ref[...] = hot_ref[lax.rem(at_ref[0] + d, heads)]
+        ref[...] = hot_ref[lax.rem(y + d, heads)]
 
 
 def pack_kernel(table_ref, q_hbm, k_hbm, v_hbm, send_hbm, x_ref, e_ref, send_ref, sems, out_sems):
@@ -104,10 +107,15 @@
     slots = devices * COLD
     part = 256
     copies = load_heads(q_hbm, k_hbm, v_hbm, x_ref, sems)
-    cols = columns_of(table_ref[...])
-    lane = lax.broadcasted_iota(jnp.int32, (tokens, LANES), 1)
-    for h in range(heads):
-        e_ref[h] = jnp.where(lane == heads + h, cols, 0.0).astype(BF16)
+    tag = lax.broadcasted_iota(jnp.int32, (TAGS, tokens), 0) + 1
+    marks = [
+        jnp.where(table_ref[heads + h : heads + h + 1].astype(jnp.int32) == tag, MARK, 0.0)
+        for h in range(heads)
+    ]
+    cols = columns_of(jnp.concatenate(marks, axis=0))
+    lane = lax.broadcasted_iota(jnp.int32, (tokens, LANES), 1) // TAGS
+    for h in range(heads):
+        e_ref[h] = jnp.where(lane == h, cols, 0.0).astype(BF16)
     label_parts = [jnp.zeros((part, LANES), F32) for _ in range(slots // part)]
     sent = []
     for h in range(heads):
@@ -165,29 +173,36 @@
     for load in loads:
         load.start()
     loads[0].wait()
-    labels = got_ref[:, 3 * heads].astype(F32).reshape(slots, hd)
-    label_rows = jnp.transpose(labels)
+    marks = got_ref[:, 3 * heads].astype(F32).reshape(slots, hd)
+    lane = lax.broadcasted_iota(jnp.int32, (slots, hd), 1) // TAGS
+    key_marks = marks.astype(BF16)
     part = 256
     causal = lax.broadcasted_iota(jnp.int32, (part, part), 1) <= lax.broadcasted_iota(
         jnp.int32, (part, part), 0
     )
+    ones = jnp.ones((slots, hd), BF16)
     sent = []
     for h in range(heads):
+        query_marks = jnp.where(lane == h, marks, 0.0).astype(BF16)
         loads[1 + h].wait()
         q, k, v = (
             got_ref[:, 3 * h + j].astype(F32).reshape(slots, hd).astype(BF16) for j in range(3)
         )
-        row = label_rows[heads + h : heads + h + 1]
+        q = jnp.concatenate([q, query_marks], axis=1)
+        k = jnp.concatenate([k, key_marks], axis=1)
+        v = jnp.concatenate([v, ones], axis=1)
         for c in range(slots // part):
             stop = (c + 1) * part
-            col = labels[c * part : stop, heads + h : heads + h + 1]
             scores = lax.dot_general(
                 q[c * part : stop], k[:stop], NT, preferred_element_type=F32
             )
-            allowed = col == row[:, :stop]
-            last = allowed[:, c * part :] & causal
-            allowed = last if c == 0 else jnp.concatenate([allowed[:, : c * part], last], axis=1)
-            out = softmax_rows(scores, allowed, scale, v[:stop])
+            last = jnp.where(causal, scores[:, c * part :], NEG_FILL)
+            if c > 0:
+                last = jnp.concatenate([scores[:, : c * part], last], axis=1)
+            top = jnp.max(last, axis=1, keepdims=True)
+            weights = jnp.exp2(last * scale - top * scale).astype(BF16)
+            out = jnp.dot(weights, v[:stop], preferred_element_type=F32)
+            out = out[:, :hd] / out[:, hd:]
             devs = slice(c * part // COLD, stop // COLD)
             out_ref[devs, h] = out.reshape(part // COLD, COLD, hd).astype(BF16)
         out = pltpu.make_async_copy(out_ref.at[:, h], out_hbm.at[:, h], out_sems.at[h])
@@ -197,10 +212,11 @@
         out.wait()
 
 
-def mid_kernel(at_ref, b0_ref, b1_ref, b2_ref, b3_ref, q_ref, kv_ref, all_ref):
+def mid_kernel(b0_ref, b1_ref, b2_ref, b3_ref, q_ref, kv_ref, all_ref):
     hd = q_ref.shape[-1]
+    y = lax.axis_index("y")
     for d, ref in enumerate((b0_ref, b1_ref, b2_ref, b3_ref)):
-        all_ref[lax.rem(at_ref[0] - d + 4, 4)] = ref[...].astype(F32)
+        all_ref[lax.rem(y + 4 - d, 4)] = ref[...].astype(F32)
     rows = 4 * HOT
     blocks = [all_ref[:, 3 * j : 3 * j + 3] for j in range(4)]
     labels = blocks[3].reshape(rows, hd)
@@ -212,11 +228,11 @@
     kv_ref[24] = flat[:COLD].astype(BF16)
 
 
-def hot_kernel(at_ref, q_ref, near_ref, far_ref, o0_ref, o1_ref, o2_ref, o3_ref, k_ref, v_ref, o_ref):
+def hot_kernel(q_ref, near_ref, far_ref, o0_ref, o1_ref, o2_ref, o3_ref, k_ref, v_ref, o_ref):
     hd = q_ref.shape[-1]
     rows = 4 * HOT
     scale = hd ** (-0.5) * LOG2E
-    y, x, core, z = (at_ref[i] for i in range(4))
+    y, x, core, z = (lax.axis_index(a) for a in ("y", "x", "core", "z"))
     mine = (z * 2 + core) * 4 + x
     q = q_ref[0:12].astype(F32).reshape(rows, hd).astype(BF16)
     label_col = q_ref[12:24].astype(F32).reshape(rows, hd)[:, 0:1]
@@ -248,7 +264,7 @@
         ref[...] = o_ref[lax.rem(y + 4 - d, 4)].astype(BF16)
 
 
-def unpack_kernel(at_ref, table_ref, back_ref, o0_ref, o1_ref, o2_ref, o3_ref, out_ref, hot_ref):
+def unpack_kernel(table_ref, back_ref, o0_ref, o1_ref, o2_ref, o3_ref, out_ref, hot_ref):
     devices, heads, _, hd = back_ref.shape
     tokens = table_ref.shape[1]
     cols = columns_of(table_ref[...])
@@ -258,7 +274,7 @@
         hot_ref[d] = ref[...].astype(F32)
     for h in range(heads):
         rows = back_ref[:, h].astype(F32).reshape(slots, hd).astype(BF16)
-        hot = hot_ref[lax.rem(h + 4 - at_ref[0], 4)].reshape(HOT, hd)
+        hot = hot_ref[lax.rem(h + 4 - lax.axis_index("y"), 4)].reshape(HOT, hd)
         hot = jnp.concatenate([hot, jnp.zeros((LANES - HOT, hd), F32)], axis=0).astype(BF16)
         for c in range(tokens // part):
             slot = cols[c * part : (c + 1) * part, h : h + 1].astype(jnp.int32)
@@ -272,7 +288,6 @@
             out_ref[c * part : (c + 1) * part, h * hd : (h + 1) * hd] = got.astype(BF16)
 
 
-SMEM = pl.BlockSpec(memory_space=pltpu.SMEM)
 VMEM = pl.BlockSpec(memory_space=pltpu.VMEM)
 HBM = pl.BlockSpec(memory_space=pltpu.HBM)
 AXES = ("z", "core", "x", "y")
@@ -300,15 +315,14 @@
     devices = lax.axis_size(AXES)
     heads, tokens = cluster_ids.shape
     hd = query_rows.shape[1] // heads
-    at = jnp.stack([lax.axis_index(a).astype(jnp.int32) for a in ("y", "x", "core", "z")])
     tile = (COLD, hd)
     x_scratch = pltpu.VMEM((heads, tokens, 3 * hd), BF16)
     x_sems = pltpu.SemaphoreType.DMA((3 * heads,))
     table, h0, h1, h2, h3 = call(
-        rank_kernel, "rank", 58, [SMEM, VMEM, HBM, HBM, HBM],
+        rank_kernel, "rank", 58, [VMEM, HBM, HBM, HBM],
         [(VMEM, (2 * heads, tokens), F32)] + [(VMEM, (12, *tile), BF16)] * 4,
         [x_scratch, pltpu.VMEM((heads, 12, *tile), BF16), x_sems],
-        at, cluster_ids, query_rows, key_rows, value_rows,
+        cluster_ids, query_rows, key_rows, value_rows,
     )
     near = [h0] + [shift(b, "y", d + 1) for d, b in enumerate((h1, h2, h3))]
     (send,) = call(
@@ -324,13 +338,13 @@
     send, near = lax.optimization_barrier((send, near))
     got = lax.all_to_all(send, AXES, split_axis=0, concat_axis=0, tiled=True)
     hot_q, kv = call(
-        mid_kernel, "mid", 24, [SMEM] + [VMEM] * 4,
+        mid_kernel, "mid", 24, [VMEM] * 4,
         [(VMEM, (24, *tile), BF16), (VMEM, (25, *tile), BF16)],
         [pltpu.VMEM((4, 12, *tile), F32)],
-        at, *near,
+        *near,
     )
     kv = jnp.concatenate([kv] + [shift(kv, "x", d) for d in (1, 2, 3)], axis=0)
-    along_z = [kv] + [shift(kv, "z", d) for d in (1, 2, 3)]
+    blocks = [kv] + [shift(kv, "z", d) for d in (1, 2, 3)]
     (answer,) = call(
         cold_kernel, "cold", 58, [HBM], [(HBM, (devices, heads, *tile), BF16)],
         [
@@ -339,23 +353,23 @@
         ],
         got,
     )
-    along_z, _ = lax.optimization_barrier((along_z, answer))
-    kv = jnp.concatenate(along_z, axis=0)
+    blocks, _ = lax.optimization_barrier((blocks, answer))
+    kv = jnp.concatenate(blocks, axis=0)
     far = shift(kv, "core", 1)
     outs = call(
-        hot_kernel, "hot", 24, [SMEM] + [VMEM] * 3, [(VMEM, (3, *tile), BF16)] * 4,
+        hot_kernel, "hot", 24, [VMEM] * 3, [(VMEM, (3, *tile), BF16)] * 4,
         [
             pltpu.VMEM((32 * LANES, hd), BF16), pltpu.VMEM((32 * LANES, hd), BF16),
             pltpu.VMEM((4, 3, *tile), F32),
         ],
-        at, hot_q, kv, far,
+        hot_q, kv, far,
     )
     hot_out = [outs[0]] + [shift(b, "y", 3 - d) for d, b in enumerate(outs[1:])]
     back = lax.all_to_all(answer, AXES, split_axis=0, concat_axis=0, tiled=True)
     (result,) = call(
-        unpack_kernel, "unpack", 24, [SMEM] + [VMEM] * 6, [(VMEM, (tokens, heads * hd), BF16)],
+        unpack_kernel, "unpack", 24, [VMEM] * 6, [(VMEM, (tokens, heads * hd), BF16)],
         [pltpu.VMEM((4, 3, *tile), F32)],
-        at, table, back, *hot_out,
+        table, back, *hot_out,
     )
     return result
 

time: 115 us -> 116 us (level)
  local copies, waits for them, and re-layouts: 0.16 us -> 8.02 us
  waiting for transfers between devices: 49.2 us -> 46.4 us
  Pallas kernels: 28.4 us -> 26.4 us
    unnamed x12, local copies, waits for them, and re-layouts: 0.12 us -> 6.45 us
    all_to_all x1, waiting for transfers between devices: 6.21 us -> 3.53 us  [local(): back = lax.all_to_all(answer, AXES, split_axis=0, concat_axis=0, tiled=True)]
    pallas_call x6, Pallas kernels: 28.4 us -> 26.4 us  [call(): pl.pallas_call(kernel, out_shape=tuple((jax.ShapeDtypeStruct(*out[1:]) fo...]
  transfers between devices with their start and end apart: 15 -> 15, of which waited for: 6 -> 5; matrix products, arithmetic and copies ran while one was open for 0% -> 5% of each run, Pallas kernels for 18% -> 16%
where the time goes in v4:
time: 116 us; the launch traced here: 115 us
  waiting for transfers between devices  46.4 us (40%)
  starting transfers between devices  34.3 us (30%)
  Pallas kernels  26.4 us (23%)
  local copies, waits for them, and re-layouts  8.02 us (7%)
    ppermute x13, waiting for transfers between devices, shift(): lax.ppermute(block, axis, [(i, (i + by) % size) for i in range(size)])  42.9 us
    pallas_call x6, Pallas kernels, call(): pl.pallas_call(kernel, out_shape=tuple((jax.ShapeDtypeStruct(*out[1:]) fo...  26.4 us
    ppermute x13, starting transfers between devices, shift(): lax.ppermute(block, axis, [(i, (i + by) % size) for i in range(size)])  18.8 us
    all_to_all x1, starting transfers between devices, local(): got = lax.all_to_all(send, AXES, split_axis=0, concat_axis=0, tiled=True)  8.55 us
    all_to_all x1, starting transfers between devices, local(): back = lax.all_to_all(answer, AXES, split_axis=0, concat_axis=0, tiled=True)  6.98 us
    unnamed x12, local copies, waits for them, and re-layouts  6.45 us
    all_to_all x1, waiting for transfers between devices, local(): back = lax.all_to_all(answer, AXES, split_axis=0, concat_axis=0, tiled=True)  3.53 us
  transfers between devices with their start and end apart: 15, of which 5 were waited for; matrix products, arithmetic and copies ran while one was open for 5% of the time, Pallas kernels for 16%

profile of v4, /device:TPU:0, one launch (start us, length us, event | category | flops | bytes accessed | tf_op | source)
XLA Modules:
  0.0 115.3 jit_solution(17956843624759283902)
XLA Ops:
  0.0 3.9 %rank.1 = (f32[8,1024]{1,0:T(8,128)}, bf16[12,8,128]{2,1,0:T(8,128)(2,1)}, bf16[12,8,128]{2,1,0:T(8,128)(2,1)}, bf16[12,8,128]{2,1,0:T(8,128)(2,1)}, bf16[12,8,128]{2,1,0:T(8,128)(2,1)}) custom-call(s32[4,1024]{1,0:T(4,128)} %ids_ref.1, bf16[1024,512]{1,0:T(8,128)(2,1)} %q_hbm.3, bf16[1024,512]{1,0:T(8,128)(2,1)} %k_hbm.3, bf16[1024,512]{1,0:T(8,128)(2,1)} %v_hbm.3), custom_call_target="tpu_custom_call" | custom-call | tf_op jit(solution)/shard_map/rank/pallas_call | solution.py:298
  3.9 1.7 %collective-permute-start = (bf16[12,8,128]{2,1,0:T(8,128)(2,1)}, bf16[12,8,128]{2,1,0:T(8,128)(2,1)S(1)}, u32[]{:S(2)}, u32[]{:S(2)}) collective-permute-start(bf16[12,8,128]{2,1,0:T(8,128)(2,1)} %get-tuple-element.27), channel_id=1, source_target_pairs={{0,1},{1,2},{2,3},{3,0},{4,5},{5,6},{6,7},{7,4},{8,9},{9,10},{10,1... | collective-permute-start | bytes 73736 | tf_op jit(solution)/shard_map/ppermute | solution.py:311
  5.7 2.9 %collective-permute-start.1 = (bf16[12,8,128]{2,1,0:T(8,128)(2,1)}, bf16[12,8,128]{2,1,0:T(8,128)(2,1)S(1)}, u32[]{:S(2)}, u32[]{:S(2)}) collective-permute-start(bf16[12,8,128]{2,1,0:T(8,128)(2,1)} %get-tuple-element.28), channel_id=1, source_target_pairs={{0,2},{1,3},{2,0},{3,1},{4,6},{5,7},{6,4},{7,5},{8,10},{9,11},{10,... | collective-permute-start | bytes 73736 | tf_op jit(solution)/shard_map/ppermute | solution.py:311
  8.6 1.3 %collective-permute-start.2 = (bf16[12,8,128]{2,1,0:T(8,128)(2,1)}, bf16[12,8,128]{2,1,0:T(8,128)(2,1)S(1)}, u32[]{:S(2)}, u32[]{:S(2)}) collective-permute-start(bf16[12,8,128]{2,1,0:T(8,128)(2,1)} %get-tuple-element.29), channel_id=1, source_target_pairs={{0,3},{1,0},{2,1},{3,2},{4,7},{5,4},{6,5},{7,6},{8,11},{9,8},{10,9... | collective-permute-start | bytes 73736 | tf_op jit(solution)/shard_map/ppermute | solution.py:311
  9.9 8.1 %pack.1 = bf16[128,13,8,128]{3,2,1,0:T(8,128)(2,1)} custom-call(f32[8,1024]{1,0:T(8,128)} %get-tuple-element.25.table_ref, bf16[1024,512]{1,0:T(8,128)(2,1)} %q_hbm.3, bf16[1024,512]{1,0:T(8,128)(2,1)} %k_hbm.3, bf16[1024,512]{1,0:T(8,128)(2,1)} %v_hbm.3), custom_call_target="tpu_custom_call" | custom-call | tf_op jit(solution)/shard_map/pack/pallas_call | solution.py:298
  18.0 8.5 %all-to-all-start = ((bf16[128,13,8,128]{3,2,1,0:T(8,128)(2,1)}), bf16[128,13,8,128]{3,2,1,0:T(8,128)(2,1)S(1)}, u32[]{:S(2)}, u32[]{:S(2)}) async-start(bf16[128,13,8,128]{3,2,1,0:T(8,128)(2,1)} %pack.1), calls=%async_computation | async-start | bytes 6815744 | tf_op jit(solution)/shard_map/all_to_all | solution.py:339
  26.7 2.2 %collective-permute-start.5 = (bf16[25,8,128]{2,1,0:T(8,128)(2,1)S(1)}, bf16[25,8,128]{2,1,0:T(8,128)(2,1)S(1)}, u32[]{:S(2)}, u32[]{:S(2)}) collective-permute-start(bf16[25,8,128]{2,1,0:T(8,128)(2,1)S(1)} %get-tuple-element.36), channel_id=1, source_target_pairs={{0,12},{4,0},{8,4},{12,8},{1,13},{5,1},{9,5},{13,9},{2,14},{6,2},{... | collective-permute-start | bytes 153608 | tf_op jit(solution)/shard_map/ppermute | solution.py:311
  28.9 0.9 collective-permute-start.4
  29.8 0.9 collective-permute-start.3
  30.6 0.6 constant_dynamic-update-slice_fusion.3
  31.2 36.6 %collective-permute-done.3 = bf16[25,8,128]{2,1,0:T(8,128)(2,1)S(1)} collective-permute-done((bf16[25,8,128]{2,1,0:T(8,128)(2,1)S(1)}, bf16[25,8,128]{2,1,0:T(8,128)(2,1)S(1)}, u32[]{:S(2)}, u32[]{:S(2)}) %collective-permute-start.3) | collective-permute-done | bytes 51232 | tf_op jit(solution)/shard_map/ppermute | solution.py:311
  67.8 0.6 constant_dynamic-update-slice_fusion.2
  68.4 0.6 constant_dynamic-update-slice_fusion.1
  69.1 0.6 constant_dynamic-update-slice_fusion
  69.7 3.4 %collective-permute-start.8 = (bf16[100,8,128]{2,1,0:T(8,128)(2,1)}, bf16[100,8,128]{2,1,0:T(8,128)(2,1)}, u32[]{:S(2)}, u32[]{:S(2)}) collective-permute-start(bf16[100,8,128]{2,1,0:T(8,128)(2,1)} %constant_dynamic-update-slice_fusion), channel_id=1, source_target_pairs={{0,96},{32,0},{64,32},{96,64},{1,97},{33,1},{65,33},{97,65},{2,98}... | collective-permute-start | bytes 614408 | tf_op jit(solution)/shard_map/ppermute | solution.py:311
  73.1 0.3 collective-permute-start.7
  73.4 1.1 collective-permute-start.6
  74.5 1.7 %copy-done.2 = bf16[128,13,8,128]{3,2,1,0:T(8,128)(2,1)} copy-done((bf16[128,13,8,128]{3,2,1,0:T(8,128)(2,1)}, bf16[128,13,8,128]{3,2,1,0:T(8,128)(2,1)S(1)}, u32[]{:S(2)}) %copy-start.2) | copy-done | bytes 3407896
  76.2 9.2 %cold.1 = bf16[128,4,8,128]{3,2,1,0:T(8,128)(2,1)} custom-call(bf16[128,13,8,128]{3,2,1,0:T(8,128)(2,1)} %copy-done.2), custom_call_target="tpu_custom_call" | custom-call | tf_op jit(solution)/shard_map/cold/pallas_call | solution.py:298
  85.4 7.0 %all-to-all-start.1 = ((bf16[128,4,8,128]{3,2,1,0:T(8,128)(2,1)}), bf16[128,4,8,128]{3,2,1,0:T(8,128)(2,1)S(1)}, u32[]{:S(2)}, u32[]{:S(2)}) async-start(bf16[128,4,8,128]{3,2,1,0:T(8,128)(2,1)} %cold.1), calls=%async_computation.1 | async-start | bytes 2097152 | tf_op jit(solution)/shard_map/all_to_all | solution.py:368
  92.4 0.9 constant_dynamic-update-slice_fusion.7
  93.4 1.0 constant_dynamic-update-slice_fusion.6
  94.3 1.0 constant_dynamic-update-slice_fusion.5
  95.3 1.0 constant_dynamic-update-slice_fusion.4.near_ref
  96.4 2.3 %collective-permute-done.9.far_ref = bf16[400,8,128]{2,1,0:T(8,128)(2,1)S(1)} collective-permute-done((bf16[400,8,128]{2,1,0:T(8,128)(2,1)S(1)}, bf16[400,8,128]{2,1,0:T(8,128)(2,1)S(1)}, u32[]{:S(2)}, u32[]{:S(2)}) %collective-permute-start.9) | collective-permute-done | bytes 819232 | tf_op jit(solution)/shard_map/ppermute | solution.py:311
  98.7 1.3 %hot.1 = (bf16[3,8,128]{2,1,0:T(8,128)(2,1)S(1)}, bf16[3,8,128]{2,1,0:T(8,128)(2,1)S(1)}, bf16[3,8,128]{2,1,0:T(8,128)(2,1)S(1)}, bf16[3,8,128]{2,1,0:T(8,128)(2,1)S(1)}) custom-call(bf16[24,8,128]{2,1,0:T(8,128)(2,1)S(1)} %get-tuple-element.35.q_ref, bf16[400,8,128]{2,1,0:T(8,128)(2,1)S(1)} %constant_dynamic-update-slice_fusion.4.near_ref, ...), custom_call_target="tpu_custom_call" | custom-call | tf_op jit(solution)/shard_map/hot/pallas_call | solution.py:298
  100.0 2.3 %collective-permute-start.10 = (bf16[3,8,128]{2,1,0:T(8,128)(2,1)S(1)}, bf16[3,8,128]{2,1,0:T(8,128)(2,1)S(1)}, u32[]{:S(2)}, u32[]{:S(2)}) collective-permute-start(bf16[3,8,128]{2,1,0:T(8,128)(2,1)S(1)} %get-tuple-element.42), channel_id=1, source_target_pairs={{0,3},{1,0},{2,1},{3,2},{4,7},{5,4},{6,5},{7,6},{8,11},{9,8},{10,9... | collective-permute-start | bytes 18440 | tf_op jit(solution)/shard_map/ppermute | solution.py:311
  102.3 0.8 collective-permute-start.11
  103.1 0.9 collective-permute-start.12
  103.9 3.7 %collective-permute-done.11.o2_ref = bf16[3,8,128]{2,1,0:T(8,128)(2,1)S(1)} collective-permute-done((bf16[3,8,128]{2,1,0:T(8,128)(2,1)S(1)}, bf16[3,8,128]{2,1,0:T(8,128)(2,1)S(1)}, u32[]{:S(2)}, u32[]{:S(2)}) %collective-permute-start.11) | collective-permute-done | bytes 6176 | tf_op jit(solution)/shard_map/ppermute | solution.py:311
  107.9 3.5 %all-to-all-done.1.back_ref = bf16[128,4,8,128]{3,2,1,0:T(8,128)(2,1)S(1)} async-done(((bf16[128,4,8,128]{3,2,1,0:T(8,128)(2,1)}), bf16[128,4,8,128]{3,2,1,0:T(8,128)(2,1)S(1)}, u32[]{:S(2)}, u32[]{:S(2)}) %all-to-all-start.1) | async-done | bytes 1048608 | tf_op jit(solution)/shard_map/all_to_all | solution.py:368
  111.5 3.9 %unpack.1 = bf16[1024,512]{1,0:T(8,128)(2,1)} custom-call(f32[8,1024]{1,0:T(8,128)S(1)} %copy-done, bf16[128,4,8,128]{3,2,1,0:T(8,128)(2,1)S(1)} %all-to-all-done.1.back_ref, bf16[3,8,128]{2,1,0:T(8,128)(2,1)S(1)} %get-tuple-element.41.o0_ref, bf16[3,8,128]{2,1,0:T(8,128)(2,1)S(1)} %collective-permute-done.10.o1_ref, ...), custom_call_target="tpu_custom_call" | custom-call | tf_op jit(solution)/shard_map/unpack/pallas_call | solution.py:298
  (18 shorter events, 0.5 us)
Async XLA Ops:
  3.9 14.1 %collective-permute-start = (bf16[12,8,128]{2,1,0:T(8,128)(2,1)}, bf16[12,8,128]{2,1,0:T(8,128)(2,1)S(1)}, u32[]{:S(2)}, u32[]{:S(2)}) collective-permute-start(bf16[12,8,128]{2,1,0:T(8,128)(2,1)} %get-tuple-element.27), channel_id=1, source_target_pairs={{0,1},{1,2},{2,3},{3,0},{4,5},{5,6},{6,7},{7,4},{8,9},{9,10},{10,1... | collective-permute-start | bytes 73736 | tf_op jit(solution)/shard_map/ppermute | solution.py:311
  5.7 12.3 %collective-permute-start.1 = (bf16[12,8,128]{2,1,0:T(8,128)(2,1)}, bf16[12,8,128]{2,1,0:T(8,128)(2,1)S(1)}, u32[]{:S(2)}, u32[]{:S(2)}) collective-permute-start(bf16[12,8,128]{2,1,0:T(8,128)(2,1)} %get-tuple-element.28), channel_id=1, source_target_pairs={{0,2},{1,3},{2,0},{3,1},{4,6},{5,7},{6,4},{7,5},{8,10},{9,11},{10,... | collective-permute-start | bytes 73736 | tf_op jit(solution)/shard_map/ppermute | solution.py:311
  8.6 9.4 %collective-permute-start.2 = (bf16[12,8,128]{2,1,0:T(8,128)(2,1)}, bf16[12,8,128]{2,1,0:T(8,128)(2,1)S(1)}, u32[]{:S(2)}, u32[]{:S(2)}) collective-permute-start(bf16[12,8,128]{2,1,0:T(8,128)(2,1)} %get-tuple-element.29), channel_id=1, source_target_pairs={{0,3},{1,0},{2,1},{3,2},{4,7},{5,4},{6,5},{7,6},{8,11},{9,8},{10,9... | collective-permute-start | bytes 73736 | tf_op jit(solution)/shard_map/ppermute | solution.py:311
  18.0 8.6 %copy-start.1 = (bf16[12,8,128]{2,1,0:T(8,128)(2,1)S(1)}, bf16[12,8,128]{2,1,0:T(8,128)(2,1)}, u32[]{:S(2)}) copy-start(bf16[12,8,128]{2,1,0:T(8,128)(2,1)} %get-tuple-element.31.b0_ref) | copy-start | bytes 73732
  18.0 56.5 %all-to-all-start = ((bf16[128,13,8,128]{3,2,1,0:T(8,128)(2,1)}), bf16[128,13,8,128]{3,2,1,0:T(8,128)(2,1)S(1)}, u32[]{:S(2)}, u32[]{:S(2)}) async-start(bf16[128,13,8,128]{3,2,1,0:T(8,128)(2,1)} %pack.1), calls=%async_computation | async-start | bytes 6815744 | tf_op jit(solution)/shard_map/all_to_all | solution.py:339
  26.7 42.4 %collective-permute-start.5 = (bf16[25,8,128]{2,1,0:T(8,128)(2,1)S(1)}, bf16[25,8,128]{2,1,0:T(8,128)(2,1)S(1)}, u32[]{:S(2)}, u32[]{:S(2)}) collective-permute-start(bf16[25,8,128]{2,1,0:T(8,128)(2,1)S(1)} %get-tuple-element.36), channel_id=1, source_target_pairs={{0,12},{4,0},{8,4},{12,8},{1,13},{5,1},{9,5},{13,9},{2,14},{6,2},{... | collective-permute-start | bytes 153608 | tf_op jit(solution)/shard_map/ppermute | solution.py:311
  28.9 39.5 %collective-permute-start.4 = (bf16[25,8,128]{2,1,0:T(8,128)(2,1)S(1)}, bf16[25,8,128]{2,1,0:T(8,128)(2,1)S(1)}, u32[]{:S(2)}, u32[]{:S(2)}) collective-permute-start(bf16[25,8,128]{2,1,0:T(8,128)(2,1)S(1)} %get-tuple-element.36), channel_id=1, source_target_pairs={{0,8},{4,12},{8,0},{12,4},{1,9},{5,13},{9,1},{13,5},{2,10},{6,14},... | collective-permute-start | bytes 153608 | tf_op jit(solution)/shard_map/ppermute | solution.py:311
  29.8 38.1 %collective-permute-start.3 = (bf16[25,8,128]{2,1,0:T(8,128)(2,1)S(1)}, bf16[25,8,128]{2,1,0:T(8,128)(2,1)S(1)}, u32[]{:S(2)}, u32[]{:S(2)}) collective-permute-start(bf16[25,8,128]{2,1,0:T(8,128)(2,1)S(1)} %get-tuple-element.36), channel_id=1, source_target_pairs={{0,4},{4,8},{8,12},{12,0},{1,5},{5,9},{9,13},{13,1},{2,6},{6,10},{... | collective-permute-start | bytes 153608 | tf_op jit(solution)/shard_map/ppermute | solution.py:311
  69.7 22.7 %collective-permute-start.8 = (bf16[100,8,128]{2,1,0:T(8,128)(2,1)}, bf16[100,8,128]{2,1,0:T(8,128)(2,1)}, u32[]{:S(2)}, u32[]{:S(2)}) collective-permute-start(bf16[100,8,128]{2,1,0:T(8,128)(2,1)} %constant_dynamic-update-slice_fusion), channel_id=1, source_target_pairs={{0,96},{32,0},{64,32},{96,64},{1,97},{33,1},{65,33},{97,65},{2,98}... | collective-permute-start | bytes 614408 | tf_op jit(solution)/shard_map/ppermute | solution.py:311
  73.1 19.3 %collective-permute-start.7 = (bf16[100,8,128]{2,1,0:T(8,128)(2,1)}, bf16[100,8,128]{2,1,0:T(8,128)(2,1)}, u32[]{:S(2)}, u32[]{:S(2)}) collective-permute-start(bf16[100,8,128]{2,1,0:T(8,128)(2,1)} %constant_dynamic-update-slice_fusion), channel_id=1, source_target_pairs={{0,64},{32,96},{64,0},{96,32},{1,65},{33,97},{65,1},{97,33},{2,66}... | collective-permute-start | bytes 614408 | tf_op jit(solution)/shard_map/ppermute | solution.py:311
  73.4 19.0 %collective-permute-start.6 = (bf16[100,8,128]{2,1,0:T(8,128)(2,1)}, bf16[100,8,128]{2,1,0:T(8,128)(2,1)}, u32[]{:S(2)}, u32[]{:S(2)}) collective-permute-start(bf16[100,8,128]{2,1,0:T(8,128)(2,1)} %constant_dynamic-update-slice_fusion), channel_id=1, source_target_pairs={{0,32},{32,64},{64,96},{96,0},{1,33},{33,65},{65,97},{97,1},{2,34}... | collective-permute-start | bytes 614408 | tf_op jit(solution)/shard_map/ppermute | solution.py:311
  74.5 1.7 %copy-start.2 = (bf16[128,13,8,128]{3,2,1,0:T(8,128)(2,1)}, bf16[128,13,8,128]{3,2,1,0:T(8,128)(2,1)S(1)}, u32[]{:S(2)}) copy-start(bf16[128,13,8,128]{3,2,1,0:T(8,128)(2,1)S(1)} %all-to-all-done.got_hbm) | copy-start | bytes 10223620
  85.4 26.1 %copy-start = (f32[8,1024]{1,0:T(8,128)S(1)}, f32[8,1024]{1,0:T(8,128)}, u32[]{:S(2)}) copy-start(f32[8,1024]{1,0:T(8,128)} %get-tuple-element.25.table_ref) | copy-start | bytes 98308
  85.4 26.0 %all-to-all-start.1 = ((bf16[128,4,8,128]{3,2,1,0:T(8,128)(2,1)}), bf16[128,4,8,128]{3,2,1,0:T(8,128)(2,1)S(1)}, u32[]{:S(2)}, u32[]{:S(2)}) async-start(bf16[128,4,8,128]{3,2,1,0:T(8,128)(2,1)} %cold.1), calls=%async_computation.1 | async-start | bytes 2097152 | tf_op jit(solution)/shard_map/all_to_all | solution.py:368
  96.3 2.4 %collective-permute-start.9 = (bf16[400,8,128]{2,1,0:T(8,128)(2,1)S(1)}, bf16[400,8,128]{2,1,0:T(8,128)(2,1)S(1)}, u32[]{:S(2)}, u32[]{:S(2)}) collective-permute-start(bf16[400,8,128]{2,1,0:T(8,128)(2,1)S(1)} %constant_dynamic-update-slice_fusion.4.near_ref), channel_id=1, source_target_pairs={{0,16},{16,0},{1,17},{17,1},{2,18},{18,2},{3,19},{19,3},{4,20},{20... | collective-permute-start | bytes 2457608 | tf_op jit(solution)/shard_map/ppermute | solution.py:311
  100.0 4.0 %collective-permute-start.10 = (bf16[3,8,128]{2,1,0:T(8,128)(2,1)S(1)}, bf16[3,8,128]{2,1,0:T(8,128)(2,1)S(1)}, u32[]{:S(2)}, u32[]{:S(2)}) collective-permute-start(bf16[3,8,128]{2,1,0:T(8,128)(2,1)S(1)} %get-tuple-element.42), channel_id=1, source_target_pairs={{0,3},{1,0},{2,1},{3,2},{4,7},{5,4},{6,5},{7,6},{8,11},{9,8},{10,9... | collective-permute-start | bytes 18440 | tf_op jit(solution)/shard_map/ppermute | solution.py:311
  102.3 5.4 %collective-permute-start.11 = (bf16[3,8,128]{2,1,0:T(8,128)(2,1)S(1)}, bf16[3,8,128]{2,1,0:T(8,128)(2,1)S(1)}, u32[]{:S(2)}, u32[]{:S(2)}) collective-permute-start(bf16[3,8,128]{2,1,0:T(8,128)(2,1)S(1)} %get-tuple-element.43), channel_id=1, source_target_pairs={{0,2},{1,3},{2,0},{3,1},{4,6},{5,7},{6,4},{7,5},{8,10},{9,11},{10,... | collective-permute-start | bytes 18440 | tf_op jit(solution)/shard_map/ppermute | solution.py:311
  103.1 4.8 %collective-permute-start.12 = (bf16[3,8,128]{2,1,0:T(8,128)(2,1)S(1)}, bf16[3,8,128]{2,1,0:T(8,128)(2,1)S(1)}, u32[]{:S(2)}, u32[]{:S(2)}) collective-permute-start(bf16[3,8,128]{2,1,0:T(8,128)(2,1)S(1)} %get-tuple-element.44), channel_id=1, source_target_pairs={{0,1},{1,2},{2,3},{3,0},{4,5},{5,6},{6,7},{7,4},{8,9},{9,10},{10,1... | collective-permute-start | bytes 18440 | tf_op jit(solution)/shard_map/ppermute | solution.py:311

commit v5 on v2

v5 whole, which is shorter than its diff:
```python
import jax
import jax.numpy as jnp
from jax import lax
from jax.experimental import pallas as pl
from jax.experimental.pallas import tpu as pltpu
from jax.sharding import PartitionSpec as P

CL_DEV = 8
COLD = 8
HOT = 24
HOT_PAD = 32
LANES = 128
NEG_FILL = -1e30
SHARE = 3
HOT_LANE = 64
LOG2E = 1.4426950408889634
F32 = jnp.float32
BF16 = jnp.bfloat16


def iota(shape, dim):
    return lax.broadcasted_iota(jnp.int32, shape, dim)


def columns_of(table):
    tokens = table.shape[1]
    return jnp.transpose(
        jnp.concatenate([table, jnp.zeros((LANES - table.shape[0], tokens), F32)], axis=0)
    )


def pack_kernel(
    ids_ref, q_hbm, k_hbm, v_hbm,
    table_ref, h0_ref, h1_ref, h2_ref, h3_ref, send_hbm,
    q_ref, k_ref, v_ref, x_ref, hot_ref, send_ref, sems, out_sems,
):
    heads, tokens = ids_ref.shape
    hd = q_ref.shape[1] // heads
    devices = send_ref.shape[0]
    slots = devices * COLD
    step = 256
    loads = [
        pltpu.make_async_copy(src, dst, sems.at[j])
        for j, (src, dst) in enumerate(((q_hbm, q_ref), (k_hbm, k_ref), (v_hbm, v_ref)))
    ]
    for load in loads:
        load.start()
    ids = ids_ref[...]
    owner = ids // CL_DEV
    tags = (ids - owner * CL_DEV + 1).astype(F32)
    upper = (iota((step, step), 0) < iota((step, step), 1)).astype(BF16)
    dev_col = iota((devices, step), 0)
    slot_rows, hot_ranks = [], []
    labels = jnp.zeros((devices, LANES), F32)
    for h in range(heads):
        carry = jnp.zeros((devices, 1), F32)
        ones, ranks = [], []
        for b in range(tokens // step):
            one = (owner[h : h + 1, b * step : (b + 1) * step] == dev_col).astype(F32)
            inside = jnp.dot(one.astype(BF16), upper, preferred_element_type=F32) + carry
            carry = carry + jnp.sum(one, axis=1, keepdims=True)
            ones.append(one)
            ranks.append(jnp.sum(one * inside, axis=0, keepdims=True))
        full = (carry > COLD).astype(F32)
        for b, one in enumerate(ones):
            ranks[b] = jnp.where(
                jnp.sum(one * full, axis=0, keepdims=True) > 0.5, ranks[b] + slots, ranks[b]
            )
            lane = jnp.where(ranks[b] < COLD, ranks[b] + COLD * h, -1.0).astype(jnp.int32)
            tag = jnp.where(
                lane == iota((LANES, step), 0), tags[h : h + 1, b * step : (b + 1) * step], 0.0
            )
            labels = labels + lax.dot_general(
                one.astype(BF16), tag.astype(BF16), NT, preferred_element_type=F32
            )
        rank = jnp.concatenate(ranks, axis=1).astype(jnp.int32)
        slot_rows.append(jnp.where(rank >= slots, rank, owner[h : h + 1] * COLD + rank))
        hot_ranks.append(jnp.where(rank >= slots, rank - slots, -SHARE))
    slot_all = jnp.concatenate(slot_rows, axis=0)
    table_ref[...] = jnp.concatenate([slot_all.astype(F32), tags], axis=0)
    shares = HOT // SHARE
    rows = shares * COLD
    row = iota((rows, 1), 0)
    row_share, row_at = row // COLD, row % COLD
    want_k = jnp.where(row_at < SHARE, SHARE * row_share + row_at, -9)
    want_v = jnp.where(
        (row_at >= SHARE) & (row_at < 2 * SHARE), SHARE * (row_share - 1) + row_at, -9
    )
    want_tag = jnp.where(row_at == 2 * SHARE, row_share, -9)
    for load in loads:
        load.wait()
    hot_tiles = []
    for h in range(heads):
        cols = slice(h * hd, (h + 1) * hd)
        for j, ref in enumerate((q_ref, k_ref, v_ref)):
            x_ref[h, :, j * hd : (j + 1) * hd] = ref[:, cols]
        hot = hot_ranks[h]
        tag_rows = jnp.broadcast_to(tags[h : h + 1], (LANES, tokens))
        share = (hot + SHARE) // SHARE - 1
        lane_tag = jnp.where(iota((LANES, tokens), 0) == HOT_LANE + hot - SHARE * share, tag_rows, 0.0)
        tiles = lax.dot_general(
            (share == want_tag).astype(BF16), lane_tag.astype(BF16), NT, preferred_element_type=F32
        )
        tiles = tiles + jnp.dot((hot == want_k).astype(BF16), k_ref[:, cols], preferred_element_type=F32)
        tiles = tiles + jnp.dot((hot == want_v).astype(BF16), v_ref[:, cols], preferred_element_type=F32)
        hot_tiles.append(tiles)
        place = (hot == iota((HOT_PAD, tokens), 0)).astype(BF16)
        asked = jnp.dot(place, q_ref[:, cols], preferred_element_type=F32)
        asked_tags = lax.dot_general(place, tag_rows.astype(BF16), NT, preferred_element_type=F32)
        hot_ref[h, 0:3] = asked[:HOT].reshape(3, COLD, hd).astype(BF16)
        hot_ref[h, 3:6] = asked_tags[:HOT].reshape(3, COLD, hd).astype(BF16)
    y = lax.axis_index("y")
    for d, ref in enumerate((h0_ref, h1_ref, h2_ref, h3_ref)):
        ref[...] = hot_ref[lax.rem(y + d, heads)]
    part = 256
    sub = iota((COLD, LANES), 0)
    sent = []
    for c in range(slots // part):
        first, stop = c * part // COLD, (c + 1) * part // COLD
        for h in range(heads):
            place = (slot_all[h : h + 1] == iota((part, tokens), 0) + c * part).astype(BF16)
            moved = jnp.dot(place, x_ref[h], preferred_element_type=F32)
            for j in range(3):
                send_ref[first:stop, 3 * h + j] = (
                    moved[:, j * hd : (j + 1) * hd].reshape(stop - first, COLD, hd).astype(BF16)
                )
        for dev in range(first, stop):
            share, head = dev // 16, dev % heads
            tile = hot_tiles[head][share * COLD : (share + 1) * COLD]
            tile = jnp.where(sub == 2 * SHARE, tile + labels[dev : dev + 1], tile)
            send_ref[dev, 3 * heads] = tile.astype(BF16)
        out = pltpu.make_async_copy(
            send_ref.at[first:stop], send_hbm.at[first:stop], out_sems.at[c]
        )
        out.start()
        sent.append(out)
    for out in sent:
        out.wait()


def softmax_rows(scores, allowed, scale, values):
    masked = jnp.where(allowed, scores, NEG_FILL)
    top = jnp.max(masked, axis=1, keepdims=True)
    weights = jnp.exp2((masked - top) * scale)
    total = jnp.sum(weights, axis=1, keepdims=True)
    out = jnp.dot(weights.astype(BF16), values, preferred_element_type=F32)
    return out / total


NT = (((1,), (1,)), ((), ()))


def cold_kernel(got_ref, out_ref):
    devices, tiles, _, hd = got_ref.shape
    heads = tiles // 3
    slots = devices * COLD
    scale = hd ** (-0.5) * LOG2E
    extra = got_ref[:, 3 * heads].astype(F32)
    spread = jnp.broadcast_to(
        extra[:, 2 * SHARE : 2 * SHARE + 1], (devices, COLD, LANES)
    ).reshape(slots, LANES)
    pick = iota((slots, LANES), 1) - iota((slots, LANES), 0) % COLD
    ones = jnp.ones((LANES, LANES), BF16)
    part = 256
    causal = iota((part, part), 1) <= iota((part, part), 0)
    for h in range(heads):
        tags = jnp.where(pick == COLD * h, spread, 0.0).astype(BF16)
        label_cols = jnp.dot(tags, ones, preferred_element_type=F32)
        label_rows = lax.dot_general(ones[:COLD], tags, NT, preferred_element_type=F32)
        q, k, v = (
            got_ref[:, 3 * h + j].astype(F32).reshape(slots, hd).astype(BF16) for j in range(3)
        )
        for c in range(slots // part):
            stop = (c + 1) * part
            scores = lax.dot_general(
                q[c * part : stop], k[:stop], NT, preferred_element_type=F32
            )
            allowed = label_cols[c * part : stop, :1] == label_rows[:1, :stop]
            last = allowed[:, c * part :] & causal
            allowed = last if c == 0 else jnp.concatenate([allowed[:, : c * part], last], axis=1)
            out = softmax_rows(scores, allowed, scale, v[:stop])
            devs = slice(c * part // COLD, stop // COLD)
            out_ref[devs, h] = out.reshape(part // COLD, COLD, hd).astype(BF16)


def mid_kernel(got_ref, kv_ref):
    devices, tiles, _, hd = got_ref.shape
    slots = devices * COLD
    keys = devices * SHARE
    extra = got_ref[:, tiles - 1].astype(F32).reshape(slots, hd).astype(BF16)
    n = iota((keys, 1), 0)
    source, at = n // SHARE, n % SHARE
    col = iota((keys, slots), 1)

    def rows_at(offset):
        place = (col == source * COLD + offset).astype(BF16)
        return jnp.dot(place, extra, preferred_element_type=F32)

    kv_ref[0:48] = rows_at(at).reshape(48, COLD, hd).astype(BF16)
    kv_ref[48:96] = rows_at(at + SHARE).reshape(48, COLD, hd).astype(BF16)
    tags = jnp.where(iota((keys, hd), 1) == HOT_LANE + at, rows_at(2 * SHARE), 0.0).astype(BF16)
    flat = lax.dot_general(jnp.ones((COLD, hd), BF16), tags, NT, preferred_element_type=F32)
    label = [flat[0:1, j * LANES : (j + 1) * LANES] for j in range(keys // LANES)]
    label.append(jnp.zeros((COLD - len(label), LANES), F32))
    kv_ref[96] = jnp.concatenate(label, axis=0).astype(BF16)


def hot_kernel(
    b0_ref, b1_ref, b2_ref, b3_ref, n0_ref, n1_ref, n2_ref, n3_ref, f0_ref, f1_ref, f2_ref, f3_ref,
    o0_ref, o1_ref, o2_ref, o3_ref, all_ref, k_ref, v_ref, o_ref,
):
    hd = b0_ref.shape[-1]
    rows = 4 * HOT
    keys = k_ref.shape[0] // 8
    scale = hd ** (-0.5) * LOG2E
    y, x, core, z = (lax.axis_index(a) for a in ("y", "x", "core", "z"))
    for d, ref in enumerate((b0_ref, b1_ref, b2_ref, b3_ref)):
        all_ref[lax.rem(y + 4 - d, 4)] = ref[...].astype(F32)
    q = all_ref[:, 0:3].reshape(rows, hd).astype(BF16)
    label_col = all_ref[:, 3:6].reshape(rows, hd)[:, 0:1]
    row = iota((rows, 1), 0)
    asked_at = (((z * 2 + core) * 16 + x * 4) * HOT + row).astype(F32)
    n = iota((1, keys), 1)
    key_at = (n // SHARE) * HOT + n % SHARE
    allowed = []
    blocks = ((n0_ref, n1_ref, n2_ref, n3_ref), (f0_ref, f1_ref, f2_ref, f3_ref))
    for dc in range(2):
        for dz in range(4):
            ref = blocks[dc][dz]
            at = slice((dc * 4 + dz) * keys, (dc * 4 + dz + 1) * keys)
            k_ref[at] = ref[0:48].astype(F32).reshape(keys, hd).astype(BF16)
            v_ref[at] = ref[48:96].astype(F32).reshape(keys, hd).astype(BF16)
            tile = ref[96].astype(F32)
            label = jnp.concatenate([tile[j : j + 1] for j in range(keys // LANES)], axis=1)
            share = lax.rem(z + 4 - dz, 4) * 2 + lax.rem(core + dc, 2)
            there = (key_at + SHARE * share).astype(F32)
            allowed.append((label_col == label) & (there <= asked_at))
    scores = lax.dot_general(q, k_ref[...], NT, preferred_element_type=F32)
    out = softmax_rows(scores, jnp.concatenate(allowed, axis=1), scale, v_ref[...])
    o_ref[...] = out.reshape(4, 3, COLD, hd)
    for d, ref in enumerate((o0_ref, o1_ref, o2_ref, o3_ref)):
        ref[...] = o_ref[lax.rem(y + 4 - d, 4)].astype(BF16)


def unpack_kernel(table_ref, back_ref, o0_ref, o1_ref, o2_ref, o3_ref, out_ref, hot_ref):
    devices, heads, _, hd = back_ref.shape
    tokens = table_ref.shape[1]
    cols = columns_of(table_ref[...])
    slots = devices * COLD
    part = 256
    for d, ref in enumerate((o0_ref, o1_ref, o2_ref, o3_ref)):
        hot_ref[d] = ref[...].astype(F32)
    for h in range(heads):
        rows = back_ref[:, h].astype(F32).reshape(slots, hd).astype(BF16)
        hot = hot_ref[lax.rem(h + 4 - lax.axis_index("y"), 4)].reshape(HOT, hd)
        hot = jnp.concatenate([hot, jnp.zeros((LANES - HOT, hd), F32)], axis=0).astype(BF16)
        for c in range(tokens // part):
            slot = cols[c * part : (c + 1) * part, h : h + 1].astype(jnp.int32)
            place = (slot == lax.broadcasted_iota(jnp.int32, (part, slots), 1)).astype(BF16)
            hot_place = (
                slot == lax.broadcasted_iota(jnp.int32, (part, LANES), 1) + slots
            ).astype(BF16)
            got = jnp.dot(place, rows, preferred_element_type=F32) + jnp.dot(
                hot_place, hot, preferred_element_type=F32
            )
            out_ref[c * part : (c + 1) * part, h * hd : (h + 1) * hd] = got.astype(BF16)


VMEM = pl.BlockSpec(memory_space=pltpu.VMEM)
HBM = pl.BlockSpec(memory_space=pl.ANY)
AXES = ("z", "core", "x", "y")
MIB = 1024 * 1024


def call(kernel, name, limit, ins, outs, scratch, *arrays):
    return pl.pallas_call(
        kernel,
        out_shape=tuple(jax.ShapeDtypeStruct(*out[1:]) for out in outs),
        in_specs=ins,
        out_specs=tuple(out[0] for out in outs),
        scratch_shapes=scratch,
        compiler_params=pltpu.CompilerParams(vmem_limit_bytes=limit * MIB),
        name=name,
    )(*arrays)


def shift(block, axis, by):
    size = lax.axis_size(axis)
    return lax.ppermute(block, axis, [(i, (i + by) % size) for i in range(size)])


def local(query_rows, key_rows, value_rows, cluster_ids):
    devices = lax.axis_size(AXES)
    heads, tokens = cluster_ids.shape
    hd = query_rows.shape[1] // heads
    tile = (COLD, hd)
    rows = pltpu.VMEM((tokens, heads * hd), BF16)
    payload = (devices, 3 * heads + 1, *tile)
    table, h0, h1, h2, h3, send = call(
        pack_kernel, "pack", 58, [VMEM, HBM, HBM, HBM],
        [(VMEM, (2 * heads, tokens), F32)] + [(VMEM, (6, *tile), BF16)] * 4 + [(HBM, payload, BF16)],
        [
            rows, rows, rows, pltpu.VMEM((heads, tokens, 3 * hd), BF16),
            pltpu.VMEM((heads, 6, *tile), BF16), pltpu.VMEM(payload, BF16),
            pltpu.SemaphoreType.DMA((3,)), pltpu.SemaphoreType.DMA((4,)),
        ],
        cluster_ids, query_rows, key_rows, value_rows,
    )
    got = lax.all_to_all(send, AXES, split_axis=0, concat_axis=0, tiled=True)
    asked = [h0] + [shift(b, "y", d + 1) for d, b in enumerate((h1, h2, h3))]
    got, asked = lax.optimization_barrier((got, asked))
    (kv,) = call(mid_kernel, "mid", 24, [VMEM], [(VMEM, (97, *tile), BF16)], [], got)
    got, kv = lax.optimization_barrier((got, kv))
    near = [kv] + [shift(kv, "z", d) for d in (1, 2, 3)]
    (answer,) = call(
        cold_kernel, "cold", 24, [VMEM], [(VMEM, (devices, heads, *tile), BF16)], [], got
    )
    near, answer = lax.optimization_barrier((near, answer))
    far = [shift(b, "core", 1) for b in near]
    outs = call(
        hot_kernel, "hot", 24, [VMEM] * 12, [(VMEM, (3, *tile), BF16)] * 4,
        [
            pltpu.VMEM((4, 6, *tile), F32), pltpu.VMEM((devices * HOT, hd), BF16),
            pltpu.VMEM((devices * HOT, hd), BF16), pltpu.VMEM((4, 3, *tile), F32),
        ],
        *asked, *near, *far,
    )
    hot_out = [outs[0]] + [shift(b, "y", 3 - d) for d, b in enumerate(outs[1:])]
    back = lax.all_to_all(answer, AXES, split_axis=0, concat_axis=0, tiled=True)
    (result,) = call(
        unpack_kernel, "unpack", 24, [VMEM] * 6, [(VMEM, (tokens, heads * hd), BF16)],
        [pltpu.VMEM((4, 3, *tile), F32)],
        table, back, *hot_out,
    )
    return result


def solution(mesh):
    split = jax.sharding.Mesh(mesh.devices.reshape(4, 2, 4, 4), AXES)
    return jax.shard_map(
        local,
        mesh=split,
        in_specs=(P(AXES, None), P(AXES, None), P(AXES, None), P(None, AXES)),
        out_specs=P(AXES, None),
        check_vma=False,
    )
```

time: 127 us -> 110 us (0.87)
  starting transfers between devices: 45.1 us -> 31.9 us
  local copies, waits for them, and re-layouts: 14.4 us -> 5.16 us
  Pallas kernels: 21.8 us -> 24.3 us
  waiting for transfers between devices: 45.3 us -> 47.6 us
    ppermute x13, starting transfers between devices: 24.2 us -> 13.5 us  [shift(): lax.ppermute(block, axis, [(i, (i + by) % size) for i in range(size)])]
    all_to_all x1, waiting for transfers between devices: 0.01 us -> 7.45 us  [local(): got = lax.all_to_all(send, AXES, split_axis=0, concat_axis=0, tiled=True)]
    unnamed x21 -> x24, local copies, waits for them, and re-layouts: 12.1 us -> 5.16 us
    ppermute x13, waiting for transfers between devices: 42.4 us -> 36.5 us  [shift(): lax.ppermute(block, axis, [(i, (i + by) % size) for i in range(size)])]
    all_to_all x1, starting transfers between devices: 9.71 us -> 7.17 us  [local(): back = lax.all_to_all(answer, AXES, split_axis=0, concat_axis=0, tiled=True)]
    pallas_call x5, Pallas kernels: 21.8 us -> 24.3 us  [call(): pl.pallas_call(kernel, out_shape=tuple((jax.ShapeDtypeStruct(*out[1:]) fo...]
    concatenate x2 -> x0, local copies, waits for them, and re-layouts: 2.3 us -> none  [local(): kv = jnp.concatenate([kv] + [shift(kv, axis, d) for d in (1, 2, 3)], axis=0)]
  transfers between devices with their start and end apart: 15 -> 15, of which waited for: 11 -> 12; matrix products, arithmetic and copies ran while one was open for 5% -> 0% of each run, Pallas kernels for 8% -> 9%
where the time goes in v5:
time: 110 us; the launch traced here: 109 us
  waiting for transfers between devices  47.6 us (43%)
  starting transfers between devices  31.9 us (29%)
  Pallas kernels  24.3 us (22%)
  local copies, waits for them, and re-layouts  5.16 us (5%)
    ppermute x13, waiting for transfers between devices, shift(): lax.ppermute(block, axis, [(i, (i + by) % size) for i in range(size)])  36.5 us
    pallas_call x5, Pallas kernels, call(): pl.pallas_call(kernel, out_shape=tuple((jax.ShapeDtypeStruct(*out[1:]) fo...  24.3 us
    ppermute x13, starting transfers between devices, shift(): lax.ppermute(block, axis, [(i, (i + by) % size) for i in range(size)])  13.5 us
    all_to_all x1, starting transfers between devices, local(): got = lax.all_to_all(send, AXES, split_axis=0, concat_axis=0, tiled=True)  11.2 us
    all_to_all x1, waiting for transfers between devices, local(): got = lax.all_to_all(send, AXES, split_axis=0, concat_axis=0, tiled=True)  7.45 us
    all_to_all x1, starting transfers between devices, local(): back = lax.all_to_all(answer, AXES, split_axis=0, concat_axis=0, tiled=True)  7.17 us
    unnamed x24, local copies, waits for them, and re-layouts  5.16 us
    all_to_all x1, waiting for transfers between devices, local(): back = lax.all_to_all(answer, AXES, split_axis=0, concat_axis=0, tiled=True)  3.66 us
  transfers between devices with their start and end apart: 15, of which 12 were waited for; matrix products, arithmetic and copies ran while one was open for 0% of the time, Pallas kernels for 9%

profile of v5, /device:TPU:0, one launch (start us, length us, event | category | flops | bytes accessed | tf_op | source)
XLA Modules:
  0.0 109.1 jit_solution(12190732732724735960)
XLA Ops:
  0.0 9.9 %pack.1 = (f32[8,1024]{1,0:T(8,128)}, bf16[6,8,128]{2,1,0:T(8,128)(2,1)}, bf16[6,8,128]{2,1,0:T(8,128)(2,1)}, bf16[6,8,128]{2,1,0:T(8,128)(2,1)}, bf16[6,8,128]{...) custom-call(s32[4,1024]{1,0:T(4,128)} %ids_ref.1, bf16[1024,512]{1,0:T(8,128)(2,1)} %q_hbm.1, bf16[1024,512]{1,0:T(8,128)(2,1)} %k_hbm.1, ...), custom_call_target="tpu_custom_call" | custom-call | tf_op jit(solution)/shard_map/pack/pallas_call | solution.py:276
  10.0 11.2 %all-to-all-start = ((bf16[128,13,8,128]{3,2,1,0:T(8,128)(2,1)}), bf16[128,13,8,128]{3,2,1,0:T(8,128)(2,1)S(1)}, u32[]{:S(2)}, u32[]{:S(2)}) async-start(bf16[128,13,8,128]{3,2,1,0:T(8,128)(2,1)} %get-tuple-element.28), calls=%async_computation | async-start | bytes 6815744 | tf_op jit(solution)/shard_map/all_to_all | solution.py:309
  21.1 1.0 collective-permute-start
  22.2 2.7 %collective-permute-start.1 = (bf16[6,8,128]{2,1,0:T(8,128)(2,1)S(1)}, bf16[6,8,128]{2,1,0:T(8,128)(2,1)S(1)}, u32[]{:S(2)}, u32[]{:S(2)}) collective-permute-start(bf16[6,8,128]{2,1,0:T(8,128)(2,1)S(1)} %copy-done.10), channel_id=1, source_target_pairs={{0,2},{1,3},{2,0},{3,1},{4,6},{5,7},{6,4},{7,5},{8,10},{9,11},{10,... | collective-permute-start | bytes 36872 | tf_op jit(solution)/shard_map/ppermute | solution.py:289
  24.9 1.4 %collective-permute-start.2 = (bf16[6,8,128]{2,1,0:T(8,128)(2,1)S(1)}, bf16[6,8,128]{2,1,0:T(8,128)(2,1)S(1)}, u32[]{:S(2)}, u32[]{:S(2)}) collective-permute-start(bf16[6,8,128]{2,1,0:T(8,128)(2,1)S(1)} %copy-done.9), channel_id=1, source_target_pairs={{0,3},{1,0},{2,1},{3,2},{4,7},{5,4},{6,5},{7,6},{8,11},{9,8},{10,9... | collective-permute-start | bytes 36872 | tf_op jit(solution)/shard_map/ppermute | solution.py:289
  26.3 29.7 %collective-permute-done.b1_ref = bf16[6,8,128]{2,1,0:T(8,128)(2,1)S(1)} collective-permute-done((bf16[6,8,128]{2,1,0:T(8,128)(2,1)S(1)}, bf16[6,8,128]{2,1,0:T(8,128)(2,1)S(1)}, u32[]{:S(2)}, u32[]{:S(2)}) %collective-permute-start) | collective-permute-done | bytes 12320 | tf_op jit(solution)/shard_map/ppermute | solution.py:289
  56.0 0.8 collective-permute-done.2.b3_ref
  56.8 7.5 %all-to-all-done.got_ref = bf16[128,13,8,128]{3,2,1,0:T(8,128)(2,1)S(1)} async-done(((bf16[128,13,8,128]{3,2,1,0:T(8,128)(2,1)}), bf16[128,13,8,128]{3,2,1,0:T(8,128)(2,1)S(1)}, u32[]{:S(2)}, u32[]{:S(2)}) %all-to-all-start) | async-done | bytes 3407904 | tf_op jit(solution)/shard_map/all_to_all | solution.py:309
  64.3 1.0 mid.1.n0_ref
  65.3 1.9 %collective-permute-start.5 = (bf16[97,8,128]{2,1,0:T(8,128)(2,1)S(1)}, bf16[97,8,128]{2,1,0:T(8,128)(2,1)S(1)}, u32[]{:S(2)}, u32[]{:S(2)}) collective-permute-start(bf16[97,8,128]{2,1,0:T(8,128)(2,1)S(1)} %mid.1.n0_ref), channel_id=1, source_target_pairs={{0,96},{32,0},{64,32},{96,64},{1,97},{33,1},{65,33},{97,65},{2,98}... | collective-permute-start | bytes 595976 | tf_op jit(solution)/shard_map/ppermute | solution.py:289
  67.1 1.1 %collective-permute-start.4 = (bf16[97,8,128]{2,1,0:T(8,128)(2,1)S(1)}, bf16[97,8,128]{2,1,0:T(8,128)(2,1)S(1)}, u32[]{:S(2)}, u32[]{:S(2)}) collective-permute-start(bf16[97,8,128]{2,1,0:T(8,128)(2,1)S(1)} %mid.1.n0_ref), channel_id=1, source_target_pairs={{0,64},{32,96},{64,0},{96,32},{1,65},{33,97},{65,1},{97,33},{2,66}... | collective-permute-start | bytes 595976 | tf_op jit(solution)/shard_map/ppermute | solution.py:289
  68.2 0.3 collective-permute-start.3
  68.6 7.5 %cold.1 = bf16[128,4,8,128]{3,2,1,0:T(8,128)(2,1)S(1)} custom-call(bf16[128,13,8,128]{3,2,1,0:T(8,128)(2,1)S(1)} %all-to-all-done.got_ref), custom_call_target="tpu_custom_call" | custom-call | tf_op jit(solution)/shard_map/cold/pallas_call | solution.py:276
  76.2 1.0 copy-done
  77.1 0.7 copy-done.3
  77.8 0.7 copy-done.5
  78.5 0.5 collective-permute-done.3.n1_ref
  79.0 7.2 %all-to-all-start.1 = ((bf16[128,4,8,128]{3,2,1,0:T(8,128)(2,1)}), bf16[128,4,8,128]{3,2,1,0:T(8,128)(2,1)S(1)}, u32[]{:S(2)}, u32[]{:S(2)}) async-start(bf16[128,4,8,128]{3,2,1,0:T(8,128)(2,1)} %copy-done), calls=%async_computation.1 | async-start | bytes 2097152 | tf_op jit(solution)/shard_map/all_to_all | solution.py:329
  86.3 0.5 collective-permute-start.7
  86.9 0.4 collective-permute-start.9
  87.3 0.6 collective-permute-done.6.f0_ref
  87.9 0.3 collective-permute-done.7.f1_ref
  88.8 0.9 copy-done.2
  89.7 0.9 copy-done.4
  90.6 0.9 copy-done.6
  91.6 2.0 %hot.1 = (bf16[3,8,128]{2,1,0:T(8,128)(2,1)S(1)}, bf16[3,8,128]{2,1,0:T(8,128)(2,1)S(1)}, bf16[3,8,128]{2,1,0:T(8,128)(2,1)S(1)}, bf16[3,8,128]{2,1,0:T(8,128)(2,1)S(1)}) custom-call(bf16[6,8,128]{2,1,0:T(8,128)(2,1)S(1)} %copy-done.8, bf16[6,8,128]{2,1,0:T(8,128)(2,1)S(1)} %collective-permute-done.b1_ref, ...), custom_call_target="tpu_custom_call" | custom-call | tf_op jit(solution)/shard_map/hot/pallas_call | solution.py:276
  93.6 2.3 %collective-permute-start.10 = (bf16[3,8,128]{2,1,0:T(8,128)(2,1)S(1)}, bf16[3,8,128]{2,1,0:T(8,128)(2,1)S(1)}, u32[]{:S(2)}, u32[]{:S(2)}) collective-permute-start(bf16[3,8,128]{2,1,0:T(8,128)(2,1)S(1)} %get-tuple-element.46), channel_id=1, source_target_pairs={{0,3},{1,0},{2,1},{3,2},{4,7},{5,4},{6,5},{7,6},{8,11},{9,8},{10,9... | collective-permute-start | bytes 18440 | tf_op jit(solution)/shard_map/ppermute | solution.py:289
  95.9 0.8 collective-permute-start.11
  96.7 0.9 collective-permute-start.12
  97.7 3.7 %collective-permute-done.11.o2_ref = bf16[3,8,128]{2,1,0:T(8,128)(2,1)S(1)} collective-permute-done((bf16[3,8,128]{2,1,0:T(8,128)(2,1)S(1)}, bf16[3,8,128]{2,1,0:T(8,128)(2,1)S(1)}, u32[]{:S(2)}, u32[]{:S(2)}) %collective-permute-start.11) | collective-permute-done | bytes 6176 | tf_op jit(solution)/shard_map/ppermute | solution.py:289
  101.6 3.7 %all-to-all-done.1.back_ref = bf16[128,4,8,128]{3,2,1,0:T(8,128)(2,1)S(1)} async-done(((bf16[128,4,8,128]{3,2,1,0:T(8,128)(2,1)}), bf16[128,4,8,128]{3,2,1,0:T(8,128)(2,1)S(1)}, u32[]{:S(2)}, u32[]{:S(2)}) %all-to-all-start.1) | async-done | bytes 1048608 | tf_op jit(solution)/shard_map/all_to_all | solution.py:329
  105.2 3.9 %unpack.1 = bf16[1024,512]{1,0:T(8,128)(2,1)} custom-call(f32[8,1024]{1,0:T(8,128)S(1)} %copy-done.7, bf16[128,4,8,128]{3,2,1,0:T(8,128)(2,1)S(1)} %all-to-all-done.1.back_ref, bf16[3,8,128]{2,1,0:T(8,128)(2,1)S(1)} %get-tuple-element.45.o0_ref, bf16[3,8,128]{2,1,0:T(8,128)(2,1)S(1)} %collective-permute-done.10.o1_ref, ...), custom_call_target="tpu_custom_call" | custom-call | tf_op jit(solution)/shard_map/unpack/pallas_call | solution.py:276
  (27 shorter events, 1.1 us)
Async XLA Ops:
  9.9 11.2 %copy-start.11 = (bf16[6,8,128]{2,1,0:T(8,128)(2,1)S(1)}, bf16[6,8,128]{2,1,0:T(8,128)(2,1)}, u32[]{:S(2)}) copy-start(bf16[6,8,128]{2,1,0:T(8,128)(2,1)} %get-tuple-element.30) | copy-start | bytes 36868
  10.0 12.2 %copy-start.10 = (bf16[6,8,128]{2,1,0:T(8,128)(2,1)S(1)}, bf16[6,8,128]{2,1,0:T(8,128)(2,1)}, u32[]{:S(2)}) copy-start(bf16[6,8,128]{2,1,0:T(8,128)(2,1)} %get-tuple-element.31) | copy-start | bytes 36868
  10.0 14.9 %copy-start.9 = (bf16[6,8,128]{2,1,0:T(8,128)(2,1)S(1)}, bf16[6,8,128]{2,1,0:T(8,128)(2,1)}, u32[]{:S(2)}) copy-start(bf16[6,8,128]{2,1,0:T(8,128)(2,1)} %get-tuple-element.32) | copy-start | bytes 36868
  10.0 54.3 %all-to-all-start = ((bf16[128,13,8,128]{3,2,1,0:T(8,128)(2,1)}), bf16[128,13,8,128]{3,2,1,0:T(8,128)(2,1)S(1)}, u32[]{:S(2)}, u32[]{:S(2)}) async-start(bf16[128,13,8,128]{3,2,1,0:T(8,128)(2,1)} %get-tuple-element.28), calls=%async_computation | async-start | bytes 6815744 | tf_op jit(solution)/shard_map/all_to_all | solution.py:309
  21.1 34.8 %collective-permute-start = (bf16[6,8,128]{2,1,0:T(8,128)(2,1)S(1)}, bf16[6,8,128]{2,1,0:T(8,128)(2,1)S(1)}, u32[]{:S(2)}, u32[]{:S(2)}) collective-permute-start(bf16[6,8,128]{2,1,0:T(8,128)(2,1)S(1)} %copy-done.11), channel_id=1, source_target_pairs={{0,1},{1,2},{2,3},{3,0},{4,5},{5,6},{6,7},{7,4},{8,9},{9,10},{10,1... | collective-permute-start | bytes 36872 | tf_op jit(solution)/shard_map/ppermute | solution.py:289
  22.2 33.8 %collective-permute-start.1 = (bf16[6,8,128]{2,1,0:T(8,128)(2,1)S(1)}, bf16[6,8,128]{2,1,0:T(8,128)(2,1)S(1)}, u32[]{:S(2)}, u32[]{:S(2)}) collective-permute-start(bf16[6,8,128]{2,1,0:T(8,128)(2,1)S(1)} %copy-done.10), channel_id=1, source_target_pairs={{0,2},{1,3},{2,0},{3,1},{4,6},{5,7},{6,4},{7,5},{8,10},{9,11},{10,... | collective-permute-start | bytes 36872 | tf_op jit(solution)/shard_map/ppermute | solution.py:289
  24.9 31.9 %collective-permute-start.2 = (bf16[6,8,128]{2,1,0:T(8,128)(2,1)S(1)}, bf16[6,8,128]{2,1,0:T(8,128)(2,1)S(1)}, u32[]{:S(2)}, u32[]{:S(2)}) collective-permute-start(bf16[6,8,128]{2,1,0:T(8,128)(2,1)S(1)} %copy-done.9), channel_id=1, source_target_pairs={{0,3},{1,0},{2,1},{3,2},{4,7},{5,4},{6,5},{7,6},{8,11},{9,8},{10,9... | collective-permute-start | bytes 36872 | tf_op jit(solution)/shard_map/ppermute | solution.py:289
  65.2 10.9 %copy-start.1 = (bf16[97,8,128]{2,1,0:T(8,128)(2,1)}, bf16[97,8,128]{2,1,0:T(8,128)(2,1)S(1)}, u32[]{:S(2)}) copy-start(bf16[97,8,128]{2,1,0:T(8,128)(2,1)S(1)} %mid.1.n0_ref) | copy-start | bytes 595972
  65.2 23.5 %copy-start.8 = (bf16[6,8,128]{2,1,0:T(8,128)(2,1)S(1)}, bf16[6,8,128]{2,1,0:T(8,128)(2,1)}, u32[]{:S(2)}) copy-start(bf16[6,8,128]{2,1,0:T(8,128)(2,1)} %get-tuple-element.37.b0_ref) | copy-start | bytes 36868
  65.2 40.0 %copy-start.7 = (f32[8,1024]{1,0:T(8,128)S(1)}, f32[8,1024]{1,0:T(8,128)}, u32[]{:S(2)}) copy-start(f32[8,1024]{1,0:T(8,128)} %get-tuple-element.27.table_ref) | copy-start | bytes 98308
  65.3 11.8 %collective-permute-start.5 = (bf16[97,8,128]{2,1,0:T(8,128)(2,1)S(1)}, bf16[97,8,128]{2,1,0:T(8,128)(2,1)S(1)}, u32[]{:S(2)}, u32[]{:S(2)}) collective-permute-start(bf16[97,8,128]{2,1,0:T(8,128)(2,1)S(1)} %mid.1.n0_ref), channel_id=1, source_target_pairs={{0,96},{32,0},{64,32},{96,64},{1,97},{33,1},{65,33},{97,65},{2,98}... | collective-permute-start | bytes 595976 | tf_op jit(solution)/shard_map/ppermute | solution.py:289
  67.1 10.0 %collective-permute-start.4 = (bf16[97,8,128]{2,1,0:T(8,128)(2,1)S(1)}, bf16[97,8,128]{2,1,0:T(8,128)(2,1)S(1)}, u32[]{:S(2)}, u32[]{:S(2)}) collective-permute-start(bf16[97,8,128]{2,1,0:T(8,128)(2,1)S(1)} %mid.1.n0_ref), channel_id=1, source_target_pairs={{0,64},{32,96},{64,0},{96,32},{1,65},{33,97},{65,1},{97,33},{2,66}... | collective-permute-start | bytes 595976 | tf_op jit(solution)/shard_map/ppermute | solution.py:289
  68.2 10.8 %collective-permute-start.3 = (bf16[97,8,128]{2,1,0:T(8,128)(2,1)S(1)}, bf16[97,8,128]{2,1,0:T(8,128)(2,1)}, u32[]{:S(2)}, u32[]{:S(2)}) collective-permute-start(bf16[97,8,128]{2,1,0:T(8,128)(2,1)S(1)} %mid.1.n0_ref), channel_id=1, source_target_pairs={{0,32},{32,64},{64,96},{96,0},{1,33},{33,65},{65,97},{97,1},{2,34}... | collective-permute-start | bytes 595976 | tf_op jit(solution)/shard_map/ppermute | solution.py:289
  76.1 1.0 copy-start
  77.1 0.7 copy-start.3
  77.8 0.7 copy-start.5
  79.0 26.2 %all-to-all-start.1 = ((bf16[128,4,8,128]{3,2,1,0:T(8,128)(2,1)}), bf16[128,4,8,128]{3,2,1,0:T(8,128)(2,1)S(1)}, u32[]{:S(2)}, u32[]{:S(2)}) async-start(bf16[128,4,8,128]{3,2,1,0:T(8,128)(2,1)} %copy-done), calls=%async_computation.1 | async-start | bytes 2097152 | tf_op jit(solution)/shard_map/all_to_all | solution.py:329
  86.2 1.7 %collective-permute-start.6 = (bf16[97,8,128]{2,1,0:T(8,128)(2,1)}, bf16[97,8,128]{2,1,0:T(8,128)(2,1)S(1)}, u32[]{:S(2)}, u32[]{:S(2)}) collective-permute-start(bf16[97,8,128]{2,1,0:T(8,128)(2,1)} %copy-done.1), channel_id=1, source_target_pairs={{0,16},{16,0},{1,17},{17,1},{2,18},{18,2},{3,19},{19,3},{4,20},{20... | collective-permute-start | bytes 595976 | tf_op jit(solution)/shard_map/ppermute | solution.py:289
  86.3 1.9 %collective-permute-start.7 = (bf16[97,8,128]{2,1,0:T(8,128)(2,1)}, bf16[97,8,128]{2,1,0:T(8,128)(2,1)S(1)}, u32[]{:S(2)}, u32[]{:S(2)}) collective-permute-start(bf16[97,8,128]{2,1,0:T(8,128)(2,1)} %collective-permute-done.3.n1_ref), channel_id=1, source_target_pairs={{0,16},{16,0},{1,17},{17,1},{2,18},{18,2},{3,19},{19,3},{4,20},{20... | collective-permute-start | bytes 595976 | tf_op jit(solution)/shard_map/ppermute | solution.py:289
  86.8 1.7 %collective-permute-start.8 = (bf16[97,8,128]{2,1,0:T(8,128)(2,1)}, bf16[97,8,128]{2,1,0:T(8,128)(2,1)S(1)}, u32[]{:S(2)}, u32[]{:S(2)}) collective-permute-start(bf16[97,8,128]{2,1,0:T(8,128)(2,1)} %copy-done.5), channel_id=1, source_target_pairs={{0,16},{16,0},{1,17},{17,1},{2,18},{18,2},{3,19},{19,3},{4,20},{20... | collective-permute-start | bytes 595976 | tf_op jit(solution)/shard_map/ppermute | solution.py:289
  86.9 1.9 %collective-permute-start.9 = (bf16[97,8,128]{2,1,0:T(8,128)(2,1)}, bf16[97,8,128]{2,1,0:T(8,128)(2,1)S(1)}, u32[]{:S(2)}, u32[]{:S(2)}) collective-permute-start(bf16[97,8,128]{2,1,0:T(8,128)(2,1)} %copy-done.3), channel_id=1, source_target_pairs={{0,16},{16,0},{1,17},{17,1},{2,18},{18,2},{3,19},{19,3},{4,20},{20... | collective-permute-start | bytes 595976 | tf_op jit(solution)/shard_map/ppermute | solution.py:289
  88.8 0.9 copy-start.2
  89.7 0.9 copy-start.4
  90.6 0.9 copy-start.6
  93.6 4.1 %collective-permute-start.10 = (bf16[3,8,128]{2,1,0:T(8,128)(2,1)S(1)}, bf16[3,8,128]{2,1,0:T(8,128)(2,1)S(1)}, u32[]{:S(2)}, u32[]{:S(2)}) collective-permute-start(bf16[3,8,128]{2,1,0:T(8,128)(2,1)S(1)} %get-tuple-element.46), channel_id=1, source_target_pairs={{0,3},{1,0},{2,1},{3,2},{4,7},{5,4},{6,5},{7,6},{8,11},{9,8},{10,9... | collective-permute-start | bytes 18440 | tf_op jit(solution)/shard_map/ppermute | solution.py:289
  95.9 5.5 %collective-permute-start.11 = (bf16[3,8,128]{2,1,0:T(8,128)(2,1)S(1)}, bf16[3,8,128]{2,1,0:T(8,128)(2,1)S(1)}, u32[]{:S(2)}, u32[]{:S(2)}) collective-permute-start(bf16[3,8,128]{2,1,0:T(8,128)(2,1)S(1)} %get-tuple-element.47), channel_id=1, source_target_pairs={{0,2},{1,3},{2,0},{3,1},{4,6},{5,7},{6,4},{7,5},{8,10},{9,11},{10,... | collective-permute-start | bytes 18440 | tf_op jit(solution)/shard_map/ppermute | solution.py:289
  96.7 4.9 %collective-permute-start.12 = (bf16[3,8,128]{2,1,0:T(8,128)(2,1)S(1)}, bf16[3,8,128]{2,1,0:T(8,128)(2,1)S(1)}, u32[]{:S(2)}, u32[]{:S(2)}) collective-permute-start(bf16[3,8,128]{2,1,0:T(8,128)(2,1)S(1)} %get-tuple-element.48), channel_id=1, source_target_pairs={{0,1},{1,2},{2,3},{3,0},{4,5},{5,6},{6,7},{7,4},{8,9},{9,10},{10,1... | collective-permute-start | bytes 18440 | tf_op jit(solution)/shard_map/ppermute | solution.py:289

commit v6 on v5

--- a/solution.py
+++ b/solution.py
@@ -12,7 +12,9 @@
 LANES = 128
 NEG_FILL = -1e30
 SHARE = 3
-HOT_LANE = 64
+HOT_LANE = 32
+MARK_Q = 104.0
+MARK_K = 100.0
 LOG2E = 1.4426950408889634
 F32 = jnp.float32
 BF16 = jnp.bfloat16
@@ -50,7 +52,7 @@
     tags = (ids - owner * CL_DEV + 1).astype(F32)
     upper = (iota((step, step), 0) < iota((step, step), 1)).astype(BF16)
     dev_col = iota((devices, step), 0)
-    slot_rows, hot_ranks = [], []
+    slot_rows = []
     labels = jnp.zeros((devices, LANES), F32)
     for h in range(heads):
         carry = jnp.zeros((devices, 1), F32)
@@ -66,7 +68,9 @@
             ranks[b] = jnp.where(
                 jnp.sum(one * full, axis=0, keepdims=True) > 0.5, ranks[b] + slots, ranks[b]
             )
-            lane = jnp.where(ranks[b] < COLD, ranks[b] + COLD * h, -1.0).astype(jnp.int32)
+            lane = jnp.where(
+                ranks[b] < COLD, ranks[b] + COLD * h, ranks[b] + (HOT_LANE + HOT * h - slots)
+            ).astype(jnp.int32)
             tag = jnp.where(
                 lane == iota((LANES, step), 0), tags[h : h + 1, b * step : (b + 1) * step], 0.0
             )
@@ -75,43 +79,38 @@
             )
         rank = jnp.concatenate(ranks, axis=1).astype(jnp.int32)
         slot_rows.append(jnp.where(rank >= slots, rank, owner[h : h + 1] * COLD + rank))
-        hot_ranks.append(jnp.where(rank >= slots, rank - slots, -SHARE))
     slot_all = jnp.concatenate(slot_rows, axis=0)
     table_ref[...] = jnp.concatenate([slot_all.astype(F32), tags], axis=0)
-    shares = HOT // SHARE
-    rows = shares * COLD
-    row = iota((rows, 1), 0)
+    asked_tags = jnp.sum(labels, axis=0, keepdims=True)
+    cold_lane = iota((1, LANES), 1) < HOT_LANE
+    for h in range(heads):
+        own = iota((HOT, LANES), 1) == iota((HOT, LANES), 0) + (HOT_LANE + HOT * h)
+        tag = jnp.sum(jnp.where(own, asked_tags, 0.0), axis=1, keepdims=True)
+        hot_ref[h, 3:6] = jnp.broadcast_to(tag, (HOT, hd)).reshape(3, COLD, hd).astype(BF16)
+    rows = HOT // SHARE * COLD
+    row = iota((rows + HOT_PAD, 1), 0)
     row_share, row_at = row // COLD, row % COLD
-    want_k = jnp.where(row_at < SHARE, SHARE * row_share + row_at, -9)
-    want_v = jnp.where(
-        (row_at >= SHARE) & (row_at < 2 * SHARE), SHARE * (row_share - 1) + row_at, -9
-    )
-    want_tag = jnp.where(row_at == 2 * SHARE, row_share, -9)
+    want = jnp.where(row_at < SHARE, SHARE * row_share + row_at, SHARE * (row_share - 1) + row_at)
+    want = jnp.where(row_at < 2 * SHARE, want, -9)
+    want = jnp.where(row < rows, want, row - rows) + slots
+    tile_at = iota((rows, hd), 0) % COLD
     for load in loads:
         load.wait()
     hot_tiles = []
     for h in range(heads):
-        cols = slice(h * hd, (h + 1) * hd)
         for j, ref in enumerate((q_ref, k_ref, v_ref)):
-            x_ref[h, :, j * hd : (j + 1) * hd] = ref[:, cols]
-        hot = hot_ranks[h]
-        tag_rows = jnp.broadcast_to(tags[h : h + 1], (LANES, tokens))
-        share = (hot + SHARE) // SHARE - 1
-        lane_tag = jnp.where(iota((LANES, tokens), 0) == HOT_LANE + hot - SHARE * share, tag_rows, 0.0)
-        tiles = lax.dot_general(
-            (share == want_tag).astype(BF16), lane_tag.astype(BF16), NT, preferred_element_type=F32
+            x_ref[h, :, j * hd : (j + 1) * hd] = ref[:, h * hd : (h + 1) * hd]
+        moved = jnp.dot(
+            (slot_all[h : h + 1] == want).astype(BF16), x_ref[h], preferred_element_type=F32
         )
-        tiles = tiles + jnp.dot((hot == want_k).astype(BF16), k_ref[:, cols], preferred_element_type=F32)
-        tiles = tiles + jnp.dot((hot == want_v).astype(BF16), v_ref[:, cols], preferred_element_type=F32)
+        tiles = jnp.where(tile_at < SHARE, moved[:rows, hd : 2 * hd], moved[:rows, 2 * hd :])
+        tiles = jnp.where(tile_at == COLD - 1, asked_tags, tiles)
         hot_tiles.append(tiles)
-        place = (hot == iota((HOT_PAD, tokens), 0)).astype(BF16)
-        asked = jnp.dot(place, q_ref[:, cols], preferred_element_type=F32)
-        asked_tags = lax.dot_general(place, tag_rows.astype(BF16), NT, preferred_element_type=F32)
-        hot_ref[h, 0:3] = asked[:HOT].reshape(3, COLD, hd).astype(BF16)
-        hot_ref[h, 3:6] = asked_tags[:HOT].reshape(3, COLD, hd).astype(BF16)
+        hot_ref[h, 0:3] = moved[rows : rows + HOT, :hd].reshape(3, COLD, hd).astype(BF16)
     y = lax.axis_index("y")
     for d, ref in enumerate((h0_ref, h1_ref, h2_ref, h3_ref)):
         ref[...] = hot_ref[lax.rem(y + d, heads)]
+    labels = jnp.where(cold_lane, labels, 0.0)
     part = 256
     sub = iota((COLD, LANES), 0)
     sent = []
@@ -127,7 +126,7 @@
         for dev in range(first, stop):
             share, head = dev // 16, dev % heads
             tile = hot_tiles[head][share * COLD : (share + 1) * COLD]
-            tile = jnp.where(sub == 2 * SHARE, tile + labels[dev : dev + 1], tile)
+            tile = jnp.where(sub == 2 * SHARE, labels[dev : dev + 1], tile)
             send_ref[dev, 3 * heads] = tile.astype(BF16)
         out = pltpu.make_async_copy(
             send_ref.at[first:stop], send_hbm.at[first:stop], out_sems.at[c]
@@ -161,24 +160,29 @@
     ).reshape(slots, LANES)
     pick = iota((slots, LANES), 1) - iota((slots, LANES), 0) % COLD
     ones = jnp.ones((LANES, LANES), BF16)
-    part = 256
+    part = 512
     causal = iota((part, part), 1) <= iota((part, part), 0)
     for h in range(heads):
         tags = jnp.where(pick == COLD * h, spread, 0.0).astype(BF16)
         label_cols = jnp.dot(tags, ones, preferred_element_type=F32)
-        label_rows = lax.dot_general(ones[:COLD], tags, NT, preferred_element_type=F32)
         q, k, v = (
             got_ref[:, 3 * h + j].astype(F32).reshape(slots, hd).astype(BF16) for j in range(3)
         )
+        marked = label_cols == (iota((slots, LANES), 1) + 1).astype(F32)
+        q = jnp.concatenate([q, jnp.where(marked, MARK_Q, 0.0).astype(BF16)], axis=1)
+        k = jnp.concatenate([k, jnp.where(marked, MARK_K, 0.0).astype(BF16)], axis=1)
         for c in range(slots // part):
             stop = (c + 1) * part
             scores = lax.dot_general(
                 q[c * part : stop], k[:stop], NT, preferred_element_type=F32
             )
-            allowed = label_cols[c * part : stop, :1] == label_rows[:1, :stop]
-            last = allowed[:, c * part :] & causal
-            allowed = last if c == 0 else jnp.concatenate([allowed[:, : c * part], last], axis=1)
-            out = softmax_rows(scores, allowed, scale, v[:stop])
+            last = jnp.where(causal, scores[:, c * part :], NEG_FILL)
+            if c > 0:
+                last = jnp.concatenate([scores[:, : c * part], last], axis=1)
+            top = jnp.max(last, axis=1, keepdims=True)
+            weights = jnp.exp2((last - top) * scale)
+            total = jnp.sum(weights, axis=1, keepdims=True)
+            out = jnp.dot(weights.astype(BF16), v[:stop], preferred_element_type=F32) / total
             devs = slice(c * part // COLD, stop // COLD)
             out_ref[devs, h] = out.reshape(part // COLD, COLD, hd).astype(BF16)
 
@@ -198,7 +202,9 @@
 
     kv_ref[0:48] = rows_at(at).reshape(48, COLD, hd).astype(BF16)
     kv_ref[48:96] = rows_at(at + SHARE).reshape(48, COLD, hd).astype(BF16)
-    tags = jnp.where(iota((keys, hd), 1) == HOT_LANE + at, rows_at(2 * SHARE), 0.0).astype(BF16)
+    y, core, z = (lax.axis_index(a) for a in ("y", "core", "z"))
+    lane = HOT_LANE + HOT * y + SHARE * (z * 2 + core) + at
+    tags = jnp.where(iota((keys, hd), 1) == lane, rows_at(COLD - 1), 0.0).astype(BF16)
     flat = lax.dot_general(jnp.ones((COLD, hd), BF16), tags, NT, preferred_element_type=F32)
     label = [flat[0:1, j * LANES : (j + 1) * LANES] for j in range(keys // LANES)]
     label.append(jnp.zeros((COLD - len(label), LANES), F32))
@@ -206,7 +212,7 @@
 
 
 def hot_kernel(
-    b0_ref, b1_ref, b2_ref, b3_ref, n0_ref, n1_ref, n2_ref, n3_ref, f0_ref, f1_ref, f2_ref, f3_ref,
+    b0_ref, b1_ref, b2_ref, b3_ref, near_ref, far_ref,
     o0_ref, o1_ref, o2_ref, o3_ref, all_ref, k_ref, v_ref, o_ref,
 ):
     hd = b0_ref.shape[-1]
@@ -223,15 +229,14 @@
     n = iota((1, keys), 1)
     key_at = (n // SHARE) * HOT + n % SHARE
     allowed = []
-    blocks = ((n0_ref, n1_ref, n2_ref, n3_ref), (f0_ref, f1_ref, f2_ref, f3_ref))
-    for dc in range(2):
+    for dc, ref in enumerate((near_ref, far_ref)):
         for dz in range(4):
-            ref = blocks[dc][dz]
+            tile = 97 * dz
             at = slice((dc * 4 + dz) * keys, (dc * 4 + dz + 1) * keys)
-            k_ref[at] = ref[0:48].astype(F32).reshape(keys, hd).astype(BF16)
-            v_ref[at] = ref[48:96].astype(F32).reshape(keys, hd).astype(BF16)
-            tile = ref[96].astype(F32)
-            label = jnp.concatenate([tile[j : j + 1] for j in range(keys // LANES)], axis=1)
+            k_ref[at] = ref[tile : tile + 48].astype(F32).reshape(keys, hd).astype(BF16)
+            v_ref[at] = ref[tile + 48 : tile + 96].astype(F32).reshape(keys, hd).astype(BF16)
+            tags = ref[tile + 96].astype(F32)
+            label = jnp.concatenate([tags[j : j + 1] for j in range(keys // LANES)], axis=1)
             share = lax.rem(z + 4 - dz, 4) * 2 + lax.rem(core + dc, 2)
             there = (key_at + SHARE * share).astype(F32)
             allowed.append((label_col == label) & (there <= asked_at))
@@ -316,14 +321,15 @@
         cold_kernel, "cold", 24, [VMEM], [(VMEM, (devices, heads, *tile), BF16)], [], got
     )
     near, answer = lax.optimization_barrier((near, answer))
-    far = [shift(b, "core", 1) for b in near]
+    near = jnp.concatenate(near, axis=0)
+    far = shift(near, "core", 1)
     outs = call(
-        hot_kernel, "hot", 24, [VMEM] * 12, [(VMEM, (3, *tile), BF16)] * 4,
+        hot_kernel, "hot", 24, [VMEM] * 6, [(VMEM, (3, *tile), BF16)] * 4,
         [
             pltpu.VMEM((4, 6, *tile), F32), pltpu.VMEM((devices * HOT, hd), BF16),
             pltpu.VMEM((devices * HOT, hd), BF16), pltpu.VMEM((4, 3, *tile), F32),
         ],
-        *asked, *near, *far,
+        *asked, near, far,
     )
     hot_out = [outs[0]] + [shift(b, "y", 3 - d) for d, b in enumerate(outs[1:])]
     back = lax.all_to_all(answer, AXES, split_axis=0, concat_axis=0, tiled=True)

time: 110 us -> 107 us (0.973)
  waiting for transfers between devices: 47.6 us -> 52.4 us
  Pallas kernels: 24.3 us -> 21.1 us
  starting transfers between devices: 31.9 us -> 28.8 us
    ppermute x13 -> x10, waiting for transfers between devices: 36.5 us -> 40.6 us  [shift(): lax.ppermute(block, axis, [(i, (i + by) % size) for i in range(size)])]
    pallas_call x5, Pallas kernels: 24.3 us -> 21.1 us  [call(): pl.pallas_call(kernel, out_shape=tuple((jax.ShapeDtypeStruct(*out[1:]) fo...]
    all_to_all x1, starting transfers between devices: 7.17 us -> 5.1 us  [local(): back = lax.all_to_all(answer, AXES, split_axis=0, concat_axis=0, tiled=True)]
    ppermute x13 -> x10, starting transfers between devices: 13.5 us -> 12.5 us  [shift(): lax.ppermute(block, axis, [(i, (i + by) % size) for i in range(size)])]
    unnamed x24 -> x23, local copies, waits for them, and re-layouts: 5.16 us -> 4.54 us
  transfers between devices with their start and end apart: 15 -> 12, of which waited for: 12 -> 9; matrix products, arithmetic and copies ran while one was open for 0% -> 3% of each run, Pallas kernels for 9% -> 6%
where the time goes in v6:
time: 107 us
  waiting for transfers between devices  52.4 us (49%)
  starting transfers between devices  28.8 us (27%)
  Pallas kernels  21.1 us (20%)
  local copies, waits for them, and re-layouts  4.57 us (4%)
    ppermute x10, waiting for transfers between devices, shift(): lax.ppermute(block, axis, [(i, (i + by) % size) for i in range(size)])  40.6 us
    pallas_call x5, Pallas kernels, call(): pl.pallas_call(kernel, out_shape=tuple((jax.ShapeDtypeStruct(*out[1:]) fo...  21.1 us
    ppermute x10, starting transfers between devices, shift(): lax.ppermute(block, axis, [(i, (i + by) % size) for i in range(size)])  12.5 us
    all_to_all x1, starting transfers between devices, local(): got = lax.all_to_all(send, AXES, split_axis=0, concat_axis=0, tiled=True)  11.1 us
    all_to_all x1, waiting for transfers between devices, local(): got = lax.all_to_all(send, AXES, split_axis=0, concat_axis=0, tiled=True)  7.45 us
    all_to_all x1, starting transfers between devices, local(): back = lax.all_to_all(answer, AXES, split_axis=0, concat_axis=0, tiled=True)  5.1 us
    unnamed x23, local copies, waits for them, and re-layouts  4.54 us
    all_to_all x1, waiting for transfers between devices, local(): back = lax.all_to_all(answer, AXES, split_axis=0, concat_axis=0, tiled=True)  4.36 us
  transfers between devices with their start and end apart: 12, of which 9 were waited for; matrix products, arithmetic and copies ran while one was open for 3% of the time, Pallas kernels for 6%

profile of v6, /device:TPU:0, one launch (start us, length us, event | category | flops | bytes accessed | tf_op | source)
XLA Modules:
  0.0 106.9 jit_solution(4939763911336452971)
XLA Ops:
  0.0 9.8 %pack.1 = (f32[8,1024]{1,0:T(8,128)}, bf16[6,8,128]{2,1,0:T(8,128)(2,1)}, bf16[6,8,128]{2,1,0:T(8,128)(2,1)}, bf16[6,8,128]{2,1,0:T(8,128)(2,1)}, bf16[6,8,128]{...) custom-call(s32[4,1024]{1,0:T(4,128)} %ids_ref.1, bf16[1024,512]{1,0:T(8,128)(2,1)} %q_hbm.1, bf16[1024,512]{1,0:T(8,128)(2,1)} %k_hbm.1, ...), custom_call_target="tpu_custom_call" | custom-call | tf_op jit(solution)/shard_map/pack/pallas_call | solution.py:281
  9.8 0.0 copy-start.9
  9.8 11.1 %all-to-all-start = ((bf16[128,13,8,128]{3,2,1,0:T(8,128)(2,1)}), bf16[128,13,8,128]{3,2,1,0:T(8,128)(2,1)S(1)}, u32[]{:S(2)}, u32[]{:S(2)}) async-start(bf16[128,13,8,128]{3,2,1,0:T(8,128)(2,1)} %get-tuple-element.28), calls=%async_computation | async-start | bytes 6815744 | tf_op jit(solution)/shard_map/all_to_all | solution.py:314
  21.0 1.0 collective-permute-start
  22.0 2.7 %collective-permute-start.1 = (bf16[6,8,128]{2,1,0:T(8,128)(2,1)S(1)}, bf16[6,8,128]{2,1,0:T(8,128)(2,1)S(1)}, u32[]{:S(2)}, u32[]{:S(2)}) collective-permute-start(bf16[6,8,128]{2,1,0:T(8,128)(2,1)S(1)} %copy-done.8), channel_id=1, source_target_pairs={{0,2},{1,3},{2,0},{3,1},{4,6},{5,7},{6,4},{7,5},{8,10},{9,11},{10,... | collective-permute-start | bytes 36872 | tf_op jit(solution)/shard_map/ppermute | solution.py:294
  24.8 1.4 %collective-permute-start.2 = (bf16[6,8,128]{2,1,0:T(8,128)(2,1)S(1)}, bf16[6,8,128]{2,1,0:T(8,128)(2,1)S(1)}, u32[]{:S(2)}, u32[]{:S(2)}) collective-permute-start(bf16[6,8,128]{2,1,0:T(8,128)(2,1)S(1)} %copy-done.7), channel_id=1, source_target_pairs={{0,3},{1,0},{2,1},{3,2},{4,7},{5,4},{6,5},{7,6},{8,11},{9,8},{10,9... | collective-permute-start | bytes 36872 | tf_op jit(solution)/shard_map/ppermute | solution.py:294
  26.2 29.7 %collective-permute-done.b1_ref = bf16[6,8,128]{2,1,0:T(8,128)(2,1)S(1)} collective-permute-done((bf16[6,8,128]{2,1,0:T(8,128)(2,1)S(1)}, bf16[6,8,128]{2,1,0:T(8,128)(2,1)S(1)}, u32[]{:S(2)}, u32[]{:S(2)}) %collective-permute-start) | collective-permute-done | bytes 12320 | tf_op jit(solution)/shard_map/ppermute | solution.py:294
  55.8 0.8 collective-permute-done.2.b3_ref
  56.7 7.5 %all-to-all-done.got_ref = bf16[128,13,8,128]{3,2,1,0:T(8,128)(2,1)S(1)} async-done(((bf16[128,13,8,128]{3,2,1,0:T(8,128)(2,1)}), bf16[128,13,8,128]{3,2,1,0:T(8,128)(2,1)S(1)}, u32[]{:S(2)}, u32[]{:S(2)}) %all-to-all-start) | async-done | bytes 3407904 | tf_op jit(solution)/shard_map/all_to_all | solution.py:314
  64.1 1.0 mid.1
  65.1 1.9 %collective-permute-start.5 = (bf16[97,8,128]{2,1,0:T(8,128)(2,1)S(1)}, bf16[97,8,128]{2,1,0:T(8,128)(2,1)S(1)}, u32[]{:S(2)}, u32[]{:S(2)}) collective-permute-start(bf16[97,8,128]{2,1,0:T(8,128)(2,1)S(1)} %mid.1), channel_id=1, source_target_pairs={{0,96},{32,0},{64,32},{96,64},{1,97},{33,1},{65,33},{97,65},{2,98}... | collective-permute-start | bytes 595976 | tf_op jit(solution)/shard_map/ppermute | solution.py:294
  67.0 1.1 %collective-permute-start.4 = (bf16[97,8,128]{2,1,0:T(8,128)(2,1)S(1)}, bf16[97,8,128]{2,1,0:T(8,128)(2,1)S(1)}, u32[]{:S(2)}, u32[]{:S(2)}) collective-permute-start(bf16[97,8,128]{2,1,0:T(8,128)(2,1)S(1)} %mid.1), channel_id=1, source_target_pairs={{0,64},{32,96},{64,0},{96,32},{1,65},{33,97},{65,1},{97,33},{2,66}... | collective-permute-start | bytes 595976 | tf_op jit(solution)/shard_map/ppermute | solution.py:294
  68.1 0.3 collective-permute-start.3
  68.4 5.3 %cold.1 = bf16[128,4,8,128]{3,2,1,0:T(8,128)(2,1)S(1)} custom-call(bf16[128,13,8,128]{3,2,1,0:T(8,128)(2,1)S(1)} %all-to-all-done.got_ref), custom_call_target="tpu_custom_call" | custom-call | tf_op jit(solution)/shard_map/cold/pallas_call | solution.py:281
  73.8 1.0 copy-done
  74.7 1.7 %collective-permute-done.4 = bf16[97,8,128]{2,1,0:T(8,128)(2,1)S(1)} collective-permute-done((bf16[97,8,128]{2,1,0:T(8,128)(2,1)S(1)}, bf16[97,8,128]{2,1,0:T(8,128)(2,1)S(1)}, u32[]{:S(2)}, u32[]{:S(2)}) %collective-permute-start.4) | collective-permute-done | bytes 198688 | tf_op jit(solution)/shard_map/ppermute | solution.py:294
  76.4 0.7 copy-done.6
  77.1 1.7 %collective-permute-done.3 = bf16[97,8,128]{2,1,0:T(8,128)(2,1)} collective-permute-done((bf16[97,8,128]{2,1,0:T(8,128)(2,1)S(1)}, bf16[97,8,128]{2,1,0:T(8,128)(2,1)}, u32[]{:S(2)}, u32[]{:S(2)}) %collective-permute-start.3) | collective-permute-done | bytes 198688 | tf_op jit(solution)/shard_map/ppermute | solution.py:294
  78.8 5.1 %all-to-all-start.1 = ((bf16[128,4,8,128]{3,2,1,0:T(8,128)(2,1)}), bf16[128,4,8,128]{3,2,1,0:T(8,128)(2,1)S(1)}, u32[]{:S(2)}, u32[]{:S(2)}) async-start(bf16[128,4,8,128]{3,2,1,0:T(8,128)(2,1)} %copy-done), calls=%async_computation.1 | async-start | bytes 2097152 | tf_op jit(solution)/shard_map/all_to_all | solution.py:335
  84.0 0.9 constant_dynamic-update-slice_fusion.3
  84.9 1.0 constant_dynamic-update-slice_fusion.2
  85.9 1.0 constant_dynamic-update-slice_fusion.1
  86.9 0.1 collective-permute-start.6
  87.0 2.3 %collective-permute-done.6.far_ref = bf16[388,8,128]{2,1,0:T(8,128)(2,1)S(1)} collective-permute-done((bf16[388,8,128]{2,1,0:T(8,128)(2,1)S(1)}, bf16[388,8,128]{2,1,0:T(8,128)(2,1)S(1)}, u32[]{:S(2)}, u32[]{:S(2)}) %collective-permute-start.6) | collective-permute-done | bytes 794656 | tf_op jit(solution)/shard_map/ppermute | solution.py:294
  89.2 1.1 %hot.1 = (bf16[3,8,128]{2,1,0:T(8,128)(2,1)S(1)}, bf16[3,8,128]{2,1,0:T(8,128)(2,1)S(1)}, bf16[3,8,128]{2,1,0:T(8,128)(2,1)S(1)}, bf16[3,8,128]{2,1,0:T(8,128)(2,1)S(1)}) custom-call(bf16[6,8,128]{2,1,0:T(8,128)(2,1)S(1)} %copy-done.3, bf16[6,8,128]{2,1,0:T(8,128)(2,1)S(1)} %collective-permute-done.b1_ref, ...), custom_call_target="tpu_custom_call" | custom-call | tf_op jit(solution)/shard_map/hot/pallas_call | solution.py:281
  90.3 2.3 %collective-permute-start.7 = (bf16[3,8,128]{2,1,0:T(8,128)(2,1)S(1)}, bf16[3,8,128]{2,1,0:T(8,128)(2,1)S(1)}, u32[]{:S(2)}, u32[]{:S(2)}) collective-permute-start(bf16[3,8,128]{2,1,0:T(8,128)(2,1)S(1)} %get-tuple-element.46), channel_id=1, source_target_pairs={{0,3},{1,0},{2,1},{3,2},{4,7},{5,4},{6,5},{7,6},{8,11},{9,8},{10,9... | collective-permute-start | bytes 18440 | tf_op jit(solution)/shard_map/ppermute | solution.py:294
  92.6 0.8 collective-permute-start.8
  93.4 0.9 collective-permute-start.9
  94.3 3.5 %collective-permute-done.8.o2_ref = bf16[3,8,128]{2,1,0:T(8,128)(2,1)S(1)} collective-permute-done((bf16[3,8,128]{2,1,0:T(8,128)(2,1)S(1)}, bf16[3,8,128]{2,1,0:T(8,128)(2,1)S(1)}, u32[]{:S(2)}, u32[]{:S(2)}) %collective-permute-start.8) | collective-permute-done | bytes 6176 | tf_op jit(solution)/shard_map/ppermute | solution.py:294
  97.8 0.8 collective-permute-done.9.o3_ref
  98.6 4.4 %all-to-all-done.1.back_ref = bf16[128,4,8,128]{3,2,1,0:T(8,128)(2,1)S(1)} async-done(((bf16[128,4,8,128]{3,2,1,0:T(8,128)(2,1)}), bf16[128,4,8,128]{3,2,1,0:T(8,128)(2,1)S(1)}, u32[]{:S(2)}, u32[]{:S(2)}) %all-to-all-start.1) | async-done | bytes 1048608 | tf_op jit(solution)/shard_map/all_to_all | solution.py:335
  103.0 3.9 %unpack.1 = bf16[1024,512]{1,0:T(8,128)(2,1)} custom-call(f32[8,1024]{1,0:T(8,128)S(1)} %copy-done.2, bf16[128,4,8,128]{3,2,1,0:T(8,128)(2,1)S(1)} %all-to-all-done.1.back_ref, bf16[3,8,128]{2,1,0:T(8,128)(2,1)S(1)} %get-tuple-element.45.o0_ref, bf16[3,8,128]{2,1,0:T(8,128)(2,1)S(1)} %collective-permute-done.7.o1_ref, ...), custom_call_target="tpu_custom_call" | custom-call | tf_op jit(solution)/shard_map/unpack/pallas_call | solution.py:281
  (21 shorter events, 0.1 us)
Async XLA Ops:
  9.8 11.2 %copy-start.9 = (bf16[6,8,128]{2,1,0:T(8,128)(2,1)S(1)}, bf16[6,8,128]{2,1,0:T(8,128)(2,1)}, u32[]{:S(2)}) copy-start(bf16[6,8,128]{2,1,0:T(8,128)(2,1)} %get-tuple-element.30) | copy-start | bytes 36868
  9.8 12.2 %copy-start.8 = (bf16[6,8,128]{2,1,0:T(8,128)(2,1)S(1)}, bf16[6,8,128]{2,1,0:T(8,128)(2,1)}, u32[]{:S(2)}) copy-start(bf16[6,8,128]{2,1,0:T(8,128)(2,1)} %get-tuple-element.31) | copy-start | bytes 36868
  9.8 14.9 %copy-start.7 = (bf16[6,8,128]{2,1,0:T(8,128)(2,1)S(1)}, bf16[6,8,128]{2,1,0:T(8,128)(2,1)}, u32[]{:S(2)}) copy-start(bf16[6,8,128]{2,1,0:T(8,128)(2,1)} %get-tuple-element.32) | copy-start | bytes 36868
  9.8 54.3 %all-to-all-start = ((bf16[128,13,8,128]{3,2,1,0:T(8,128)(2,1)}), bf16[128,13,8,128]{3,2,1,0:T(8,128)(2,1)S(1)}, u32[]{:S(2)}, u32[]{:S(2)}) async-start(bf16[128,13,8,128]{3,2,1,0:T(8,128)(2,1)} %get-tuple-element.28), calls=%async_computation | async-start | bytes 6815744 | tf_op jit(solution)/shard_map/all_to_all | solution.py:314
  21.0 34.8 %collective-permute-start = (bf16[6,8,128]{2,1,0:T(8,128)(2,1)S(1)}, bf16[6,8,128]{2,1,0:T(8,128)(2,1)S(1)}, u32[]{:S(2)}, u32[]{:S(2)}) collective-permute-start(bf16[6,8,128]{2,1,0:T(8,128)(2,1)S(1)} %copy-done.9), channel_id=1, source_target_pairs={{0,1},{1,2},{2,3},{3,0},{4,5},{5,6},{6,7},{7,4},{8,9},{9,10},{10,1... | collective-permute-start | bytes 36872 | tf_op jit(solution)/shard_map/ppermute | solution.py:294
  22.0 33.8 %collective-permute-start.1 = (bf16[6,8,128]{2,1,0:T(8,128)(2,1)S(1)}, bf16[6,8,128]{2,1,0:T(8,128)(2,1)S(1)}, u32[]{:S(2)}, u32[]{:S(2)}) collective-permute-start(bf16[6,8,128]{2,1,0:T(8,128)(2,1)S(1)} %copy-done.8), channel_id=1, source_target_pairs={{0,2},{1,3},{2,0},{3,1},{4,6},{5,7},{6,4},{7,5},{8,10},{9,11},{10,... | collective-permute-start | bytes 36872 | tf_op jit(solution)/shard_map/ppermute | solution.py:294
  24.8 31.9 %collective-permute-start.2 = (bf16[6,8,128]{2,1,0:T(8,128)(2,1)S(1)}, bf16[6,8,128]{2,1,0:T(8,128)(2,1)S(1)}, u32[]{:S(2)}, u32[]{:S(2)}) collective-permute-start(bf16[6,8,128]{2,1,0:T(8,128)(2,1)S(1)} %copy-done.7), channel_id=1, source_target_pairs={{0,3},{1,0},{2,1},{3,2},{4,7},{5,4},{6,5},{7,6},{8,11},{9,8},{10,9... | collective-permute-start | bytes 36872 | tf_op jit(solution)/shard_map/ppermute | solution.py:294
  65.1 8.6 %copy-start.1 = (bf16[97,8,128]{2,1,0:T(8,128)(2,1)}, bf16[97,8,128]{2,1,0:T(8,128)(2,1)S(1)}, u32[]{:S(2)}) copy-start(bf16[97,8,128]{2,1,0:T(8,128)(2,1)S(1)} %mid.1) | copy-start | bytes 595972
  65.1 24.1 %copy-start.3 = (bf16[6,8,128]{2,1,0:T(8,128)(2,1)S(1)}, bf16[6,8,128]{2,1,0:T(8,128)(2,1)}, u32[]{:S(2)}) copy-start(bf16[6,8,128]{2,1,0:T(8,128)(2,1)} %get-tuple-element.37.b0_ref) | copy-start | bytes 36868
  65.1 9.6 %collective-permute-start.5 = (bf16[97,8,128]{2,1,0:T(8,128)(2,1)S(1)}, bf16[97,8,128]{2,1,0:T(8,128)(2,1)S(1)}, u32[]{:S(2)}, u32[]{:S(2)}) collective-permute-start(bf16[97,8,128]{2,1,0:T(8,128)(2,1)S(1)} %mid.1), channel_id=1, source_target_pairs={{0,96},{32,0},{64,32},{96,64},{1,97},{33,1},{65,33},{97,65},{2,98}... | collective-permute-start | bytes 595976 | tf_op jit(solution)/shard_map/ppermute | solution.py:294
  67.0 9.4 %collective-permute-start.4 = (bf16[97,8,128]{2,1,0:T(8,128)(2,1)S(1)}, bf16[97,8,128]{2,1,0:T(8,128)(2,1)S(1)}, u32[]{:S(2)}, u32[]{:S(2)}) collective-permute-start(bf16[97,8,128]{2,1,0:T(8,128)(2,1)S(1)} %mid.1), channel_id=1, source_target_pairs={{0,64},{32,96},{64,0},{96,32},{1,65},{33,97},{65,1},{97,33},{2,66}... | collective-permute-start | bytes 595976 | tf_op jit(solution)/shard_map/ppermute | solution.py:294
  68.1 10.8 %collective-permute-start.3 = (bf16[97,8,128]{2,1,0:T(8,128)(2,1)S(1)}, bf16[97,8,128]{2,1,0:T(8,128)(2,1)}, u32[]{:S(2)}, u32[]{:S(2)}) collective-permute-start(bf16[97,8,128]{2,1,0:T(8,128)(2,1)S(1)} %mid.1), channel_id=1, source_target_pairs={{0,32},{32,64},{64,96},{96,0},{1,33},{33,65},{65,97},{97,1},{2,34}... | collective-permute-start | bytes 595976 | tf_op jit(solution)/shard_map/ppermute | solution.py:294
  73.7 1.0 copy-start
  74.7 28.3 %copy-start.2 = (f32[8,1024]{1,0:T(8,128)S(1)}, f32[8,1024]{1,0:T(8,128)}, u32[]{:S(2)}) copy-start(f32[8,1024]{1,0:T(8,128)} %get-tuple-element.27.table_ref) | copy-start | bytes 98308
  74.7 1.7 %copy-start.4 = (bf16[97,8,128]{2,1,0:T(8,128)(2,1)}, bf16[97,8,128]{2,1,0:T(8,128)(2,1)S(1)}, u32[]{:S(2)}) copy-start(bf16[97,8,128]{2,1,0:T(8,128)(2,1)S(1)} %collective-permute-done.5) | copy-start | bytes 595972
  76.4 0.7 copy-start.6
  78.8 8.0 %copy-start.5 = (bf16[97,8,128]{2,1,0:T(8,128)(2,1)S(1)}, bf16[97,8,128]{2,1,0:T(8,128)(2,1)}, u32[]{:S(2)}) copy-start(bf16[97,8,128]{2,1,0:T(8,128)(2,1)} %copy-done.4) | copy-start | bytes 595972
  78.8 24.2 %all-to-all-start.1 = ((bf16[128,4,8,128]{3,2,1,0:T(8,128)(2,1)}), bf16[128,4,8,128]{3,2,1,0:T(8,128)(2,1)S(1)}, u32[]{:S(2)}, u32[]{:S(2)}) async-start(bf16[128,4,8,128]{3,2,1,0:T(8,128)(2,1)} %copy-done), calls=%async_computation.1 | async-start | bytes 2097152 | tf_op jit(solution)/shard_map/all_to_all | solution.py:335
  86.9 2.4 %collective-permute-start.6 = (bf16[388,8,128]{2,1,0:T(8,128)(2,1)S(1)}, bf16[388,8,128]{2,1,0:T(8,128)(2,1)S(1)}, u32[]{:S(2)}, u32[]{:S(2)}) collective-permute-start(bf16[388,8,128]{2,1,0:T(8,128)(2,1)S(1)} %constant_dynamic-update-slice_fusion.near_ref), channel_id=1, source_target_pairs={{0,16},{16,0},{1,17},{17,1},{2,18},{18,2},{3,19},{19,3},{4,20},{20... | collective-permute-start | bytes 2383880 | tf_op jit(solution)/shard_map/ppermute | solution.py:294
  90.3 4.0 %collective-permute-start.7 = (bf16[3,8,128]{2,1,0:T(8,128)(2,1)S(1)}, bf16[3,8,128]{2,1,0:T(8,128)(2,1)S(1)}, u32[]{:S(2)}, u32[]{:S(2)}) collective-permute-start(bf16[3,8,128]{2,1,0:T(8,128)(2,1)S(1)} %get-tuple-element.46), channel_id=1, source_target_pairs={{0,3},{1,0},{2,1},{3,2},{4,7},{5,4},{6,5},{7,6},{8,11},{9,8},{10,9... | collective-permute-start | bytes 18440 | tf_op jit(solution)/shard_map/ppermute | solution.py:294
  92.6 5.2 %collective-permute-start.8 = (bf16[3,8,128]{2,1,0:T(8,128)(2,1)S(1)}, bf16[3,8,128]{2,1,0:T(8,128)(2,1)S(1)}, u32[]{:S(2)}, u32[]{:S(2)}) collective-permute-start(bf16[3,8,128]{2,1,0:T(8,128)(2,1)S(1)} %get-tuple-element.47), channel_id=1, source_target_pairs={{0,2},{1,3},{2,0},{3,1},{4,6},{5,7},{6,4},{7,5},{8,10},{9,11},{10,... | collective-permute-start | bytes 18440 | tf_op jit(solution)/shard_map/ppermute | solution.py:294
  93.4 5.2 %collective-permute-start.9 = (bf16[3,8,128]{2,1,0:T(8,128)(2,1)S(1)}, bf16[3,8,128]{2,1,0:T(8,128)(2,1)S(1)}, u32[]{:S(2)}, u32[]{:S(2)}) collective-permute-start(bf16[3,8,128]{2,1,0:T(8,128)(2,1)S(1)} %get-tuple-element.48), channel_id=1, source_target_pairs={{0,1},{1,2},{2,3},{3,0},{4,5},{5,6},{6,7},{7,4},{8,9},{9,10},{10,1... | collective-permute-start | bytes 18440 | tf_op jit(solution)/shard_map/ppermute | solution.py:294

commit v7 on v6

--- a/solution.py
+++ b/solution.py
@@ -34,19 +34,25 @@
 def pack_kernel(
     ids_ref, q_hbm, k_hbm, v_hbm,
     table_ref, h0_ref, h1_ref, h2_ref, h3_ref, send_hbm,
-    q_ref, k_ref, v_ref, x_ref, hot_ref, send_ref, sems, out_sems,
+    x_ref, hot_ref, send_ref, sems, out_sems,
 ):
     heads, tokens = ids_ref.shape
-    hd = q_ref.shape[1] // heads
+    hd = q_hbm.shape[1] // heads
     devices = send_ref.shape[0]
     slots = devices * COLD
     step = 256
     loads = [
-        pltpu.make_async_copy(src, dst, sems.at[j])
-        for j, (src, dst) in enumerate(((q_hbm, q_ref), (k_hbm, k_ref), (v_hbm, v_ref)))
+        [
+            pltpu.make_async_copy(
+                src.at[:, h * hd : (h + 1) * hd], x_ref.at[h, :, j * hd : (j + 1) * hd], sems.at[3 * h + j]
+            )
+            for j, src in enumerate((q_hbm, k_hbm, v_hbm))
+        ]
+        for h in range(heads)
     ]
-    for load in loads:
-        load.start()
+    for row in loads:
+        for load in row:
+            load.start()
     ids = ids_ref[...]
     owner = ids // CL_DEV
     tags = (ids - owner * CL_DEV + 1).astype(F32)
@@ -94,12 +100,10 @@
     want = jnp.where(row_at < 2 * SHARE, want, -9)
     want = jnp.where(row < rows, want, row - rows) + slots
     tile_at = iota((rows, hd), 0) % COLD
-    for load in loads:
-        load.wait()
     hot_tiles = []
     for h in range(heads):
-        for j, ref in enumerate((q_ref, k_ref, v_ref)):
-            x_ref[h, :, j * hd : (j + 1) * hd] = ref[:, h * hd : (h + 1) * hd]
+        for load in loads[h]:
+            load.wait()
         moved = jnp.dot(
             (slot_all[h : h + 1] == want).astype(BF16), x_ref[h], preferred_element_type=F32
         )
@@ -299,15 +303,14 @@
     heads, tokens = cluster_ids.shape
     hd = query_rows.shape[1] // heads
     tile = (COLD, hd)
-    rows = pltpu.VMEM((tokens, heads * hd), BF16)
     payload = (devices, 3 * heads + 1, *tile)
     table, h0, h1, h2, h3, send = call(
         pack_kernel, "pack", 58, [VMEM, HBM, HBM, HBM],
         [(VMEM, (2 * heads, tokens), F32)] + [(VMEM, (6, *tile), BF16)] * 4 + [(HBM, payload, BF16)],
         [
-            rows, rows, rows, pltpu.VMEM((heads, tokens, 3 * hd), BF16),
+            pltpu.VMEM((heads, tokens, 3 * hd), BF16),
             pltpu.VMEM((heads, 6, *tile), BF16), pltpu.VMEM(payload, BF16),
-            pltpu.SemaphoreType.DMA((3,)), pltpu.SemaphoreType.DMA((4,)),
+            pltpu.SemaphoreType.DMA((3 * heads,)), pltpu.SemaphoreType.DMA((4,)),
         ],
         cluster_ids, query_rows, key_rows, value_rows,
     )
@@ -316,12 +319,13 @@
     got, asked = lax.optimization_barrier((got, asked))
     (kv,) = call(mid_kernel, "mid", 24, [VMEM], [(VMEM, (97, *tile), BF16)], [], got)
     got, kv = lax.optimization_barrier((got, kv))
-    near = [kv] + [shift(kv, "z", d) for d in (1, 2, 3)]
+    below, above = shift(kv, "z", 1), shift(kv, "z", 3)
     (answer,) = call(
         cold_kernel, "cold", 24, [VMEM], [(VMEM, (devices, heads, *tile), BF16)], [], got
     )
-    near, answer = lax.optimization_barrier((near, answer))
-    near = jnp.concatenate(near, axis=0)
+    below, above, answer = lax.optimization_barrier((below, above, answer))
+    beyond = [shift(below[:49], "z", 1), shift(above[49:], "z", 3)]
+    near = jnp.concatenate([kv, below, *beyond, above], axis=0)
     far = shift(near, "core", 1)
     outs = call(
         hot_kernel, "hot", 24, [VMEM] * 6, [(VMEM, (3, *tile), BF16)] * 4,

time: 107 us -> 114 us (1.065)
  waiting for transfers between devices: 52.4 us -> 57.1 us
  starting transfers between devices: 28.8 us -> 30.7 us
    ppermute x10 -> x11, waiting for transfers between devices: 40.6 us -> 49.7 us  [shift(): lax.ppermute(block, axis, [(i, (i + by) % size) for i in range(size)])]
    all_to_all x1, waiting for transfers between devices: 4.36 us -> 0.01 us  [local(): back = lax.all_to_all(answer, AXES, split_axis=0, concat_axis=0, tiled=True)]
    unnamed x23 -> x16, local copies, waits for them, and re-layouts: 4.54 us -> 1.98 us
    slice x0 -> x2, local copies, waits for them, and re-layouts: none -> 1.8 us  [local(): beyond = [shift(below[:49], 'z', 1), shift(above[49:], 'z', 3)]]
    ppermute x10 -> x11, starting transfers between devices: 12.5 us -> 13.9 us  [shift(): lax.ppermute(block, axis, [(i, (i + by) % size) for i in range(size)])]
  transfers between devices with their start and end apart: 12 -> 13, of which waited for: 9 -> 8; matrix products, arithmetic and copies ran while one was open for 3% -> 3% of each run, Pallas kernels for 6% -> 6%
where the time goes in v7:
time: 114 us; the launch traced here: 113 us
  waiting for transfers between devices  57.1 us (50%)
  starting transfers between devices  30.7 us (27%)
  Pallas kernels  20.6 us (18%)
  local copies, waits for them, and re-layouts  4.74 us (4%)
    ppermute x11, waiting for transfers between devices, shift(): lax.ppermute(block, axis, [(i, (i + by) % size) for i in range(size)])  49.7 us
    pallas_call x5, Pallas kernels, call(): pl.pallas_call(kernel, out_shape=tuple((jax.ShapeDtypeStruct(*out[1:]) fo...  20.6 us
    ppermute x11, starting transfers between devices, shift(): lax.ppermute(block, axis, [(i, (i + by) % size) for i in range(size)])  13.9 us
    all_to_all x1, starting transfers between devices, local(): got = lax.all_to_all(send, AXES, split_axis=0, concat_axis=0, tiled=True)  11.2 us
    all_to_all x1, waiting for transfers between devices, local(): got = lax.all_to_all(send, AXES, split_axis=0, concat_axis=0, tiled=True)  7.45 us
    all_to_all x1, starting transfers between devices, local(): back = lax.all_to_all(answer, AXES, split_axis=0, concat_axis=0, tiled=True)  5.67 us
  transfers between devices with their start and end apart: 13, of which 8 were waited for; matrix products, arithmetic and copies ran while one was open for 3% of the time, Pallas kernels for 6%

profile of v7, /device:TPU:0, one launch (start us, length us, event | category | flops | bytes accessed | tf_op | source)
XLA Modules:
  0.0 113.3 jit_solution(13817767071281648446)
XLA Ops:
  0.0 9.5 %pack.1 = (f32[8,1024]{1,0:T(8,128)}, bf16[6,8,128]{2,1,0:T(8,128)(2,1)}, bf16[6,8,128]{2,1,0:T(8,128)(2,1)}, bf16[6,8,128]{2,1,0:T(8,128)(2,1)}, bf16[6,8,128]{...) custom-call(s32[4,1024]{1,0:T(4,128)} %ids_ref.1, bf16[1024,512]{1,0:T(8,128)(2,1)} %q_hbm.1, bf16[1024,512]{1,0:T(8,128)(2,1)} %k_hbm.1, ...), custom_call_target="tpu_custom_call" | custom-call | tf_op jit(solution)/shard_map/pack/pallas_call | solution.py:285
  9.5 0.0 copy-start.5
  9.5 11.2 %all-to-all-start = ((bf16[128,13,8,128]{3,2,1,0:T(8,128)(2,1)}), bf16[128,13,8,128]{3,2,1,0:T(8,128)(2,1)S(1)}, u32[]{:S(2)}, u32[]{:S(2)}) async-start(bf16[128,13,8,128]{3,2,1,0:T(8,128)(2,1)} %get-tuple-element.26), calls=%async_computation | async-start | bytes 6815744 | tf_op jit(solution)/shard_map/all_to_all | solution.py:317
  20.7 1.0 collective-permute-start
  21.7 2.7 %collective-permute-start.1 = (bf16[6,8,128]{2,1,0:T(8,128)(2,1)S(1)}, bf16[6,8,128]{2,1,0:T(8,128)(2,1)S(1)}, u32[]{:S(2)}, u32[]{:S(2)}) collective-permute-start(bf16[6,8,128]{2,1,0:T(8,128)(2,1)S(1)} %copy-done.4), channel_id=1, source_target_pairs={{0,2},{1,3},{2,0},{3,1},{4,6},{5,7},{6,4},{7,5},{8,10},{9,11},{10,... | collective-permute-start | bytes 36872 | tf_op jit(solution)/shard_map/ppermute | solution.py:298
  24.5 1.4 %collective-permute-start.2 = (bf16[6,8,128]{2,1,0:T(8,128)(2,1)S(1)}, bf16[6,8,128]{2,1,0:T(8,128)(2,1)S(1)}, u32[]{:S(2)}, u32[]{:S(2)}) collective-permute-start(bf16[6,8,128]{2,1,0:T(8,128)(2,1)S(1)} %copy-done.3), channel_id=1, source_target_pairs={{0,3},{1,0},{2,1},{3,2},{4,7},{5,4},{6,5},{7,6},{8,11},{9,8},{10,9... | collective-permute-start | bytes 36872 | tf_op jit(solution)/shard_map/ppermute | solution.py:298
  25.9 29.7 %collective-permute-done.b1_ref = bf16[6,8,128]{2,1,0:T(8,128)(2,1)S(1)} collective-permute-done((bf16[6,8,128]{2,1,0:T(8,128)(2,1)S(1)}, bf16[6,8,128]{2,1,0:T(8,128)(2,1)S(1)}, u32[]{:S(2)}, u32[]{:S(2)}) %collective-permute-start) | collective-permute-done | bytes 12320 | tf_op jit(solution)/shard_map/ppermute | solution.py:298
  55.5 0.8 collective-permute-done.2.b3_ref
  56.4 7.5 %all-to-all-done.got_ref = bf16[128,13,8,128]{3,2,1,0:T(8,128)(2,1)S(1)} async-done(((bf16[128,13,8,128]{3,2,1,0:T(8,128)(2,1)}), bf16[128,13,8,128]{3,2,1,0:T(8,128)(2,1)S(1)}, u32[]{:S(2)}, u32[]{:S(2)}) %all-to-all-start) | async-done | bytes 3407904 | tf_op jit(solution)/shard_map/all_to_all | solution.py:317
  63.8 1.0 mid.1
  64.8 1.8 %collective-permute-start.4 = (bf16[97,8,128]{2,1,0:T(8,128)(2,1)S(1)}, bf16[97,8,128]{2,1,0:T(8,128)(2,1)}, u32[]{:S(2)}, u32[]{:S(2)}) collective-permute-start(bf16[97,8,128]{2,1,0:T(8,128)(2,1)S(1)} %mid.1), channel_id=1, source_target_pairs={{0,96},{32,0},{64,32},{96,64},{1,97},{33,1},{65,33},{97,65},{2,98}... | collective-permute-start | bytes 595976 | tf_op jit(solution)/shard_map/ppermute | solution.py:298
  66.6 0.2 collective-permute-start.3
  66.9 5.2 %cold.1 = bf16[128,4,8,128]{3,2,1,0:T(8,128)(2,1)S(1)} custom-call(bf16[128,13,8,128]{3,2,1,0:T(8,128)(2,1)S(1)} %all-to-all-done.got_ref), custom_call_target="tpu_custom_call" | custom-call | tf_op jit(solution)/shard_map/cold/pallas_call | solution.py:285
  72.0 1.0 copy-done
  73.0 0.9 collective-permute-done.3
  73.9 5.7 %all-to-all-start.1 = ((bf16[128,4,8,128]{3,2,1,0:T(8,128)(2,1)}), bf16[128,4,8,128]{3,2,1,0:T(8,128)(2,1)S(1)}, u32[]{:S(2)}, u32[]{:S(2)}) async-start(bf16[128,4,8,128]{3,2,1,0:T(8,128)(2,1)} %copy-done), calls=%async_computation.1 | async-start | bytes 2097152 | tf_op jit(solution)/shard_map/all_to_all | solution.py:339
  79.6 0.9 slice.7
  80.5 0.9 slice.6
  81.4 2.8 %collective-permute-start.6 = (bf16[48,8,128]{2,1,0:T(8,128)(2,1)S(1)}, bf16[48,8,128]{2,1,0:T(8,128)(2,1)S(1)}, u32[]{:S(2)}, u32[]{:S(2)}) collective-permute-start(bf16[48,8,128]{2,1,0:T(8,128)(2,1)S(1)} %slice.7), channel_id=1, source_target_pairs={{0,96},{32,0},{64,32},{96,64},{1,97},{33,1},{65,33},{97,65},{2,98}... | collective-permute-start | bytes 294920 | tf_op jit(solution)/shard_map/ppermute | solution.py:298
  84.3 1.0 constant_dynamic-update-slice_fusion.3
  85.2 12.0 %collective-permute-done.5 = bf16[49,8,128]{2,1,0:T(8,128)(2,1)S(1)} collective-permute-done((bf16[49,8,128]{2,1,0:T(8,128)(2,1)S(1)}, bf16[49,8,128]{2,1,0:T(8,128)(2,1)S(1)}, u32[]{:S(2)}, u32[]{:S(2)}) %collective-permute-start.5) | collective-permute-done | bytes 100384 | tf_op jit(solution)/shard_map/ppermute | solution.py:298
  97.3 1.0 constant_dynamic-update-slice_fusion.near_ref
  98.2 0.2 collective-permute-start.7
  98.4 2.2 %collective-permute-done.7.far_ref = bf16[388,8,128]{2,1,0:T(8,128)(2,1)S(1)} collective-permute-done((bf16[388,8,128]{2,1,0:T(8,128)(2,1)S(1)}, bf16[388,8,128]{2,1,0:T(8,128)(2,1)S(1)}, u32[]{:S(2)}, u32[]{:S(2)}) %collective-permute-start.7) | collective-permute-done | bytes 794656 | tf_op jit(solution)/shard_map/ppermute | solution.py:298
  100.6 1.1 hot.1
  101.7 1.9 %collective-permute-start.8 = (bf16[3,8,128]{2,1,0:T(8,128)(2,1)S(1)}, bf16[3,8,128]{2,1,0:T(8,128)(2,1)S(1)}, u32[]{:S(2)}, u32[]{:S(2)}) collective-permute-start(bf16[3,8,128]{2,1,0:T(8,128)(2,1)S(1)} %get-tuple-element.42), channel_id=1, source_target_pairs={{0,3},{1,0},{2,1},{3,2},{4,7},{5,4},{6,5},{7,6},{8,11},{9,8},{10,9... | collective-permute-start | bytes 18440 | tf_op jit(solution)/shard_map/ppermute | solution.py:298
  103.6 1.0 collective-permute-start.9
  104.6 0.8 collective-permute-start.10
  105.4 0.0 collective-permute-done.8.o1_ref
  105.4 3.4 %collective-permute-done.9.o2_ref = bf16[3,8,128]{2,1,0:T(8,128)(2,1)S(1)} collective-permute-done((bf16[3,8,128]{2,1,0:T(8,128)(2,1)S(1)}, bf16[3,8,128]{2,1,0:T(8,128)(2,1)S(1)}, u32[]{:S(2)}, u32[]{:S(2)}) %collective-permute-start.9) | collective-permute-done | bytes 6176 | tf_op jit(solution)/shard_map/ppermute | solution.py:298
  108.7 0.7 collective-permute-done.10.o3_ref
  109.4 3.9 %unpack.1 = bf16[1024,512]{1,0:T(8,128)(2,1)} custom-call(f32[8,1024]{1,0:T(8,128)S(1)} %copy-done.1, bf16[128,4,8,128]{3,2,1,0:T(8,128)(2,1)S(1)} %all-to-all-done.1.back_ref, bf16[3,8,128]{2,1,0:T(8,128)(2,1)S(1)} %get-tuple-element.41.o0_ref, bf16[3,8,128]{2,1,0:T(8,128)(2,1)S(1)} %collective-permute-done.8.o1_ref, ...), custom_call_target="tpu_custom_call" | custom-call | tf_op jit(solution)/shard_map/unpack/pallas_call | solution.py:285
  (18 shorter events, 0.1 us)
Async XLA Ops:
  9.5 11.2 %copy-start.5 = (bf16[6,8,128]{2,1,0:T(8,128)(2,1)S(1)}, bf16[6,8,128]{2,1,0:T(8,128)(2,1)}, u32[]{:S(2)}) copy-start(bf16[6,8,128]{2,1,0:T(8,128)(2,1)} %get-tuple-element.28) | copy-start | bytes 36868
  9.5 12.2 %copy-start.4 = (bf16[6,8,128]{2,1,0:T(8,128)(2,1)S(1)}, bf16[6,8,128]{2,1,0:T(8,128)(2,1)}, u32[]{:S(2)}) copy-start(bf16[6,8,128]{2,1,0:T(8,128)(2,1)} %get-tuple-element.29) | copy-start | bytes 36868
  9.5 14.9 %copy-start.3 = (bf16[6,8,128]{2,1,0:T(8,128)(2,1)S(1)}, bf16[6,8,128]{2,1,0:T(8,128)(2,1)}, u32[]{:S(2)}) copy-start(bf16[6,8,128]{2,1,0:T(8,128)(2,1)} %get-tuple-element.30) | copy-start | bytes 36868
  9.5 54.3 %all-to-all-start = ((bf16[128,13,8,128]{3,2,1,0:T(8,128)(2,1)}), bf16[128,13,8,128]{3,2,1,0:T(8,128)(2,1)S(1)}, u32[]{:S(2)}, u32[]{:S(2)}) async-start(bf16[128,13,8,128]{3,2,1,0:T(8,128)(2,1)} %get-tuple-element.26), calls=%async_computation | async-start | bytes 6815744 | tf_op jit(solution)/shard_map/all_to_all | solution.py:317
  20.7 34.8 %collective-permute-start = (bf16[6,8,128]{2,1,0:T(8,128)(2,1)S(1)}, bf16[6,8,128]{2,1,0:T(8,128)(2,1)S(1)}, u32[]{:S(2)}, u32[]{:S(2)}) collective-permute-start(bf16[6,8,128]{2,1,0:T(8,128)(2,1)S(1)} %copy-done.5), channel_id=1, source_target_pairs={{0,1},{1,2},{2,3},{3,0},{4,5},{5,6},{6,7},{7,4},{8,9},{9,10},{10,1... | collective-permute-start | bytes 36872 | tf_op jit(solution)/shard_map/ppermute | solution.py:298
  21.7 33.8 %collective-permute-start.1 = (bf16[6,8,128]{2,1,0:T(8,128)(2,1)S(1)}, bf16[6,8,128]{2,1,0:T(8,128)(2,1)S(1)}, u32[]{:S(2)}, u32[]{:S(2)}) collective-permute-start(bf16[6,8,128]{2,1,0:T(8,128)(2,1)S(1)} %copy-done.4), channel_id=1, source_target_pairs={{0,2},{1,3},{2,0},{3,1},{4,6},{5,7},{6,4},{7,5},{8,10},{9,11},{10,... | collective-permute-start | bytes 36872 | tf_op jit(solution)/shard_map/ppermute | solution.py:298
  24.5 31.9 %collective-permute-start.2 = (bf16[6,8,128]{2,1,0:T(8,128)(2,1)S(1)}, bf16[6,8,128]{2,1,0:T(8,128)(2,1)S(1)}, u32[]{:S(2)}, u32[]{:S(2)}) collective-permute-start(bf16[6,8,128]{2,1,0:T(8,128)(2,1)S(1)} %copy-done.3), channel_id=1, source_target_pairs={{0,3},{1,0},{2,1},{3,2},{4,7},{5,4},{6,5},{7,6},{8,11},{9,8},{10,9... | collective-permute-start | bytes 36872 | tf_op jit(solution)/shard_map/ppermute | solution.py:298
  64.8 35.8 %copy-start.2 = (bf16[6,8,128]{2,1,0:T(8,128)(2,1)S(1)}, bf16[6,8,128]{2,1,0:T(8,128)(2,1)}, u32[]{:S(2)}) copy-start(bf16[6,8,128]{2,1,0:T(8,128)(2,1)} %get-tuple-element.35.b0_ref) | copy-start | bytes 36868
  64.8 8.2 %collective-permute-start.4 = (bf16[97,8,128]{2,1,0:T(8,128)(2,1)S(1)}, bf16[97,8,128]{2,1,0:T(8,128)(2,1)}, u32[]{:S(2)}, u32[]{:S(2)}) collective-permute-start(bf16[97,8,128]{2,1,0:T(8,128)(2,1)S(1)} %mid.1), channel_id=1, source_target_pairs={{0,96},{32,0},{64,32},{96,64},{1,97},{33,1},{65,33},{97,65},{2,98}... | collective-permute-start | bytes 595976 | tf_op jit(solution)/shard_map/ppermute | solution.py:298
  66.6 7.3 %collective-permute-start.3 = (bf16[97,8,128]{2,1,0:T(8,128)(2,1)S(1)}, bf16[97,8,128]{2,1,0:T(8,128)(2,1)}, u32[]{:S(2)}, u32[]{:S(2)}) collective-permute-start(bf16[97,8,128]{2,1,0:T(8,128)(2,1)S(1)} %mid.1), channel_id=1, source_target_pairs={{0,32},{32,64},{64,96},{96,0},{1,33},{33,65},{65,97},{97,1},{2,34}... | collective-permute-start | bytes 595976 | tf_op jit(solution)/shard_map/ppermute | solution.py:298
  72.0 1.0 copy-start
  73.0 36.4 %copy-start.1 = (f32[8,1024]{1,0:T(8,128)S(1)}, f32[8,1024]{1,0:T(8,128)}, u32[]{:S(2)}) copy-start(f32[8,1024]{1,0:T(8,128)} %get-tuple-element.25.table_ref) | copy-start | bytes 98308
  73.9 35.5 %all-to-all-start.1 = ((bf16[128,4,8,128]{3,2,1,0:T(8,128)(2,1)}), bf16[128,4,8,128]{3,2,1,0:T(8,128)(2,1)S(1)}, u32[]{:S(2)}, u32[]{:S(2)}) async-start(bf16[128,4,8,128]{3,2,1,0:T(8,128)(2,1)} %copy-done), calls=%async_computation.1 | async-start | bytes 2097152 | tf_op jit(solution)/shard_map/all_to_all | solution.py:339
  81.4 15.8 %collective-permute-start.6 = (bf16[48,8,128]{2,1,0:T(8,128)(2,1)S(1)}, bf16[48,8,128]{2,1,0:T(8,128)(2,1)S(1)}, u32[]{:S(2)}, u32[]{:S(2)}) collective-permute-start(bf16[48,8,128]{2,1,0:T(8,128)(2,1)S(1)} %slice.7), channel_id=1, source_target_pairs={{0,96},{32,0},{64,32},{96,64},{1,97},{33,1},{65,33},{97,65},{2,98}... | collective-permute-start | bytes 294920 | tf_op jit(solution)/shard_map/ppermute | solution.py:298
  84.3 13.0 %collective-permute-start.5 = (bf16[49,8,128]{2,1,0:T(8,128)(2,1)S(1)}, bf16[49,8,128]{2,1,0:T(8,128)(2,1)S(1)}, u32[]{:S(2)}, u32[]{:S(2)}) collective-permute-start(bf16[49,8,128]{2,1,0:T(8,128)(2,1)S(1)} %slice.6), channel_id=1, source_target_pairs={{0,32},{32,64},{64,96},{96,0},{1,33},{33,65},{65,97},{97,1},{2,34}... | collective-permute-start | bytes 301064 | tf_op jit(solution)/shard_map/ppermute | solution.py:298
  98.2 2.4 %collective-permute-start.7 = (bf16[388,8,128]{2,1,0:T(8,128)(2,1)S(1)}, bf16[388,8,128]{2,1,0:T(8,128)(2,1)S(1)}, u32[]{:S(2)}, u32[]{:S(2)}) collective-permute-start(bf16[388,8,128]{2,1,0:T(8,128)(2,1)S(1)} %constant_dynamic-update-slice_fusion.near_ref), channel_id=1, source_target_pairs={{0,16},{16,0},{1,17},{17,1},{2,18},{18,2},{3,19},{19,3},{4,20},{20... | collective-permute-start | bytes 2383880 | tf_op jit(solution)/shard_map/ppermute | solution.py:298
  101.7 3.7 %collective-permute-start.8 = (bf16[3,8,128]{2,1,0:T(8,128)(2,1)S(1)}, bf16[3,8,128]{2,1,0:T(8,128)(2,1)S(1)}, u32[]{:S(2)}, u32[]{:S(2)}) collective-permute-start(bf16[3,8,128]{2,1,0:T(8,128)(2,1)S(1)} %get-tuple-element.42), channel_id=1, source_target_pairs={{0,3},{1,0},{2,1},{3,2},{4,7},{5,4},{6,5},{7,6},{8,11},{9,8},{10,9... | collective-permute-start | bytes 18440 | tf_op jit(solution)/shard_map/ppermute | solution.py:298
  103.6 5.1 %collective-permute-start.9 = (bf16[3,8,128]{2,1,0:T(8,128)(2,1)S(1)}, bf16[3,8,128]{2,1,0:T(8,128)(2,1)S(1)}, u32[]{:S(2)}, u32[]{:S(2)}) collective-permute-start(bf16[3,8,128]{2,1,0:T(8,128)(2,1)S(1)} %get-tuple-element.43), channel_id=1, source_target_pairs={{0,2},{1,3},{2,0},{3,1},{4,6},{5,7},{6,4},{7,5},{8,10},{9,11},{10,... | collective-permute-start | bytes 18440 | tf_op jit(solution)/shard_map/ppermute | solution.py:298
  104.6 4.8 %collective-permute-start.10 = (bf16[3,8,128]{2,1,0:T(8,128)(2,1)S(1)}, bf16[3,8,128]{2,1,0:T(8,128)(2,1)S(1)}, u32[]{:S(2)}, u32[]{:S(2)}) collective-permute-start(bf16[3,8,128]{2,1,0:T(8,128)(2,1)S(1)} %get-tuple-element.44), channel_id=1, source_target_pairs={{0,1},{1,2},{2,3},{3,0},{4,5},{5,6},{6,7},{7,4},{8,9},{9,10},{10,1... | collective-permute-start | bytes 18440 | tf_op jit(solution)/shard_map/ppermute | solution.py:298

commit v8 on v7

--- a/solution.py
+++ b/solution.py
@@ -281,7 +281,7 @@
 MIB = 1024 * 1024
 
 
-def call(kernel, name, limit, ins, outs, scratch, *arrays):
+def call(kernel, name, limit, ins, outs, scratch, *arrays, flops=None):
     return pl.pallas_call(
         kernel,
         out_shape=tuple(jax.ShapeDtypeStruct(*out[1:]) for out in outs),
@@ -290,6 +290,7 @@
         scratch_shapes=scratch,
         compiler_params=pltpu.CompilerParams(vmem_limit_bytes=limit * MIB),
         name=name,
+        cost_estimate=None if flops is None else pl.CostEstimate(flops=flops, bytes_accessed=0, transcendentals=0),
     )(*arrays)
 
 
@@ -319,13 +320,12 @@
     got, asked = lax.optimization_barrier((got, asked))
     (kv,) = call(mid_kernel, "mid", 24, [VMEM], [(VMEM, (97, *tile), BF16)], [], got)
     got, kv = lax.optimization_barrier((got, kv))
-    below, above = shift(kv, "z", 1), shift(kv, "z", 3)
+    near = [kv] + [shift(kv, "z", d) for d in (1, 2, 3)]
     (answer,) = call(
-        cold_kernel, "cold", 24, [VMEM], [(VMEM, (devices, heads, *tile), BF16)], [], got
-    )
-    below, above, answer = lax.optimization_barrier((below, above, answer))
-    beyond = [shift(below[:49], "z", 1), shift(above[49:], "z", 3)]
-    near = jnp.concatenate([kv, below, *beyond, above], axis=0)
+        cold_kernel, "cold", 24, [VMEM], [(VMEM, (devices, heads, *tile), BF16)], [], got, flops=20_000_000_000,
+    )
+    near, _ = lax.optimization_barrier((near, answer))
+    near = jnp.concatenate(near, axis=0)
     far = shift(near, "core", 1)
     outs = call(
         hot_kernel, "hot", 24, [VMEM] * 6, [(VMEM, (3, *tile), BF16)] * 4,
@@ -334,6 +334,7 @@
             pltpu.VMEM((devices * HOT, hd), BF16), pltpu.VMEM((4, 3, *tile), F32),
         ],
         *asked, near, far,
+        flops=2_000_000_000,
     )
     hot_out = [outs[0]] + [shift(b, "y", 3 - d) for d, b in enumerate(outs[1:])]
     back = lax.all_to_all(answer, AXES, split_axis=0, concat_axis=0, tiled=True)

time: 114 us -> 106 us (0.930)
  waiting for transfers between devices: 57.1 us -> 48 us
    ppermute x11 -> x10, waiting for transfers between devices: 49.7 us -> 36.9 us  [shift(): lax.ppermute(block, axis, [(i, (i + by) % size) for i in range(size)])]
    all_to_all x1, waiting for transfers between devices: 0.01 us -> 3.66 us  [local(): back = lax.all_to_all(answer, AXES, split_axis=0, concat_axis=0, tiled=True)]
    all_to_all x1, starting transfers between devices: 5.67 us -> 7.67 us  [local(): back = lax.all_to_all(answer, AXES, split_axis=0, concat_axis=0, tiled=True)]
    unnamed x16 -> x15, local copies, waits for them, and re-layouts: 1.98 us -> 3.84 us
    slice x2 -> x0, local copies, waits for them, and re-layouts: 1.8 us -> none  [local(): beyond = [shift(below[:49], 'z', 1), shift(above[49:], 'z', 3)]]
    ppermute x11 -> x10, starting transfers between devices: 13.9 us -> 12.5 us  [shift(): lax.ppermute(block, axis, [(i, (i + by) % size) for i in range(size)])]
  transfers between devices with their start and end apart: 13 -> 12, of which waited for: 8 -> 7; matrix products, arithmetic and copies ran while one was open for 3% -> 4% of each run, Pallas kernels for 6% -> 6%
where the time goes in v8:
time: 106 us; the launch traced here: 105 us
  waiting for transfers between devices  48 us (45%)
  starting transfers between devices  31.3 us (30%)
  Pallas kernels  21.3 us (20%)
  local copies, waits for them, and re-layouts  4.8 us (5%)
    ppermute x10, waiting for transfers between devices, shift(): lax.ppermute(block, axis, [(i, (i + by) % size) for i in range(size)])  36.9 us
    pallas_call x5, Pallas kernels, call(): pl.pallas_call(kernel, out_shape=tuple((jax.ShapeDtypeStruct(*out[1:]) fo...  21.3 us
    ppermute x10, starting transfers between devices, shift(): lax.ppermute(block, axis, [(i, (i + by) % size) for i in range(size)])  12.5 us
    all_to_all x1, starting transfers between devices, local(): got = lax.all_to_all(send, AXES, split_axis=0, concat_axis=0, tiled=True)  11.2 us
    all_to_all x1, starting transfers between devices, local(): back = lax.all_to_all(answer, AXES, split_axis=0, concat_axis=0, tiled=True)  7.67 us
    all_to_all x1, waiting for transfers between devices, local(): got = lax.all_to_all(send, AXES, split_axis=0, concat_axis=0, tiled=True)  7.45 us
    unnamed x15, local copies, waits for them, and re-layouts  3.84 us
    all_to_all x1, waiting for transfers between devices, local(): back = lax.all_to_all(answer, AXES, split_axis=0, concat_axis=0, tiled=True)  3.66 us
  transfers between devices with their start and end apart: 12, of which 7 were waited for; matrix products, arithmetic and copies ran while one was open for 4% of the time, Pallas kernels for 6%

profile of v8, /device:TPU:0, one launch (start us, length us, event | category | flops | bytes accessed | tf_op | source)
XLA Modules:
  0.0 105.5 jit_solution(2378878688132230377)
XLA Ops:
  0.0 9.5 %pack.1 = (f32[8,1024]{1,0:T(8,128)}, bf16[6,8,128]{2,1,0:T(8,128)(2,1)}, bf16[6,8,128]{2,1,0:T(8,128)(2,1)}, bf16[6,8,128]{2,1,0:T(8,128)(2,1)}, bf16[6,8,128]{...) custom-call(s32[4,1024]{1,0:T(4,128)} %ids_ref.1, bf16[1024,512]{1,0:T(8,128)(2,1)} %q_hbm.1, bf16[1024,512]{1,0:T(8,128)(2,1)} %k_hbm.1, ...), custom_call_target="tpu_custom_call" | custom-call | tf_op jit(solution)/shard_map/pack/pallas_call | solution.py:285
  9.5 0.0 copy-start.5
  9.5 11.2 %all-to-all-start = ((bf16[128,13,8,128]{3,2,1,0:T(8,128)(2,1)}), bf16[128,13,8,128]{3,2,1,0:T(8,128)(2,1)S(1)}, u32[]{:S(2)}, u32[]{:S(2)}) async-start(bf16[128,13,8,128]{3,2,1,0:T(8,128)(2,1)} %get-tuple-element.27), calls=%async_computation | async-start | bytes 6815744 | tf_op jit(solution)/shard_map/all_to_all | solution.py:318
  20.7 1.0 collective-permute-start
  21.7 2.7 %collective-permute-start.1 = (bf16[6,8,128]{2,1,0:T(8,128)(2,1)S(1)}, bf16[6,8,128]{2,1,0:T(8,128)(2,1)S(1)}, u32[]{:S(2)}, u32[]{:S(2)}) collective-permute-start(bf16[6,8,128]{2,1,0:T(8,128)(2,1)S(1)} %copy-done.4), channel_id=1, source_target_pairs={{0,2},{1,3},{2,0},{3,1},{4,6},{5,7},{6,4},{7,5},{8,10},{9,11},{10,... | collective-permute-start | bytes 36872 | tf_op jit(solution)/shard_map/ppermute | solution.py:299
  24.4 1.4 %collective-permute-start.2 = (bf16[6,8,128]{2,1,0:T(8,128)(2,1)S(1)}, bf16[6,8,128]{2,1,0:T(8,128)(2,1)S(1)}, u32[]{:S(2)}, u32[]{:S(2)}) collective-permute-start(bf16[6,8,128]{2,1,0:T(8,128)(2,1)S(1)} %copy-done.3), channel_id=1, source_target_pairs={{0,3},{1,0},{2,1},{3,2},{4,7},{5,4},{6,5},{7,6},{8,11},{9,8},{10,9... | collective-permute-start | bytes 36872 | tf_op jit(solution)/shard_map/ppermute | solution.py:299
  25.9 29.7 %collective-permute-done.b1_ref = bf16[6,8,128]{2,1,0:T(8,128)(2,1)S(1)} collective-permute-done((bf16[6,8,128]{2,1,0:T(8,128)(2,1)S(1)}, bf16[6,8,128]{2,1,0:T(8,128)(2,1)S(1)}, u32[]{:S(2)}, u32[]{:S(2)}) %collective-permute-start) | collective-permute-done | bytes 12320 | tf_op jit(solution)/shard_map/ppermute | solution.py:299
  55.5 0.8 collective-permute-done.2.b3_ref
  56.4 7.5 %all-to-all-done.got_ref = bf16[128,13,8,128]{3,2,1,0:T(8,128)(2,1)S(1)} async-done(((bf16[128,13,8,128]{3,2,1,0:T(8,128)(2,1)}), bf16[128,13,8,128]{3,2,1,0:T(8,128)(2,1)S(1)}, u32[]{:S(2)}, u32[]{:S(2)}) %all-to-all-start) | async-done | bytes 3407904 | tf_op jit(solution)/shard_map/all_to_all | solution.py:318
  63.8 1.7 %mid.1 = bf16[97,8,128]{2,1,0:T(8,128)(2,1)} custom-call(bf16[128,13,8,128]{3,2,1,0:T(8,128)(2,1)S(1)} %all-to-all-done.got_ref), custom_call_target="tpu_custom_call" | custom-call | tf_op jit(solution)/shard_map/mid/pallas_call | solution.py:285
  65.5 1.8 %collective-permute-start.5 = (bf16[97,8,128]{2,1,0:T(8,128)(2,1)}, bf16[97,8,128]{2,1,0:T(8,128)(2,1)}, u32[]{:S(2)}, u32[]{:S(2)}) collective-permute-start(bf16[97,8,128]{2,1,0:T(8,128)(2,1)} %mid.1), channel_id=1, source_target_pairs={{0,96},{32,0},{64,32},{96,64},{1,97},{33,1},{65,33},{97,65},{2,98}... | collective-permute-start | bytes 595976 | tf_op jit(solution)/shard_map/ppermute | solution.py:299
  67.3 1.1 %collective-permute-start.4 = (bf16[97,8,128]{2,1,0:T(8,128)(2,1)}, bf16[97,8,128]{2,1,0:T(8,128)(2,1)}, u32[]{:S(2)}, u32[]{:S(2)}) collective-permute-start(bf16[97,8,128]{2,1,0:T(8,128)(2,1)} %mid.1), channel_id=1, source_target_pairs={{0,64},{32,96},{64,0},{96,32},{1,65},{33,97},{65,1},{97,33},{2,66}... | collective-permute-start | bytes 595976 | tf_op jit(solution)/shard_map/ppermute | solution.py:299
  68.4 0.3 collective-permute-start.3
  68.7 5.2 %cold.1 = bf16[128,4,8,128]{3,2,1,0:T(8,128)(2,1)S(1)} custom-call(bf16[128,13,8,128]{3,2,1,0:T(8,128)(2,1)S(1)} %all-to-all-done.got_ref), custom_call_target="tpu_custom_call" | custom-call | flops 20000000000 | tf_op jit(solution)/shard_map/cold/pallas_call | solution.py:285
  73.9 0.0 copy-start
  73.9 1.0 copy-done
  74.9 7.7 %all-to-all-start.1 = ((bf16[128,4,8,128]{3,2,1,0:T(8,128)(2,1)}), bf16[128,4,8,128]{3,2,1,0:T(8,128)(2,1)S(1)}, u32[]{:S(2)}, u32[]{:S(2)}) async-start(bf16[128,4,8,128]{3,2,1,0:T(8,128)(2,1)} %copy-done), calls=%async_computation.1 | async-start | bytes 2097152 | tf_op jit(solution)/shard_map/all_to_all | solution.py:340
  82.6 0.0 collective-permute-done.5
  82.6 0.9 constant_dynamic-update-slice_fusion.3
  83.5 1.0 constant_dynamic-update-slice_fusion.2
  84.5 1.0 constant_dynamic-update-slice_fusion.1
  85.5 1.0 constant_dynamic-update-slice_fusion.near_ref
  86.4 0.1 collective-permute-start.6
  86.5 2.3 %collective-permute-done.6.far_ref = bf16[388,8,128]{2,1,0:T(8,128)(2,1)S(1)} collective-permute-done((bf16[388,8,128]{2,1,0:T(8,128)(2,1)S(1)}, bf16[388,8,128]{2,1,0:T(8,128)(2,1)S(1)}, u32[]{:S(2)}, u32[]{:S(2)}) %collective-permute-start.6) | collective-permute-done | bytes 794656 | tf_op jit(solution)/shard_map/ppermute | solution.py:299
  88.8 1.1 %hot.1 = (bf16[3,8,128]{2,1,0:T(8,128)(2,1)S(1)}, bf16[3,8,128]{2,1,0:T(8,128)(2,1)S(1)}, bf16[3,8,128]{2,1,0:T(8,128)(2,1)S(1)}, bf16[3,8,128]{2,1,0:T(8,128)(2,1)S(1)}) custom-call(bf16[6,8,128]{2,1,0:T(8,128)(2,1)S(1)} %copy-done.2, bf16[6,8,128]{2,1,0:T(8,128)(2,1)S(1)} %collective-permute-done.b1_ref, ...), custom_call_target="tpu_custom_call" | custom-call | flops 2000000000 | tf_op jit(solution)/shard_map/hot/pallas_call | solution.py:285
  89.9 2.3 %collective-permute-start.7 = (bf16[3,8,128]{2,1,0:T(8,128)(2,1)S(1)}, bf16[3,8,128]{2,1,0:T(8,128)(2,1)S(1)}, u32[]{:S(2)}, u32[]{:S(2)}) collective-permute-start(bf16[3,8,128]{2,1,0:T(8,128)(2,1)S(1)} %get-tuple-element.44), channel_id=1, source_target_pairs={{0,3},{1,0},{2,1},{3,2},{4,7},{5,4},{6,5},{7,6},{8,11},{9,8},{10,9... | collective-permute-start | bytes 18440 | tf_op jit(solution)/shard_map/ppermute | solution.py:299
  92.2 0.8 collective-permute-start.8
  93.0 0.9 collective-permute-start.9
  93.8 3.9 %collective-permute-done.8.o2_ref = bf16[3,8,128]{2,1,0:T(8,128)(2,1)S(1)} collective-permute-done((bf16[3,8,128]{2,1,0:T(8,128)(2,1)S(1)}, bf16[3,8,128]{2,1,0:T(8,128)(2,1)S(1)}, u32[]{:S(2)}, u32[]{:S(2)}) %collective-permute-start.8) | collective-permute-done | bytes 6176 | tf_op jit(solution)/shard_map/ppermute | solution.py:299
  97.8 0.2 collective-permute-done.9.o3_ref
  98.0 3.7 %all-to-all-done.1.back_ref = bf16[128,4,8,128]{3,2,1,0:T(8,128)(2,1)S(1)} async-done(((bf16[128,4,8,128]{3,2,1,0:T(8,128)(2,1)}), bf16[128,4,8,128]{3,2,1,0:T(8,128)(2,1)S(1)}, u32[]{:S(2)}, u32[]{:S(2)}) %all-to-all-start.1) | async-done | bytes 1048608 | tf_op jit(solution)/shard_map/all_to_all | solution.py:340
  101.6 3.9 %unpack.1 = bf16[1024,512]{1,0:T(8,128)(2,1)} custom-call(f32[8,1024]{1,0:T(8,128)S(1)} %copy-done.1, bf16[128,4,8,128]{3,2,1,0:T(8,128)(2,1)S(1)} %all-to-all-done.1.back_ref, bf16[3,8,128]{2,1,0:T(8,128)(2,1)S(1)} %get-tuple-element.43.o0_ref, bf16[3,8,128]{2,1,0:T(8,128)(2,1)S(1)} %collective-permute-done.7.o1_ref, ...), custom_call_target="tpu_custom_call" | custom-call | tf_op jit(solution)/shard_map/unpack/pallas_call | solution.py:285
  (13 shorter events, 0.0 us)
Async XLA Ops:
  9.5 11.2 %copy-start.5 = (bf16[6,8,128]{2,1,0:T(8,128)(2,1)S(1)}, bf16[6,8,128]{2,1,0:T(8,128)(2,1)}, u32[]{:S(2)}) copy-start(bf16[6,8,128]{2,1,0:T(8,128)(2,1)} %get-tuple-element.29) | copy-start | bytes 36868
  9.5 12.2 %copy-start.4 = (bf16[6,8,128]{2,1,0:T(8,128)(2,1)S(1)}, bf16[6,8,128]{2,1,0:T(8,128)(2,1)}, u32[]{:S(2)}) copy-start(bf16[6,8,128]{2,1,0:T(8,128)(2,1)} %get-tuple-element.30) | copy-start | bytes 36868
  9.5 14.9 %copy-start.3 = (bf16[6,8,128]{2,1,0:T(8,128)(2,1)S(1)}, bf16[6,8,128]{2,1,0:T(8,128)(2,1)}, u32[]{:S(2)}) copy-start(bf16[6,8,128]{2,1,0:T(8,128)(2,1)} %get-tuple-element.31) | copy-start | bytes 36868
  9.5 54.3 %all-to-all-start = ((bf16[128,13,8,128]{3,2,1,0:T(8,128)(2,1)}), bf16[128,13,8,128]{3,2,1,0:T(8,128)(2,1)S(1)}, u32[]{:S(2)}, u32[]{:S(2)}) async-start(bf16[128,13,8,128]{3,2,1,0:T(8,128)(2,1)} %get-tuple-element.27), calls=%async_computation | async-start | bytes 6815744 | tf_op jit(solution)/shard_map/all_to_all | solution.py:318
  20.7 34.8 %collective-permute-start = (bf16[6,8,128]{2,1,0:T(8,128)(2,1)S(1)}, bf16[6,8,128]{2,1,0:T(8,128)(2,1)S(1)}, u32[]{:S(2)}, u32[]{:S(2)}) collective-permute-start(bf16[6,8,128]{2,1,0:T(8,128)(2,1)S(1)} %copy-done.5), channel_id=1, source_target_pairs={{0,1},{1,2},{2,3},{3,0},{4,5},{5,6},{6,7},{7,4},{8,9},{9,10},{10,1... | collective-permute-start | bytes 36872 | tf_op jit(solution)/shard_map/ppermute | solution.py:299
  21.7 33.8 %collective-permute-start.1 = (bf16[6,8,128]{2,1,0:T(8,128)(2,1)S(1)}, bf16[6,8,128]{2,1,0:T(8,128)(2,1)S(1)}, u32[]{:S(2)}, u32[]{:S(2)}) collective-permute-start(bf16[6,8,128]{2,1,0:T(8,128)(2,1)S(1)} %copy-done.4), channel_id=1, source_target_pairs={{0,2},{1,3},{2,0},{3,1},{4,6},{5,7},{6,4},{7,5},{8,10},{9,11},{10,... | collective-permute-start | bytes 36872 | tf_op jit(solution)/shard_map/ppermute | solution.py:299
  24.4 31.9 %collective-permute-start.2 = (bf16[6,8,128]{2,1,0:T(8,128)(2,1)S(1)}, bf16[6,8,128]{2,1,0:T(8,128)(2,1)S(1)}, u32[]{:S(2)}, u32[]{:S(2)}) collective-permute-start(bf16[6,8,128]{2,1,0:T(8,128)(2,1)S(1)} %copy-done.3), channel_id=1, source_target_pairs={{0,3},{1,0},{2,1},{3,2},{4,7},{5,4},{6,5},{7,6},{8,11},{9,8},{10,9... | collective-permute-start | bytes 36872 | tf_op jit(solution)/shard_map/ppermute | solution.py:299
  65.5 17.1 %collective-permute-start.5 = (bf16[97,8,128]{2,1,0:T(8,128)(2,1)}, bf16[97,8,128]{2,1,0:T(8,128)(2,1)}, u32[]{:S(2)}, u32[]{:S(2)}) collective-permute-start(bf16[97,8,128]{2,1,0:T(8,128)(2,1)} %mid.1), channel_id=1, source_target_pairs={{0,96},{32,0},{64,32},{96,64},{1,97},{33,1},{65,33},{97,65},{2,98}... | collective-permute-start | bytes 595976 | tf_op jit(solution)/shard_map/ppermute | solution.py:299
  67.3 15.3 %collective-permute-start.4 = (bf16[97,8,128]{2,1,0:T(8,128)(2,1)}, bf16[97,8,128]{2,1,0:T(8,128)(2,1)}, u32[]{:S(2)}, u32[]{:S(2)}) collective-permute-start(bf16[97,8,128]{2,1,0:T(8,128)(2,1)} %mid.1), channel_id=1, source_target_pairs={{0,64},{32,96},{64,0},{96,32},{1,65},{33,97},{65,1},{97,33},{2,66}... | collective-permute-start | bytes 595976 | tf_op jit(solution)/shard_map/ppermute | solution.py:299
  68.4 14.2 %collective-permute-start.3 = (bf16[97,8,128]{2,1,0:T(8,128)(2,1)}, bf16[97,8,128]{2,1,0:T(8,128)(2,1)}, u32[]{:S(2)}, u32[]{:S(2)}) collective-permute-start(bf16[97,8,128]{2,1,0:T(8,128)(2,1)} %mid.1), channel_id=1, source_target_pairs={{0,32},{32,64},{64,96},{96,0},{1,33},{33,65},{65,97},{97,1},{2,34}... | collective-permute-start | bytes 595976 | tf_op jit(solution)/shard_map/ppermute | solution.py:299
  73.9 1.0 copy-start
  74.9 13.9 %copy-start.2 = (bf16[6,8,128]{2,1,0:T(8,128)(2,1)S(1)}, bf16[6,8,128]{2,1,0:T(8,128)(2,1)}, u32[]{:S(2)}) copy-start(bf16[6,8,128]{2,1,0:T(8,128)(2,1)} %get-tuple-element.34.b0_ref) | copy-start | bytes 36868
  74.9 26.7 %all-to-all-start.1 = ((bf16[128,4,8,128]{3,2,1,0:T(8,128)(2,1)}), bf16[128,4,8,128]{3,2,1,0:T(8,128)(2,1)S(1)}, u32[]{:S(2)}, u32[]{:S(2)}) async-start(bf16[128,4,8,128]{3,2,1,0:T(8,128)(2,1)} %copy-done), calls=%async_computation.1 | async-start | bytes 2097152 | tf_op jit(solution)/shard_map/all_to_all | solution.py:340
  86.4 15.2 %copy-start.1 = (f32[8,1024]{1,0:T(8,128)S(1)}, f32[8,1024]{1,0:T(8,128)}, u32[]{:S(2)}) copy-start(f32[8,1024]{1,0:T(8,128)} %get-tuple-element.26.table_ref) | copy-start | bytes 98308
  86.4 2.4 %collective-permute-start.6 = (bf16[388,8,128]{2,1,0:T(8,128)(2,1)S(1)}, bf16[388,8,128]{2,1,0:T(8,128)(2,1)S(1)}, u32[]{:S(2)}, u32[]{:S(2)}) collective-permute-start(bf16[388,8,128]{2,1,0:T(8,128)(2,1)S(1)} %constant_dynamic-update-slice_fusion.near_ref), channel_id=1, source_target_pairs={{0,16},{16,0},{1,17},{17,1},{2,18},{18,2},{3,19},{19,3},{4,20},{20... | collective-permute-start | bytes 2383880 | tf_op jit(solution)/shard_map/ppermute | solution.py:299
  89.9 4.0 %collective-permute-start.7 = (bf16[3,8,128]{2,1,0:T(8,128)(2,1)S(1)}, bf16[3,8,128]{2,1,0:T(8,128)(2,1)S(1)}, u32[]{:S(2)}, u32[]{:S(2)}) collective-permute-start(bf16[3,8,128]{2,1,0:T(8,128)(2,1)S(1)} %get-tuple-element.44), channel_id=1, source_target_pairs={{0,3},{1,0},{2,1},{3,2},{4,7},{5,4},{6,5},{7,6},{8,11},{9,8},{10,9... | collective-permute-start | bytes 18440 | tf_op jit(solution)/shard_map/ppermute | solution.py:299
  92.2 5.6 %collective-permute-start.8 = (bf16[3,8,128]{2,1,0:T(8,128)(2,1)S(1)}, bf16[3,8,128]{2,1,0:T(8,128)(2,1)S(1)}, u32[]{:S(2)}, u32[]{:S(2)}) collective-permute-start(bf16[3,8,128]{2,1,0:T(8,128)(2,1)S(1)} %get-tuple-element.45), channel_id=1, source_target_pairs={{0,2},{1,3},{2,0},{3,1},{4,6},{5,7},{6,4},{7,5},{8,10},{9,11},{10,... | collective-permute-start | bytes 18440 | tf_op jit(solution)/shard_map/ppermute | solution.py:299
  93.0 5.0 %collective-permute-start.9 = (bf16[3,8,128]{2,1,0:T(8,128)(2,1)S(1)}, bf16[3,8,128]{2,1,0:T(8,128)(2,1)S(1)}, u32[]{:S(2)}, u32[]{:S(2)}) collective-permute-start(bf16[3,8,128]{2,1,0:T(8,128)(2,1)S(1)} %get-tuple-element.46), channel_id=1, source_target_pairs={{0,1},{1,2},{2,3},{3,0},{4,5},{5,6},{6,7},{7,4},{8,9},{9,10},{10,1... | collective-permute-start | bytes 18440 | tf_op jit(solution)/shard_map/ppermute | solution.py:299

commit v9 on v8

--- a/solution.py
+++ b/solution.py
@@ -32,15 +32,17 @@
 
 
 def pack_kernel(
-    ids_ref, q_hbm, k_hbm, v_hbm,
-    table_ref, h0_ref, h1_ref, h2_ref, h3_ref, send_hbm,
-    x_ref, hot_ref, send_ref, sems, out_sems,
+    ids_hbm, q_hbm, k_hbm, v_hbm,
+    table_hbm, h0_hbm, h1_hbm, h2_hbm, h3_hbm, send_hbm,
+    ids_ref, table_ref, x_ref, hot_ref, send_ref, sems, out_sems,
 ):
     heads, tokens = ids_ref.shape
     hd = q_hbm.shape[1] // heads
     devices = send_ref.shape[0]
     slots = devices * COLD
     step = 256
+    ids_load = pltpu.make_async_copy(ids_hbm, ids_ref, sems.at[3 * heads])
+    ids_load.start()
     loads = [
         [
             pltpu.make_async_copy(
@@ -53,6 +55,7 @@
     for row in loads:
         for load in row:
             load.start()
+    ids_load.wait()
     ids = ids_ref[...]
     owner = ids // CL_DEV
     tags = (ids - owner * CL_DEV + 1).astype(F32)
@@ -87,6 +90,8 @@
         slot_rows.append(jnp.where(rank >= slots, rank, owner[h : h + 1] * COLD + rank))
     slot_all = jnp.concatenate(slot_rows, axis=0)
     table_ref[...] = jnp.concatenate([slot_all.astype(F32), tags], axis=0)
+    sent = [pltpu.make_async_copy(table_ref, table_hbm, out_sems.at[4])]
+    sent[0].start()
     asked_tags = jnp.sum(labels, axis=0, keepdims=True)
     cold_lane = iota((1, LANES), 1) < HOT_LANE
     for h in range(heads):
@@ -112,12 +117,12 @@
         hot_tiles.append(tiles)
         hot_ref[h, 0:3] = moved[rows : rows + HOT, :hd].reshape(3, COLD, hd).astype(BF16)
     y = lax.axis_index("y")
-    for d, ref in enumerate((h0_ref, h1_ref, h2_ref, h3_ref)):
-        ref[...] = hot_ref[lax.rem(y + d, heads)]
+    for d, ref in enumerate((h0_hbm, h1_hbm, h2_hbm, h3_hbm)):
+        sent.append(pltpu.make_async_copy(hot_ref.at[lax.rem(y + d, heads)], ref, out_sems.at[5 + d]))
+        sent[-1].start()
     labels = jnp.where(cold_lane, labels, 0.0)
     part = 256
     sub = iota((COLD, LANES), 0)
-    sent = []
     for c in range(slots // part):
         first, stop = c * part // COLD, (c + 1) * part // COLD
         for h in range(heads):
@@ -153,7 +158,7 @@
 NT = (((1,), (1,)), ((), ()))
 
 
-def cold_kernel(got_ref, out_ref):
+def cold_kernel(got_ref, out_hbm, out_ref, out_sems):
     devices, tiles, _, hd = got_ref.shape
     heads = tiles // 3
     slots = devices * COLD
@@ -166,6 +171,7 @@
     ones = jnp.ones((LANES, LANES), BF16)
     part = 512
     causal = iota((part, part), 1) <= iota((part, part), 0)
+    sent = []
     for h in range(heads):
         tags = jnp.where(pick == COLD * h, spread, 0.0).astype(BF16)
         label_cols = jnp.dot(tags, ones, preferred_element_type=F32)
@@ -189,6 +195,11 @@
             out = jnp.dot(weights.astype(BF16), v[:stop], preferred_element_type=F32) / total
             devs = slice(c * part // COLD, stop // COLD)
             out_ref[devs, h] = out.reshape(part // COLD, COLD, hd).astype(BF16)
+        out = pltpu.make_async_copy(out_ref.at[:, h], out_hbm.at[:, h], out_sems.at[h])
+        out.start()
+        sent.append(out)
+    for out in sent:
+        out.wait()
 
 
 def mid_kernel(got_ref, kv_ref):
@@ -251,7 +262,7 @@
         ref[...] = o_ref[lax.rem(y + 4 - d, 4)].astype(BF16)
 
 
-def unpack_kernel(table_ref, back_ref, o0_ref, o1_ref, o2_ref, o3_ref, out_ref, hot_ref):
+def unpack_kernel(table_ref, back_ref, o0_ref, o1_ref, o2_ref, o3_ref, out_hbm, hot_ref, out_ref, sems):
     devices, heads, _, hd = back_ref.shape
     tokens = table_ref.shape[1]
     cols = columns_of(table_ref[...])
@@ -259,20 +270,28 @@
     part = 256
     for d, ref in enumerate((o0_ref, o1_ref, o2_ref, o3_ref)):
         hot_ref[d] = ref[...].astype(F32)
-    for h in range(heads):
-        rows = back_ref[:, h].astype(F32).reshape(slots, hd).astype(BF16)
-        hot = hot_ref[lax.rem(h + 4 - lax.axis_index("y"), 4)].reshape(HOT, hd)
-        hot = jnp.concatenate([hot, jnp.zeros((LANES - HOT, hd), F32)], axis=0).astype(BF16)
-        for c in range(tokens // part):
-            slot = cols[c * part : (c + 1) * part, h : h + 1].astype(jnp.int32)
-            place = (slot == lax.broadcasted_iota(jnp.int32, (part, slots), 1)).astype(BF16)
-            hot_place = (
-                slot == lax.broadcasted_iota(jnp.int32, (part, LANES), 1) + slots
-            ).astype(BF16)
-            got = jnp.dot(place, rows, preferred_element_type=F32) + jnp.dot(
-                hot_place, hot, preferred_element_type=F32
-            )
-            out_ref[c * part : (c + 1) * part, h * hd : (h + 1) * hd] = got.astype(BF16)
+    y = lax.axis_index("y")
+    rows, hots = [], []
+    for h in range(heads):
+        rows.append(back_ref[:, h].astype(F32).reshape(slots, hd).astype(BF16))
+        hot = hot_ref[lax.rem(h + 4 - y, 4)].reshape(HOT, hd)
+        hots.append(jnp.concatenate([hot, jnp.zeros((LANES - HOT, hd), F32)], axis=0).astype(BF16))
+    sent = []
+    for c in range(tokens // part):
+        at = slice(c * part, (c + 1) * part)
+        for h in range(heads):
+            slot = cols[at, h : h + 1].astype(jnp.int32)
+            place = (slot == iota((part, slots), 1)).astype(BF16)
+            hot_place = (slot == iota((part, LANES), 1) + slots).astype(BF16)
+            got = jnp.dot(place, rows[h], preferred_element_type=F32) + jnp.dot(
+                hot_place, hots[h], preferred_element_type=F32
+            )
+            out_ref[at, h * hd : (h + 1) * hd] = got.astype(BF16)
+        out = pltpu.make_async_copy(out_ref.at[at], out_hbm.at[at], sems.at[c])
+        out.start()
+        sent.append(out)
+    for out in sent:
+        out.wait()
 
 
 VMEM = pl.BlockSpec(memory_space=pltpu.VMEM)
@@ -284,7 +303,9 @@
 def call(kernel, name, limit, ins, outs, scratch, *arrays, flops=None):
     return pl.pallas_call(
         kernel,
-        out_shape=tuple(jax.ShapeDtypeStruct(*out[1:]) for out in outs),
+        out_shape=tuple(
+            pltpu.HBM(*out[1:]) if out[0] is HBM else jax.ShapeDtypeStruct(*out[1:]) for out in outs
+        ),
         in_specs=ins,
         out_specs=tuple(out[0] for out in outs),
         scratch_shapes=scratch,
@@ -306,12 +327,13 @@
     tile = (COLD, hd)
     payload = (devices, 3 * heads + 1, *tile)
     table, h0, h1, h2, h3, send = call(
-        pack_kernel, "pack", 58, [VMEM, HBM, HBM, HBM],
-        [(VMEM, (2 * heads, tokens), F32)] + [(VMEM, (6, *tile), BF16)] * 4 + [(HBM, payload, BF16)],
+        pack_kernel, "pack", 58, [HBM] * 4,
+        [(HBM, (2 * heads, tokens), F32)] + [(HBM, (6, *tile), BF16)] * 4 + [(HBM, payload, BF16)],
         [
+            pltpu.VMEM((heads, tokens), jnp.int32), pltpu.VMEM((2 * heads, tokens), F32),
             pltpu.VMEM((heads, tokens, 3 * hd), BF16),
             pltpu.VMEM((heads, 6, *tile), BF16), pltpu.VMEM(payload, BF16),
-            pltpu.SemaphoreType.DMA((3 * heads,)), pltpu.SemaphoreType.DMA((4,)),
+            pltpu.SemaphoreType.DMA((3 * heads + 1,)), pltpu.SemaphoreType.DMA((9,)),
         ],
         cluster_ids, query_rows, key_rows, value_rows,
     )
@@ -322,7 +344,9 @@
     got, kv = lax.optimization_barrier((got, kv))
     near = [kv] + [shift(kv, "z", d) for d in (1, 2, 3)]
     (answer,) = call(
-        cold_kernel, "cold", 24, [VMEM], [(VMEM, (devices, heads, *tile), BF16)], [], got, flops=20_000_000_000,
+        cold_kernel, "cold", 24, [VMEM], [(HBM, (devices, heads, *tile), BF16)],
+        [pltpu.VMEM((devices, heads, *tile), BF16), pltpu.SemaphoreType.DMA((heads,))],
+        got, flops=20_000_000_000,
     )
     near, _ = lax.optimization_barrier((near, answer))
     near = jnp.concatenate(near, axis=0)
@@ -339,8 +363,11 @@
     hot_out = [outs[0]] + [shift(b, "y", 3 - d) for d, b in enumerate(outs[1:])]
     back = lax.all_to_all(answer, AXES, split_axis=0, concat_axis=0, tiled=True)
     (result,) = call(
-        unpack_kernel, "unpack", 24, [VMEM] * 6, [(VMEM, (tokens, heads * hd), BF16)],
-        [pltpu.VMEM((4, 3, *tile), F32)],
+        unpack_kernel, "unpack", 24, [VMEM] * 6, [(HBM, (tokens, heads * hd), BF16)],
+        [
+            pltpu.VMEM((4, 3, *tile), F32), pltpu.VMEM((tokens, heads * hd), BF16),
+            pltpu.SemaphoreType.DMA((4,)),
+        ],
         table, back, *hot_out,
     )
     return result

time: 106 us -> 105 us (level)
    unnamed x15 -> x13, local copies, waits for them, and re-layouts: 3.84 us -> 2.88 us
  transfers between devices with their start and end apart: 12 -> 12, of which waited for: 7 -> 7; matrix products, arithmetic and copies ran while one was open for 4% -> 4% of each run, Pallas kernels for 6% -> 7%
where the time goes in v9:
time: 105 us
  waiting for transfers between devices  48 us (46%)
  starting transfers between devices  31.3 us (30%)
  Pallas kernels  21.4 us (20%)
  local copies, waits for them, and re-layouts  3.83 us (4%)
    ppermute x10, waiting for transfers between devices, shift(): lax.ppermute(block, axis, [(i, (i + by) % size) for i in range(size)])  36.9 us
    pallas_call x5, Pallas kernels, call(): pl.pallas_call(kernel, out_shape=tuple((pltpu.HBM(*out[1:]) if out[0] is...  21.4 us
    ppermute x10, starting transfers between devices, shift(): lax.ppermute(block, axis, [(i, (i + by) % size) for i in range(size)])  12.5 us
    all_to_all x1, starting transfers between devices, local(): got = lax.all_to_all(send, AXES, split_axis=0, concat_axis=0, tiled=True)  11.1 us
    all_to_all x1, starting transfers between devices, local(): back = lax.all_to_all(answer, AXES, split_axis=0, concat_axis=0, tiled=True)  7.68 us
    all_to_all x1, waiting for transfers between devices, local(): got = lax.all_to_all(send, AXES, split_axis=0, concat_axis=0, tiled=True)  7.45 us
    all_to_all x1, waiting for transfers between devices, local(): back = lax.all_to_all(answer, AXES, split_axis=0, concat_axis=0, tiled=True)  3.66 us
    unnamed x13, local copies, waits for them, and re-layouts  2.88 us
  transfers between devices with their start and end apart: 12, of which 7 were waited for; matrix products, arithmetic and copies ran while one was open for 4% of the time, Pallas kernels for 7%

profile of v9, /device:TPU:0, one launch (start us, length us, event | category | flops | bytes accessed | tf_op | source)
XLA Modules:
  0.0 104.8 jit_solution(11144174718852051801)
XLA Ops:
  0.0 8.9 %pack.1 = (f32[8,1024]{1,0:T(8,128)}, bf16[6,8,128]{2,1,0:T(8,128)(2,1)}, bf16[6,8,128]{2,1,0:T(8,128)(2,1)}, bf16[6,8,128]{2,1,0:T(8,128)(2,1)}, bf16[6,8,128]{...) custom-call(s32[4,1024]{1,0:T(4,128)} %ids_hbm.1, bf16[1024,512]{1,0:T(8,128)(2,1)} %q_hbm.1, bf16[1024,512]{1,0:T(8,128)(2,1)} %k_hbm.1, ...), custom_call_target="tpu_custom_call" | custom-call | tf_op jit(solution)/shard_map/pack/pallas_call | solution.py:304
  8.9 0.0 copy-start.4
  8.9 11.1 %all-to-all-start = ((bf16[128,13,8,128]{3,2,1,0:T(8,128)(2,1)}), bf16[128,13,8,128]{3,2,1,0:T(8,128)(2,1)S(1)}, u32[]{:S(2)}, u32[]{:S(2)}) async-start(bf16[128,13,8,128]{3,2,1,0:T(8,128)(2,1)} %get-tuple-element.27), calls=%async_computation | async-start | bytes 6815744 | tf_op jit(solution)/shard_map/all_to_all | solution.py:340
  20.1 1.0 collective-permute-start
  21.1 2.7 %collective-permute-start.1 = (bf16[6,8,128]{2,1,0:T(8,128)(2,1)S(1)}, bf16[6,8,128]{2,1,0:T(8,128)(2,1)S(1)}, u32[]{:S(2)}, u32[]{:S(2)}) collective-permute-start(bf16[6,8,128]{2,1,0:T(8,128)(2,1)S(1)} %copy-done.3), channel_id=1, source_target_pairs={{0,2},{1,3},{2,0},{3,1},{4,6},{5,7},{6,4},{7,5},{8,10},{9,11},{10,... | collective-permute-start | bytes 36872 | tf_op jit(solution)/shard_map/ppermute | solution.py:320
  23.9 1.4 %collective-permute-start.2 = (bf16[6,8,128]{2,1,0:T(8,128)(2,1)S(1)}, bf16[6,8,128]{2,1,0:T(8,128)(2,1)S(1)}, u32[]{:S(2)}, u32[]{:S(2)}) collective-permute-start(bf16[6,8,128]{2,1,0:T(8,128)(2,1)S(1)} %copy-done.2), channel_id=1, source_target_pairs={{0,3},{1,0},{2,1},{3,2},{4,7},{5,4},{6,5},{7,6},{8,11},{9,8},{10,9... | collective-permute-start | bytes 36872 | tf_op jit(solution)/shard_map/ppermute | solution.py:320
  25.3 29.7 %collective-permute-done.b1_ref = bf16[6,8,128]{2,1,0:T(8,128)(2,1)S(1)} collective-permute-done((bf16[6,8,128]{2,1,0:T(8,128)(2,1)S(1)}, bf16[6,8,128]{2,1,0:T(8,128)(2,1)S(1)}, u32[]{:S(2)}, u32[]{:S(2)}) %collective-permute-start) | collective-permute-done | bytes 12320 | tf_op jit(solution)/shard_map/ppermute | solution.py:320
  54.9 0.8 collective-permute-done.2.b3_ref
  55.8 7.5 %all-to-all-done.got_ref = bf16[128,13,8,128]{3,2,1,0:T(8,128)(2,1)S(1)} async-done(((bf16[128,13,8,128]{3,2,1,0:T(8,128)(2,1)}), bf16[128,13,8,128]{3,2,1,0:T(8,128)(2,1)S(1)}, u32[]{:S(2)}, u32[]{:S(2)}) %all-to-all-start) | async-done | bytes 3407904 | tf_op jit(solution)/shard_map/all_to_all | solution.py:340
  63.2 1.7 %mid.1 = bf16[97,8,128]{2,1,0:T(8,128)(2,1)} custom-call(bf16[128,13,8,128]{3,2,1,0:T(8,128)(2,1)S(1)} %all-to-all-done.got_ref), custom_call_target="tpu_custom_call" | custom-call | tf_op jit(solution)/shard_map/mid/pallas_call | solution.py:304
  64.9 1.8 %collective-permute-start.5 = (bf16[97,8,128]{2,1,0:T(8,128)(2,1)}, bf16[97,8,128]{2,1,0:T(8,128)(2,1)}, u32[]{:S(2)}, u32[]{:S(2)}) collective-permute-start(bf16[97,8,128]{2,1,0:T(8,128)(2,1)} %mid.1), channel_id=1, source_target_pairs={{0,96},{32,0},{64,32},{96,64},{1,97},{33,1},{65,33},{97,65},{2,98}... | collective-permute-start | bytes 595976 | tf_op jit(solution)/shard_map/ppermute | solution.py:320
  66.7 1.1 %collective-permute-start.4 = (bf16[97,8,128]{2,1,0:T(8,128)(2,1)}, bf16[97,8,128]{2,1,0:T(8,128)(2,1)}, u32[]{:S(2)}, u32[]{:S(2)}) collective-permute-start(bf16[97,8,128]{2,1,0:T(8,128)(2,1)} %mid.1), channel_id=1, source_target_pairs={{0,64},{32,96},{64,0},{96,32},{1,65},{33,97},{65,1},{97,33},{2,66}... | collective-permute-start | bytes 595976 | tf_op jit(solution)/shard_map/ppermute | solution.py:320
  67.8 0.3 collective-permute-start.3
  68.2 5.9 %cold.1 = bf16[128,4,8,128]{3,2,1,0:T(8,128)(2,1)} custom-call(bf16[128,13,8,128]{3,2,1,0:T(8,128)(2,1)S(1)} %all-to-all-done.got_ref), custom_call_target="tpu_custom_call" | custom-call | flops 20000000000 | tf_op jit(solution)/shard_map/cold/pallas_call | solution.py:304
  74.1 7.7 %all-to-all-start.1 = ((bf16[128,4,8,128]{3,2,1,0:T(8,128)(2,1)}), bf16[128,4,8,128]{3,2,1,0:T(8,128)(2,1)S(1)}, u32[]{:S(2)}, u32[]{:S(2)}) async-start(bf16[128,4,8,128]{3,2,1,0:T(8,128)(2,1)} %cold.1), calls=%async_computation.1 | async-start | bytes 2097152 | tf_op jit(solution)/shard_map/all_to_all | solution.py:364
  81.8 0.0 collective-permute-done.5
  81.8 0.0 collective-permute-done.4
  81.8 0.9 constant_dynamic-update-slice_fusion.3
  82.8 1.0 constant_dynamic-update-slice_fusion.2
  83.7 1.0 constant_dynamic-update-slice_fusion.1
  84.7 1.0 constant_dynamic-update-slice_fusion.near_ref
  85.6 0.1 collective-permute-start.6
  85.7 2.3 %collective-permute-done.6.far_ref = bf16[388,8,128]{2,1,0:T(8,128)(2,1)S(1)} collective-permute-done((bf16[388,8,128]{2,1,0:T(8,128)(2,1)S(1)}, bf16[388,8,128]{2,1,0:T(8,128)(2,1)S(1)}, u32[]{:S(2)}, u32[]{:S(2)}) %collective-permute-start.6) | collective-permute-done | bytes 794656 | tf_op jit(solution)/shard_map/ppermute | solution.py:320
  88.0 1.1 %hot.1 = (bf16[3,8,128]{2,1,0:T(8,128)(2,1)S(1)}, bf16[3,8,128]{2,1,0:T(8,128)(2,1)S(1)}, bf16[3,8,128]{2,1,0:T(8,128)(2,1)S(1)}, bf16[3,8,128]{2,1,0:T(8,128)(2,1)S(1)}) custom-call(bf16[6,8,128]{2,1,0:T(8,128)(2,1)S(1)} %copy-done.1, bf16[6,8,128]{2,1,0:T(8,128)(2,1)S(1)} %collective-permute-done.b1_ref, ...), custom_call_target="tpu_custom_call" | custom-call | flops 2000000000 | tf_op jit(solution)/shard_map/hot/pallas_call | solution.py:304
  89.1 2.3 %collective-permute-start.7 = (bf16[3,8,128]{2,1,0:T(8,128)(2,1)S(1)}, bf16[3,8,128]{2,1,0:T(8,128)(2,1)S(1)}, u32[]{:S(2)}, u32[]{:S(2)}) collective-permute-start(bf16[3,8,128]{2,1,0:T(8,128)(2,1)S(1)} %get-tuple-element.44), channel_id=1, source_target_pairs={{0,3},{1,0},{2,1},{3,2},{4,7},{5,4},{6,5},{7,6},{8,11},{9,8},{10,9... | collective-permute-start | bytes 18440 | tf_op jit(solution)/shard_map/ppermute | solution.py:320
  91.4 0.8 collective-permute-start.8
  92.2 0.9 collective-permute-start.9
  93.1 0.0 collective-permute-done.7.o1_ref
  93.1 3.9 %collective-permute-done.8.o2_ref = bf16[3,8,128]{2,1,0:T(8,128)(2,1)S(1)} collective-permute-done((bf16[3,8,128]{2,1,0:T(8,128)(2,1)S(1)}, bf16[3,8,128]{2,1,0:T(8,128)(2,1)S(1)}, u32[]{:S(2)}, u32[]{:S(2)}) %collective-permute-start.8) | collective-permute-done | bytes 6176 | tf_op jit(solution)/shard_map/ppermute | solution.py:320
  97.0 0.2 collective-permute-done.9.o3_ref
  97.2 3.7 %all-to-all-done.1.back_ref = bf16[128,4,8,128]{3,2,1,0:T(8,128)(2,1)S(1)} async-done(((bf16[128,4,8,128]{3,2,1,0:T(8,128)(2,1)}), bf16[128,4,8,128]{3,2,1,0:T(8,128)(2,1)S(1)}, u32[]{:S(2)}, u32[]{:S(2)}) %all-to-all-start.1) | async-done | bytes 1048608 | tf_op jit(solution)/shard_map/all_to_all | solution.py:364
  100.8 3.8 %unpack.1 = bf16[1024,512]{1,0:T(8,128)(2,1)} custom-call(f32[8,1024]{1,0:T(8,128)S(1)} %copy-done, bf16[128,4,8,128]{3,2,1,0:T(8,128)(2,1)S(1)} %all-to-all-done.1.back_ref, bf16[3,8,128]{2,1,0:T(8,128)(2,1)S(1)} %get-tuple-element.43.o0_ref, bf16[3,8,128]{2,1,0:T(8,128)(2,1)S(1)} %collective-permute-done.7.o1_ref, ...), custom_call_target="tpu_custom_call" | custom-call | tf_op jit(solution)/shard_map/unpack/pallas_call | solution.py:304
  (11 shorter events, 0.0 us)
Async XLA Ops:
  8.9 11.2 %copy-start.4 = (bf16[6,8,128]{2,1,0:T(8,128)(2,1)S(1)}, bf16[6,8,128]{2,1,0:T(8,128)(2,1)}, u32[]{:S(2)}) copy-start(bf16[6,8,128]{2,1,0:T(8,128)(2,1)} %get-tuple-element.29) | copy-start | bytes 36868
  8.9 12.2 %copy-start.3 = (bf16[6,8,128]{2,1,0:T(8,128)(2,1)S(1)}, bf16[6,8,128]{2,1,0:T(8,128)(2,1)}, u32[]{:S(2)}) copy-start(bf16[6,8,128]{2,1,0:T(8,128)(2,1)} %get-tuple-element.30) | copy-start | bytes 36868
  8.9 14.9 %copy-start.2 = (bf16[6,8,128]{2,1,0:T(8,128)(2,1)S(1)}, bf16[6,8,128]{2,1,0:T(8,128)(2,1)}, u32[]{:S(2)}) copy-start(bf16[6,8,128]{2,1,0:T(8,128)(2,1)} %get-tuple-element.31) | copy-start | bytes 36868
  8.9 54.3 %all-to-all-start = ((bf16[128,13,8,128]{3,2,1,0:T(8,128)(2,1)}), bf16[128,13,8,128]{3,2,1,0:T(8,128)(2,1)S(1)}, u32[]{:S(2)}, u32[]{:S(2)}) async-start(bf16[128,13,8,128]{3,2,1,0:T(8,128)(2,1)} %get-tuple-element.27), calls=%async_computation | async-start | bytes 6815744 | tf_op jit(solution)/shard_map/all_to_all | solution.py:340
  20.1 34.8 %collective-permute-start = (bf16[6,8,128]{2,1,0:T(8,128)(2,1)S(1)}, bf16[6,8,128]{2,1,0:T(8,128)(2,1)S(1)}, u32[]{:S(2)}, u32[]{:S(2)}) collective-permute-start(bf16[6,8,128]{2,1,0:T(8,128)(2,1)S(1)} %copy-done.4), channel_id=1, source_target_pairs={{0,1},{1,2},{2,3},{3,0},{4,5},{5,6},{6,7},{7,4},{8,9},{9,10},{10,1... | collective-permute-start | bytes 36872 | tf_op jit(solution)/shard_map/ppermute | solution.py:320
  21.1 33.8 %collective-permute-start.1 = (bf16[6,8,128]{2,1,0:T(8,128)(2,1)S(1)}, bf16[6,8,128]{2,1,0:T(8,128)(2,1)S(1)}, u32[]{:S(2)}, u32[]{:S(2)}) collective-permute-start(bf16[6,8,128]{2,1,0:T(8,128)(2,1)S(1)} %copy-done.3), channel_id=1, source_target_pairs={{0,2},{1,3},{2,0},{3,1},{4,6},{5,7},{6,4},{7,5},{8,10},{9,11},{10,... | collective-permute-start | bytes 36872 | tf_op jit(solution)/shard_map/ppermute | solution.py:320
  23.9 31.9 %collective-permute-start.2 = (bf16[6,8,128]{2,1,0:T(8,128)(2,1)S(1)}, bf16[6,8,128]{2,1,0:T(8,128)(2,1)S(1)}, u32[]{:S(2)}, u32[]{:S(2)}) collective-permute-start(bf16[6,8,128]{2,1,0:T(8,128)(2,1)S(1)} %copy-done.2), channel_id=1, source_target_pairs={{0,3},{1,0},{2,1},{3,2},{4,7},{5,4},{6,5},{7,6},{8,11},{9,8},{10,9... | collective-permute-start | bytes 36872 | tf_op jit(solution)/shard_map/ppermute | solution.py:320
  64.9 16.9 %collective-permute-start.5 = (bf16[97,8,128]{2,1,0:T(8,128)(2,1)}, bf16[97,8,128]{2,1,0:T(8,128)(2,1)}, u32[]{:S(2)}, u32[]{:S(2)}) collective-permute-start(bf16[97,8,128]{2,1,0:T(8,128)(2,1)} %mid.1), channel_id=1, source_target_pairs={{0,96},{32,0},{64,32},{96,64},{1,97},{33,1},{65,33},{97,65},{2,98}... | collective-permute-start | bytes 595976 | tf_op jit(solution)/shard_map/ppermute | solution.py:320
  66.7 15.1 %collective-permute-start.4 = (bf16[97,8,128]{2,1,0:T(8,128)(2,1)}, bf16[97,8,128]{2,1,0:T(8,128)(2,1)}, u32[]{:S(2)}, u32[]{:S(2)}) collective-permute-start(bf16[97,8,128]{2,1,0:T(8,128)(2,1)} %mid.1), channel_id=1, source_target_pairs={{0,64},{32,96},{64,0},{96,32},{1,65},{33,97},{65,1},{97,33},{2,66}... | collective-permute-start | bytes 595976 | tf_op jit(solution)/shard_map/ppermute | solution.py:320
  67.8 14.0 %collective-permute-start.3 = (bf16[97,8,128]{2,1,0:T(8,128)(2,1)}, bf16[97,8,128]{2,1,0:T(8,128)(2,1)}, u32[]{:S(2)}, u32[]{:S(2)}) collective-permute-start(bf16[97,8,128]{2,1,0:T(8,128)(2,1)} %mid.1), channel_id=1, source_target_pairs={{0,32},{32,64},{64,96},{96,0},{1,33},{33,65},{65,97},{97,1},{2,34}... | collective-permute-start | bytes 595976 | tf_op jit(solution)/shard_map/ppermute | solution.py:320
  74.1 13.9 %copy-start.1 = (bf16[6,8,128]{2,1,0:T(8,128)(2,1)S(1)}, bf16[6,8,128]{2,1,0:T(8,128)(2,1)}, u32[]{:S(2)}) copy-start(bf16[6,8,128]{2,1,0:T(8,128)(2,1)} %get-tuple-element.34.b0_ref) | copy-start | bytes 36868
  74.1 26.7 %all-to-all-start.1 = ((bf16[128,4,8,128]{3,2,1,0:T(8,128)(2,1)}), bf16[128,4,8,128]{3,2,1,0:T(8,128)(2,1)S(1)}, u32[]{:S(2)}, u32[]{:S(2)}) async-start(bf16[128,4,8,128]{3,2,1,0:T(8,128)(2,1)} %cold.1), calls=%async_computation.1 | async-start | bytes 2097152 | tf_op jit(solution)/shard_map/all_to_all | solution.py:364
  85.6 15.2 %copy-start = (f32[8,1024]{1,0:T(8,128)S(1)}, f32[8,1024]{1,0:T(8,128)}, u32[]{:S(2)}) copy-start(f32[8,1024]{1,0:T(8,128)} %get-tuple-element.26.table_ref) | copy-start | bytes 98308
  85.6 2.4 %collective-permute-start.6 = (bf16[388,8,128]{2,1,0:T(8,128)(2,1)S(1)}, bf16[388,8,128]{2,1,0:T(8,128)(2,1)S(1)}, u32[]{:S(2)}, u32[]{:S(2)}) collective-permute-start(bf16[388,8,128]{2,1,0:T(8,128)(2,1)S(1)} %constant_dynamic-update-slice_fusion.near_ref), channel_id=1, source_target_pairs={{0,16},{16,0},{1,17},{17,1},{2,18},{18,2},{3,19},{19,3},{4,20},{20... | collective-permute-start | bytes 2383880 | tf_op jit(solution)/shard_map/ppermute | solution.py:320
  89.1 4.0 %collective-permute-start.7 = (bf16[3,8,128]{2,1,0:T(8,128)(2,1)S(1)}, bf16[3,8,128]{2,1,0:T(8,128)(2,1)S(1)}, u32[]{:S(2)}, u32[]{:S(2)}) collective-permute-start(bf16[3,8,128]{2,1,0:T(8,128)(2,1)S(1)} %get-tuple-element.44), channel_id=1, source_target_pairs={{0,3},{1,0},{2,1},{3,2},{4,7},{5,4},{6,5},{7,6},{8,11},{9,8},{10,9... | collective-permute-start | bytes 18440 | tf_op jit(solution)/shard_map/ppermute | solution.py:320
  91.4 5.6 %collective-permute-start.8 = (bf16[3,8,128]{2,1,0:T(8,128)(2,1)S(1)}, bf16[3,8,128]{2,1,0:T(8,128)(2,1)S(1)}, u32[]{:S(2)}, u32[]{:S(2)}) collective-permute-start(bf16[3,8,128]{2,1,0:T(8,128)(2,1)S(1)} %get-tuple-element.45), channel_id=1, source_target_pairs={{0,2},{1,3},{2,0},{3,1},{4,6},{5,7},{6,4},{7,5},{8,10},{9,11},{10,... | collective-permute-start | bytes 18440 | tf_op jit(solution)/shard_map/ppermute | solution.py:320
  92.2 5.0 %collective-permute-start.9 = (bf16[3,8,128]{2,1,0:T(8,128)(2,1)S(1)}, bf16[3,8,128]{2,1,0:T(8,128)(2,1)S(1)}, u32[]{:S(2)}, u32[]{:S(2)}) collective-permute-start(bf16[3,8,128]{2,1,0:T(8,128)(2,1)S(1)} %get-tuple-element.46), channel_id=1, source_target_pairs={{0,1},{1,2},{2,3},{3,0},{4,5},{5,6},{6,7},{7,4},{8,9},{9,10},{10,1... | collective-permute-start | bytes 18440 | tf_op jit(solution)/shard_map/ppermute | solution.py:320

commit v10 on v9

--- a/solution.py
+++ b/solution.py
@@ -34,7 +34,7 @@
 def pack_kernel(
     ids_hbm, q_hbm, k_hbm, v_hbm,
     table_hbm, h0_hbm, h1_hbm, h2_hbm, h3_hbm, send_hbm,
-    ids_ref, table_ref, x_ref, hot_ref, send_ref, sems, out_sems,
+    ids_ref, table_ref, q_ref, k_ref, v_ref, hot_ref, send_ref, sems, out_sems,
 ):
     heads, tokens = ids_ref.shape
     hd = q_hbm.shape[1] // heads
@@ -44,17 +44,12 @@
     ids_load = pltpu.make_async_copy(ids_hbm, ids_ref, sems.at[3 * heads])
     ids_load.start()
     loads = [
-        [
-            pltpu.make_async_copy(
-                src.at[:, h * hd : (h + 1) * hd], x_ref.at[h, :, j * hd : (j + 1) * hd], sems.at[3 * h + j]
-            )
-            for j, src in enumerate((q_hbm, k_hbm, v_hbm))
-        ]
-        for h in range(heads)
+        pltpu.make_async_copy(src.at[r * 512 : (r + 1) * 512], dst.at[r * 512 : (r + 1) * 512], sems.at[2 * j + r])
+        for j, (src, dst) in enumerate(((q_hbm, q_ref), (k_hbm, k_ref), (v_hbm, v_ref)))
+        for r in range(2)
     ]
-    for row in loads:
-        for load in row:
-            load.start()
+    for load in loads:
+        load.start()
     ids_load.wait()
     ids = ids_ref[...]
     owner = ids // CL_DEV
@@ -106,11 +101,13 @@
     want = jnp.where(row < rows, want, row - rows) + slots
     tile_at = iota((rows, hd), 0) % COLD
     hot_tiles = []
-    for h in range(heads):
-        for load in loads[h]:
-            load.wait()
+    xs = []
+    for load in loads:
+        load.wait()
+    for h in range(heads):
+        xs.append(jnp.concatenate([ref[:, h * hd : (h + 1) * hd] for ref in (q_ref, k_ref, v_ref)], axis=1))
         moved = jnp.dot(
-            (slot_all[h : h + 1] == want).astype(BF16), x_ref[h], preferred_element_type=F32
+            (slot_all[h : h + 1] == want).astype(BF16), xs[h], preferred_element_type=F32
         )
         tiles = jnp.where(tile_at < SHARE, moved[:rows, hd : 2 * hd], moved[:rows, 2 * hd :])
         tiles = jnp.where(tile_at == COLD - 1, asked_tags, tiles)
@@ -127,7 +124,7 @@
         first, stop = c * part // COLD, (c + 1) * part // COLD
         for h in range(heads):
             place = (slot_all[h : h + 1] == iota((part, tokens), 0) + c * part).astype(BF16)
-            moved = jnp.dot(place, x_ref[h], preferred_element_type=F32)
+            moved = jnp.dot(place, xs[h], preferred_element_type=F32)
             for j in range(3):
                 send_ref[first:stop, 3 * h + j] = (
                     moved[:, j * hd : (j + 1) * hd].reshape(stop - first, COLD, hd).astype(BF16)
@@ -202,7 +199,7 @@
         out.wait()
 
 
-def mid_kernel(got_ref, kv_ref):
+def mid_kernel(got_ref, kv_hbm, kv_ref, sems):
     devices, tiles, _, hd = got_ref.shape
     slots = devices * COLD
     keys = devices * SHARE
@@ -215,8 +212,15 @@
         place = (col == source * COLD + offset).astype(BF16)
         return jnp.dot(place, extra, preferred_element_type=F32)
 
+    parts = (slice(0, 48), slice(48, 96), slice(96, 97))
+    sent = [
+        pltpu.make_async_copy(kv_ref.at[part], kv_hbm.at[part], sems.at[i])
+        for i, part in enumerate(parts)
+    ]
     kv_ref[0:48] = rows_at(at).reshape(48, COLD, hd).astype(BF16)
+    sent[0].start()
     kv_ref[48:96] = rows_at(at + SHARE).reshape(48, COLD, hd).astype(BF16)
+    sent[1].start()
     y, core, z = (lax.axis_index(a) for a in ("y", "core", "z"))
     lane = HOT_LANE + HOT * y + SHARE * (z * 2 + core) + at
     tags = jnp.where(iota((keys, hd), 1) == lane, rows_at(COLD - 1), 0.0).astype(BF16)
@@ -224,6 +228,9 @@
     label = [flat[0:1, j * LANES : (j + 1) * LANES] for j in range(keys // LANES)]
     label.append(jnp.zeros((COLD - len(label), LANES), F32))
     kv_ref[96] = jnp.concatenate(label, axis=0).astype(BF16)
+    sent[2].start()
+    for out in sent:
+        out.wait()
 
 
 def hot_kernel(
@@ -331,7 +338,7 @@
         [(HBM, (2 * heads, tokens), F32)] + [(HBM, (6, *tile), BF16)] * 4 + [(HBM, payload, BF16)],
         [
             pltpu.VMEM((heads, tokens), jnp.int32), pltpu.VMEM((2 * heads, tokens), F32),
-            pltpu.VMEM((heads, tokens, 3 * hd), BF16),
+            *[pltpu.VMEM((tokens, heads * hd), BF16)] * 3,
             pltpu.VMEM((heads, 6, *tile), BF16), pltpu.VMEM(payload, BF16),
             pltpu.SemaphoreType.DMA((3 * heads + 1,)), pltpu.SemaphoreType.DMA((9,)),
         ],
@@ -340,7 +347,10 @@
     got = lax.all_to_all(send, AXES, split_axis=0, concat_axis=0, tiled=True)
     asked = [h0] + [shift(b, "y", d + 1) for d, b in enumerate((h1, h2, h3))]
     got, asked = lax.optimization_barrier((got, asked))
-    (kv,) = call(mid_kernel, "mid", 24, [VMEM], [(VMEM, (97, *tile), BF16)], [], got)
+    (kv,) = call(
+        mid_kernel, "mid", 24, [VMEM], [(HBM, (97, *tile), BF16)],
+        [pltpu.VMEM((97, *tile), BF16), pltpu.SemaphoreType.DMA((3,))], got,
+    )
     got, kv = lax.optimization_barrier((got, kv))
     near = [kv] + [shift(kv, "z", d) for d in (1, 2, 3)]
     (answer,) = call(

time: 105 us -> 105 us (level)
  no operation moved by 1% of the time
where the time goes in v10:
time: 105 us; the launch traced here: 104 us
  waiting for transfers between devices  48 us (46%)
  starting transfers between devices  31.4 us (30%)
  Pallas kernels  20.8 us (20%)
  local copies, waits for them, and re-layouts  3.83 us (4%)
    ppermute x10, waiting for transfers between devices, shift(): lax.ppermute(block, axis, [(i, (i + by) % size) for i in range(size)])  36.9 us
    pallas_call x5, Pallas kernels, call(): pl.pallas_call(kernel, out_shape=tuple((pltpu.HBM(*out[1:]) if out[0] is...  20.8 us
    ppermute x10, starting transfers between devices, shift(): lax.ppermute(block, axis, [(i, (i + by) % size) for i in range(size)])  12.5 us
    all_to_all x1, starting transfers between devices, local(): got = lax.all_to_all(send, AXES, split_axis=0, concat_axis=0, tiled=True)  11.2 us
    all_to_all x1, starting transfers between devices, local(): back = lax.all_to_all(answer, AXES, split_axis=0, concat_axis=0, tiled=True)  7.68 us
    all_to_all x1, waiting for transfers between devices, local(): got = lax.all_to_all(send, AXES, split_axis=0, concat_axis=0, tiled=True)  7.45 us
    all_to_all x1, waiting for transfers between devices, local(): back = lax.all_to_all(answer, AXES, split_axis=0, concat_axis=0, tiled=True)  3.66 us
    unnamed x13, local copies, waits for them, and re-layouts  2.88 us
  transfers between devices with their start and end apart: 12, of which 7 were waited for; matrix products, arithmetic and copies ran while one was open for 4% of the time, Pallas kernels for 7%

profile of v10, /device:TPU:0, one launch (start us, length us, event | category | flops | bytes accessed | tf_op | source)
XLA Modules:
  0.0 104.4 jit_solution(5126642118529529271)
XLA Ops:
  0.0 8.5 %pack.1 = (f32[8,1024]{1,0:T(8,128)}, bf16[6,8,128]{2,1,0:T(8,128)(2,1)}, bf16[6,8,128]{2,1,0:T(8,128)(2,1)}, bf16[6,8,128]{2,1,0:T(8,128)(2,1)}, bf16[6,8,128]{...) custom-call(s32[4,1024]{1,0:T(4,128)} %ids_hbm.1, bf16[1024,512]{1,0:T(8,128)(2,1)} %q_hbm.1, bf16[1024,512]{1,0:T(8,128)(2,1)} %k_hbm.1, ...), custom_call_target="tpu_custom_call" | custom-call | tf_op jit(solution)/shard_map/pack/pallas_call | solution.py:311
  8.5 0.0 copy-start.4
  8.5 11.2 %all-to-all-start = ((bf16[128,13,8,128]{3,2,1,0:T(8,128)(2,1)}), bf16[128,13,8,128]{3,2,1,0:T(8,128)(2,1)S(1)}, u32[]{:S(2)}, u32[]{:S(2)}) async-start(bf16[128,13,8,128]{3,2,1,0:T(8,128)(2,1)} %get-tuple-element.27), calls=%async_computation | async-start | bytes 6815744 | tf_op jit(solution)/shard_map/all_to_all | solution.py:347
  19.7 1.0 collective-permute-start
  20.7 2.7 %collective-permute-start.1 = (bf16[6,8,128]{2,1,0:T(8,128)(2,1)S(1)}, bf16[6,8,128]{2,1,0:T(8,128)(2,1)S(1)}, u32[]{:S(2)}, u32[]{:S(2)}) collective-permute-start(bf16[6,8,128]{2,1,0:T(8,128)(2,1)S(1)} %copy-done.3), channel_id=1, source_target_pairs={{0,2},{1,3},{2,0},{3,1},{4,6},{5,7},{6,4},{7,5},{8,10},{9,11},{10,... | collective-permute-start | bytes 36872 | tf_op jit(solution)/shard_map/ppermute | solution.py:327
  23.4 1.4 %collective-permute-start.2 = (bf16[6,8,128]{2,1,0:T(8,128)(2,1)S(1)}, bf16[6,8,128]{2,1,0:T(8,128)(2,1)S(1)}, u32[]{:S(2)}, u32[]{:S(2)}) collective-permute-start(bf16[6,8,128]{2,1,0:T(8,128)(2,1)S(1)} %copy-done.2), channel_id=1, source_target_pairs={{0,3},{1,0},{2,1},{3,2},{4,7},{5,4},{6,5},{7,6},{8,11},{9,8},{10,9... | collective-permute-start | bytes 36872 | tf_op jit(solution)/shard_map/ppermute | solution.py:327
  24.8 29.7 %collective-permute-done.b1_ref = bf16[6,8,128]{2,1,0:T(8,128)(2,1)S(1)} collective-permute-done((bf16[6,8,128]{2,1,0:T(8,128)(2,1)S(1)}, bf16[6,8,128]{2,1,0:T(8,128)(2,1)S(1)}, u32[]{:S(2)}, u32[]{:S(2)}) %collective-permute-start) | collective-permute-done | bytes 12320 | tf_op jit(solution)/shard_map/ppermute | solution.py:327
  54.5 0.8 collective-permute-done.2.b3_ref
  55.3 7.5 %all-to-all-done.got_ref = bf16[128,13,8,128]{3,2,1,0:T(8,128)(2,1)S(1)} async-done(((bf16[128,13,8,128]{3,2,1,0:T(8,128)(2,1)}), bf16[128,13,8,128]{3,2,1,0:T(8,128)(2,1)S(1)}, u32[]{:S(2)}, u32[]{:S(2)}) %all-to-all-start) | async-done | bytes 3407904 | tf_op jit(solution)/shard_map/all_to_all | solution.py:347
  62.8 1.6 %mid.1 = bf16[97,8,128]{2,1,0:T(8,128)(2,1)} custom-call(bf16[128,13,8,128]{3,2,1,0:T(8,128)(2,1)S(1)} %all-to-all-done.got_ref), custom_call_target="tpu_custom_call" | custom-call | tf_op jit(solution)/shard_map/mid/pallas_call | solution.py:311
  64.4 1.9 %collective-permute-start.5 = (bf16[97,8,128]{2,1,0:T(8,128)(2,1)}, bf16[97,8,128]{2,1,0:T(8,128)(2,1)}, u32[]{:S(2)}, u32[]{:S(2)}) collective-permute-start(bf16[97,8,128]{2,1,0:T(8,128)(2,1)} %mid.1), channel_id=1, source_target_pairs={{0,96},{32,0},{64,32},{96,64},{1,97},{33,1},{65,33},{97,65},{2,98}... | collective-permute-start | bytes 595976 | tf_op jit(solution)/shard_map/ppermute | solution.py:327
  66.3 1.1 %collective-permute-start.4 = (bf16[97,8,128]{2,1,0:T(8,128)(2,1)}, bf16[97,8,128]{2,1,0:T(8,128)(2,1)}, u32[]{:S(2)}, u32[]{:S(2)}) collective-permute-start(bf16[97,8,128]{2,1,0:T(8,128)(2,1)} %mid.1), channel_id=1, source_target_pairs={{0,64},{32,96},{64,0},{96,32},{1,65},{33,97},{65,1},{97,33},{2,66}... | collective-permute-start | bytes 595976 | tf_op jit(solution)/shard_map/ppermute | solution.py:327
  67.4 0.3 collective-permute-start.3
  67.7 5.9 %cold.1 = bf16[128,4,8,128]{3,2,1,0:T(8,128)(2,1)} custom-call(bf16[128,13,8,128]{3,2,1,0:T(8,128)(2,1)S(1)} %all-to-all-done.got_ref), custom_call_target="tpu_custom_call" | custom-call | flops 20000000000 | tf_op jit(solution)/shard_map/cold/pallas_call | solution.py:311
  73.6 7.7 %all-to-all-start.1 = ((bf16[128,4,8,128]{3,2,1,0:T(8,128)(2,1)}), bf16[128,4,8,128]{3,2,1,0:T(8,128)(2,1)S(1)}, u32[]{:S(2)}, u32[]{:S(2)}) async-start(bf16[128,4,8,128]{3,2,1,0:T(8,128)(2,1)} %cold.1), calls=%async_computation.1 | async-start | bytes 2097152 | tf_op jit(solution)/shard_map/all_to_all | solution.py:374
  81.3 0.0 collective-permute-done.5
  81.3 0.0 collective-permute-done.3
  81.4 0.9 constant_dynamic-update-slice_fusion.3
  82.3 1.0 constant_dynamic-update-slice_fusion.2
  83.3 1.0 constant_dynamic-update-slice_fusion.1
  84.2 1.0 constant_dynamic-update-slice_fusion.near_ref
  85.2 0.1 collective-permute-start.6
  85.3 2.3 %collective-permute-done.6.far_ref = bf16[388,8,128]{2,1,0:T(8,128)(2,1)S(1)} collective-permute-done((bf16[388,8,128]{2,1,0:T(8,128)(2,1)S(1)}, bf16[388,8,128]{2,1,0:T(8,128)(2,1)S(1)}, u32[]{:S(2)}, u32[]{:S(2)}) %collective-permute-start.6) | collective-permute-done | bytes 794656 | tf_op jit(solution)/shard_map/ppermute | solution.py:327
  87.6 1.1 %hot.1 = (bf16[3,8,128]{2,1,0:T(8,128)(2,1)S(1)}, bf16[3,8,128]{2,1,0:T(8,128)(2,1)S(1)}, bf16[3,8,128]{2,1,0:T(8,128)(2,1)S(1)}, bf16[3,8,128]{2,1,0:T(8,128)(2,1)S(1)}) custom-call(bf16[6,8,128]{2,1,0:T(8,128)(2,1)S(1)} %copy-done.1, bf16[6,8,128]{2,1,0:T(8,128)(2,1)S(1)} %collective-permute-done.b1_ref, ...), custom_call_target="tpu_custom_call" | custom-call | flops 2000000000 | tf_op jit(solution)/shard_map/hot/pallas_call | solution.py:311
  88.6 2.3 %collective-permute-start.7 = (bf16[3,8,128]{2,1,0:T(8,128)(2,1)S(1)}, bf16[3,8,128]{2,1,0:T(8,128)(2,1)S(1)}, u32[]{:S(2)}, u32[]{:S(2)}) collective-permute-start(bf16[3,8,128]{2,1,0:T(8,128)(2,1)S(1)} %get-tuple-element.44), channel_id=1, source_target_pairs={{0,3},{1,0},{2,1},{3,2},{4,7},{5,4},{6,5},{7,6},{8,11},{9,8},{10,9... | collective-permute-start | bytes 18440 | tf_op jit(solution)/shard_map/ppermute | solution.py:327
  90.9 0.8 collective-permute-start.8
  91.7 0.9 collective-permute-start.9
  92.6 0.0 collective-permute-done.7.o1_ref
  92.6 3.9 %collective-permute-done.8.o2_ref = bf16[3,8,128]{2,1,0:T(8,128)(2,1)S(1)} collective-permute-done((bf16[3,8,128]{2,1,0:T(8,128)(2,1)S(1)}, bf16[3,8,128]{2,1,0:T(8,128)(2,1)S(1)}, u32[]{:S(2)}, u32[]{:S(2)}) %collective-permute-start.8) | collective-permute-done | bytes 6176 | tf_op jit(solution)/shard_map/ppermute | solution.py:327
  96.6 0.2 collective-permute-done.9.o3_ref
  96.7 3.7 %all-to-all-done.1.back_ref = bf16[128,4,8,128]{3,2,1,0:T(8,128)(2,1)S(1)} async-done(((bf16[128,4,8,128]{3,2,1,0:T(8,128)(2,1)}), bf16[128,4,8,128]{3,2,1,0:T(8,128)(2,1)S(1)}, u32[]{:S(2)}, u32[]{:S(2)}) %all-to-all-start.1) | async-done | bytes 1048608 | tf_op jit(solution)/shard_map/all_to_all | solution.py:374
  100.4 3.8 %unpack.1 = bf16[1024,512]{1,0:T(8,128)(2,1)} custom-call(f32[8,1024]{1,0:T(8,128)S(1)} %copy-done, bf16[128,4,8,128]{3,2,1,0:T(8,128)(2,1)S(1)} %all-to-all-done.1.back_ref, bf16[3,8,128]{2,1,0:T(8,128)(2,1)S(1)} %get-tuple-element.43.o0_ref, bf16[3,8,128]{2,1,0:T(8,128)(2,1)S(1)} %collective-permute-done.7.o1_ref, ...), custom_call_target="tpu_custom_call" | custom-call | tf_op jit(solution)/shard_map/unpack/pallas_call | solution.py:311
  (11 shorter events, 0.0 us)
Async XLA Ops:
  8.5 11.2 %copy-start.4 = (bf16[6,8,128]{2,1,0:T(8,128)(2,1)S(1)}, bf16[6,8,128]{2,1,0:T(8,128)(2,1)}, u32[]{:S(2)}) copy-start(bf16[6,8,128]{2,1,0:T(8,128)(2,1)} %get-tuple-element.29) | copy-start | bytes 36868
  8.5 12.2 %copy-start.3 = (bf16[6,8,128]{2,1,0:T(8,128)(2,1)S(1)}, bf16[6,8,128]{2,1,0:T(8,128)(2,1)}, u32[]{:S(2)}) copy-start(bf16[6,8,128]{2,1,0:T(8,128)(2,1)} %get-tuple-element.30) | copy-start | bytes 36868
  8.5 14.9 %copy-start.2 = (bf16[6,8,128]{2,1,0:T(8,128)(2,1)S(1)}, bf16[6,8,128]{2,1,0:T(8,128)(2,1)}, u32[]{:S(2)}) copy-start(bf16[6,8,128]{2,1,0:T(8,128)(2,1)} %get-tuple-element.31) | copy-start | bytes 36868
  8.5 54.3 %all-to-all-start = ((bf16[128,13,8,128]{3,2,1,0:T(8,128)(2,1)}), bf16[128,13,8,128]{3,2,1,0:T(8,128)(2,1)S(1)}, u32[]{:S(2)}, u32[]{:S(2)}) async-start(bf16[128,13,8,128]{3,2,1,0:T(8,128)(2,1)} %get-tuple-element.27), calls=%async_computation | async-start | bytes 6815744 | tf_op jit(solution)/shard_map/all_to_all | solution.py:347
  19.7 34.8 %collective-permute-start = (bf16[6,8,128]{2,1,0:T(8,128)(2,1)S(1)}, bf16[6,8,128]{2,1,0:T(8,128)(2,1)S(1)}, u32[]{:S(2)}, u32[]{:S(2)}) collective-permute-start(bf16[6,8,128]{2,1,0:T(8,128)(2,1)S(1)} %copy-done.4), channel_id=1, source_target_pairs={{0,1},{1,2},{2,3},{3,0},{4,5},{5,6},{6,7},{7,4},{8,9},{9,10},{10,1... | collective-permute-start | bytes 36872 | tf_op jit(solution)/shard_map/ppermute | solution.py:327
  20.7 33.8 %collective-permute-start.1 = (bf16[6,8,128]{2,1,0:T(8,128)(2,1)S(1)}, bf16[6,8,128]{2,1,0:T(8,128)(2,1)S(1)}, u32[]{:S(2)}, u32[]{:S(2)}) collective-permute-start(bf16[6,8,128]{2,1,0:T(8,128)(2,1)S(1)} %copy-done.3), channel_id=1, source_target_pairs={{0,2},{1,3},{2,0},{3,1},{4,6},{5,7},{6,4},{7,5},{8,10},{9,11},{10,... | collective-permute-start | bytes 36872 | tf_op jit(solution)/shard_map/ppermute | solution.py:327
  23.4 31.9 %collective-permute-start.2 = (bf16[6,8,128]{2,1,0:T(8,128)(2,1)S(1)}, bf16[6,8,128]{2,1,0:T(8,128)(2,1)S(1)}, u32[]{:S(2)}, u32[]{:S(2)}) collective-permute-start(bf16[6,8,128]{2,1,0:T(8,128)(2,1)S(1)} %copy-done.2), channel_id=1, source_target_pairs={{0,3},{1,0},{2,1},{3,2},{4,7},{5,4},{6,5},{7,6},{8,11},{9,8},{10,9... | collective-permute-start | bytes 36872 | tf_op jit(solution)/shard_map/ppermute | solution.py:327
  64.4 16.9 %collective-permute-start.5 = (bf16[97,8,128]{2,1,0:T(8,128)(2,1)}, bf16[97,8,128]{2,1,0:T(8,128)(2,1)}, u32[]{:S(2)}, u32[]{:S(2)}) collective-permute-start(bf16[97,8,128]{2,1,0:T(8,128)(2,1)} %mid.1), channel_id=1, source_target_pairs={{0,96},{32,0},{64,32},{96,64},{1,97},{33,1},{65,33},{97,65},{2,98}... | collective-permute-start | bytes 595976 | tf_op jit(solution)/shard_map/ppermute | solution.py:327
  66.3 15.1 %collective-permute-start.4 = (bf16[97,8,128]{2,1,0:T(8,128)(2,1)}, bf16[97,8,128]{2,1,0:T(8,128)(2,1)}, u32[]{:S(2)}, u32[]{:S(2)}) collective-permute-start(bf16[97,8,128]{2,1,0:T(8,128)(2,1)} %mid.1), channel_id=1, source_target_pairs={{0,64},{32,96},{64,0},{96,32},{1,65},{33,97},{65,1},{97,33},{2,66}... | collective-permute-start | bytes 595976 | tf_op jit(solution)/shard_map/ppermute | solution.py:327
  67.4 14.0 %collective-permute-start.3 = (bf16[97,8,128]{2,1,0:T(8,128)(2,1)}, bf16[97,8,128]{2,1,0:T(8,128)(2,1)}, u32[]{:S(2)}, u32[]{:S(2)}) collective-permute-start(bf16[97,8,128]{2,1,0:T(8,128)(2,1)} %mid.1), channel_id=1, source_target_pairs={{0,32},{32,64},{64,96},{96,0},{1,33},{33,65},{65,97},{97,1},{2,34}... | collective-permute-start | bytes 595976 | tf_op jit(solution)/shard_map/ppermute | solution.py:327
  73.6 13.9 %copy-start.1 = (bf16[6,8,128]{2,1,0:T(8,128)(2,1)S(1)}, bf16[6,8,128]{2,1,0:T(8,128)(2,1)}, u32[]{:S(2)}) copy-start(bf16[6,8,128]{2,1,0:T(8,128)(2,1)} %get-tuple-element.34.b0_ref) | copy-start | bytes 36868
  73.6 26.7 %all-to-all-start.1 = ((bf16[128,4,8,128]{3,2,1,0:T(8,128)(2,1)}), bf16[128,4,8,128]{3,2,1,0:T(8,128)(2,1)S(1)}, u32[]{:S(2)}, u32[]{:S(2)}) async-start(bf16[128,4,8,128]{3,2,1,0:T(8,128)(2,1)} %cold.1), calls=%async_computation.1 | async-start | bytes 2097152 | tf_op jit(solution)/shard_map/all_to_all | solution.py:374
  85.2 15.2 %copy-start = (f32[8,1024]{1,0:T(8,128)S(1)}, f32[8,1024]{1,0:T(8,128)}, u32[]{:S(2)}) copy-start(f32[8,1024]{1,0:T(8,128)} %get-tuple-element.26.table_ref) | copy-start | bytes 98308
  85.2 2.4 %collective-permute-start.6 = (bf16[388,8,128]{2,1,0:T(8,128)(2,1)S(1)}, bf16[388,8,128]{2,1,0:T(8,128)(2,1)S(1)}, u32[]{:S(2)}, u32[]{:S(2)}) collective-permute-start(bf16[388,8,128]{2,1,0:T(8,128)(2,1)S(1)} %constant_dynamic-update-slice_fusion.near_ref), channel_id=1, source_target_pairs={{0,16},{16,0},{1,17},{17,1},{2,18},{18,2},{3,19},{19,3},{4,20},{20... | collective-permute-start | bytes 2383880 | tf_op jit(solution)/shard_map/ppermute | solution.py:327
  88.6 4.0 %collective-permute-start.7 = (bf16[3,8,128]{2,1,0:T(8,128)(2,1)S(1)}, bf16[3,8,128]{2,1,0:T(8,128)(2,1)S(1)}, u32[]{:S(2)}, u32[]{:S(2)}) collective-permute-start(bf16[3,8,128]{2,1,0:T(8,128)(2,1)S(1)} %get-tuple-element.44), channel_id=1, source_target_pairs={{0,3},{1,0},{2,1},{3,2},{4,7},{5,4},{6,5},{7,6},{8,11},{9,8},{10,9... | collective-permute-start | bytes 18440 | tf_op jit(solution)/shard_map/ppermute | solution.py:327
  90.9 5.6 %collective-permute-start.8 = (bf16[3,8,128]{2,1,0:T(8,128)(2,1)S(1)}, bf16[3,8,128]{2,1,0:T(8,128)(2,1)S(1)}, u32[]{:S(2)}, u32[]{:S(2)}) collective-permute-start(bf16[3,8,128]{2,1,0:T(8,128)(2,1)S(1)} %get-tuple-element.45), channel_id=1, source_target_pairs={{0,2},{1,3},{2,0},{3,1},{4,6},{5,7},{6,4},{7,5},{8,10},{9,11},{10,... | collective-permute-start | bytes 18440 | tf_op jit(solution)/shard_map/ppermute | solution.py:327
  91.7 5.0 %collective-permute-start.9 = (bf16[3,8,128]{2,1,0:T(8,128)(2,1)S(1)}, bf16[3,8,128]{2,1,0:T(8,128)(2,1)S(1)}, u32[]{:S(2)}, u32[]{:S(2)}) collective-permute-start(bf16[3,8,128]{2,1,0:T(8,128)(2,1)S(1)} %get-tuple-element.46), channel_id=1, source_target_pairs={{0,1},{1,2},{2,3},{3,0},{4,5},{5,6},{6,7},{7,4},{8,9},{9,10},{10,1... | collective-permute-start | bytes 18440 | tf_op jit(solution)/shard_map/ppermute | solution.py:327

commit v11 on v10

--- a/solution.py
+++ b/solution.py
@@ -192,9 +192,11 @@
             out = jnp.dot(weights.astype(BF16), v[:stop], preferred_element_type=F32) / total
             devs = slice(c * part // COLD, stop // COLD)
             out_ref[devs, h] = out.reshape(part // COLD, COLD, hd).astype(BF16)
-        out = pltpu.make_async_copy(out_ref.at[:, h], out_hbm.at[:, h], out_sems.at[h])
-        out.start()
-        sent.append(out)
+            copy = pltpu.make_async_copy(
+                out_ref.at[devs, h], out_hbm.at[devs, h], out_sems.at[h * (slots // part) + c]
+            )
+            copy.start()
+            sent.append(copy)
     for out in sent:
         out.wait()
 
@@ -204,31 +206,35 @@
     slots = devices * COLD
     keys = devices * SHARE
     extra = got_ref[:, tiles - 1].astype(F32).reshape(slots, hd).astype(BF16)
-    n = iota((keys, 1), 0)
-    source, at = n // SHARE, n % SHARE
-    col = iota((keys, slots), 1)
-
-    def rows_at(offset):
-        place = (col == source * COLD + offset).astype(BF16)
-        return jnp.dot(place, extra, preferred_element_type=F32)
-
-    parts = (slice(0, 48), slice(48, 96), slice(96, 97))
-    sent = [
-        pltpu.make_async_copy(kv_ref.at[part], kv_hbm.at[part], sems.at[i])
-        for i, part in enumerate(parts)
-    ]
-    kv_ref[0:48] = rows_at(at).reshape(48, COLD, hd).astype(BF16)
+    runs = slots // LANES
+    each = keys // runs
+    row = iota((3 * each, 1), 0)
+    kind, n = row // each, row % each
+    at = n % SHARE
+    col = n // SHARE * COLD + jnp.where(kind == 0, at, jnp.where(kind == 1, at + SHARE, COLD - 1))
+    place = (col == iota((3 * each, LANES), 1)).astype(BF16)
+    y, core, z = (lax.axis_index(a) for a in ("y", "core", "z"))
+    lane = HOT_LANE + HOT * y + SHARE * (z * 2 + core) + iota((each, 1), 0) % SHARE
+    own = iota((each, hd), 1) == lane
+    tiles_each = each // COLD
+    tags = []
+    for b in range(runs):
+        moved = jnp.dot(place, extra[b * LANES : (b + 1) * LANES], preferred_element_type=F32)
+        first = b * tiles_each
+        kv_ref[first : first + tiles_each] = moved[:each].reshape(tiles_each, COLD, hd).astype(BF16)
+        kv_ref[48 + first : 48 + first + tiles_each] = (
+            moved[each : 2 * each].reshape(tiles_each, COLD, hd).astype(BF16)
+        )
+        tags.append(jnp.where(own, moved[2 * each :], 0.0))
+    sent = [pltpu.make_async_copy(kv_ref.at[0:96], kv_hbm.at[0:96], sems.at[0])]
     sent[0].start()
-    kv_ref[48:96] = rows_at(at + SHARE).reshape(48, COLD, hd).astype(BF16)
-    sent[1].start()
-    y, core, z = (lax.axis_index(a) for a in ("y", "core", "z"))
-    lane = HOT_LANE + HOT * y + SHARE * (z * 2 + core) + at
-    tags = jnp.where(iota((keys, hd), 1) == lane, rows_at(COLD - 1), 0.0).astype(BF16)
+    tags = jnp.concatenate(tags, axis=0).astype(BF16)
     flat = lax.dot_general(jnp.ones((COLD, hd), BF16), tags, NT, preferred_element_type=F32)
     label = [flat[0:1, j * LANES : (j + 1) * LANES] for j in range(keys // LANES)]
     label.append(jnp.zeros((COLD - len(label), LANES), F32))
     kv_ref[96] = jnp.concatenate(label, axis=0).astype(BF16)
-    sent[2].start()
+    sent.append(pltpu.make_async_copy(kv_ref.at[96:97], kv_hbm.at[96:97], sems.at[1]))
+    sent[1].start()
     for out in sent:
         out.wait()
 
@@ -349,13 +355,13 @@
     got, asked = lax.optimization_barrier((got, asked))
     (kv,) = call(
         mid_kernel, "mid", 24, [VMEM], [(HBM, (97, *tile), BF16)],
-        [pltpu.VMEM((97, *tile), BF16), pltpu.SemaphoreType.DMA((3,))], got,
+        [pltpu.VMEM((97, *tile), BF16), pltpu.SemaphoreType.DMA((2,))], got,
     )
     got, kv = lax.optimization_barrier((got, kv))
     near = [kv] + [shift(kv, "z", d) for d in (1, 2, 3)]
     (answer,) = call(
         cold_kernel, "cold", 24, [VMEM], [(HBM, (devices, heads, *tile), BF16)],
-        [pltpu.VMEM((devices, heads, *tile), BF16), pltpu.SemaphoreType.DMA((heads,))],
+        [pltpu.VMEM((devices, heads, *tile), BF16), pltpu.SemaphoreType.DMA((2 * heads,))],
         got, flops=20_000_000_000,
     )
     near, _ = lax.optimization_barrier((near, answer))

time: 105 us -> 104 us (level)
  no operation moved by 1% of the time
where the time goes in v11:
time: 104 us
  waiting for transfers between devices  48 us (46%)
  starting transfers between devices  31.4 us (30%)
  Pallas kernels  20.3 us (20%)
  local copies, waits for them, and re-layouts  3.83 us (4%)
    ppermute x10, waiting for transfers between devices, shift(): lax.ppermute(block, axis, [(i, (i + by) % size) for i in range(size)])  36.9 us
    pallas_call x5, Pallas kernels, call(): pl.pallas_call(kernel, out_shape=tuple((pltpu.HBM(*out[1:]) if out[0] is...  20.3 us
    ppermute x10, starting transfers between devices, shift(): lax.ppermute(block, axis, [(i, (i + by) % size) for i in range(size)])  12.5 us
    all_to_all x1, starting transfers between devices, local(): got = lax.all_to_all(send, AXES, split_axis=0, concat_axis=0, tiled=True)  11.2 us
    all_to_all x1, starting transfers between devices, local(): back = lax.all_to_all(answer, AXES, split_axis=0, concat_axis=0, tiled=True)  7.68 us
    all_to_all x1, waiting for transfers between devices, local(): got = lax.all_to_all(send, AXES, split_axis=0, concat_axis=0, tiled=True)  7.45 us
    all_to_all x1, waiting for transfers between devices, local(): back = lax.all_to_all(answer, AXES, split_axis=0, concat_axis=0, tiled=True)  3.66 us
    unnamed x13, local copies, waits for them, and re-layouts  2.88 us
  transfers between devices with their start and end apart: 12, of which 7 were waited for; matrix products, arithmetic and copies ran while one was open for 4% of the time, Pallas kernels for 7%

profile of v11, /device:TPU:0, one launch (start us, length us, event | category | flops | bytes accessed | tf_op | source)
XLA Modules:
  0.0 103.9 jit_solution(13986131425968780307)
XLA Ops:
  0.0 8.5 %pack.1 = (f32[8,1024]{1,0:T(8,128)}, bf16[6,8,128]{2,1,0:T(8,128)(2,1)}, bf16[6,8,128]{2,1,0:T(8,128)(2,1)}, bf16[6,8,128]{2,1,0:T(8,128)(2,1)}, bf16[6,8,128]{...) custom-call(s32[4,1024]{1,0:T(4,128)} %ids_hbm.1, bf16[1024,512]{1,0:T(8,128)(2,1)} %q_hbm.1, bf16[1024,512]{1,0:T(8,128)(2,1)} %k_hbm.1, ...), custom_call_target="tpu_custom_call" | custom-call | tf_op jit(solution)/shard_map/pack/pallas_call | solution.py:317
  8.5 0.0 copy-start.4
  8.5 11.2 %all-to-all-start = ((bf16[128,13,8,128]{3,2,1,0:T(8,128)(2,1)}), bf16[128,13,8,128]{3,2,1,0:T(8,128)(2,1)S(1)}, u32[]{:S(2)}, u32[]{:S(2)}) async-start(bf16[128,13,8,128]{3,2,1,0:T(8,128)(2,1)} %get-tuple-element.27), calls=%async_computation | async-start | bytes 6815744 | tf_op jit(solution)/shard_map/all_to_all | solution.py:353
  19.7 1.0 collective-permute-start
  20.7 2.7 %collective-permute-start.1 = (bf16[6,8,128]{2,1,0:T(8,128)(2,1)S(1)}, bf16[6,8,128]{2,1,0:T(8,128)(2,1)S(1)}, u32[]{:S(2)}, u32[]{:S(2)}) collective-permute-start(bf16[6,8,128]{2,1,0:T(8,128)(2,1)S(1)} %copy-done.3), channel_id=1, source_target_pairs={{0,2},{1,3},{2,0},{3,1},{4,6},{5,7},{6,4},{7,5},{8,10},{9,11},{10,... | collective-permute-start | bytes 36872 | tf_op jit(solution)/shard_map/ppermute | solution.py:333
  23.4 1.4 %collective-permute-start.2 = (bf16[6,8,128]{2,1,0:T(8,128)(2,1)S(1)}, bf16[6,8,128]{2,1,0:T(8,128)(2,1)S(1)}, u32[]{:S(2)}, u32[]{:S(2)}) collective-permute-start(bf16[6,8,128]{2,1,0:T(8,128)(2,1)S(1)} %copy-done.2), channel_id=1, source_target_pairs={{0,3},{1,0},{2,1},{3,2},{4,7},{5,4},{6,5},{7,6},{8,11},{9,8},{10,9... | collective-permute-start | bytes 36872 | tf_op jit(solution)/shard_map/ppermute | solution.py:333
  24.8 29.7 %collective-permute-done.b1_ref = bf16[6,8,128]{2,1,0:T(8,128)(2,1)S(1)} collective-permute-done((bf16[6,8,128]{2,1,0:T(8,128)(2,1)S(1)}, bf16[6,8,128]{2,1,0:T(8,128)(2,1)S(1)}, u32[]{:S(2)}, u32[]{:S(2)}) %collective-permute-start) | collective-permute-done | bytes 12320 | tf_op jit(solution)/shard_map/ppermute | solution.py:333
  54.5 0.8 collective-permute-done.2.b3_ref
  55.3 7.5 %all-to-all-done.got_ref = bf16[128,13,8,128]{3,2,1,0:T(8,128)(2,1)S(1)} async-done(((bf16[128,13,8,128]{3,2,1,0:T(8,128)(2,1)}), bf16[128,13,8,128]{3,2,1,0:T(8,128)(2,1)S(1)}, u32[]{:S(2)}, u32[]{:S(2)}) %all-to-all-start) | async-done | bytes 3407904 | tf_op jit(solution)/shard_map/all_to_all | solution.py:353
  62.8 1.1 %mid.1 = bf16[97,8,128]{2,1,0:T(8,128)(2,1)} custom-call(bf16[128,13,8,128]{3,2,1,0:T(8,128)(2,1)S(1)} %all-to-all-done.got_ref), custom_call_target="tpu_custom_call" | custom-call | tf_op jit(solution)/shard_map/mid/pallas_call | solution.py:317
  63.9 1.9 %collective-permute-start.5 = (bf16[97,8,128]{2,1,0:T(8,128)(2,1)}, bf16[97,8,128]{2,1,0:T(8,128)(2,1)}, u32[]{:S(2)}, u32[]{:S(2)}) collective-permute-start(bf16[97,8,128]{2,1,0:T(8,128)(2,1)} %mid.1), channel_id=1, source_target_pairs={{0,96},{32,0},{64,32},{96,64},{1,97},{33,1},{65,33},{97,65},{2,98}... | collective-permute-start | bytes 595976 | tf_op jit(solution)/shard_map/ppermute | solution.py:333
  65.8 1.1 %collective-permute-start.4 = (bf16[97,8,128]{2,1,0:T(8,128)(2,1)}, bf16[97,8,128]{2,1,0:T(8,128)(2,1)}, u32[]{:S(2)}, u32[]{:S(2)}) collective-permute-start(bf16[97,8,128]{2,1,0:T(8,128)(2,1)} %mid.1), channel_id=1, source_target_pairs={{0,64},{32,96},{64,0},{96,32},{1,65},{33,97},{65,1},{97,33},{2,66}... | collective-permute-start | bytes 595976 | tf_op jit(solution)/shard_map/ppermute | solution.py:333
  66.9 0.3 collective-permute-start.3
  67.2 5.9 %cold.1 = bf16[128,4,8,128]{3,2,1,0:T(8,128)(2,1)} custom-call(bf16[128,13,8,128]{3,2,1,0:T(8,128)(2,1)S(1)} %all-to-all-done.got_ref), custom_call_target="tpu_custom_call" | custom-call | flops 20000000000 | tf_op jit(solution)/shard_map/cold/pallas_call | solution.py:317
  73.1 7.7 %all-to-all-start.1 = ((bf16[128,4,8,128]{3,2,1,0:T(8,128)(2,1)}), bf16[128,4,8,128]{3,2,1,0:T(8,128)(2,1)S(1)}, u32[]{:S(2)}, u32[]{:S(2)}) async-start(bf16[128,4,8,128]{3,2,1,0:T(8,128)(2,1)} %cold.1), calls=%async_computation.1 | async-start | bytes 2097152 | tf_op jit(solution)/shard_map/all_to_all | solution.py:380
  80.8 0.0 collective-permute-done.4
  80.9 0.0 collective-permute-done.3
  80.9 0.9 constant_dynamic-update-slice_fusion.3
  81.8 1.0 constant_dynamic-update-slice_fusion.2
  82.8 1.0 constant_dynamic-update-slice_fusion.1
  83.7 1.0 constant_dynamic-update-slice_fusion.near_ref
  84.7 0.1 collective-permute-start.6
  84.8 2.3 %collective-permute-done.6.far_ref = bf16[388,8,128]{2,1,0:T(8,128)(2,1)S(1)} collective-permute-done((bf16[388,8,128]{2,1,0:T(8,128)(2,1)S(1)}, bf16[388,8,128]{2,1,0:T(8,128)(2,1)S(1)}, u32[]{:S(2)}, u32[]{:S(2)}) %collective-permute-start.6) | collective-permute-done | bytes 794656 | tf_op jit(solution)/shard_map/ppermute | solution.py:333
  87.1 1.1 %hot.1 = (bf16[3,8,128]{2,1,0:T(8,128)(2,1)S(1)}, bf16[3,8,128]{2,1,0:T(8,128)(2,1)S(1)}, bf16[3,8,128]{2,1,0:T(8,128)(2,1)S(1)}, bf16[3,8,128]{2,1,0:T(8,128)(2,1)S(1)}) custom-call(bf16[6,8,128]{2,1,0:T(8,128)(2,1)S(1)} %copy-done.1, bf16[6,8,128]{2,1,0:T(8,128)(2,1)S(1)} %collective-permute-done.b1_ref, ...), custom_call_target="tpu_custom_call" | custom-call | flops 2000000000 | tf_op jit(solution)/shard_map/hot/pallas_call | solution.py:317
  88.1 2.3 %collective-permute-start.7 = (bf16[3,8,128]{2,1,0:T(8,128)(2,1)S(1)}, bf16[3,8,128]{2,1,0:T(8,128)(2,1)S(1)}, u32[]{:S(2)}, u32[]{:S(2)}) collective-permute-start(bf16[3,8,128]{2,1,0:T(8,128)(2,1)S(1)} %get-tuple-element.44), channel_id=1, source_target_pairs={{0,3},{1,0},{2,1},{3,2},{4,7},{5,4},{6,5},{7,6},{8,11},{9,8},{10,9... | collective-permute-start | bytes 18440 | tf_op jit(solution)/shard_map/ppermute | solution.py:333
  90.4 0.8 collective-permute-start.8
  91.2 0.9 collective-permute-start.9
  92.1 0.0 collective-permute-done.7.o1_ref
  92.1 3.9 %collective-permute-done.8.o2_ref = bf16[3,8,128]{2,1,0:T(8,128)(2,1)S(1)} collective-permute-done((bf16[3,8,128]{2,1,0:T(8,128)(2,1)S(1)}, bf16[3,8,128]{2,1,0:T(8,128)(2,1)S(1)}, u32[]{:S(2)}, u32[]{:S(2)}) %collective-permute-start.8) | collective-permute-done | bytes 6176 | tf_op jit(solution)/shard_map/ppermute | solution.py:333
  96.1 0.2 collective-permute-done.9.o3_ref
  96.2 3.7 %all-to-all-done.1.back_ref = bf16[128,4,8,128]{3,2,1,0:T(8,128)(2,1)S(1)} async-done(((bf16[128,4,8,128]{3,2,1,0:T(8,128)(2,1)}), bf16[128,4,8,128]{3,2,1,0:T(8,128)(2,1)S(1)}, u32[]{:S(2)}, u32[]{:S(2)}) %all-to-all-start.1) | async-done | bytes 1048608 | tf_op jit(solution)/shard_map/all_to_all | solution.py:380
  99.9 3.8 %unpack.1 = bf16[1024,512]{1,0:T(8,128)(2,1)} custom-call(f32[8,1024]{1,0:T(8,128)S(1)} %copy-done, bf16[128,4,8,128]{3,2,1,0:T(8,128)(2,1)S(1)} %all-to-all-done.1.back_ref, bf16[3,8,128]{2,1,0:T(8,128)(2,1)S(1)} %get-tuple-element.43.o0_ref, bf16[3,8,128]{2,1,0:T(8,128)(2,1)S(1)} %collective-permute-done.7.o1_ref, ...), custom_call_target="tpu_custom_call" | custom-call | tf_op jit(solution)/shard_map/unpack/pallas_call | solution.py:317
  (11 shorter events, 0.0 us)
Async XLA Ops:
  8.5 11.2 %copy-start.4 = (bf16[6,8,128]{2,1,0:T(8,128)(2,1)S(1)}, bf16[6,8,128]{2,1,0:T(8,128)(2,1)}, u32[]{:S(2)}) copy-start(bf16[6,8,128]{2,1,0:T(8,128)(2,1)} %get-tuple-element.29) | copy-start | bytes 36868
  8.5 12.2 %copy-start.3 = (bf16[6,8,128]{2,1,0:T(8,128)(2,1)S(1)}, bf16[6,8,128]{2,1,0:T(8,128)(2,1)}, u32[]{:S(2)}) copy-start(bf16[6,8,128]{2,1,0:T(8,128)(2,1)} %get-tuple-element.30) | copy-start | bytes 36868
  8.5 14.9 %copy-start.2 = (bf16[6,8,128]{2,1,0:T(8,128)(2,1)S(1)}, bf16[6,8,128]{2,1,0:T(8,128)(2,1)}, u32[]{:S(2)}) copy-start(bf16[6,8,128]{2,1,0:T(8,128)(2,1)} %get-tuple-element.31) | copy-start | bytes 36868
  8.5 54.3 %all-to-all-start = ((bf16[128,13,8,128]{3,2,1,0:T(8,128)(2,1)}), bf16[128,13,8,128]{3,2,1,0:T(8,128)(2,1)S(1)}, u32[]{:S(2)}, u32[]{:S(2)}) async-start(bf16[128,13,8,128]{3,2,1,0:T(8,128)(2,1)} %get-tuple-element.27), calls=%async_computation | async-start | bytes 6815744 | tf_op jit(solution)/shard_map/all_to_all | solution.py:353
  19.7 34.8 %collective-permute-start = (bf16[6,8,128]{2,1,0:T(8,128)(2,1)S(1)}, bf16[6,8,128]{2,1,0:T(8,128)(2,1)S(1)}, u32[]{:S(2)}, u32[]{:S(2)}) collective-permute-start(bf16[6,8,128]{2,1,0:T(8,128)(2,1)S(1)} %copy-done.4), channel_id=1, source_target_pairs={{0,1},{1,2},{2,3},{3,0},{4,5},{5,6},{6,7},{7,4},{8,9},{9,10},{10,1... | collective-permute-start | bytes 36872 | tf_op jit(solution)/shard_map/ppermute | solution.py:333
  20.7 33.8 %collective-permute-start.1 = (bf16[6,8,128]{2,1,0:T(8,128)(2,1)S(1)}, bf16[6,8,128]{2,1,0:T(8,128)(2,1)S(1)}, u32[]{:S(2)}, u32[]{:S(2)}) collective-permute-start(bf16[6,8,128]{2,1,0:T(8,128)(2,1)S(1)} %copy-done.3), channel_id=1, source_target_pairs={{0,2},{1,3},{2,0},{3,1},{4,6},{5,7},{6,4},{7,5},{8,10},{9,11},{10,... | collective-permute-start | bytes 36872 | tf_op jit(solution)/shard_map/ppermute | solution.py:333
  23.4 31.9 %collective-permute-start.2 = (bf16[6,8,128]{2,1,0:T(8,128)(2,1)S(1)}, bf16[6,8,128]{2,1,0:T(8,128)(2,1)S(1)}, u32[]{:S(2)}, u32[]{:S(2)}) collective-permute-start(bf16[6,8,128]{2,1,0:T(8,128)(2,1)S(1)} %copy-done.2), channel_id=1, source_target_pairs={{0,3},{1,0},{2,1},{3,2},{4,7},{5,4},{6,5},{7,6},{8,11},{9,8},{10,9... | collective-permute-start | bytes 36872 | tf_op jit(solution)/shard_map/ppermute | solution.py:333
  63.9 16.9 %collective-permute-start.5 = (bf16[97,8,128]{2,1,0:T(8,128)(2,1)}, bf16[97,8,128]{2,1,0:T(8,128)(2,1)}, u32[]{:S(2)}, u32[]{:S(2)}) collective-permute-start(bf16[97,8,128]{2,1,0:T(8,128)(2,1)} %mid.1), channel_id=1, source_target_pairs={{0,96},{32,0},{64,32},{96,64},{1,97},{33,1},{65,33},{97,65},{2,98}... | collective-permute-start | bytes 595976 | tf_op jit(solution)/shard_map/ppermute | solution.py:333
  65.8 15.1 %collective-permute-start.4 = (bf16[97,8,128]{2,1,0:T(8,128)(2,1)}, bf16[97,8,128]{2,1,0:T(8,128)(2,1)}, u32[]{:S(2)}, u32[]{:S(2)}) collective-permute-start(bf16[97,8,128]{2,1,0:T(8,128)(2,1)} %mid.1), channel_id=1, source_target_pairs={{0,64},{32,96},{64,0},{96,32},{1,65},{33,97},{65,1},{97,33},{2,66}... | collective-permute-start | bytes 595976 | tf_op jit(solution)/shard_map/ppermute | solution.py:333
  66.9 14.0 %collective-permute-start.3 = (bf16[97,8,128]{2,1,0:T(8,128)(2,1)}, bf16[97,8,128]{2,1,0:T(8,128)(2,1)}, u32[]{:S(2)}, u32[]{:S(2)}) collective-permute-start(bf16[97,8,128]{2,1,0:T(8,128)(2,1)} %mid.1), channel_id=1, source_target_pairs={{0,32},{32,64},{64,96},{96,0},{1,33},{33,65},{65,97},{97,1},{2,34}... | collective-permute-start | bytes 595976 | tf_op jit(solution)/shard_map/ppermute | solution.py:333
  73.1 13.9 %copy-start.1 = (bf16[6,8,128]{2,1,0:T(8,128)(2,1)S(1)}, bf16[6,8,128]{2,1,0:T(8,128)(2,1)}, u32[]{:S(2)}) copy-start(bf16[6,8,128]{2,1,0:T(8,128)(2,1)} %get-tuple-element.34.b0_ref) | copy-start | bytes 36868
  73.1 26.7 %all-to-all-start.1 = ((bf16[128,4,8,128]{3,2,1,0:T(8,128)(2,1)}), bf16[128,4,8,128]{3,2,1,0:T(8,128)(2,1)S(1)}, u32[]{:S(2)}, u32[]{:S(2)}) async-start(bf16[128,4,8,128]{3,2,1,0:T(8,128)(2,1)} %cold.1), calls=%async_computation.1 | async-start | bytes 2097152 | tf_op jit(solution)/shard_map/all_to_all | solution.py:380
  84.7 15.2 %copy-start = (f32[8,1024]{1,0:T(8,128)S(1)}, f32[8,1024]{1,0:T(8,128)}, u32[]{:S(2)}) copy-start(f32[8,1024]{1,0:T(8,128)} %get-tuple-element.26.table_ref) | copy-start | bytes 98308
  84.7 2.4 %collective-permute-start.6 = (bf16[388,8,128]{2,1,0:T(8,128)(2,1)S(1)}, bf16[388,8,128]{2,1,0:T(8,128)(2,1)S(1)}, u32[]{:S(2)}, u32[]{:S(2)}) collective-permute-start(bf16[388,8,128]{2,1,0:T(8,128)(2,1)S(1)} %constant_dynamic-update-slice_fusion.near_ref), channel_id=1, source_target_pairs={{0,16},{16,0},{1,17},{17,1},{2,18},{18,2},{3,19},{19,3},{4,20},{20... | collective-permute-start | bytes 2383880 | tf_op jit(solution)/shard_map/ppermute | solution.py:333
  88.1 4.0 %collective-permute-start.7 = (bf16[3,8,128]{2,1,0:T(8,128)(2,1)S(1)}, bf16[3,8,128]{2,1,0:T(8,128)(2,1)S(1)}, u32[]{:S(2)}, u32[]{:S(2)}) collective-permute-start(bf16[3,8,128]{2,1,0:T(8,128)(2,1)S(1)} %get-tuple-element.44), channel_id=1, source_target_pairs={{0,3},{1,0},{2,1},{3,2},{4,7},{5,4},{6,5},{7,6},{8,11},{9,8},{10,9... | collective-permute-start | bytes 18440 | tf_op jit(solution)/shard_map/ppermute | solution.py:333
  90.4 5.6 %collective-permute-start.8 = (bf16[3,8,128]{2,1,0:T(8,128)(2,1)S(1)}, bf16[3,8,128]{2,1,0:T(8,128)(2,1)S(1)}, u32[]{:S(2)}, u32[]{:S(2)}) collective-permute-start(bf16[3,8,128]{2,1,0:T(8,128)(2,1)S(1)} %get-tuple-element.45), channel_id=1, source_target_pairs={{0,2},{1,3},{2,0},{3,1},{4,6},{5,7},{6,4},{7,5},{8,10},{9,11},{10,... | collective-permute-start | bytes 18440 | tf_op jit(solution)/shard_map/ppermute | solution.py:333
  91.2 5.0 %collective-permute-start.9 = (bf16[3,8,128]{2,1,0:T(8,128)(2,1)S(1)}, bf16[3,8,128]{2,1,0:T(8,128)(2,1)S(1)}, u32[]{:S(2)}, u32[]{:S(2)}) collective-permute-start(bf16[3,8,128]{2,1,0:T(8,128)(2,1)S(1)} %get-tuple-element.46), channel_id=1, source_target_pairs={{0,1},{1,2},{2,3},{3,0},{4,5},{5,6},{6,7},{7,4},{8,9},{9,10},{10,1... | collective-permute-start | bytes 18440 | tf_op jit(solution)/shard_map/ppermute | solution.py:333

commit v12 on v11

--- a/solution.py
+++ b/solution.py
@@ -284,21 +284,19 @@
     for d, ref in enumerate((o0_ref, o1_ref, o2_ref, o3_ref)):
         hot_ref[d] = ref[...].astype(F32)
     y = lax.axis_index("y")
-    rows, hots = [], []
+    rows = []
     for h in range(heads):
         rows.append(back_ref[:, h].astype(F32).reshape(slots, hd).astype(BF16))
         hot = hot_ref[lax.rem(h + 4 - y, 4)].reshape(HOT, hd)
-        hots.append(jnp.concatenate([hot, jnp.zeros((LANES - HOT, hd), F32)], axis=0).astype(BF16))
+        spare = jnp.zeros((LANES - HOT, hd), F32)
+        rows[h] = jnp.concatenate([rows[h], jnp.concatenate([hot, spare], axis=0).astype(BF16)], axis=0)
     sent = []
     for c in range(tokens // part):
         at = slice(c * part, (c + 1) * part)
         for h in range(heads):
             slot = cols[at, h : h + 1].astype(jnp.int32)
-            place = (slot == iota((part, slots), 1)).astype(BF16)
-            hot_place = (slot == iota((part, LANES), 1) + slots).astype(BF16)
-            got = jnp.dot(place, rows[h], preferred_element_type=F32) + jnp.dot(
-                hot_place, hots[h], preferred_element_type=F32
-            )
+            place = (slot == iota((part, slots + LANES), 1)).astype(BF16)
+            got = jnp.dot(place, rows[h], preferred_element_type=F32)
             out_ref[at, h * hd : (h + 1) * hd] = got.astype(BF16)
         out = pltpu.make_async_copy(out_ref.at[at], out_hbm.at[at], sems.at[c])
         out.start()

time: 104 us -> 104 us (level)
  no operation moved by 1% of the time
where the time goes in v12:
time: 104 us
  waiting for transfers between devices  48 us (46%)
  starting transfers between devices  31.4 us (30%)
  Pallas kernels  20.2 us (19%)
  local copies, waits for them, and re-layouts  3.83 us (4%)
    ppermute x10, waiting for transfers between devices, shift(): lax.ppermute(block, axis, [(i, (i + by) % size) for i in range(size)])  36.9 us
    pallas_call x5, Pallas kernels, call(): pl.pallas_call(kernel, out_shape=tuple((pltpu.HBM(*out[1:]) if out[0] is...  20.2 us
    ppermute x10, starting transfers between devices, shift(): lax.ppermute(block, axis, [(i, (i + by) % size) for i in range(size)])  12.5 us
    all_to_all x1, starting transfers between devices, local(): got = lax.all_to_all(send, AXES, split_axis=0, concat_axis=0, tiled=True)  11.2 us
    all_to_all x1, starting transfers between devices, local(): back = lax.all_to_all(answer, AXES, split_axis=0, concat_axis=0, tiled=True)  7.68 us
    all_to_all x1, waiting for transfers between devices, local(): got = lax.all_to_all(send, AXES, split_axis=0, concat_axis=0, tiled=True)  7.45 us
    all_to_all x1, waiting for transfers between devices, local(): back = lax.all_to_all(answer, AXES, split_axis=0, concat_axis=0, tiled=True)  3.66 us
    unnamed x13, local copies, waits for them, and re-layouts  2.88 us
  transfers between devices with their start and end apart: 12, of which 7 were waited for; matrix products, arithmetic and copies ran while one was open for 4% of the time, Pallas kernels for 7%

profile of v12, /device:TPU:0, one launch (start us, length us, event | category | flops | bytes accessed | tf_op | source)
XLA Modules:
  0.0 103.8 jit_solution(15780760378046637246)
XLA Ops:
  0.0 8.5 %pack.1 = (f32[8,1024]{1,0:T(8,128)}, bf16[6,8,128]{2,1,0:T(8,128)(2,1)}, bf16[6,8,128]{2,1,0:T(8,128)(2,1)}, bf16[6,8,128]{2,1,0:T(8,128)(2,1)}, bf16[6,8,128]{...) custom-call(s32[4,1024]{1,0:T(4,128)} %ids_hbm.1, bf16[1024,512]{1,0:T(8,128)(2,1)} %q_hbm.1, bf16[1024,512]{1,0:T(8,128)(2,1)} %k_hbm.1, ...), custom_call_target="tpu_custom_call" | custom-call | tf_op jit(solution)/shard_map/pack/pallas_call | solution.py:315
  8.5 0.0 copy-start.4
  8.5 11.2 %all-to-all-start = ((bf16[128,13,8,128]{3,2,1,0:T(8,128)(2,1)}), bf16[128,13,8,128]{3,2,1,0:T(8,128)(2,1)S(1)}, u32[]{:S(2)}, u32[]{:S(2)}) async-start(bf16[128,13,8,128]{3,2,1,0:T(8,128)(2,1)} %get-tuple-element.27), calls=%async_computation | async-start | bytes 6815744 | tf_op jit(solution)/shard_map/all_to_all | solution.py:351
  19.7 1.0 collective-permute-start
  20.7 2.7 %collective-permute-start.1 = (bf16[6,8,128]{2,1,0:T(8,128)(2,1)S(1)}, bf16[6,8,128]{2,1,0:T(8,128)(2,1)S(1)}, u32[]{:S(2)}, u32[]{:S(2)}) collective-permute-start(bf16[6,8,128]{2,1,0:T(8,128)(2,1)S(1)} %copy-done.3), channel_id=1, source_target_pairs={{0,2},{1,3},{2,0},{3,1},{4,6},{5,7},{6,4},{7,5},{8,10},{9,11},{10,... | collective-permute-start | bytes 36872 | tf_op jit(solution)/shard_map/ppermute | solution.py:331
  23.4 1.4 %collective-permute-start.2 = (bf16[6,8,128]{2,1,0:T(8,128)(2,1)S(1)}, bf16[6,8,128]{2,1,0:T(8,128)(2,1)S(1)}, u32[]{:S(2)}, u32[]{:S(2)}) collective-permute-start(bf16[6,8,128]{2,1,0:T(8,128)(2,1)S(1)} %copy-done.2), channel_id=1, source_target_pairs={{0,3},{1,0},{2,1},{3,2},{4,7},{5,4},{6,5},{7,6},{8,11},{9,8},{10,9... | collective-permute-start | bytes 36872 | tf_op jit(solution)/shard_map/ppermute | solution.py:331
  24.8 29.7 %collective-permute-done.b1_ref = bf16[6,8,128]{2,1,0:T(8,128)(2,1)S(1)} collective-permute-done((bf16[6,8,128]{2,1,0:T(8,128)(2,1)S(1)}, bf16[6,8,128]{2,1,0:T(8,128)(2,1)S(1)}, u32[]{:S(2)}, u32[]{:S(2)}) %collective-permute-start) | collective-permute-done | bytes 12320 | tf_op jit(solution)/shard_map/ppermute | solution.py:331
  54.5 0.8 collective-permute-done.2.b3_ref
  55.3 7.5 %all-to-all-done.got_ref = bf16[128,13,8,128]{3,2,1,0:T(8,128)(2,1)S(1)} async-done(((bf16[128,13,8,128]{3,2,1,0:T(8,128)(2,1)}), bf16[128,13,8,128]{3,2,1,0:T(8,128)(2,1)S(1)}, u32[]{:S(2)}, u32[]{:S(2)}) %all-to-all-start) | async-done | bytes 3407904 | tf_op jit(solution)/shard_map/all_to_all | solution.py:351
  62.8 1.1 %mid.1 = bf16[97,8,128]{2,1,0:T(8,128)(2,1)} custom-call(bf16[128,13,8,128]{3,2,1,0:T(8,128)(2,1)S(1)} %all-to-all-done.got_ref), custom_call_target="tpu_custom_call" | custom-call | tf_op jit(solution)/shard_map/mid/pallas_call | solution.py:315
  63.9 1.9 %collective-permute-start.5 = (bf16[97,8,128]{2,1,0:T(8,128)(2,1)}, bf16[97,8,128]{2,1,0:T(8,128)(2,1)}, u32[]{:S(2)}, u32[]{:S(2)}) collective-permute-start(bf16[97,8,128]{2,1,0:T(8,128)(2,1)} %mid.1), channel_id=1, source_target_pairs={{0,96},{32,0},{64,32},{96,64},{1,97},{33,1},{65,33},{97,65},{2,98}... | collective-permute-start | bytes 595976 | tf_op jit(solution)/shard_map/ppermute | solution.py:331
  65.8 1.1 %collective-permute-start.4 = (bf16[97,8,128]{2,1,0:T(8,128)(2,1)}, bf16[97,8,128]{2,1,0:T(8,128)(2,1)}, u32[]{:S(2)}, u32[]{:S(2)}) collective-permute-start(bf16[97,8,128]{2,1,0:T(8,128)(2,1)} %mid.1), channel_id=1, source_target_pairs={{0,64},{32,96},{64,0},{96,32},{1,65},{33,97},{65,1},{97,33},{2,66}... | collective-permute-start | bytes 595976 | tf_op jit(solution)/shard_map/ppermute | solution.py:331
  66.9 0.3 collective-permute-start.3
  67.2 5.9 %cold.1 = bf16[128,4,8,128]{3,2,1,0:T(8,128)(2,1)} custom-call(bf16[128,13,8,128]{3,2,1,0:T(8,128)(2,1)S(1)} %all-to-all-done.got_ref), custom_call_target="tpu_custom_call" | custom-call | flops 20000000000 | tf_op jit(solution)/shard_map/cold/pallas_call | solution.py:315
  73.1 7.7 %all-to-all-start.1 = ((bf16[128,4,8,128]{3,2,1,0:T(8,128)(2,1)}), bf16[128,4,8,128]{3,2,1,0:T(8,128)(2,1)S(1)}, u32[]{:S(2)}, u32[]{:S(2)}) async-start(bf16[128,4,8,128]{3,2,1,0:T(8,128)(2,1)} %cold.1), calls=%async_computation.1 | async-start | bytes 2097152 | tf_op jit(solution)/shard_map/all_to_all | solution.py:378
  80.8 0.0 collective-permute-done.4
  80.9 0.0 collective-permute-done.3
  80.9 0.9 constant_dynamic-update-slice_fusion.3
  81.8 1.0 constant_dynamic-update-slice_fusion.2
  82.8 1.0 constant_dynamic-update-slice_fusion.1
  83.7 1.0 constant_dynamic-update-slice_fusion.near_ref
  84.7 0.1 collective-permute-start.6
  84.8 2.3 %collective-permute-done.6.far_ref = bf16[388,8,128]{2,1,0:T(8,128)(2,1)S(1)} collective-permute-done((bf16[388,8,128]{2,1,0:T(8,128)(2,1)S(1)}, bf16[388,8,128]{2,1,0:T(8,128)(2,1)S(1)}, u32[]{:S(2)}, u32[]{:S(2)}) %collective-permute-start.6) | collective-permute-done | bytes 794656 | tf_op jit(solution)/shard_map/ppermute | solution.py:331
  87.1 1.1 %hot.1 = (bf16[3,8,128]{2,1,0:T(8,128)(2,1)S(1)}, bf16[3,8,128]{2,1,0:T(8,128)(2,1)S(1)}, bf16[3,8,128]{2,1,0:T(8,128)(2,1)S(1)}, bf16[3,8,128]{2,1,0:T(8,128)(2,1)S(1)}) custom-call(bf16[6,8,128]{2,1,0:T(8,128)(2,1)S(1)} %copy-done.1, bf16[6,8,128]{2,1,0:T(8,128)(2,1)S(1)} %collective-permute-done.b1_ref, ...), custom_call_target="tpu_custom_call" | custom-call | flops 2000000000 | tf_op jit(solution)/shard_map/hot/pallas_call | solution.py:315
  88.1 2.3 %collective-permute-start.7 = (bf16[3,8,128]{2,1,0:T(8,128)(2,1)S(1)}, bf16[3,8,128]{2,1,0:T(8,128)(2,1)S(1)}, u32[]{:S(2)}, u32[]{:S(2)}) collective-permute-start(bf16[3,8,128]{2,1,0:T(8,128)(2,1)S(1)} %get-tuple-element.44), channel_id=1, source_target_pairs={{0,3},{1,0},{2,1},{3,2},{4,7},{5,4},{6,5},{7,6},{8,11},{9,8},{10,9... | collective-permute-start | bytes 18440 | tf_op jit(solution)/shard_map/ppermute | solution.py:331
  90.4 0.8 collective-permute-start.8
  91.2 0.9 collective-permute-start.9
  92.1 0.0 collective-permute-done.7.o1_ref
  92.1 3.9 %collective-permute-done.8.o2_ref = bf16[3,8,128]{2,1,0:T(8,128)(2,1)S(1)} collective-permute-done((bf16[3,8,128]{2,1,0:T(8,128)(2,1)S(1)}, bf16[3,8,128]{2,1,0:T(8,128)(2,1)S(1)}, u32[]{:S(2)}, u32[]{:S(2)}) %collective-permute-start.8) | collective-permute-done | bytes 6176 | tf_op jit(solution)/shard_map/ppermute | solution.py:331
  96.1 0.2 collective-permute-done.9.o3_ref
  96.2 3.7 %all-to-all-done.1.back_ref = bf16[128,4,8,128]{3,2,1,0:T(8,128)(2,1)S(1)} async-done(((bf16[128,4,8,128]{3,2,1,0:T(8,128)(2,1)}), bf16[128,4,8,128]{3,2,1,0:T(8,128)(2,1)S(1)}, u32[]{:S(2)}, u32[]{:S(2)}) %all-to-all-start.1) | async-done | bytes 1048608 | tf_op jit(solution)/shard_map/all_to_all | solution.py:378
  99.9 3.7 %unpack.1 = bf16[1024,512]{1,0:T(8,128)(2,1)} custom-call(f32[8,1024]{1,0:T(8,128)S(1)} %copy-done, bf16[128,4,8,128]{3,2,1,0:T(8,128)(2,1)S(1)} %all-to-all-done.1.back_ref, bf16[3,8,128]{2,1,0:T(8,128)(2,1)S(1)} %get-tuple-element.43.o0_ref, bf16[3,8,128]{2,1,0:T(8,128)(2,1)S(1)} %collective-permute-done.7.o1_ref, ...), custom_call_target="tpu_custom_call" | custom-call | tf_op jit(solution)/shard_map/unpack/pallas_call | solution.py:315
  (11 shorter events, 0.0 us)
Async XLA Ops:
  8.5 11.2 %copy-start.4 = (bf16[6,8,128]{2,1,0:T(8,128)(2,1)S(1)}, bf16[6,8,128]{2,1,0:T(8,128)(2,1)}, u32[]{:S(2)}) copy-start(bf16[6,8,128]{2,1,0:T(8,128)(2,1)} %get-tuple-element.29) | copy-start | bytes 36868
  8.5 12.2 %copy-start.3 = (bf16[6,8,128]{2,1,0:T(8,128)(2,1)S(1)}, bf16[6,8,128]{2,1,0:T(8,128)(2,1)}, u32[]{:S(2)}) copy-start(bf16[6,8,128]{2,1,0:T(8,128)(2,1)} %get-tuple-element.30) | copy-start | bytes 36868
  8.5 14.9 %copy-start.2 = (bf16[6,8,128]{2,1,0:T(8,128)(2,1)S(1)}, bf16[6,8,128]{2,1,0:T(8,128)(2,1)}, u32[]{:S(2)}) copy-start(bf16[6,8,128]{2,1,0:T(8,128)(2,1)} %get-tuple-element.31) | copy-start | bytes 36868
  8.5 54.3 %all-to-all-start = ((bf16[128,13,8,128]{3,2,1,0:T(8,128)(2,1)}), bf16[128,13,8,128]{3,2,1,0:T(8,128)(2,1)S(1)}, u32[]{:S(2)}, u32[]{:S(2)}) async-start(bf16[128,13,8,128]{3,2,1,0:T(8,128)(2,1)} %get-tuple-element.27), calls=%async_computation | async-start | bytes 6815744 | tf_op jit(solution)/shard_map/all_to_all | solution.py:351
  19.7 34.8 %collective-permute-start = (bf16[6,8,128]{2,1,0:T(8,128)(2,1)S(1)}, bf16[6,8,128]{2,1,0:T(8,128)(2,1)S(1)}, u32[]{:S(2)}, u32[]{:S(2)}) collective-permute-start(bf16[6,8,128]{2,1,0:T(8,128)(2,1)S(1)} %copy-done.4), channel_id=1, source_target_pairs={{0,1},{1,2},{2,3},{3,0},{4,5},{5,6},{6,7},{7,4},{8,9},{9,10},{10,1... | collective-permute-start | bytes 36872 | tf_op jit(solution)/shard_map/ppermute | solution.py:331
  20.7 33.8 %collective-permute-start.1 = (bf16[6,8,128]{2,1,0:T(8,128)(2,1)S(1)}, bf16[6,8,128]{2,1,0:T(8,128)(2,1)S(1)}, u32[]{:S(2)}, u32[]{:S(2)}) collective-permute-start(bf16[6,8,128]{2,1,0:T(8,128)(2,1)S(1)} %copy-done.3), channel_id=1, source_target_pairs={{0,2},{1,3},{2,0},{3,1},{4,6},{5,7},{6,4},{7,5},{8,10},{9,11},{10,... | collective-permute-start | bytes 36872 | tf_op jit(solution)/shard_map/ppermute | solution.py:331
  23.4 31.9 %collective-permute-start.2 = (bf16[6,8,128]{2,1,0:T(8,128)(2,1)S(1)}, bf16[6,8,128]{2,1,0:T(8,128)(2,1)S(1)}, u32[]{:S(2)}, u32[]{:S(2)}) collective-permute-start(bf16[6,8,128]{2,1,0:T(8,128)(2,1)S(1)} %copy-done.2), channel_id=1, source_target_pairs={{0,3},{1,0},{2,1},{3,2},{4,7},{5,4},{6,5},{7,6},{8,11},{9,8},{10,9... | collective-permute-start | bytes 36872 | tf_op jit(solution)/shard_map/ppermute | solution.py:331
  63.9 16.9 %collective-permute-start.5 = (bf16[97,8,128]{2,1,0:T(8,128)(2,1)}, bf16[97,8,128]{2,1,0:T(8,128)(2,1)}, u32[]{:S(2)}, u32[]{:S(2)}) collective-permute-start(bf16[97,8,128]{2,1,0:T(8,128)(2,1)} %mid.1), channel_id=1, source_target_pairs={{0,96},{32,0},{64,32},{96,64},{1,97},{33,1},{65,33},{97,65},{2,98}... | collective-permute-start | bytes 595976 | tf_op jit(solution)/shard_map/ppermute | solution.py:331
  65.8 15.1 %collective-permute-start.4 = (bf16[97,8,128]{2,1,0:T(8,128)(2,1)}, bf16[97,8,128]{2,1,0:T(8,128)(2,1)}, u32[]{:S(2)}, u32[]{:S(2)}) collective-permute-start(bf16[97,8,128]{2,1,0:T(8,128)(2,1)} %mid.1), channel_id=1, source_target_pairs={{0,64},{32,96},{64,0},{96,32},{1,65},{33,97},{65,1},{97,33},{2,66}... | collective-permute-start | bytes 595976 | tf_op jit(solution)/shard_map/ppermute | solution.py:331
  66.9 14.0 %collective-permute-start.3 = (bf16[97,8,128]{2,1,0:T(8,128)(2,1)}, bf16[97,8,128]{2,1,0:T(8,128)(2,1)}, u32[]{:S(2)}, u32[]{:S(2)}) collective-permute-start(bf16[97,8,128]{2,1,0:T(8,128)(2,1)} %mid.1), channel_id=1, source_target_pairs={{0,32},{32,64},{64,96},{96,0},{1,33},{33,65},{65,97},{97,1},{2,34}... | collective-permute-start | bytes 595976 | tf_op jit(solution)/shard_map/ppermute | solution.py:331
  73.1 13.9 %copy-start.1 = (bf16[6,8,128]{2,1,0:T(8,128)(2,1)S(1)}, bf16[6,8,128]{2,1,0:T(8,128)(2,1)}, u32[]{:S(2)}) copy-start(bf16[6,8,128]{2,1,0:T(8,128)(2,1)} %get-tuple-element.34.b0_ref) | copy-start | bytes 36868
  73.1 26.7 %all-to-all-start.1 = ((bf16[128,4,8,128]{3,2,1,0:T(8,128)(2,1)}), bf16[128,4,8,128]{3,2,1,0:T(8,128)(2,1)S(1)}, u32[]{:S(2)}, u32[]{:S(2)}) async-start(bf16[128,4,8,128]{3,2,1,0:T(8,128)(2,1)} %cold.1), calls=%async_computation.1 | async-start | bytes 2097152 | tf_op jit(solution)/shard_map/all_to_all | solution.py:378
  84.7 15.2 %copy-start = (f32[8,1024]{1,0:T(8,128)S(1)}, f32[8,1024]{1,0:T(8,128)}, u32[]{:S(2)}) copy-start(f32[8,1024]{1,0:T(8,128)} %get-tuple-element.26.table_ref) | copy-start | bytes 98308
  84.7 2.4 %collective-permute-start.6 = (bf16[388,8,128]{2,1,0:T(8,128)(2,1)S(1)}, bf16[388,8,128]{2,1,0:T(8,128)(2,1)S(1)}, u32[]{:S(2)}, u32[]{:S(2)}) collective-permute-start(bf16[388,8,128]{2,1,0:T(8,128)(2,1)S(1)} %constant_dynamic-update-slice_fusion.near_ref), channel_id=1, source_target_pairs={{0,16},{16,0},{1,17},{17,1},{2,18},{18,2},{3,19},{19,3},{4,20},{20... | collective-permute-start | bytes 2383880 | tf_op jit(solution)/shard_map/ppermute | solution.py:331
  88.1 4.0 %collective-permute-start.7 = (bf16[3,8,128]{2,1,0:T(8,128)(2,1)S(1)}, bf16[3,8,128]{2,1,0:T(8,128)(2,1)S(1)}, u32[]{:S(2)}, u32[]{:S(2)}) collective-permute-start(bf16[3,8,128]{2,1,0:T(8,128)(2,1)S(1)} %get-tuple-element.44), channel_id=1, source_target_pairs={{0,3},{1,0},{2,1},{3,2},{4,7},{5,4},{6,5},{7,6},{8,11},{9,8},{10,9... | collective-permute-start | bytes 18440 | tf_op jit(solution)/shard_map/ppermute | solution.py:331
  90.4 5.6 %collective-permute-start.8 = (bf16[3,8,128]{2,1,0:T(8,128)(2,1)S(1)}, bf16[3,8,128]{2,1,0:T(8,128)(2,1)S(1)}, u32[]{:S(2)}, u32[]{:S(2)}) collective-permute-start(bf16[3,8,128]{2,1,0:T(8,128)(2,1)S(1)} %get-tuple-element.45), channel_id=1, source_target_pairs={{0,2},{1,3},{2,0},{3,1},{4,6},{5,7},{6,4},{7,5},{8,10},{9,11},{10,... | collective-permute-start | bytes 18440 | tf_op jit(solution)/shard_map/ppermute | solution.py:331
  91.2 5.0 %collective-permute-start.9 = (bf16[3,8,128]{2,1,0:T(8,128)(2,1)S(1)}, bf16[3,8,128]{2,1,0:T(8,128)(2,1)S(1)}, u32[]{:S(2)}, u32[]{:S(2)}) collective-permute-start(bf16[3,8,128]{2,1,0:T(8,128)(2,1)S(1)} %get-tuple-element.46), channel_id=1, source_target_pairs={{0,1},{1,2},{2,3},{3,0},{4,5},{5,6},{6,7},{7,4},{8,9},{9,10},{10,1... | collective-permute-start | bytes 18440 | tf_op jit(solution)/shard_map/ppermute | solution.py:331

commit v13 on v12

--- a/solution.py
+++ b/solution.py
@@ -90,9 +90,7 @@
     asked_tags = jnp.sum(labels, axis=0, keepdims=True)
     cold_lane = iota((1, LANES), 1) < HOT_LANE
     for h in range(heads):
-        own = iota((HOT, LANES), 1) == iota((HOT, LANES), 0) + (HOT_LANE + HOT * h)
-        tag = jnp.sum(jnp.where(own, asked_tags, 0.0), axis=1, keepdims=True)
-        hot_ref[h, 3:6] = jnp.broadcast_to(tag, (HOT, hd)).reshape(3, COLD, hd).astype(BF16)
+        hot_ref[h, 3] = jnp.broadcast_to(asked_tags, (COLD, LANES)).astype(BF16)
     rows = HOT // SHARE * COLD
     row = iota((rows + HOT_PAD, 1), 0)
     row_share, row_at = row // COLD, row % COLD
@@ -251,8 +249,10 @@
     for d, ref in enumerate((b0_ref, b1_ref, b2_ref, b3_ref)):
         all_ref[lax.rem(y + 4 - d, 4)] = ref[...].astype(F32)
     q = all_ref[:, 0:3].reshape(rows, hd).astype(BF16)
-    label_col = all_ref[:, 3:6].reshape(rows, hd)[:, 0:1]
     row = iota((rows, 1), 0)
+    tags = jnp.broadcast_to(all_ref[:, 3, 0:1], (4, HOT, LANES)).reshape(rows, LANES)
+    own = iota((rows, LANES), 1) == HOT_LANE + HOT * y + row % HOT
+    label_col = jnp.sum(jnp.where(own, tags, 0.0), axis=1, keepdims=True)
     asked_at = (((z * 2 + core) * 16 + x * 4) * HOT + row).astype(F32)
     n = iota((1, keys), 1)
     key_at = (n // SHARE) * HOT + n % SHARE
@@ -339,11 +339,11 @@
     payload = (devices, 3 * heads + 1, *tile)
     table, h0, h1, h2, h3, send = call(
         pack_kernel, "pack", 58, [HBM] * 4,
-        [(HBM, (2 * heads, tokens), F32)] + [(HBM, (6, *tile), BF16)] * 4 + [(HBM, payload, BF16)],
+        [(HBM, (2 * heads, tokens), F32)] + [(HBM, (4, *tile), BF16)] * 4 + [(HBM, payload, BF16)],
         [
             pltpu.VMEM((heads, tokens), jnp.int32), pltpu.VMEM((2 * heads, tokens), F32),
             *[pltpu.VMEM((tokens, heads * hd), BF16)] * 3,
-            pltpu.VMEM((heads, 6, *tile), BF16), pltpu.VMEM(payload, BF16),
+            pltpu.VMEM((heads, 4, *tile), BF16), pltpu.VMEM(payload, BF16),
             pltpu.SemaphoreType.DMA((3 * heads + 1,)), pltpu.SemaphoreType.DMA((9,)),
         ],
         cluster_ids, query_rows, key_rows, value_rows,
@@ -368,7 +368,7 @@
     outs = call(
         hot_kernel, "hot", 24, [VMEM] * 6, [(VMEM, (3, *tile), BF16)] * 4,
         [
-            pltpu.VMEM((4, 6, *tile), F32), pltpu.VMEM((devices * HOT, hd), BF16),
+            pltpu.VMEM((4, 4, *tile), F32), pltpu.VMEM((devices * HOT, hd), BF16),
             pltpu.VMEM((devices * HOT, hd), BF16), pltpu.VMEM((4, 3, *tile), F32),
         ],
         *asked, near, far,

time: 104 us -> 104 us (level)
  transfers between devices with their start and end apart: 12 -> 12, of which waited for: 7 -> 8; matrix products, arithmetic and copies ran while one was open for 4% -> 4% of each run, Pallas kernels for 7% -> 7%
where the time goes in v13:
time: 104 us
  waiting for transfers between devices  48 us (46%)
  starting transfers between devices  31.4 us (30%)
  Pallas kernels  20.2 us (19%)
  local copies, waits for them, and re-layouts  3.83 us (4%)
    ppermute x10, waiting for transfers between devices, shift(): lax.ppermute(block, axis, [(i, (i + by) % size) for i in range(size)])  36.7 us
    pallas_call x5, Pallas kernels, call(): pl.pallas_call(kernel, out_shape=tuple((pltpu.HBM(*out[1:]) if out[0] is...  20.2 us
    ppermute x10, starting transfers between devices, shift(): lax.ppermute(block, axis, [(i, (i + by) % size) for i in range(size)])  12.5 us
    all_to_all x1, starting transfers between devices, local(): got = lax.all_to_all(send, AXES, split_axis=0, concat_axis=0, tiled=True)  11.2 us
    all_to_all x1, starting transfers between devices, local(): back = lax.all_to_all(answer, AXES, split_axis=0, concat_axis=0, tiled=True)  7.68 us
    all_to_all x1, waiting for transfers between devices, local(): got = lax.all_to_all(send, AXES, split_axis=0, concat_axis=0, tiled=True)  7.65 us
    all_to_all x1, waiting for transfers between devices, local(): back = lax.all_to_all(answer, AXES, split_axis=0, concat_axis=0, tiled=True)  3.66 us
    unnamed x13, local copies, waits for them, and re-layouts  2.88 us
  transfers between devices with their start and end apart: 12, of which 8 were waited for; matrix products, arithmetic and copies ran while one was open for 4% of the time, Pallas kernels for 7%

profile of v13, /device:TPU:0, one launch (start us, length us, event | category | flops | bytes accessed | tf_op | source)
XLA Modules:
  0.0 103.7 jit_solution(1209788407788090561)
XLA Ops:
  0.0 8.4 %pack.1 = (f32[8,1024]{1,0:T(8,128)}, bf16[4,8,128]{2,1,0:T(8,128)(2,1)}, bf16[4,8,128]{2,1,0:T(8,128)(2,1)}, bf16[4,8,128]{2,1,0:T(8,128)(2,1)}, bf16[4,8,128]{...) custom-call(s32[4,1024]{1,0:T(4,128)} %ids_hbm.1, bf16[1024,512]{1,0:T(8,128)(2,1)} %q_hbm.1, bf16[1024,512]{1,0:T(8,128)(2,1)} %k_hbm.1, ...), custom_call_target="tpu_custom_call" | custom-call | tf_op jit(solution)/shard_map/pack/pallas_call | solution.py:315
  8.4 0.0 copy-start.4
  8.4 11.2 %all-to-all-start = ((bf16[128,13,8,128]{3,2,1,0:T(8,128)(2,1)}), bf16[128,13,8,128]{3,2,1,0:T(8,128)(2,1)S(1)}, u32[]{:S(2)}, u32[]{:S(2)}) async-start(bf16[128,13,8,128]{3,2,1,0:T(8,128)(2,1)} %get-tuple-element.27), calls=%async_computation | async-start | bytes 6815744 | tf_op jit(solution)/shard_map/all_to_all | solution.py:351
  19.6 1.0 collective-permute-start
  20.6 2.7 %collective-permute-start.1 = (bf16[4,8,128]{2,1,0:T(8,128)(2,1)S(1)}, bf16[4,8,128]{2,1,0:T(8,128)(2,1)S(1)}, u32[]{:S(2)}, u32[]{:S(2)}) collective-permute-start(bf16[4,8,128]{2,1,0:T(8,128)(2,1)S(1)} %copy-done.3), channel_id=1, source_target_pairs={{0,2},{1,3},{2,0},{3,1},{4,6},{5,7},{6,4},{7,5},{8,10},{9,11},{10,... | collective-permute-start | bytes 24584 | tf_op jit(solution)/shard_map/ppermute | solution.py:331
  23.3 1.4 %collective-permute-start.2 = (bf16[4,8,128]{2,1,0:T(8,128)(2,1)S(1)}, bf16[4,8,128]{2,1,0:T(8,128)(2,1)S(1)}, u32[]{:S(2)}, u32[]{:S(2)}) collective-permute-start(bf16[4,8,128]{2,1,0:T(8,128)(2,1)S(1)} %copy-done.2), channel_id=1, source_target_pairs={{0,3},{1,0},{2,1},{3,2},{4,7},{5,4},{6,5},{7,6},{8,11},{9,8},{10,9... | collective-permute-start | bytes 24584 | tf_op jit(solution)/shard_map/ppermute | solution.py:331
  24.8 27.7 %collective-permute-done.b1_ref = bf16[4,8,128]{2,1,0:T(8,128)(2,1)S(1)} collective-permute-done((bf16[4,8,128]{2,1,0:T(8,128)(2,1)S(1)}, bf16[4,8,128]{2,1,0:T(8,128)(2,1)S(1)}, u32[]{:S(2)}, u32[]{:S(2)}) %collective-permute-start) | collective-permute-done | bytes 8224 | tf_op jit(solution)/shard_map/ppermute | solution.py:331
  52.5 1.4 %collective-permute-done.1.b2_ref = bf16[4,8,128]{2,1,0:T(8,128)(2,1)S(1)} collective-permute-done((bf16[4,8,128]{2,1,0:T(8,128)(2,1)S(1)}, bf16[4,8,128]{2,1,0:T(8,128)(2,1)S(1)}, u32[]{:S(2)}, u32[]{:S(2)}) %collective-permute-start.1) | collective-permute-done | bytes 8224 | tf_op jit(solution)/shard_map/ppermute | solution.py:331
  53.8 1.2 %collective-permute-done.2.b3_ref = bf16[4,8,128]{2,1,0:T(8,128)(2,1)S(1)} collective-permute-done((bf16[4,8,128]{2,1,0:T(8,128)(2,1)S(1)}, bf16[4,8,128]{2,1,0:T(8,128)(2,1)S(1)}, u32[]{:S(2)}, u32[]{:S(2)}) %collective-permute-start.2) | collective-permute-done | bytes 8224 | tf_op jit(solution)/shard_map/ppermute | solution.py:331
  55.1 7.7 %all-to-all-done.got_ref = bf16[128,13,8,128]{3,2,1,0:T(8,128)(2,1)S(1)} async-done(((bf16[128,13,8,128]{3,2,1,0:T(8,128)(2,1)}), bf16[128,13,8,128]{3,2,1,0:T(8,128)(2,1)S(1)}, u32[]{:S(2)}, u32[]{:S(2)}) %all-to-all-start) | async-done | bytes 3407904 | tf_op jit(solution)/shard_map/all_to_all | solution.py:351
  62.7 1.1 %mid.1 = bf16[97,8,128]{2,1,0:T(8,128)(2,1)} custom-call(bf16[128,13,8,128]{3,2,1,0:T(8,128)(2,1)S(1)} %all-to-all-done.got_ref), custom_call_target="tpu_custom_call" | custom-call | tf_op jit(solution)/shard_map/mid/pallas_call | solution.py:315
  63.8 1.9 %collective-permute-start.5 = (bf16[97,8,128]{2,1,0:T(8,128)(2,1)}, bf16[97,8,128]{2,1,0:T(8,128)(2,1)}, u32[]{:S(2)}, u32[]{:S(2)}) collective-permute-start(bf16[97,8,128]{2,1,0:T(8,128)(2,1)} %mid.1), channel_id=1, source_target_pairs={{0,96},{32,0},{64,32},{96,64},{1,97},{33,1},{65,33},{97,65},{2,98}... | collective-permute-start | bytes 595976 | tf_op jit(solution)/shard_map/ppermute | solution.py:331
  65.7 1.1 %collective-permute-start.4 = (bf16[97,8,128]{2,1,0:T(8,128)(2,1)}, bf16[97,8,128]{2,1,0:T(8,128)(2,1)}, u32[]{:S(2)}, u32[]{:S(2)}) collective-permute-start(bf16[97,8,128]{2,1,0:T(8,128)(2,1)} %mid.1), channel_id=1, source_target_pairs={{0,64},{32,96},{64,0},{96,32},{1,65},{33,97},{65,1},{97,33},{2,66}... | collective-permute-start | bytes 595976 | tf_op jit(solution)/shard_map/ppermute | solution.py:331
  66.8 0.3 collective-permute-start.3
  67.1 5.9 %cold.1 = bf16[128,4,8,128]{3,2,1,0:T(8,128)(2,1)} custom-call(bf16[128,13,8,128]{3,2,1,0:T(8,128)(2,1)S(1)} %all-to-all-done.got_ref), custom_call_target="tpu_custom_call" | custom-call | flops 20000000000 | tf_op jit(solution)/shard_map/cold/pallas_call | solution.py:315
  73.1 7.7 %all-to-all-start.1 = ((bf16[128,4,8,128]{3,2,1,0:T(8,128)(2,1)}), bf16[128,4,8,128]{3,2,1,0:T(8,128)(2,1)S(1)}, u32[]{:S(2)}, u32[]{:S(2)}) async-start(bf16[128,4,8,128]{3,2,1,0:T(8,128)(2,1)} %cold.1), calls=%async_computation.1 | async-start | bytes 2097152 | tf_op jit(solution)/shard_map/all_to_all | solution.py:378
  80.7 0.0 collective-permute-done.5
  80.8 0.0 collective-permute-done.4
  80.8 0.9 constant_dynamic-update-slice_fusion.3
  81.7 1.0 constant_dynamic-update-slice_fusion.2
  82.7 1.0 constant_dynamic-update-slice_fusion.1
  83.6 1.0 constant_dynamic-update-slice_fusion.near_ref
  84.6 0.1 collective-permute-start.6
  84.7 2.3 %collective-permute-done.6.far_ref = bf16[388,8,128]{2,1,0:T(8,128)(2,1)S(1)} collective-permute-done((bf16[388,8,128]{2,1,0:T(8,128)(2,1)S(1)}, bf16[388,8,128]{2,1,0:T(8,128)(2,1)S(1)}, u32[]{:S(2)}, u32[]{:S(2)}) %collective-permute-start.6) | collective-permute-done | bytes 794656 | tf_op jit(solution)/shard_map/ppermute | solution.py:331
  87.0 1.1 %hot.1 = (bf16[3,8,128]{2,1,0:T(8,128)(2,1)S(1)}, bf16[3,8,128]{2,1,0:T(8,128)(2,1)S(1)}, bf16[3,8,128]{2,1,0:T(8,128)(2,1)S(1)}, bf16[3,8,128]{2,1,0:T(8,128)(2,1)S(1)}) custom-call(bf16[4,8,128]{2,1,0:T(8,128)(2,1)S(1)} %copy-done.1, bf16[4,8,128]{2,1,0:T(8,128)(2,1)S(1)} %collective-permute-done.b1_ref, ...), custom_call_target="tpu_custom_call" | custom-call | flops 2000000000 | tf_op jit(solution)/shard_map/hot/pallas_call | solution.py:315
  88.1 2.3 %collective-permute-start.7 = (bf16[3,8,128]{2,1,0:T(8,128)(2,1)S(1)}, bf16[3,8,128]{2,1,0:T(8,128)(2,1)S(1)}, u32[]{:S(2)}, u32[]{:S(2)}) collective-permute-start(bf16[3,8,128]{2,1,0:T(8,128)(2,1)S(1)} %get-tuple-element.44), channel_id=1, source_target_pairs={{0,3},{1,0},{2,1},{3,2},{4,7},{5,4},{6,5},{7,6},{8,11},{9,8},{10,9... | collective-permute-start | bytes 18440 | tf_op jit(solution)/shard_map/ppermute | solution.py:331
  90.4 0.8 collective-permute-start.8
  91.2 0.9 collective-permute-start.9
  92.0 3.9 %collective-permute-done.8.o2_ref = bf16[3,8,128]{2,1,0:T(8,128)(2,1)S(1)} collective-permute-done((bf16[3,8,128]{2,1,0:T(8,128)(2,1)S(1)}, bf16[3,8,128]{2,1,0:T(8,128)(2,1)S(1)}, u32[]{:S(2)}, u32[]{:S(2)}) %collective-permute-start.8) | collective-permute-done | bytes 6176 | tf_op jit(solution)/shard_map/ppermute | solution.py:331
  96.0 0.2 collective-permute-done.9.o3_ref
  96.1 3.7 %all-to-all-done.1.back_ref = bf16[128,4,8,128]{3,2,1,0:T(8,128)(2,1)S(1)} async-done(((bf16[128,4,8,128]{3,2,1,0:T(8,128)(2,1)}), bf16[128,4,8,128]{3,2,1,0:T(8,128)(2,1)S(1)}, u32[]{:S(2)}, u32[]{:S(2)}) %all-to-all-start.1) | async-done | bytes 1048608 | tf_op jit(solution)/shard_map/all_to_all | solution.py:378
  99.8 3.7 %unpack.1 = bf16[1024,512]{1,0:T(8,128)(2,1)} custom-call(f32[8,1024]{1,0:T(8,128)S(1)} %copy-done, bf16[128,4,8,128]{3,2,1,0:T(8,128)(2,1)S(1)} %all-to-all-done.1.back_ref, bf16[3,8,128]{2,1,0:T(8,128)(2,1)S(1)} %get-tuple-element.43.o0_ref, bf16[3,8,128]{2,1,0:T(8,128)(2,1)S(1)} %collective-permute-done.7.o1_ref, ...), custom_call_target="tpu_custom_call" | custom-call | tf_op jit(solution)/shard_map/unpack/pallas_call | solution.py:315
  (11 shorter events, 0.0 us)
Async XLA Ops:
  8.4 11.2 %copy-start.4 = (bf16[4,8,128]{2,1,0:T(8,128)(2,1)S(1)}, bf16[4,8,128]{2,1,0:T(8,128)(2,1)}, u32[]{:S(2)}) copy-start(bf16[4,8,128]{2,1,0:T(8,128)(2,1)} %get-tuple-element.29) | copy-start | bytes 24580
  8.4 12.2 %copy-start.3 = (bf16[4,8,128]{2,1,0:T(8,128)(2,1)S(1)}, bf16[4,8,128]{2,1,0:T(8,128)(2,1)}, u32[]{:S(2)}) copy-start(bf16[4,8,128]{2,1,0:T(8,128)(2,1)} %get-tuple-element.30) | copy-start | bytes 24580
  8.4 14.9 %copy-start.2 = (bf16[4,8,128]{2,1,0:T(8,128)(2,1)S(1)}, bf16[4,8,128]{2,1,0:T(8,128)(2,1)}, u32[]{:S(2)}) copy-start(bf16[4,8,128]{2,1,0:T(8,128)(2,1)} %get-tuple-element.31) | copy-start | bytes 24580
  8.4 54.3 %all-to-all-start = ((bf16[128,13,8,128]{3,2,1,0:T(8,128)(2,1)}), bf16[128,13,8,128]{3,2,1,0:T(8,128)(2,1)S(1)}, u32[]{:S(2)}, u32[]{:S(2)}) async-start(bf16[128,13,8,128]{3,2,1,0:T(8,128)(2,1)} %get-tuple-element.27), calls=%async_computation | async-start | bytes 6815744 | tf_op jit(solution)/shard_map/all_to_all | solution.py:351
  19.6 32.9 %collective-permute-start = (bf16[4,8,128]{2,1,0:T(8,128)(2,1)S(1)}, bf16[4,8,128]{2,1,0:T(8,128)(2,1)S(1)}, u32[]{:S(2)}, u32[]{:S(2)}) collective-permute-start(bf16[4,8,128]{2,1,0:T(8,128)(2,1)S(1)} %copy-done.4), channel_id=1, source_target_pairs={{0,1},{1,2},{2,3},{3,0},{4,5},{5,6},{6,7},{7,4},{8,9},{9,10},{10,1... | collective-permute-start | bytes 24584 | tf_op jit(solution)/shard_map/ppermute | solution.py:331
  20.6 33.2 %collective-permute-start.1 = (bf16[4,8,128]{2,1,0:T(8,128)(2,1)S(1)}, bf16[4,8,128]{2,1,0:T(8,128)(2,1)S(1)}, u32[]{:S(2)}, u32[]{:S(2)}) collective-permute-start(bf16[4,8,128]{2,1,0:T(8,128)(2,1)S(1)} %copy-done.3), channel_id=1, source_target_pairs={{0,2},{1,3},{2,0},{3,1},{4,6},{5,7},{6,4},{7,5},{8,10},{9,11},{10,... | collective-permute-start | bytes 24584 | tf_op jit(solution)/shard_map/ppermute | solution.py:331
  23.3 31.7 %collective-permute-start.2 = (bf16[4,8,128]{2,1,0:T(8,128)(2,1)S(1)}, bf16[4,8,128]{2,1,0:T(8,128)(2,1)S(1)}, u32[]{:S(2)}, u32[]{:S(2)}) collective-permute-start(bf16[4,8,128]{2,1,0:T(8,128)(2,1)S(1)} %copy-done.2), channel_id=1, source_target_pairs={{0,3},{1,0},{2,1},{3,2},{4,7},{5,4},{6,5},{7,6},{8,11},{9,8},{10,9... | collective-permute-start | bytes 24584 | tf_op jit(solution)/shard_map/ppermute | solution.py:331
  63.8 16.9 %collective-permute-start.5 = (bf16[97,8,128]{2,1,0:T(8,128)(2,1)}, bf16[97,8,128]{2,1,0:T(8,128)(2,1)}, u32[]{:S(2)}, u32[]{:S(2)}) collective-permute-start(bf16[97,8,128]{2,1,0:T(8,128)(2,1)} %mid.1), channel_id=1, source_target_pairs={{0,96},{32,0},{64,32},{96,64},{1,97},{33,1},{65,33},{97,65},{2,98}... | collective-permute-start | bytes 595976 | tf_op jit(solution)/shard_map/ppermute | solution.py:331
  65.7 15.1 %collective-permute-start.4 = (bf16[97,8,128]{2,1,0:T(8,128)(2,1)}, bf16[97,8,128]{2,1,0:T(8,128)(2,1)}, u32[]{:S(2)}, u32[]{:S(2)}) collective-permute-start(bf16[97,8,128]{2,1,0:T(8,128)(2,1)} %mid.1), channel_id=1, source_target_pairs={{0,64},{32,96},{64,0},{96,32},{1,65},{33,97},{65,1},{97,33},{2,66}... | collective-permute-start | bytes 595976 | tf_op jit(solution)/shard_map/ppermute | solution.py:331
  66.8 14.0 %collective-permute-start.3 = (bf16[97,8,128]{2,1,0:T(8,128)(2,1)}, bf16[97,8,128]{2,1,0:T(8,128)(2,1)}, u32[]{:S(2)}, u32[]{:S(2)}) collective-permute-start(bf16[97,8,128]{2,1,0:T(8,128)(2,1)} %mid.1), channel_id=1, source_target_pairs={{0,32},{32,64},{64,96},{96,0},{1,33},{33,65},{65,97},{97,1},{2,34}... | collective-permute-start | bytes 595976 | tf_op jit(solution)/shard_map/ppermute | solution.py:331
  73.0 13.9 %copy-start.1 = (bf16[4,8,128]{2,1,0:T(8,128)(2,1)S(1)}, bf16[4,8,128]{2,1,0:T(8,128)(2,1)}, u32[]{:S(2)}) copy-start(bf16[4,8,128]{2,1,0:T(8,128)(2,1)} %get-tuple-element.34.b0_ref) | copy-start | bytes 24580
  73.1 26.7 %all-to-all-start.1 = ((bf16[128,4,8,128]{3,2,1,0:T(8,128)(2,1)}), bf16[128,4,8,128]{3,2,1,0:T(8,128)(2,1)S(1)}, u32[]{:S(2)}, u32[]{:S(2)}) async-start(bf16[128,4,8,128]{3,2,1,0:T(8,128)(2,1)} %cold.1), calls=%async_computation.1 | async-start | bytes 2097152 | tf_op jit(solution)/shard_map/all_to_all | solution.py:378
  84.6 15.2 %copy-start = (f32[8,1024]{1,0:T(8,128)S(1)}, f32[8,1024]{1,0:T(8,128)}, u32[]{:S(2)}) copy-start(f32[8,1024]{1,0:T(8,128)} %get-tuple-element.26.table_ref) | copy-start | bytes 98308
  84.6 2.4 %collective-permute-start.6 = (bf16[388,8,128]{2,1,0:T(8,128)(2,1)S(1)}, bf16[388,8,128]{2,1,0:T(8,128)(2,1)S(1)}, u32[]{:S(2)}, u32[]{:S(2)}) collective-permute-start(bf16[388,8,128]{2,1,0:T(8,128)(2,1)S(1)} %constant_dynamic-update-slice_fusion.near_ref), channel_id=1, source_target_pairs={{0,16},{16,0},{1,17},{17,1},{2,18},{18,2},{3,19},{19,3},{4,20},{20... | collective-permute-start | bytes 2383880 | tf_op jit(solution)/shard_map/ppermute | solution.py:331
  88.1 4.0 %collective-permute-start.7 = (bf16[3,8,128]{2,1,0:T(8,128)(2,1)S(1)}, bf16[3,8,128]{2,1,0:T(8,128)(2,1)S(1)}, u32[]{:S(2)}, u32[]{:S(2)}) collective-permute-start(bf16[3,8,128]{2,1,0:T(8,128)(2,1)S(1)} %get-tuple-element.44), channel_id=1, source_target_pairs={{0,3},{1,0},{2,1},{3,2},{4,7},{5,4},{6,5},{7,6},{8,11},{9,8},{10,9... | collective-permute-start | bytes 18440 | tf_op jit(solution)/shard_map/ppermute | solution.py:331
  90.4 5.6 %collective-permute-start.8 = (bf16[3,8,128]{2,1,0:T(8,128)(2,1)S(1)}, bf16[3,8,128]{2,1,0:T(8,128)(2,1)S(1)}, u32[]{:S(2)}, u32[]{:S(2)}) collective-permute-start(bf16[3,8,128]{2,1,0:T(8,128)(2,1)S(1)} %get-tuple-element.45), channel_id=1, source_target_pairs={{0,2},{1,3},{2,0},{3,1},{4,6},{5,7},{6,4},{7,5},{8,10},{9,11},{10,... | collective-permute-start | bytes 18440 | tf_op jit(solution)/shard_map/ppermute | solution.py:331
  91.2 4.9 %collective-permute-start.9 = (bf16[3,8,128]{2,1,0:T(8,128)(2,1)S(1)}, bf16[3,8,128]{2,1,0:T(8,128)(2,1)S(1)}, u32[]{:S(2)}, u32[]{:S(2)}) collective-permute-start(bf16[3,8,128]{2,1,0:T(8,128)(2,1)S(1)} %get-tuple-element.46), channel_id=1, source_target_pairs={{0,1},{1,2},{2,3},{3,0},{4,5},{5,6},{6,7},{7,4},{8,9},{9,10},{10,1... | collective-permute-start | bytes 18440 | tf_op jit(solution)/shard_map/ppermute | solution.py:331

commit v14 on v13

--- a/solution.py
+++ b/solution.py
@@ -104,17 +104,6 @@
         load.wait()
     for h in range(heads):
         xs.append(jnp.concatenate([ref[:, h * hd : (h + 1) * hd] for ref in (q_ref, k_ref, v_ref)], axis=1))
-        moved = jnp.dot(
-            (slot_all[h : h + 1] == want).astype(BF16), xs[h], preferred_element_type=F32
-        )
-        tiles = jnp.where(tile_at < SHARE, moved[:rows, hd : 2 * hd], moved[:rows, 2 * hd :])
-        tiles = jnp.where(tile_at == COLD - 1, asked_tags, tiles)
-        hot_tiles.append(tiles)
-        hot_ref[h, 0:3] = moved[rows : rows + HOT, :hd].reshape(3, COLD, hd).astype(BF16)
-    y = lax.axis_index("y")
-    for d, ref in enumerate((h0_hbm, h1_hbm, h2_hbm, h3_hbm)):
-        sent.append(pltpu.make_async_copy(hot_ref.at[lax.rem(y + d, heads)], ref, out_sems.at[5 + d]))
-        sent[-1].start()
     labels = jnp.where(cold_lane, labels, 0.0)
     part = 256
     sub = iota((COLD, LANES), 0)
@@ -122,7 +111,17 @@
         first, stop = c * part // COLD, (c + 1) * part // COLD
         for h in range(heads):
             place = (slot_all[h : h + 1] == iota((part, tokens), 0) + c * part).astype(BF16)
-            moved = jnp.dot(place, xs[h], preferred_element_type=F32)
+            if c == 0:
+                hot = (slot_all[h : h + 1] == want).astype(BF16)
+                moved = jnp.dot(
+                    jnp.concatenate([place, hot], axis=0), xs[h], preferred_element_type=F32
+                )
+                hot, moved = moved[part:], moved[:part]
+                tiles = jnp.where(tile_at < SHARE, hot[:rows, hd : 2 * hd], hot[:rows, 2 * hd :])
+                hot_tiles.append(jnp.where(tile_at == COLD - 1, asked_tags, tiles))
+                hot_ref[h, 0:3] = hot[rows : rows + HOT, :hd].reshape(3, COLD, hd).astype(BF16)
+            else:
+                moved = jnp.dot(place, xs[h], preferred_element_type=F32)
             for j in range(3):
                 send_ref[first:stop, 3 * h + j] = (
                     moved[:, j * hd : (j + 1) * hd].reshape(stop - first, COLD, hd).astype(BF16)
@@ -137,6 +136,10 @@
         )
         out.start()
         sent.append(out)
+    y = lax.axis_index("y")
+    for d, ref in enumerate((h0_hbm, h1_hbm, h2_hbm, h3_hbm)):
+        sent.append(pltpu.make_async_copy(hot_ref.at[lax.rem(y + d, heads)], ref, out_sems.at[5 + d]))
+        sent[-1].start()
     for out in sent:
         out.wait()
 

time: 104 us -> 104 us (level)
  no operation moved by 1% of the time
where the time goes in v14:
time: 104 us
  waiting for transfers between devices  48 us (46%)
  starting transfers between devices  31.4 us (30%)
  Pallas kernels  20.1 us (19%)
  local copies, waits for them, and re-layouts  3.83 us (4%)
    ppermute x10, waiting for transfers between devices, shift(): lax.ppermute(block, axis, [(i, (i + by) % size) for i in range(size)])  36.7 us
    pallas_call x5, Pallas kernels, call(): pl.pallas_call(kernel, out_shape=tuple((pltpu.HBM(*out[1:]) if out[0] is...  20.1 us
    ppermute x10, starting transfers between devices, shift(): lax.ppermute(block, axis, [(i, (i + by) % size) for i in range(size)])  12.5 us
    all_to_all x1, starting transfers between devices, local(): got = lax.all_to_all(send, AXES, split_axis=0, concat_axis=0, tiled=True)  11.2 us
    all_to_all x1, starting transfers between devices, local(): back = lax.all_to_all(answer, AXES, split_axis=0, concat_axis=0, tiled=True)  7.68 us
    all_to_all x1, waiting for transfers between devices, local(): got = lax.all_to_all(send, AXES, split_axis=0, concat_axis=0, tiled=True)  7.65 us
    all_to_all x1, waiting for transfers between devices, local(): back = lax.all_to_all(answer, AXES, split_axis=0, concat_axis=0, tiled=True)  3.66 us
    unnamed x13, local copies, waits for them, and re-layouts  2.88 us
  transfers between devices with their start and end apart: 12, of which 8 were waited for; matrix products, arithmetic and copies ran while one was open for 4% of the time, Pallas kernels for 7%

profile of v14, /device:TPU:0, one launch (start us, length us, event | category | flops | bytes accessed | tf_op | source)
XLA Modules:
  0.0 103.6 jit_solution(3397899892904528596)
XLA Ops:
  0.0 8.3 %pack.1 = (f32[8,1024]{1,0:T(8,128)}, bf16[4,8,128]{2,1,0:T(8,128)(2,1)}, bf16[4,8,128]{2,1,0:T(8,128)(2,1)}, bf16[4,8,128]{2,1,0:T(8,128)(2,1)}, bf16[4,8,128]{...) custom-call(s32[4,1024]{1,0:T(4,128)} %ids_hbm.1, bf16[1024,512]{1,0:T(8,128)(2,1)} %q_hbm.1, bf16[1024,512]{1,0:T(8,128)(2,1)} %k_hbm.1, ...), custom_call_target="tpu_custom_call" | custom-call | tf_op jit(solution)/shard_map/pack/pallas_call | solution.py:318
  8.3 0.0 copy-start.4
  8.3 11.2 %all-to-all-start = ((bf16[128,13,8,128]{3,2,1,0:T(8,128)(2,1)}), bf16[128,13,8,128]{3,2,1,0:T(8,128)(2,1)S(1)}, u32[]{:S(2)}, u32[]{:S(2)}) async-start(bf16[128,13,8,128]{3,2,1,0:T(8,128)(2,1)} %get-tuple-element.27), calls=%async_computation | async-start | bytes 6815744 | tf_op jit(solution)/shard_map/all_to_all | solution.py:354
  19.5 1.0 collective-permute-start
  20.5 2.7 %collective-permute-start.1 = (bf16[4,8,128]{2,1,0:T(8,128)(2,1)S(1)}, bf16[4,8,128]{2,1,0:T(8,128)(2,1)S(1)}, u32[]{:S(2)}, u32[]{:S(2)}) collective-permute-start(bf16[4,8,128]{2,1,0:T(8,128)(2,1)S(1)} %copy-done.3), channel_id=1, source_target_pairs={{0,2},{1,3},{2,0},{3,1},{4,6},{5,7},{6,4},{7,5},{8,10},{9,11},{10,... | collective-permute-start | bytes 24584 | tf_op jit(solution)/shard_map/ppermute | solution.py:334
  23.2 1.4 %collective-permute-start.2 = (bf16[4,8,128]{2,1,0:T(8,128)(2,1)S(1)}, bf16[4,8,128]{2,1,0:T(8,128)(2,1)S(1)}, u32[]{:S(2)}, u32[]{:S(2)}) collective-permute-start(bf16[4,8,128]{2,1,0:T(8,128)(2,1)S(1)} %copy-done.2), channel_id=1, source_target_pairs={{0,3},{1,0},{2,1},{3,2},{4,7},{5,4},{6,5},{7,6},{8,11},{9,8},{10,9... | collective-permute-start | bytes 24584 | tf_op jit(solution)/shard_map/ppermute | solution.py:334
  24.7 27.7 %collective-permute-done.b1_ref = bf16[4,8,128]{2,1,0:T(8,128)(2,1)S(1)} collective-permute-done((bf16[4,8,128]{2,1,0:T(8,128)(2,1)S(1)}, bf16[4,8,128]{2,1,0:T(8,128)(2,1)S(1)}, u32[]{:S(2)}, u32[]{:S(2)}) %collective-permute-start) | collective-permute-done | bytes 8224 | tf_op jit(solution)/shard_map/ppermute | solution.py:334
  52.4 1.4 %collective-permute-done.1.b2_ref = bf16[4,8,128]{2,1,0:T(8,128)(2,1)S(1)} collective-permute-done((bf16[4,8,128]{2,1,0:T(8,128)(2,1)S(1)}, bf16[4,8,128]{2,1,0:T(8,128)(2,1)S(1)}, u32[]{:S(2)}, u32[]{:S(2)}) %collective-permute-start.1) | collective-permute-done | bytes 8224 | tf_op jit(solution)/shard_map/ppermute | solution.py:334
  53.7 1.2 %collective-permute-done.2.b3_ref = bf16[4,8,128]{2,1,0:T(8,128)(2,1)S(1)} collective-permute-done((bf16[4,8,128]{2,1,0:T(8,128)(2,1)S(1)}, bf16[4,8,128]{2,1,0:T(8,128)(2,1)S(1)}, u32[]{:S(2)}, u32[]{:S(2)}) %collective-permute-start.2) | collective-permute-done | bytes 8224 | tf_op jit(solution)/shard_map/ppermute | solution.py:334
  55.0 7.7 %all-to-all-done.got_ref = bf16[128,13,8,128]{3,2,1,0:T(8,128)(2,1)S(1)} async-done(((bf16[128,13,8,128]{3,2,1,0:T(8,128)(2,1)}), bf16[128,13,8,128]{3,2,1,0:T(8,128)(2,1)S(1)}, u32[]{:S(2)}, u32[]{:S(2)}) %all-to-all-start) | async-done | bytes 3407904 | tf_op jit(solution)/shard_map/all_to_all | solution.py:354
  62.6 1.1 %mid.1 = bf16[97,8,128]{2,1,0:T(8,128)(2,1)} custom-call(bf16[128,13,8,128]{3,2,1,0:T(8,128)(2,1)S(1)} %all-to-all-done.got_ref), custom_call_target="tpu_custom_call" | custom-call | tf_op jit(solution)/shard_map/mid/pallas_call | solution.py:318
  63.7 1.9 %collective-permute-start.5 = (bf16[97,8,128]{2,1,0:T(8,128)(2,1)}, bf16[97,8,128]{2,1,0:T(8,128)(2,1)}, u32[]{:S(2)}, u32[]{:S(2)}) collective-permute-start(bf16[97,8,128]{2,1,0:T(8,128)(2,1)} %mid.1), channel_id=1, source_target_pairs={{0,96},{32,0},{64,32},{96,64},{1,97},{33,1},{65,33},{97,65},{2,98}... | collective-permute-start | bytes 595976 | tf_op jit(solution)/shard_map/ppermute | solution.py:334
  65.6 1.1 %collective-permute-start.4 = (bf16[97,8,128]{2,1,0:T(8,128)(2,1)}, bf16[97,8,128]{2,1,0:T(8,128)(2,1)}, u32[]{:S(2)}, u32[]{:S(2)}) collective-permute-start(bf16[97,8,128]{2,1,0:T(8,128)(2,1)} %mid.1), channel_id=1, source_target_pairs={{0,64},{32,96},{64,0},{96,32},{1,65},{33,97},{65,1},{97,33},{2,66}... | collective-permute-start | bytes 595976 | tf_op jit(solution)/shard_map/ppermute | solution.py:334
  66.7 0.3 collective-permute-start.3
  67.0 5.9 %cold.1 = bf16[128,4,8,128]{3,2,1,0:T(8,128)(2,1)} custom-call(bf16[128,13,8,128]{3,2,1,0:T(8,128)(2,1)S(1)} %all-to-all-done.got_ref), custom_call_target="tpu_custom_call" | custom-call | flops 20000000000 | tf_op jit(solution)/shard_map/cold/pallas_call | solution.py:318
  73.0 7.7 %all-to-all-start.1 = ((bf16[128,4,8,128]{3,2,1,0:T(8,128)(2,1)}), bf16[128,4,8,128]{3,2,1,0:T(8,128)(2,1)S(1)}, u32[]{:S(2)}, u32[]{:S(2)}) async-start(bf16[128,4,8,128]{3,2,1,0:T(8,128)(2,1)} %cold.1), calls=%async_computation.1 | async-start | bytes 2097152 | tf_op jit(solution)/shard_map/all_to_all | solution.py:381
  80.6 0.0 collective-permute-done.4
  80.7 0.0 collective-permute-done.3
  80.7 0.9 constant_dynamic-update-slice_fusion.3
  81.6 1.0 constant_dynamic-update-slice_fusion.2
  82.6 1.0 constant_dynamic-update-slice_fusion.1
  83.5 1.0 constant_dynamic-update-slice_fusion.near_ref
  84.5 0.1 collective-permute-start.6
  84.6 2.3 %collective-permute-done.6.far_ref = bf16[388,8,128]{2,1,0:T(8,128)(2,1)S(1)} collective-permute-done((bf16[388,8,128]{2,1,0:T(8,128)(2,1)S(1)}, bf16[388,8,128]{2,1,0:T(8,128)(2,1)S(1)}, u32[]{:S(2)}, u32[]{:S(2)}) %collective-permute-start.6) | collective-permute-done | bytes 794656 | tf_op jit(solution)/shard_map/ppermute | solution.py:334
  86.9 1.1 %hot.1 = (bf16[3,8,128]{2,1,0:T(8,128)(2,1)S(1)}, bf16[3,8,128]{2,1,0:T(8,128)(2,1)S(1)}, bf16[3,8,128]{2,1,0:T(8,128)(2,1)S(1)}, bf16[3,8,128]{2,1,0:T(8,128)(2,1)S(1)}) custom-call(bf16[4,8,128]{2,1,0:T(8,128)(2,1)S(1)} %copy-done.1, bf16[4,8,128]{2,1,0:T(8,128)(2,1)S(1)} %collective-permute-done.b1_ref, ...), custom_call_target="tpu_custom_call" | custom-call | flops 2000000000 | tf_op jit(solution)/shard_map/hot/pallas_call | solution.py:318
  88.0 2.3 %collective-permute-start.7 = (bf16[3,8,128]{2,1,0:T(8,128)(2,1)S(1)}, bf16[3,8,128]{2,1,0:T(8,128)(2,1)S(1)}, u32[]{:S(2)}, u32[]{:S(2)}) collective-permute-start(bf16[3,8,128]{2,1,0:T(8,128)(2,1)S(1)} %get-tuple-element.44), channel_id=1, source_target_pairs={{0,3},{1,0},{2,1},{3,2},{4,7},{5,4},{6,5},{7,6},{8,11},{9,8},{10,9... | collective-permute-start | bytes 18440 | tf_op jit(solution)/shard_map/ppermute | solution.py:334
  90.3 0.8 collective-permute-start.8
  91.1 0.9 collective-permute-start.9
  91.9 3.9 %collective-permute-done.8.o2_ref = bf16[3,8,128]{2,1,0:T(8,128)(2,1)S(1)} collective-permute-done((bf16[3,8,128]{2,1,0:T(8,128)(2,1)S(1)}, bf16[3,8,128]{2,1,0:T(8,128)(2,1)S(1)}, u32[]{:S(2)}, u32[]{:S(2)}) %collective-permute-start.8) | collective-permute-done | bytes 6176 | tf_op jit(solution)/shard_map/ppermute | solution.py:334
  95.9 0.2 collective-permute-done.9.o3_ref
  96.0 3.7 %all-to-all-done.1.back_ref = bf16[128,4,8,128]{3,2,1,0:T(8,128)(2,1)S(1)} async-done(((bf16[128,4,8,128]{3,2,1,0:T(8,128)(2,1)}), bf16[128,4,8,128]{3,2,1,0:T(8,128)(2,1)S(1)}, u32[]{:S(2)}, u32[]{:S(2)}) %all-to-all-start.1) | async-done | bytes 1048608 | tf_op jit(solution)/shard_map/all_to_all | solution.py:381
  99.7 3.7 %unpack.1 = bf16[1024,512]{1,0:T(8,128)(2,1)} custom-call(f32[8,1024]{1,0:T(8,128)S(1)} %copy-done, bf16[128,4,8,128]{3,2,1,0:T(8,128)(2,1)S(1)} %all-to-all-done.1.back_ref, bf16[3,8,128]{2,1,0:T(8,128)(2,1)S(1)} %get-tuple-element.43.o0_ref, bf16[3,8,128]{2,1,0:T(8,128)(2,1)S(1)} %collective-permute-done.7.o1_ref, ...), custom_call_target="tpu_custom_call" | custom-call | tf_op jit(solution)/shard_map/unpack/pallas_call | solution.py:318
  (11 shorter events, 0.0 us)
Async XLA Ops:
  8.3 11.2 %copy-start.4 = (bf16[4,8,128]{2,1,0:T(8,128)(2,1)S(1)}, bf16[4,8,128]{2,1,0:T(8,128)(2,1)}, u32[]{:S(2)}) copy-start(bf16[4,8,128]{2,1,0:T(8,128)(2,1)} %get-tuple-element.29) | copy-start | bytes 24580
  8.3 12.2 %copy-start.3 = (bf16[4,8,128]{2,1,0:T(8,128)(2,1)S(1)}, bf16[4,8,128]{2,1,0:T(8,128)(2,1)}, u32[]{:S(2)}) copy-start(bf16[4,8,128]{2,1,0:T(8,128)(2,1)} %get-tuple-element.30) | copy-start | bytes 24580
  8.3 14.9 %copy-start.2 = (bf16[4,8,128]{2,1,0:T(8,128)(2,1)S(1)}, bf16[4,8,128]{2,1,0:T(8,128)(2,1)}, u32[]{:S(2)}) copy-start(bf16[4,8,128]{2,1,0:T(8,128)(2,1)} %get-tuple-element.31) | copy-start | bytes 24580
  8.3 54.3 %all-to-all-start = ((bf16[128,13,8,128]{3,2,1,0:T(8,128)(2,1)}), bf16[128,13,8,128]{3,2,1,0:T(8,128)(2,1)S(1)}, u32[]{:S(2)}, u32[]{:S(2)}) async-start(bf16[128,13,8,128]{3,2,1,0:T(8,128)(2,1)} %get-tuple-element.27), calls=%async_computation | async-start | bytes 6815744 | tf_op jit(solution)/shard_map/all_to_all | solution.py:354
  19.5 32.9 %collective-permute-start = (bf16[4,8,128]{2,1,0:T(8,128)(2,1)S(1)}, bf16[4,8,128]{2,1,0:T(8,128)(2,1)S(1)}, u32[]{:S(2)}, u32[]{:S(2)}) collective-permute-start(bf16[4,8,128]{2,1,0:T(8,128)(2,1)S(1)} %copy-done.4), channel_id=1, source_target_pairs={{0,1},{1,2},{2,3},{3,0},{4,5},{5,6},{6,7},{7,4},{8,9},{9,10},{10,1... | collective-permute-start | bytes 24584 | tf_op jit(solution)/shard_map/ppermute | solution.py:334
  20.5 33.2 %collective-permute-start.1 = (bf16[4,8,128]{2,1,0:T(8,128)(2,1)S(1)}, bf16[4,8,128]{2,1,0:T(8,128)(2,1)S(1)}, u32[]{:S(2)}, u32[]{:S(2)}) collective-permute-start(bf16[4,8,128]{2,1,0:T(8,128)(2,1)S(1)} %copy-done.3), channel_id=1, source_target_pairs={{0,2},{1,3},{2,0},{3,1},{4,6},{5,7},{6,4},{7,5},{8,10},{9,11},{10,... | collective-permute-start | bytes 24584 | tf_op jit(solution)/shard_map/ppermute | solution.py:334
  23.2 31.7 %collective-permute-start.2 = (bf16[4,8,128]{2,1,0:T(8,128)(2,1)S(1)}, bf16[4,8,128]{2,1,0:T(8,128)(2,1)S(1)}, u32[]{:S(2)}, u32[]{:S(2)}) collective-permute-start(bf16[4,8,128]{2,1,0:T(8,128)(2,1)S(1)} %copy-done.2), channel_id=1, source_target_pairs={{0,3},{1,0},{2,1},{3,2},{4,7},{5,4},{6,5},{7,6},{8,11},{9,8},{10,9... | collective-permute-start | bytes 24584 | tf_op jit(solution)/shard_map/ppermute | solution.py:334
  63.7 16.9 %collective-permute-start.5 = (bf16[97,8,128]{2,1,0:T(8,128)(2,1)}, bf16[97,8,128]{2,1,0:T(8,128)(2,1)}, u32[]{:S(2)}, u32[]{:S(2)}) collective-permute-start(bf16[97,8,128]{2,1,0:T(8,128)(2,1)} %mid.1), channel_id=1, source_target_pairs={{0,96},{32,0},{64,32},{96,64},{1,97},{33,1},{65,33},{97,65},{2,98}... | collective-permute-start | bytes 595976 | tf_op jit(solution)/shard_map/ppermute | solution.py:334
  65.6 15.1 %collective-permute-start.4 = (bf16[97,8,128]{2,1,0:T(8,128)(2,1)}, bf16[97,8,128]{2,1,0:T(8,128)(2,1)}, u32[]{:S(2)}, u32[]{:S(2)}) collective-permute-start(bf16[97,8,128]{2,1,0:T(8,128)(2,1)} %mid.1), channel_id=1, source_target_pairs={{0,64},{32,96},{64,0},{96,32},{1,65},{33,97},{65,1},{97,33},{2,66}... | collective-permute-start | bytes 595976 | tf_op jit(solution)/shard_map/ppermute | solution.py:334
  66.7 14.0 %collective-permute-start.3 = (bf16[97,8,128]{2,1,0:T(8,128)(2,1)}, bf16[97,8,128]{2,1,0:T(8,128)(2,1)}, u32[]{:S(2)}, u32[]{:S(2)}) collective-permute-start(bf16[97,8,128]{2,1,0:T(8,128)(2,1)} %mid.1), channel_id=1, source_target_pairs={{0,32},{32,64},{64,96},{96,0},{1,33},{33,65},{65,97},{97,1},{2,34}... | collective-permute-start | bytes 595976 | tf_op jit(solution)/shard_map/ppermute | solution.py:334
  72.9 13.9 %copy-start.1 = (bf16[4,8,128]{2,1,0:T(8,128)(2,1)S(1)}, bf16[4,8,128]{2,1,0:T(8,128)(2,1)}, u32[]{:S(2)}) copy-start(bf16[4,8,128]{2,1,0:T(8,128)(2,1)} %get-tuple-element.34.b0_ref) | copy-start | bytes 24580
  73.0 26.7 %all-to-all-start.1 = ((bf16[128,4,8,128]{3,2,1,0:T(8,128)(2,1)}), bf16[128,4,8,128]{3,2,1,0:T(8,128)(2,1)S(1)}, u32[]{:S(2)}, u32[]{:S(2)}) async-start(bf16[128,4,8,128]{3,2,1,0:T(8,128)(2,1)} %cold.1), calls=%async_computation.1 | async-start | bytes 2097152 | tf_op jit(solution)/shard_map/all_to_all | solution.py:381
  84.5 15.2 %copy-start = (f32[8,1024]{1,0:T(8,128)S(1)}, f32[8,1024]{1,0:T(8,128)}, u32[]{:S(2)}) copy-start(f32[8,1024]{1,0:T(8,128)} %get-tuple-element.26.table_ref) | copy-start | bytes 98308
  84.5 2.4 %collective-permute-start.6 = (bf16[388,8,128]{2,1,0:T(8,128)(2,1)S(1)}, bf16[388,8,128]{2,1,0:T(8,128)(2,1)S(1)}, u32[]{:S(2)}, u32[]{:S(2)}) collective-permute-start(bf16[388,8,128]{2,1,0:T(8,128)(2,1)S(1)} %constant_dynamic-update-slice_fusion.near_ref), channel_id=1, source_target_pairs={{0,16},{16,0},{1,17},{17,1},{2,18},{18,2},{3,19},{19,3},{4,20},{20... | collective-permute-start | bytes 2383880 | tf_op jit(solution)/shard_map/ppermute | solution.py:334
  88.0 4.0 %collective-permute-start.7 = (bf16[3,8,128]{2,1,0:T(8,128)(2,1)S(1)}, bf16[3,8,128]{2,1,0:T(8,128)(2,1)S(1)}, u32[]{:S(2)}, u32[]{:S(2)}) collective-permute-start(bf16[3,8,128]{2,1,0:T(8,128)(2,1)S(1)} %get-tuple-element.44), channel_id=1, source_target_pairs={{0,3},{1,0},{2,1},{3,2},{4,7},{5,4},{6,5},{7,6},{8,11},{9,8},{10,9... | collective-permute-start | bytes 18440 | tf_op jit(solution)/shard_map/ppermute | solution.py:334
  90.3 5.6 %collective-permute-start.8 = (bf16[3,8,128]{2,1,0:T(8,128)(2,1)S(1)}, bf16[3,8,128]{2,1,0:T(8,128)(2,1)S(1)}, u32[]{:S(2)}, u32[]{:S(2)}) collective-permute-start(bf16[3,8,128]{2,1,0:T(8,128)(2,1)S(1)} %get-tuple-element.45), channel_id=1, source_target_pairs={{0,2},{1,3},{2,0},{3,1},{4,6},{5,7},{6,4},{7,5},{8,10},{9,11},{10,... | collective-permute-start | bytes 18440 | tf_op jit(solution)/shard_map/ppermute | solution.py:334
  91.1 5.0 %collective-permute-start.9 = (bf16[3,8,128]{2,1,0:T(8,128)(2,1)S(1)}, bf16[3,8,128]{2,1,0:T(8,128)(2,1)S(1)}, u32[]{:S(2)}, u32[]{:S(2)}) collective-permute-start(bf16[3,8,128]{2,1,0:T(8,128)(2,1)S(1)} %get-tuple-element.46), channel_id=1, source_target_pairs={{0,1},{1,2},{2,3},{3,0},{4,5},{5,6},{6,7},{7,4},{8,9},{9,10},{10,1... | collective-permute-start | bytes 18440 | tf_op jit(solution)/shard_map/ppermute | solution.py:334
